TPU v7x, 128 devices: a whole 4x4x4 slice. The times are simulated.
128 devices in a mesh: gx: 4 (over x), gy: 4 (over z), gz: 8 (over y, core).
Axes of the slice: x: 4, y: 4, z: 4, core: 2. Of those that a mesh axis runs over, the one named last changes fastest.
Arguments:
- fields: float32 [24, 32, 128, 1024], P(None, 'gx', 'gy', 'gz'), may hold values from -8.5 to 8.5
- velocity: float32 [3, 32, 128, 1024], P(None, 'gx', 'gy', 'gz'), may hold values from -0.4 to 0.4
- diffusivity: float32 [24], replicated, may hold values from 0.02 to 0.15
- weight_in: bfloat16 [24, 1600], replicated, may hold values from -1.25 to 1.25
- bias_in: float32 [1600], replicated, may hold values from -3 to 3
- weight_mid: bfloat16 [1600, 800], replicated, may hold values from -0.15625 to 0.15625
- bias_mid: float32 [800], replicated, may hold values from -3 to 3
- weight_low: bfloat16 [800, 400], replicated, may hold values from -0.21875 to 0.21875
- bias_low: float32 [400], replicated, may hold values from -3 to 3
- weight_out: bfloat16 [400, 24], replicated, may hold values from -0.3125 to 0.3125
- bias_out: float32 [24], replicated, may hold values from -3 to 3
- react_list: int32 [128, 96], P(('gx', 'gy', 'gz')), may hold values from -1 to 255, as said below
- owner_table: int32 [128, 96], P(('gx', 'gy', 'gz')), may hold values from -1 to 127, as said below
Outputs:
- updated: float32 [24, 32, 128, 1024], P(None, 'gx', 'gy', 'gz')
- owner_activity: float32 [128], P(('gx', 'gy', 'gz'))
Inputs may be any that keep to these rules, and one draw needn't show every extreme that they name: `react_list`: row d lists distinct blocks of brick d, valid entries first and -1 after them; a brick lists at most 96 blocks and some brick lists exactly 96; all bricks together list 32 times the number of devices. owner_table[d, i] is -1 exactly where react_list[d, i] is, else the owner's index over gx+gy+gz; every device owns exactly 32 blocks; no brick sends more than 1 block to one owner, and some brick sends exactly 1 to some owner.
All inputs are finite; a program needn't handle non-finite values.
Results may differ from a plain program's by a relative error of at most 0.00058.
Values may be sent and summed in bfloat16 or wider, within the bound.
No kernel may reach another device: no remote copies, remote signals or barrier semaphores. Data moves between devices by JAX's collectives and lax.ppermute only.
A program may use at most 256 MiB of HBM per device.

v0:
```python
import math

import jax
import jax.numpy as jnp
from jax import lax
from jax.sharding import PartitionSpec as P

OWNED = 32


viscous = 0.05
third_part = 1.0 / 3.0


def extended(value, sides, width):
    edges = {}
    for axis, dim in sides:
        devices, length = (lax.axis_size(axis), value.shape[dim])
        up = [(i, (i + 1) % devices) for i in range(devices)]
        last = lax.slice_in_dim(value, length - width, length, axis=dim)
        leading = lax.slice_in_dim(value, 0, width, axis=dim)
        edges[dim] = (
            lax.ppermute(last, axis, up),
            lax.ppermute(leading, axis, [(b, a) for a, b in up]),
        )
    done = []
    for _, dim in sides:
        low, high = edges[dim]
        around = [(width, width) if d in done else (0, 0) for d in range(value.ndim)]
        value = jnp.concatenate([jnp.pad(low, around), value, jnp.pad(high, around)], axis=dim)
        done.append(dim)
    return value


def split_up(value, dim, devices):
    dims = value.shape
    tiles = value.reshape(*dims[:dim], devices, dims[dim] // devices, *dims[dim + 1 :])
    return jnp.moveaxis(tiles, dim, 0)


def joined_along(tiles, dim):
    dims = list(tiles.shape[1:])
    dims[dim] *= tiles.shape[0]
    return jnp.moveaxis(tiles, 0, dim).reshape(dims)


def one_exchange(value, axis, axes, splits, concats):
    sizes = [lax.axis_size(a) for a in axes]
    tiles = split_up(value, splits[0], sizes[0])
    tiles = jnp.moveaxis(split_up(tiles, splits[1] + 1, sizes[1]), 0, 1)
    inside = tiles.shape[2:]
    tiles = tiles.reshape(-1, *inside)
    tiles = lax.all_to_all(tiles, axis, split_axis=0, concat_axis=0, tiled=True)
    tiles = joined_along(tiles.reshape(*sizes, *inside), concats[0] + 1)
    return joined_along(tiles, concats[1])


def pad_cells(array):
    return extended(array, (("gx", 1), ("gy", 2), ("gz", 3)), 1)


def interior(padded, axis_dim, offset):
    window = [slice(None)] + [slice(1, -1)] * 3
    window[axis_dim] = slice(1 + offset, padded.shape[axis_dim] - 1 + offset)
    return padded[tuple(window)]


def laplace(padded):
    summed = -6.0 * interior(padded, 1, 0)
    for axis_dim in (1, 2, 3):
        summed = summed + interior(padded, axis_dim, 1) + interior(padded, axis_dim, -1)
    return summed


def transport(padded, speeds):
    centre = interior(padded, 1, 0)
    spread = -6.0 * centre
    flux_sum = jnp.zeros_like(centre)
    for axis_dim in (1, 2, 3):
        carried = speeds[axis_dim - 1][None] * padded
        flux_sum = flux_sum + 0.5 * (
            interior(carried, axis_dim, 1) - interior(carried, axis_dim, -1)
        )
        spread = spread + interior(padded, axis_dim, 1) + interior(padded, axis_dim, -1)
    return viscous * spread - flux_sum


def network(
    block_in, weight_in, bias_in, weight_mid, bias_mid, weight_low, bias_low, weight_out, bias_out
):
    hidden = jnp.einsum("bfz,fh->bhz", block_in, weight_in, preferred_element_type=jnp.float32)
    hidden = jax.nn.silu(hidden + bias_in[None, :, None]).astype(jnp.bfloat16)
    hidden = jnp.einsum("bhz,hk->bkz", hidden, weight_mid, preferred_element_type=jnp.float32)
    hidden = jax.nn.silu(hidden + bias_mid[None, :, None]).astype(jnp.bfloat16)
    hidden = jnp.einsum("bkz,kl->blz", hidden, weight_low, preferred_element_type=jnp.float32)
    hidden = jax.nn.silu(hidden + bias_low[None, :, None]).astype(jnp.bfloat16)
    result = jnp.einsum("blz,lf->bfz", hidden, weight_out, preferred_element_type=jnp.float32)
    return result + bias_out[None, :, None]


def local(
    fields,
    velocity,
    diffusivity,
    weight_in,
    bias_in,
    weight_mid,
    bias_mid,
    weight_low,
    bias_low,
    weight_out,
    bias_out,
    react_list,
    owner_table,
):
    field_count, cells_x, cells_y, cells_z = fields.shape
    padded = pad_cells(jnp.concatenate([fields, velocity], axis=0))
    speeds = padded[field_count:]
    section_one = fields + transport(padded[:field_count], speeds)
    section_two = 0.75 * fields + 0.25 * (section_one + transport(pad_cells(section_one), speeds))
    flowed = third_part * fields + 2.0 / 3.0 * (
        section_two + transport(pad_cells(section_two), speeds)
    )
    devices = lax.axis_size(("gx", "gy", "gz"))
    block_ids = react_list[0]
    owners = owner_table[0]
    listed = block_ids.shape[0]
    capacity = (listed + devices - 1) // devices
    slots_all = devices * capacity
    block_count = cells_x * cells_y
    present = block_ids >= 0
    positions = jnp.arange(listed, dtype=jnp.int32)
    earlier = (
        (owners[None, :] == owners[:, None])
        & present[None, :]
        & (positions[None, :] < positions[:, None])
    )
    earlier_count = jnp.sum(earlier.astype(jnp.int32), axis=1)
    target_slot = jnp.where(present, owners * capacity + earlier_count, -1)
    slot_hot = (target_slot[None, :] == jnp.arange(slots_all, dtype=jnp.int32)[:, None]).astype(
        jnp.float32
    )
    block_hot = (block_ids[:, None] == jnp.arange(block_count, dtype=jnp.int32)[None, :]).astype(
        jnp.float32
    )
    routing_table = jnp.dot(slot_hot, block_hot, precision=lax.Precision.HIGHEST)
    slot_mask = (jnp.sum(slot_hot, axis=1) > 0.5).astype(jnp.int32)
    brick_blocks = flowed.reshape(field_count, block_count, cells_z).astype(jnp.bfloat16)
    outgoing = jnp.einsum(
        "sb,fbz->sfz",
        routing_table.astype(jnp.bfloat16),
        brick_blocks,
        preferred_element_type=jnp.float32,
    ).astype(jnp.bfloat16)
    outgoing = outgoing.reshape(devices, capacity, field_count, cells_z)
    slot_mask = slot_mask.reshape(devices, capacity)
    plane_count = lax.axis_size("gx") * lax.axis_size("gy")
    depth_count = lax.axis_size("gz")
    arrived, arrived_mask = (
        one_exchange(
            outgoing.reshape(plane_count, depth_count, capacity, field_count, cells_z),
            ("gx", "gy", "gz"),
            (("gx", "gy"), "gz"),
            (0, 1),
            (0, 1),
        ),
        one_exchange(
            slot_mask.reshape(plane_count, depth_count, capacity),
            ("gx", "gy", "gz"),
            (("gx", "gy"), "gz"),
            (0, 1),
            (0, 1),
        ),
    )
    arrived = arrived.reshape(slots_all, field_count, cells_z)
    occupied = arrived_mask.reshape(slots_all)
    position = jnp.cumsum(occupied) - 1
    selector = (
        (position[None, :] == jnp.arange(OWNED, dtype=jnp.int32)[:, None])
        & (occupied[None, :] == 1)
    ).astype(jnp.float32)
    compact = jnp.einsum(
        "rs,sfz->rfz", selector.astype(jnp.bfloat16), arrived, preferred_element_type=jnp.float32
    ).astype(jnp.bfloat16)
    group_size = math.gcd(OWNED, 8)

    def run_group(blockset):
        return network(
            blockset,
            weight_in,
            bias_in,
            weight_mid,
            bias_mid,
            weight_low,
            bias_low,
            weight_out,
            bias_out,
        )

    chemistry = lax.map(
        run_group, compact.reshape(OWNED // group_size, group_size, field_count, cells_z)
    )
    chemistry = chemistry.reshape(OWNED, field_count, cells_z)
    owner_activity = (jnp.sum(jnp.mean(chemistry[:, 0, :] ** 2, axis=-1)) / 8.0).reshape(1)
    returning = jnp.einsum("rs,rfz->sfz", selector, chemistry, precision=lax.Precision.HIGHEST)
    returning = returning.reshape(devices, capacity, field_count, cells_z)
    plane_count = lax.axis_size("gx") * lax.axis_size("gy")
    depth_count = lax.axis_size("gz")
    came_back = one_exchange(
        returning.reshape(plane_count, depth_count, capacity, field_count, cells_z),
        ("gx", "gy", "gz"),
        (("gx", "gy"), "gz"),
        (0, 1),
        (0, 1),
    )
    came_back = came_back.reshape(slots_all, field_count, cells_z)
    added = jnp.einsum("sb,sfz->fbz", routing_table, came_back, precision=lax.Precision.HIGHEST)
    added = added.reshape(field_count, cells_x, cells_y, cells_z)
    reacted = flowed + added
    rates = diffusivity[:, None, None, None]
    updated = reacted + rates * laplace(pad_cells(reacted))
    return (updated, owner_activity)


def solution(mesh):
    return jax.shard_map(
        local,
        mesh=mesh,
        in_specs=(
            P(None, "gx", "gy", "gz"),
            P(None, "gx", "gy", "gz"),
            P(),
            P(),
            P(),
            P(),
            P(),
            P(),
            P(),
            P(),
            P(),
            P(("gx", "gy", "gz"), None),
            P(("gx", "gy", "gz"), None),
        ),
        out_specs=(P(None, "gx", "gy", "gz"), P(("gx", "gy", "gz"))),
        check_vma=False,
    )
```

profile of v0, /device:TPU:1, one launch (start us, length us, event | category | flops | bytes accessed | tf_op | source)
XLA Modules:
  0.0 422.9 jit_solution(1608193543118292917)
XLA Ops:
  0.6 2.4 constant_dynamic-update-slice_fusion.1
  3.1 4.2 fusion.107
  7.2 3.6 copy.60
  12.2 3.6 copy.62
  18.1 2.5 collective-permute-start
  21.4 3.8 collective-permute-start.2
  25.9 3.5 copy.61
  29.4 5.0 %pad.54 = f32[27,10,34,1]{3,2,1,0:T(8,128)} pad(f32[27,8,32,1]{3,2,1,0:T(8,128)} %copy.61, f32[]{:T(128)} %constant.24.clone.1), padding=0_0x1_1x1_1x0_0 | pad | bytes 64372 | tf_op jit(solution)/shard_map/jit(_pad)/pad | solution.py:30
  34.4 3.5 copy.63
  37.9 2.6 pad.55
  41.9 2.9 pad.53
  47.6 10.2 %pad_maximum_fusion = f32[27,10,34,130]{3,2,1,0:T(8,128)S(1)} fusion(f32[27,10,34,1]{3,2,1,0:T(8,128)S(1)} %bitcast.169, f32[27,10,1,128]{3,2,1,0:T(1,128)S(1)} %pad.52, f32[27,1,32,128]{3,2,1,0:T(8,128)} %collective-permute-done, f32[27,8,32,128]{3,2,1,0:T(8,128)S(1)} %constant_dynamic-update-slice_fusion, f32[27,1,32,128]{3,2,1,0:T(8,128)} %collective-permute-done.1, ...), kind=kLoop, calls=%fused_computation.30 | loop fusion | flops 7160400 | bytes 9547200 | tf_op jit(solution)/shard_map/concatenate | solution.py:30
  57.9 9.9 %slice_multiply_fusion.2 = (f32[24,10,34,130]{3,2,1,0:T(8,128)}, f32[24,10,34,130]{3,2,1,0:T(8,128)}, f32[24,10,34,130]{3,2,1,0:T(8,128)}) fusion(f32[27,10,34,130]{3,2,1,0:T(8,128)S(1)} %pad_maximum_fusion, f32[10,34,130]{2,1,0:T(8,128)S(1)} %get-tuple-element.128, f32[10,34,130]{2,1,0:T(8,128)S(1)} %get-tuple-element.129, ...), kind=kLoop, calls=%fused_computation.35 | loop fusion | flops 3182400 | bytes 17503200 | tf_op jit(solution)/shard_map/mul | solution.py:80
  67.8 23.1 %fusion.71 = f32[24,8,32,128]{3,2,1,0:T(8,128)} fusion(f32[24,8,32,128]{3,2,1,0:T(8,128)} %param.15, f32[24,10,34,130]{3,2,1,0:T(8,128)} %get-tuple-element.136, f32[24,10,34,130]{3,2,1,0:T(8,128)} %get-tuple-element.135, f32[24,10,34,130]{3,2,1,0:T(8,128)} %get-tuple-element.134, f32[27,10,34,1]{3,2,1,0:T(8,128)} %copy-done, ...), kind=kLoop, calls=%fused_computation.146 | loop fusion | flops 26738688 | bytes 29939424 | tf_op jit(solution)/shard_map/add | solution.py:119
  90.9 6.6 %fusion.116 = (f32[24,8,32,1]{3,2,1,0:T(8,128)}, f32[24,8,32,1]{3,2,1,0:T(8,128)}) fusion(f32[24,8,32,128]{3,2,1,0:T(8,128)} %fusion.71), kind=kLoop, calls=%fused_computation.232 | loop fusion | bytes 98304 | tf_op jit(solution)/shard_map/slice | solution.py:20
  98.5 2.7 copy.64
  101.2 1.8 collective-permute-start.10
  103.0 3.0 collective-permute-start.6
  106.8 2.7 copy.66
  109.5 2.8 collective-permute-start.8
  113.1 11.4 %all-to-all-start = ((s32[128,1,1,1]{3,2,1,0:T(1,128)}), s32[128,1,1,1]{3,2,1,0:T(1,128)}, u32[]{:S(2)}, u32[]{:S(2)}) async-start(s32[128,1,1,1]{3,2,1,0:T(1,128)} %copy.72), calls=%async_computation | async-start | bytes 131072 | tf_op jit(solution)/shard_map/all_to_all | solution.py:53
  124.4 2.5 copy.65
  126.9 4.6 %pad.58 = f32[24,10,34,1]{3,2,1,0:T(8,128)} pad(f32[24,8,32,1]{3,2,1,0:T(8,128)} %copy.65, f32[]{:T(128)} %constant.24.clone.1), padding=0_0x1_1x1_1x0_0 | pad | bytes 57220 | tf_op jit(solution)/shard_map/jit(_pad)/pad | solution.py:30
  131.5 2.4 copy.67
  134.0 2.6 pad.59
  137.9 13.0 %broadcast_multiply_fusion.5 = (f32[24,10,34,130]{3,2,1,0:T(8,128)}, f32[24,10,34,130]{3,2,1,0:T(8,128)}) fusion(f32[10,34,130]{2,1,0:T(8,128)S(1)} %copy-done.8, f32[24,10,34,1]{3,2,1,0:T(8,128)} %pad.58, f32[24,10,1,128]{3,2,1,0:T(1,128)S(1)} %pad.56, f32[24,1,32,128]{3,2,1,0:T(8,128)} %collective-permute-done.6, f32[24,8,32,128]{3,2,1,0:T(8,128)S(1)} %copy-done.1, ...), kind=kLoop, calls=%fused_computation.41 | loop fusion | flops 8486400 | bytes 13083200 | tf_op jit(solution)/shard_map/mul | solution.py:80
  150.9 10.9 %broadcast_multiply_fusion.1 = f32[24,10,34,130]{3,2,1,0:T(8,128)} fusion(f32[10,34,130]{2,1,0:T(8,128)S(1)} %copy-done.6, f32[24,10,34,1]{3,2,1,0:T(8,128)S(1)} %bitcast.171, f32[24,10,1,128]{3,2,1,0:T(1,128)S(1)} %pad.56, f32[24,1,32,128]{3,2,1,0:T(8,128)} %collective-permute-done.6, f32[24,8,32,128]{3,2,1,0:T(8,128)S(1)} %copy-done.1, ...), kind=kLoop, calls=%fused_computation.37 | loop fusion | flops 7425600 | bytes 8663200 | tf_op jit(solution)/shard_map/mul | solution.py:80
  161.8 21.6 %fusion.59 = f32[24,8,32,128]{3,2,1,0:T(8,128)} fusion(f32[24,8,32,128]{3,2,1,0:T(8,128)S(1)} %copy-done.1, f32[24,10,34,130]{3,2,1,0:T(8,128)} %broadcast_multiply_fusion.1, f32[24,10,34,130]{3,2,1,0:T(8,128)} %get-tuple-element.133, f32[24,10,34,130]{3,2,1,0:T(8,128)} %get-tuple-element.132, f32[24,10,34,1]{3,2,1,0:T(8,128)} %copy-done.3, ...), kind=kLoop, calls=%fused_computation.113 | loop fusion | flops 29097984 | bytes 29409024 | tf_op jit(solution)/shard_map/add | solution.py:120
  183.4 6.6 %fusion.113 = (f32[24,8,32,1]{3,2,1,0:T(8,128)}, f32[24,8,32,1]{3,2,1,0:T(8,128)}) fusion(f32[24,8,32,128]{3,2,1,0:T(8,128)} %fusion.59), kind=kLoop, calls=%fused_computation.229 | loop fusion | bytes 98304 | tf_op jit(solution)/shard_map/slice | solution.py:20
  190.9 3.3 copy.68
  198.0 3.3 copy.70
  202.9 3.1 collective-permute-start.14
  207.7 3.2 copy.69
  210.9 4.6 %pad.62 = f32[24,10,34,1]{3,2,1,0:T(8,128)} pad(f32[24,8,32,1]{3,2,1,0:T(8,128)} %copy.69, f32[]{:T(128)} %constant.24.clone.1), padding=0_0x1_1x1_1x0_0 | pad | bytes 57220 | tf_op jit(solution)/shard_map/jit(_pad)/pad | solution.py:30
  215.5 3.2 copy.71
  218.7 2.6 pad.63
  223.6 12.5 %broadcast_multiply_fusion.4 = (f32[24,10,34,130]{3,2,1,0:T(8,128)}, f32[24,10,34,130]{3,2,1,0:T(8,128)}) fusion(f32[10,34,130]{2,1,0:T(8,128)S(1)} %copy-done.9, f32[24,10,34,1]{3,2,1,0:T(8,128)} %pad.62, f32[24,10,1,128]{3,2,1,0:T(1,128)S(1)} %pad.60, f32[24,1,32,128]{3,2,1,0:T(8,128)} %collective-permute-done.12, f32[24,8,32,128]{3,2,1,0:T(8,128)S(1)} %copy-done.2, ...), kind=kLoop, calls=%fused_computation.40 | loop fusion | flops 8486400 | bytes 13083200 | tf_op jit(solution)/shard_map/mul | solution.py:80
  236.2 10.8 %broadcast_multiply_fusion = f32[24,10,34,130]{3,2,1,0:T(8,128)} fusion(f32[10,34,130]{2,1,0:T(8,128)S(1)} %copy-done.6, f32[24,10,34,1]{3,2,1,0:T(8,128)S(1)} %bitcast.173, f32[24,10,1,128]{3,2,1,0:T(1,128)S(1)} %pad.60, f32[24,1,32,128]{3,2,1,0:T(8,128)} %collective-permute-done.12, f32[24,8,32,128]{3,2,1,0:T(8,128)S(1)} %copy-done.2, ...), kind=kLoop, calls=%fused_computation.36 | loop fusion | flops 7425600 | bytes 8663200 | tf_op jit(solution)/shard_map/mul | solution.py:80
  247.0 22.0 %fusion.105 = (bf16[24,8,32,128]{3,2,1,0:T(8,128)(2,1)}, f32[24,8,32,128]{3,2,1,0:T(8,128)}) fusion(f32[24,8,32,128]{3,2,1,0:T(8,128)S(1)} %copy-done.2, f32[24,10,34,130]{3,2,1,0:T(8,128)} %broadcast_multiply_fusion, f32[24,10,34,130]{3,2,1,0:T(8,128)} %get-tuple-element.131, f32[24,10,34,130]{3,2,1,0:T(8,128)} %get-tuple-element.130, ...), kind=kLoop, calls=%fused_computation.222 | loop fusion | flops 29884416 | bytes 30981888 | tf_op jit(solution)/shard_map/convert_element_type | solution.py:148
  269.1 1.8 fusion.81
  272.4 10.1 %all-to-all-start.1 = ((bf16[128,1,1,1,24,128]{5,4,3,2,1,0:T(8,128)(2,1)}), bf16[128,1,1,1,24,128]{5,4,3,2,1,0:T(8,128)(2,1)S(1)}, u32[]{:S(2)}, u32[]{:S(2)}) async-start(bf16[128,1,1,1,24,128]{5,4,3,2,1,0:T(8,128)(2,1)} %copy.77), calls=%async_computation.1 | async-start | bytes 1572864 | tf_op jit(solution)/shard_map/all_to_all | solution.py:53
  282.6 3.2 reduce.1
  286.6 12.3 %all-to-all-done.1 = bf16[128,1,1,1,24,128]{5,4,3,2,1,0:T(8,128)(2,1)S(1)} async-done(((bf16[128,1,1,1,24,128]{5,4,3,2,1,0:T(8,128)(2,1)}), bf16[128,1,1,1,24,128]{5,4,3,2,1,0:T(8,128)(2,1)S(1)}, u32[]{:S(2)}, u32[]{:S(2)}) %all-to-all-start.1) | async-done | bytes 786464 | tf_op jit(solution)/shard_map/all_to_all | solution.py:53
  299.2 43.7 %while.10 = (s32[]{:T(128)}, f32[4,8,24,128]{3,2,1,0:T(8,128)S(1)}, bf16[4,8,24,128]{3,1,0,2:T(8,128)(2,1)S(1)}, bf16[24,1600]{1,0:T(8,128)(2,1)S(1)}, f32[1600]...) while((s32[]{:T(128)}, f32[4,8,24,128]{3,2,1,0:T(8,128)S(1)}, ...), condition=%wide.region_4.5_spmd, body=%wide.region_3.4_spmd.sunk | while | flops 3392331776 | bytes 11750973 | solution.py:200
  299.3 3.7 fusion.139
  303.0 7.0 %fusion.140 = bf16[8,400,128]{2,1,0:T(8,128)(2,1)S(1)} fusion(f32[800]{0:T(1024)S(1)} %get-tuple-element.258, bf16[8,1600,128]{2,1,0:T(8,128)(2,1)} %fusion.139, bf16[1600,800]{0,1:T(8,128)(2,1)} %get-tuple-element.257, f32[400]{0:T(512)S(1)} %get-tuple-element.260, bf16[800,400]{0,1:T(8,128)(2,1)S(1)} %get-tuple-element.259), kind=kOutput, calls=%fused_computation.19.clone.1 | convolution fusion | flops 3284172800 | bytes 7300800 | tf_op jit(solution)/shard_map/while/body/eval_jaxpr/bkz,kl->blz/dot_general | solution.py:95
  310.2 3.7 fusion.139
  313.9 7.0 %fusion.140 = bf16[8,400,128]{2,1,0:T(8,128)(2,1)S(1)} fusion(f32[800]{0:T(1024)S(1)} %get-tuple-element.258, bf16[8,1600,128]{2,1,0:T(8,128)(2,1)} %fusion.139, bf16[1600,800]{0,1:T(8,128)(2,1)} %get-tuple-element.257, f32[400]{0:T(512)S(1)} %get-tuple-element.260, bf16[800,400]{0,1:T(8,128)(2,1)S(1)} %get-tuple-element.259), kind=kOutput, calls=%fused_computation.19.clone.1 | convolution fusion | flops 3284172800 | bytes 7300800 | tf_op jit(solution)/shard_map/while/body/eval_jaxpr/bkz,kl->blz/dot_general | solution.py:95
  321.1 3.7 fusion.139
  324.8 7.0 %fusion.140 = bf16[8,400,128]{2,1,0:T(8,128)(2,1)S(1)} fusion(f32[800]{0:T(1024)S(1)} %get-tuple-element.258, bf16[8,1600,128]{2,1,0:T(8,128)(2,1)} %fusion.139, bf16[1600,800]{0,1:T(8,128)(2,1)} %get-tuple-element.257, f32[400]{0:T(512)S(1)} %get-tuple-element.260, bf16[800,400]{0,1:T(8,128)(2,1)S(1)} %get-tuple-element.259), kind=kOutput, calls=%fused_computation.19.clone.1 | convolution fusion | flops 3284172800 | bytes 7300800 | tf_op jit(solution)/shard_map/while/body/eval_jaxpr/bkz,kl->blz/dot_general | solution.py:95
  332.1 3.7 fusion.139
  335.8 7.0 %fusion.140 = bf16[8,400,128]{2,1,0:T(8,128)(2,1)S(1)} fusion(f32[800]{0:T(1024)S(1)} %get-tuple-element.258, bf16[8,1600,128]{2,1,0:T(8,128)(2,1)} %fusion.139, bf16[1600,800]{0,1:T(8,128)(2,1)} %get-tuple-element.257, f32[400]{0:T(512)S(1)} %get-tuple-element.260, bf16[800,400]{0,1:T(8,128)(2,1)S(1)} %get-tuple-element.259), kind=kOutput, calls=%fused_computation.19.clone.1 | convolution fusion | flops 3284172800 | bytes 7300800 | tf_op jit(solution)/shard_map/while/body/eval_jaxpr/bkz,kl->blz/dot_general | solution.py:95
  343.8 2.1 copy.81
  345.9 5.0 %all-to-all-start.2 = ((f32[128,1,1,1,24,128]{5,4,3,2,1,0:T(8,128)}), f32[128,1,1,1,24,128]{5,4,3,2,1,0:T(8,128)S(1)}, u32[]{:S(2)}, u32[]{:S(2)}) async-start(f32[128,1,1,1,24,128]{5,4,3,2,1,0:T(8,128)} %copy.81), calls=%async_computation.2 | async-start | bytes 3145728 | tf_op jit(solution)/shard_map/all_to_all | solution.py:53
  351.3 24.3 %all-to-all-done.2 = f32[128,1,1,1,24,128]{5,4,3,2,1,0:T(8,128)S(1)} async-done(((f32[128,1,1,1,24,128]{5,4,3,2,1,0:T(8,128)}), f32[128,1,1,1,24,128]{5,4,3,2,1,0:T(8,128)S(1)}, u32[]{:S(2)}, u32[]{:S(2)}) %all-to-all-start.2) | async-done | bytes 1572896 | tf_op jit(solution)/shard_map/all_to_all | solution.py:53
  376.7 4.1 convolution_bitcast_fusion
  380.8 2.3 copy.83
  383.1 3.7 add.248
  389.0 3.9 fusion.110
  392.9 3.3 copy.84
  398.8 3.3 copy.86
  404.8 3.2 copy.85
  408.0 3.3 copy.87
  413.3 8.1 %fusion.33 = f32[24,8,32,128]{3,2,1,0:T(8,128)} fusion(f32[24,8,32,128]{3,2,1,0:T(8,128)S(1)} %add.248, f32[24,8,32,1]{3,2,1,0:T(8,128)} %copy.87, f32[24,10,1,128]{3,2,1,0:T(1,128)S(1)} %pad.64, f32[24,10,1,128]{3,2,1,0:T(1,128)S(1)} %pad.65, f32[24,1,32,128]{3,2,1,0:T(8,128)} %collective-permute-done.18, f32[24,1,32,128]{3,2,1,0:T(8,128)} %collective-permute-done.19, ...), kind=kLoop, calls=%fused_computation.46 | loop fusion | flops 25952256 | bytes 7372896 | tf_op jit(solution)/shard_map/add | solution.py:221
  (172 shorter events, 38.0 us)
Async XLA Ops:
  0.6 2.4 copy-start.22
  10.8 14.3 %copy-start.25 = (s32[1,96]{1,0:T(1,128)S(1)}, s32[1,96]{1,0:T(1,128)}, u32[]{:S(2)}) copy-start(s32[1,96]{1,0:T(1,128)} %param.26) | copy-start | bytes 1156
  10.8 14.4 %copy-start.24 = (s32[1,96]{1,0:T(1,128)S(1)}, s32[1,96]{1,0:T(1,128)}, u32[]{:S(2)}) copy-start(s32[1,96]{1,0:T(1,128)} %param.27) | copy-start | bytes 1156
  10.8 14.6 %collective-permute-start.4 = (f32[27,8,32,1]{2,1,3,0:T(8,128)}, f32[27,8,32,1]{2,1,3,0:T(8,128)}, u32[]{:S(2)}, u32[]{:S(2)}) collective-permute-start(f32[27,8,32,1]{2,1,3,0:T(8,128)} %copy.60), channel_id=1, source_target_pairs={{1,0},{2,1},{3,2},{4,3},{5,4},{6,5},{7,6},{0,7},{9,8},{10,9},{11,1... | collective-permute-start | bytes 82952 | tf_op jit(solution)/shard_map/ppermute | solution.py:24
  15.8 18.6 %collective-permute-start.5 = (f32[27,8,32,1]{2,1,3,0:T(8,128)}, f32[27,8,32,1]{2,1,3,0:T(8,128)}, u32[]{:S(2)}, u32[]{:S(2)}) collective-permute-start(f32[27,8,32,1]{2,1,3,0:T(8,128)} %copy.62), channel_id=1, source_target_pairs={{0,1},{1,2},{2,3},{3,4},{4,5},{5,6},{6,7},{7,0},{8,9},{9,10},{10,1... | collective-permute-start | bytes 82952 | tf_op jit(solution)/shard_map/ppermute | solution.py:23
  18.1 26.7 %collective-permute-start = (f32[27,1,32,128]{3,2,1,0:T(8,128)}, f32[27,1,32,128]{3,2,1,0:T(8,128)}, u32[]{:S(2)}, u32[]{:S(2)}) collective-permute-start(f32[27,1,32,128]{3,2,1,0:T(8,128)} %get-tuple-element.142), channel_id=1, source_target_pairs={{32,0},{64,32},{96,64},{0,96},{33,1},{65,33},{97,65},{1,97},{34,2}... | collective-permute-start | bytes 1327112 | tf_op jit(solution)/shard_map/ppermute | solution.py:24
  20.5 24.3 %collective-permute-start.1 = (f32[27,1,32,128]{3,2,1,0:T(8,128)}, f32[27,1,32,128]{3,2,1,0:T(8,128)}, u32[]{:S(2)}, u32[]{:S(2)}) collective-permute-start(f32[27,1,32,128]{3,2,1,0:T(8,128)} %get-tuple-element.141), channel_id=1, source_target_pairs={{0,32},{32,64},{64,96},{96,0},{1,33},{33,65},{65,97},{97,1},{2,34}... | collective-permute-start | bytes 1327112 | tf_op jit(solution)/shard_map/ppermute | solution.py:23
  21.4 19.2 %collective-permute-start.2 = (f32[27,8,1,128]{3,2,1,0:T(1,128)}, f32[27,8,1,128]{3,2,1,0:T(1,128)}, u32[]{:S(2)}, u32[]{:S(2)}) collective-permute-start(f32[27,8,1,128]{3,2,1,0:T(1,128)} %get-tuple-element.140), channel_id=1, source_target_pairs={{8,0},{16,8},{24,16},{0,24},{9,1},{17,9},{25,17},{1,25},{10,2},{18... | collective-permute-start | bytes 331784 | tf_op jit(solution)/shard_map/ppermute | solution.py:24
  25.4 16.5 %collective-permute-start.3 = (f32[27,8,1,128]{3,2,1,0:T(1,128)}, f32[27,8,1,128]{3,2,1,0:T(1,128)}, u32[]{:S(2)}, u32[]{:S(2)}) collective-permute-start(f32[27,8,1,128]{3,2,1,0:T(1,128)} %get-tuple-element.139), channel_id=1, source_target_pairs={{0,8},{8,16},{16,24},{24,0},{1,9},{9,17},{17,25},{25,1},{2,10},{10... | collective-permute-start | bytes 331784 | tf_op jit(solution)/shard_map/ppermute | solution.py:23
  40.5 7.0 %copy-start = (f32[27,10,34,1]{3,2,1,0:T(8,128)}, f32[27,10,34,1]{3,2,1,0:T(8,128)S(1)}, u32[]{:S(2)}) copy-start(f32[27,10,34,1]{3,2,1,0:T(8,128)S(1)} %pad.55) | copy-start | bytes 110164
  40.6 5.9 %slice-start = ((s8[5529600]{0:T(1024)(128)(4,1)}), s8[4194304]{0:T(1024)(128)(4,1)S(1)}, s32[]{:S(2)}) async-start(s8[5529600]{0:T(1024)(128)(4,1)} %bitcast.168), calls=%async_computation.3 | async-start | bytes 8388608
  41.9 5.7 %copy-start.14 = (f32[27,10,1,128]{3,2,1,0:T(1,128)}, f32[27,10,1,128]{3,2,1,0:T(1,128)S(1)}, u32[]{:S(2)}) copy-start(f32[27,10,1,128]{3,2,1,0:T(1,128)S(1)} %pad.52) | copy-start | bytes 414724
  44.8 2.8 copy-start.15
  44.8 1.7 slice-start.1
  46.5 11.4 %copy-start.7 = (f32[10,34,130]{2,1,0:T(8,128)}, f32[10,34,130]{2,1,0:T(8,128)S(1)}, u32[]{:S(2)}) copy-start(f32[10,34,130]{2,1,0:T(8,128)S(1)} %get-tuple-element.128) | copy-start | bytes 530404
  46.5 11.4 %copy-start.10 = (f32[10,34,130]{2,1,0:T(8,128)}, f32[10,34,130]{2,1,0:T(8,128)S(1)}, u32[]{:S(2)}) copy-start(f32[10,34,130]{2,1,0:T(8,128)S(1)} %get-tuple-element.129) | copy-start | bytes 530404
  47.6 10.3 %copy-start.5 = (f32[10,34,130]{2,1,0:T(8,128)}, f32[10,34,130]{2,1,0:T(8,128)S(1)}, u32[]{:S(2)}) copy-start(f32[10,34,130]{2,1,0:T(8,128)S(1)} %maximum_bitcast_fusion) | copy-start | bytes 530404
  90.9 6.6 %copy-start.1 = (f32[24,8,32,128]{3,2,1,0:T(8,128)S(1)}, f32[24,8,32,128]{3,2,1,0:T(8,128)}, u32[]{:S(2)}) copy-start(f32[24,8,32,128]{3,2,1,0:T(8,128)} %fusion.71) | copy-start | bytes 9437188
  101.2 11.1 %collective-permute-start.10 = (f32[24,8,32,1]{2,1,3,0:T(8,128)S(1)}, f32[24,8,32,1]{2,1,3,0:T(8,128)S(1)}, u32[]{:S(2)}, u32[]{:S(2)}) collective-permute-start(f32[24,8,32,1]{2,1,3,0:T(8,128)S(1)} %copy.64), channel_id=1, source_target_pairs={{1,0},{2,1},{3,2},{4,3},{5,4},{6,5},{7,6},{0,7},{9,8},{10,9},{11,1... | collective-permute-start | bytes 73736 | tf_op jit(solution)/shard_map/ppermute | solution.py:24
  103.0 34.8 %collective-permute-start.6 = (f32[24,1,32,128]{3,2,1,0:T(8,128)}, f32[24,1,32,128]{3,2,1,0:T(8,128)}, u32[]{:S(2)}, u32[]{:S(2)}) collective-permute-start(f32[24,1,32,128]{3,2,1,0:T(8,128)} %get-tuple-element.160), channel_id=1, source_target_pairs={{32,0},{64,32},{96,64},{0,96},{33,1},{65,33},{97,65},{1,97},{34,2}... | collective-permute-start | bytes 1179656 | tf_op jit(solution)/shard_map/ppermute | solution.py:24
  106.0 31.9 %collective-permute-start.7 = (f32[24,1,32,128]{3,2,1,0:T(8,128)}, f32[24,1,32,128]{3,2,1,0:T(8,128)}, u32[]{:S(2)}, u32[]{:S(2)}) collective-permute-start(f32[24,1,32,128]{3,2,1,0:T(8,128)} %get-tuple-element.159), channel_id=1, source_target_pairs={{0,32},{32,64},{64,96},{96,0},{1,33},{33,65},{65,97},{97,1},{2,34}... | collective-permute-start | bytes 1179656 | tf_op jit(solution)/shard_map/ppermute | solution.py:23
  109.5 22.1 %collective-permute-start.11 = (f32[24,8,32,1]{2,1,3,0:T(8,128)S(1)}, f32[24,8,32,1]{2,1,3,0:T(8,128)S(1)}, u32[]{:S(2)}, u32[]{:S(2)}) collective-permute-start(f32[24,8,32,1]{2,1,3,0:T(8,128)S(1)} %copy.66), channel_id=1, source_target_pairs={{0,1},{1,2},{2,3},{3,4},{4,5},{5,6},{6,7},{7,0},{8,9},{9,10},{10,1... | collective-permute-start | bytes 73736 | tf_op jit(solution)/shard_map/ppermute | solution.py:23
  109.5 27.1 %collective-permute-start.8 = (f32[24,8,1,128]{3,2,1,0:T(1,128)}, f32[24,8,1,128]{3,2,1,0:T(1,128)}, u32[]{:S(2)}, u32[]{:S(2)}) collective-permute-start(f32[24,8,1,128]{3,2,1,0:T(1,128)} %get-tuple-element.158), channel_id=1, source_target_pairs={{8,0},{16,8},{24,16},{0,24},{9,1},{17,9},{25,17},{1,25},{10,2},{18... | collective-permute-start | bytes 294920 | tf_op jit(solution)/shard_map/ppermute | solution.py:24
  112.3 25.4 %collective-permute-start.9 = (f32[24,8,1,128]{3,2,1,0:T(1,128)}, f32[24,8,1,128]{3,2,1,0:T(1,128)S(1)}, u32[]{:S(2)}, u32[]{:S(2)}) collective-permute-start(f32[24,8,1,128]{3,2,1,0:T(1,128)} %get-tuple-element.157), channel_id=1, source_target_pairs={{0,8},{8,16},{16,24},{24,0},{1,9},{9,17},{17,25},{25,1},{2,10},{10... | collective-permute-start | bytes 294920 | tf_op jit(solution)/shard_map/ppermute | solution.py:23
  113.1 159.4 %all-to-all-start = ((s32[128,1,1,1]{3,2,1,0:T(1,128)}), s32[128,1,1,1]{3,2,1,0:T(1,128)}, u32[]{:S(2)}, u32[]{:S(2)}) async-start(s32[128,1,1,1]{3,2,1,0:T(1,128)} %copy.72), calls=%async_computation | async-start | bytes 131072 | tf_op jit(solution)/shard_map/all_to_all | solution.py:53
  134.0 3.9 copy-start.8
  134.0 3.9 copy-start.11
  134.0 16.9 %slice-start.2 = ((s8[4915200]{0:T(1024)(128)(4,1)}), s8[4194304]{0:T(1024)(128)(4,1)S(1)}, s32[]{:S(2)}) async-start(s8[4915200]{0:T(1024)(128)(4,1)} %bitcast.170), calls=%async_computation.5 | async-start | bytes 8388608
  136.6 14.3 %copy-start.3 = (f32[24,10,34,1]{3,2,1,0:T(8,128)}, f32[24,10,34,1]{3,2,1,0:T(8,128)S(1)}, u32[]{:S(2)}) copy-start(f32[24,10,34,1]{3,2,1,0:T(8,128)S(1)} %pad.59) | copy-start | bytes 97924
  137.7 13.2 %copy-start.16 = (f32[24,10,1,128]{3,2,1,0:T(1,128)}, f32[24,10,1,128]{3,2,1,0:T(1,128)S(1)}, u32[]{:S(2)}) copy-start(f32[24,10,1,128]{3,2,1,0:T(1,128)S(1)} %pad.56) | copy-start | bytes 368644
  137.8 13.1 %copy-start.17 = (f32[24,10,1,128]{3,2,1,0:T(1,128)}, f32[24,10,1,128]{3,2,1,0:T(1,128)S(1)}, u32[]{:S(2)}) copy-start(f32[24,10,1,128]{3,2,1,0:T(1,128)S(1)} %pad.57) | copy-start | bytes 368644
  137.8 13.1 %slice-start.3 = ((s8[4915200]{0:T(1024)(128)(4,1)}), s8[720896]{0:T(1024)(128)(4,1)S(1)}, s32[]{:S(2)}) async-start(s8[4915200]{0:T(1024)(128)(4,1)} %bitcast.170), calls=%async_computation.6 | async-start | bytes 1441792
  137.8 13.1 %copy-start.6 = (f32[10,34,130]{2,1,0:T(8,128)S(1)}, f32[10,34,130]{2,1,0:T(8,128)}, u32[]{:S(2)}) copy-start(f32[10,34,130]{2,1,0:T(8,128)} %copy-done.5) | copy-start | bytes 530404
  183.4 6.6 %copy-start.2 = (f32[24,8,32,128]{3,2,1,0:T(8,128)S(1)}, f32[24,8,32,128]{3,2,1,0:T(8,128)}, u32[]{:S(2)}) copy-start(f32[24,8,32,128]{3,2,1,0:T(8,128)} %fusion.59) | copy-start | bytes 9437188
  194.2 11.8 %collective-permute-start.16 = (f32[24,8,32,1]{2,1,3,0:T(8,128)}, f32[24,8,32,1]{2,1,3,0:T(8,128)}, u32[]{:S(2)}, u32[]{:S(2)}) collective-permute-start(f32[24,8,32,1]{2,1,3,0:T(8,128)} %copy.68), channel_id=1, source_target_pairs={{1,0},{2,1},{3,2},{4,3},{5,4},{6,5},{7,6},{0,7},{9,8},{10,9},{11,1... | collective-permute-start | bytes 73736 | tf_op jit(solution)/shard_map/ppermute | solution.py:24
  195.3 28.2 %collective-permute-start.12 = (f32[24,1,32,128]{3,2,1,0:T(8,128)}, f32[24,1,32,128]{3,2,1,0:T(8,128)}, u32[]{:S(2)}, u32[]{:S(2)}) collective-permute-start(f32[24,1,32,128]{3,2,1,0:T(8,128)} %get-tuple-element.154), channel_id=1, source_target_pairs={{32,0},{64,32},{96,64},{0,96},{33,1},{65,33},{97,65},{1,97},{34,2}... | collective-permute-start | bytes 1179656 | tf_op jit(solution)/shard_map/ppermute | solution.py:24
  197.2 26.4 %collective-permute-start.13 = (f32[24,1,32,128]{3,2,1,0:T(8,128)}, f32[24,1,32,128]{3,2,1,0:T(8,128)}, u32[]{:S(2)}, u32[]{:S(2)}) collective-permute-start(f32[24,1,32,128]{3,2,1,0:T(8,128)} %get-tuple-element.153), channel_id=1, source_target_pairs={{0,32},{32,64},{64,96},{96,0},{1,33},{33,65},{65,97},{97,1},{2,34}... | collective-permute-start | bytes 1179656 | tf_op jit(solution)/shard_map/ppermute | solution.py:23
  201.3 14.2 %collective-permute-start.17 = (f32[24,8,32,1]{2,1,3,0:T(8,128)}, f32[24,8,32,1]{2,1,3,0:T(8,128)}, u32[]{:S(2)}, u32[]{:S(2)}) collective-permute-start(f32[24,8,32,1]{2,1,3,0:T(8,128)} %copy.70), channel_id=1, source_target_pairs={{0,1},{1,2},{2,3},{3,4},{4,5},{5,6},{6,7},{7,0},{8,9},{9,10},{10,1... | collective-permute-start | bytes 73736 | tf_op jit(solution)/shard_map/ppermute | solution.py:23
  202.9 18.4 %collective-permute-start.14 = (f32[24,8,1,128]{3,2,1,0:T(1,128)}, f32[24,8,1,128]{3,2,1,0:T(1,128)}, u32[]{:S(2)}, u32[]{:S(2)}) collective-permute-start(f32[24,8,1,128]{3,2,1,0:T(1,128)} %get-tuple-element.152), channel_id=1, source_target_pairs={{8,0},{16,8},{24,16},{0,24},{9,1},{17,9},{25,17},{1,25},{10,2},{18... | collective-permute-start | bytes 294920 | tf_op jit(solution)/shard_map/ppermute | solution.py:24
  206.0 16.4 %collective-permute-start.15 = (f32[24,8,1,128]{3,2,1,0:T(1,128)}, f32[24,8,1,128]{3,2,1,0:T(1,128)}, u32[]{:S(2)}, u32[]{:S(2)}) collective-permute-start(f32[24,8,1,128]{3,2,1,0:T(1,128)} %get-tuple-element.151), channel_id=1, source_target_pairs={{0,8},{8,16},{16,24},{24,0},{1,9},{9,17},{17,25},{25,1},{2,10},{10... | collective-permute-start | bytes 294920 | tf_op jit(solution)/shard_map/ppermute | solution.py:23
  218.7 4.9 %copy-start.9 = (f32[10,34,130]{2,1,0:T(8,128)S(1)}, f32[10,34,130]{2,1,0:T(8,128)}, u32[]{:S(2)}) copy-start(f32[10,34,130]{2,1,0:T(8,128)} %copy-done.7) | copy-start | bytes 530404
  218.7 4.9 %copy-start.12 = (f32[10,34,130]{2,1,0:T(8,128)S(1)}, f32[10,34,130]{2,1,0:T(8,128)}, u32[]{:S(2)}) copy-start(f32[10,34,130]{2,1,0:T(8,128)} %copy-done.10) | copy-start | bytes 530404
  218.7 17.4 %slice-start.4 = ((s8[4915200]{0:T(1024)(128)(4,1)}), s8[4194304]{0:T(1024)(128)(4,1)S(1)}, s32[]{:S(2)}) async-start(s8[4915200]{0:T(1024)(128)(4,1)} %bitcast.172), calls=%async_computation.7 | async-start | bytes 8388608
  221.3 14.8 %copy-start.4 = (f32[24,10,34,1]{3,2,1,0:T(8,128)}, f32[24,10,34,1]{3,2,1,0:T(8,128)S(1)}, u32[]{:S(2)}) copy-start(f32[24,10,34,1]{3,2,1,0:T(8,128)S(1)} %pad.63) | copy-start | bytes 97924
  222.4 13.7 %copy-start.18 = (f32[24,10,1,128]{3,2,1,0:T(1,128)}, f32[24,10,1,128]{3,2,1,0:T(1,128)S(1)}, u32[]{:S(2)}) copy-start(f32[24,10,1,128]{3,2,1,0:T(1,128)S(1)} %pad.60) | copy-start | bytes 368644
  223.6 12.6 %copy-start.19 = (f32[24,10,1,128]{3,2,1,0:T(1,128)}, f32[24,10,1,128]{3,2,1,0:T(1,128)S(1)}, u32[]{:S(2)}) copy-start(f32[24,10,1,128]{3,2,1,0:T(1,128)S(1)} %pad.61) | copy-start | bytes 368644
  223.6 12.6 %slice-start.5 = ((s8[4915200]{0:T(1024)(128)(4,1)}), s8[720896]{0:T(1024)(128)(4,1)S(1)}, s32[]{:S(2)}) async-start(s8[4915200]{0:T(1024)(128)(4,1)} %bitcast.172), calls=%async_computation.8 | async-start | bytes 1441792
  247.0 22.0 %copy-start.20 = (f32[128,256]{1,0:T(8,128)S(1)}, f32[128,256]{1,0:T(8,128)}, u32[]{:S(2)}) copy-start(f32[128,256]{1,0:T(8,128)} %fusion.87) | copy-start | bytes 393220
  269.1 30.1 %copy-start.21 = (bf16[400,24]{0,1:T(8,128)(2,1)S(1)}, bf16[400,24]{0,1:T(8,128)(2,1)}, u32[]{:S(2)}) copy-start(bf16[400,24]{0,1:T(8,128)(2,1)} %param.24) | copy-start | bytes 57604
  269.1 30.1 %copy-start.23 = (f32[24]{0:T(128)S(1)}, f32[24]{0:T(128)}, u32[]{:S(2)}) copy-start(f32[24]{0:T(128)} %param.25) | copy-start | bytes 292
  269.1 30.1 %copy-start.28 = (bf16[800,400]{0,1:T(8,128)(2,1)S(1)}, bf16[800,400]{0,1:T(8,128)(2,1)}, u32[]{:S(2)}) copy-start(bf16[800,400]{0,1:T(8,128)(2,1)} %param.22) | copy-start | bytes 1920004
  269.1 30.1 %copy-start.29 = (bf16[24,1600]{1,0:T(8,128)(2,1)S(1)}, bf16[24,1600]{1,0:T(8,128)(2,1)}, u32[]{:S(2)}) copy-start(bf16[24,1600]{1,0:T(8,128)(2,1)} %param.18) | copy-start | bytes 230404
  269.1 30.1 %copy-start.30 = (f32[1600]{0:T(1024)S(1)}, f32[1600]{0:T(1024)}, u32[]{:S(2)}) copy-start(f32[1600]{0:T(1024)} %param.19) | copy-start | bytes 19204
  269.1 30.1 %copy-start.31 = (f32[800]{0:T(1024)S(1)}, f32[800]{0:T(1024)}, u32[]{:S(2)}) copy-start(f32[800]{0:T(1024)} %param.21) | copy-start | bytes 9604
  269.1 30.1 %copy-start.32 = (f32[400]{0:T(512)S(1)}, f32[400]{0:T(512)}, u32[]{:S(2)}) copy-start(f32[400]{0:T(512)} %param.23) | copy-start | bytes 4804
  272.4 26.5 %all-to-all-start.1 = ((bf16[128,1,1,1,24,128]{5,4,3,2,1,0:T(8,128)(2,1)}), bf16[128,1,1,1,24,128]{5,4,3,2,1,0:T(8,128)(2,1)S(1)}, u32[]{:S(2)}, u32[]{:S(2)}) async-start(bf16[128,1,1,1,24,128]{5,4,3,2,1,0:T(8,128)(2,1)} %copy.77), calls=%async_computation.1 | async-start | bytes 1572864 | tf_op jit(solution)/shard_map/all_to_all | solution.py:53
  345.9 29.6 %all-to-all-start.2 = ((f32[128,1,1,1,24,128]{5,4,3,2,1,0:T(8,128)}), f32[128,1,1,1,24,128]{5,4,3,2,1,0:T(8,128)S(1)}, u32[]{:S(2)}, u32[]{:S(2)}) async-start(f32[128,1,1,1,24,128]{5,4,3,2,1,0:T(8,128)} %copy.81), calls=%async_computation.2 | async-start | bytes 3145728 | tf_op jit(solution)/shard_map/all_to_all | solution.py:53
  387.6 25.7 %collective-permute-start.18 = (f32[24,1,32,128]{3,2,1,0:T(8,128)}, f32[24,1,32,128]{3,2,1,0:T(8,128)}, u32[]{:S(2)}, u32[]{:S(2)}) collective-permute-start(f32[24,1,32,128]{3,2,1,0:T(8,128)} %get-tuple-element.146), channel_id=1, source_target_pairs={{32,0},{64,32},{96,64},{0,96},{33,1},{65,33},{97,65},{1,97},{34,2}... | collective-permute-start | bytes 1179656 | tf_op jit(solution)/shard_map/ppermute | solution.py:24
  388.5 24.7 %collective-permute-start.19 = (f32[24,1,32,128]{3,2,1,0:T(8,128)S(1)}, f32[24,1,32,128]{3,2,1,0:T(8,128)}, u32[]{:S(2)}, u32[]{:S(2)}) collective-permute-start(f32[24,1,32,128]{3,2,1,0:T(8,128)S(1)} %get-tuple-element.145), channel_id=1, source_target_pairs={{0,32},{32,64},{64,96},{96,0},{1,33},{33,65},{65,97},{97,1},{2,34}... | collective-permute-start | bytes 1179656 | tf_op jit(solution)/shard_map/ppermute | solution.py:23
  396.2 6.6 %collective-permute-start.22 = (f32[24,8,32,1]{2,1,3,0:T(8,128)}, f32[24,8,32,1]{2,1,3,0:T(8,128)}, u32[]{:S(2)}, u32[]{:S(2)}) collective-permute-start(f32[24,8,32,1]{2,1,3,0:T(8,128)} %copy.84), channel_id=1, source_target_pairs={{1,0},{2,1},{3,2},{4,3},{5,4},{6,5},{7,6},{0,7},{9,8},{10,9},{11,1... | collective-permute-start | bytes 73736 | tf_op jit(solution)/shard_map/ppermute | solution.py:24
  402.0 6.0 %collective-permute-start.23 = (f32[24,8,32,1]{2,1,3,0:T(8,128)}, f32[24,8,32,1]{2,1,3,0:T(8,128)}, u32[]{:S(2)}, u32[]{:S(2)}) collective-permute-start(f32[24,8,32,1]{2,1,3,0:T(8,128)} %copy.86), channel_id=1, source_target_pairs={{0,1},{1,2},{2,3},{3,4},{4,5},{5,6},{6,7},{7,0},{8,9},{9,10},{10,1... | collective-permute-start | bytes 73736 | tf_op jit(solution)/shard_map/ppermute | solution.py:23
  402.1 9.2 %collective-permute-start.20 = (f32[24,8,1,128]{3,2,1,0:T(1,128)}, f32[24,8,1,128]{3,2,1,0:T(1,128)}, u32[]{:S(2)}, u32[]{:S(2)}) collective-permute-start(f32[24,8,1,128]{3,2,1,0:T(1,128)} %get-tuple-element.148), channel_id=1, source_target_pairs={{8,0},{16,8},{24,16},{0,24},{9,1},{17,9},{25,17},{1,25},{10,2},{18... | collective-permute-start | bytes 294920 | tf_op jit(solution)/shard_map/ppermute | solution.py:24
  402.9 9.4 %collective-permute-start.21 = (f32[24,8,1,128]{3,2,1,0:T(1,128)}, f32[24,8,1,128]{3,2,1,0:T(1,128)}, u32[]{:S(2)}, u32[]{:S(2)}) collective-permute-start(f32[24,8,1,128]{3,2,1,0:T(1,128)} %get-tuple-element.147), channel_id=1, source_target_pairs={{0,8},{8,16},{16,24},{24,0},{1,9},{9,17},{17,25},{25,1},{2,10},{10... | collective-permute-start | bytes 294920 | tf_op jit(solution)/shard_map/ppermute | solution.py:23
  404.8 8.5 %copy-start.27 = (f32[24]{0:T(128)S(1)}, f32[24]{0:T(128)}, u32[]{:S(2)}) copy-start(f32[24]{0:T(128)} %param.17) | copy-start | bytes 292
  (2 other events, 1.7 us)
where the time goes:
time: 428 us; the launch traced here: 423 us
  other arithmetic  153 us (36%)
  local copies, waits for them, and re-layouts  121 us (28%)
  starting transfers between devices  55.8 us (13%)
  matrix products  52.1 us (12%)
  waiting for transfers between devices  36.7 us (9%)
    mul x7, other arithmetic, transport(): carried = speeds[axis_dim - 1][None] * padded  59.9 us
    slice x15, local copies, waits for them, and re-layouts, extended(): last = lax.slice_in_dim(value, length - width, length, axis=dim)  37.2 us
    all_to_all x3, waiting for transfers between devices, one_exchange(): tiles = lax.all_to_all(tiles, axis, split_axis=0, concat_axis=0, tiled=True)  36.6 us
    dot_general x4, matrix products, network(): jnp.einsum('bkz,kl->blz', hidden, weight_low, preferred_element_type=jnp....  27.8 us
    all_to_all x3, starting transfers between devices, one_exchange(): tiles = lax.all_to_all(tiles, axis, split_axis=0, concat_axis=0, tiled=True)  26.5 us
    ppermute x12, starting transfers between devices, extended(): lax.ppermute(leading, axis, [(b, a) for a, b in up])  24.8 us
    add x1, other arithmetic, local(): section_one = fields + transport(padded[:field_count], speeds)  23.1 us
    convert_element_type x1, other arithmetic, local(): flowed.reshape(field_count, block_count, cells_z).astype(jnp.bfloat16)  22 us
  transfers between devices with their start and end apart: 27, of which 2 were waited for; matrix products, arithmetic and copies ran while one was open for 46% of the time, Pallas kernels for 0%

commit v1 on v0

--- a/solution.py
+++ b/solution.py
@@ -174,7 +174,10 @@
     )
     arrived = arrived.reshape(slots_all, field_count, cells_z)
     occupied = arrived_mask.reshape(slots_all)
-    position = jnp.cumsum(occupied) - 1
+    slot_numbers = jnp.arange(slots_all, dtype=jnp.int32)
+    position = (
+        jnp.sum(jnp.where(slot_numbers[None, :] <= slot_numbers[:, None], occupied[None, :], 0), axis=1) - 1
+    )
     selector = (
         (position[None, :] == jnp.arange(OWNED, dtype=jnp.int32)[:, None])
         & (occupied[None, :] == 1)

time: 428 us -> 428 us (level)
  no operation moved by 1% of the time
where the time goes in v1:
time: 428 us; the launch traced here: 423 us
  other arithmetic  153 us (36%)
  local copies, waits for them, and re-layouts  121 us (28%)
  starting transfers between devices  55.8 us (13%)
  matrix products  52 us (12%)
  waiting for transfers between devices  37 us (9%)
    mul x7, other arithmetic, transport(): carried = speeds[axis_dim - 1][None] * padded  59.9 us
    slice x15, local copies, waits for them, and re-layouts, extended(): last = lax.slice_in_dim(value, length - width, length, axis=dim)  37.2 us
    all_to_all x3, waiting for transfers between devices, one_exchange(): tiles = lax.all_to_all(tiles, axis, split_axis=0, concat_axis=0, tiled=True)  36.9 us
    dot_general x4, matrix products, network(): jnp.einsum('bkz,kl->blz', hidden, weight_low, preferred_element_type=jnp....  27.9 us
    all_to_all x3, starting transfers between devices, one_exchange(): tiles = lax.all_to_all(tiles, axis, split_axis=0, concat_axis=0, tiled=True)  26.5 us
    ppermute x12, starting transfers between devices, extended(): lax.ppermute(leading, axis, [(b, a) for a, b in up])  24.8 us
    add x1, other arithmetic, local(): section_one = fields + transport(padded[:field_count], speeds)  23.1 us
    convert_element_type x1, other arithmetic, local(): flowed.reshape(field_count, block_count, cells_z).astype(jnp.bfloat16)  22 us
  transfers between devices with their start and end apart: 27, of which 2 were waited for; matrix products, arithmetic and copies ran while one was open for 46% of the time, Pallas kernels for 0%

profile of v1, /device:TPU:1, one launch (start us, length us, event | category | flops | bytes accessed | tf_op | source)
XLA Modules:
  0.0 422.9 jit_solution(18064026312104321927)
XLA Ops:
  0.6 2.4 constant_dynamic-update-slice_fusion.1
  3.1 4.2 fusion.107
  7.2 3.6 copy.54
  12.2 3.6 copy.56
  18.1 2.5 collective-permute-start
  21.4 3.8 collective-permute-start.2
  26.0 3.5 copy.55
  29.5 5.0 %pad.54 = f32[27,10,34,1]{3,2,1,0:T(8,128)} pad(f32[27,8,32,1]{3,2,1,0:T(8,128)} %copy.55, f32[]{:T(128)} %constant.24.clone.1), padding=0_0x1_1x1_1x0_0 | pad | bytes 64372 | tf_op jit(solution)/shard_map/jit(_pad)/pad | solution.py:30
  34.5 3.5 copy.57
  38.0 2.6 pad.55
  42.0 2.9 pad.53
  47.7 10.2 %pad_maximum_fusion = f32[27,10,34,130]{3,2,1,0:T(8,128)S(1)} fusion(f32[27,10,34,1]{3,2,1,0:T(8,128)S(1)} %bitcast.164, f32[27,10,1,128]{3,2,1,0:T(1,128)S(1)} %pad.52, f32[27,1,32,128]{3,2,1,0:T(8,128)} %collective-permute-done, f32[27,8,32,128]{3,2,1,0:T(8,128)S(1)} %constant_dynamic-update-slice_fusion, f32[27,1,32,128]{3,2,1,0:T(8,128)} %collective-permute-done.1, ...), kind=kLoop, calls=%fused_computation.30 | loop fusion | flops 7160400 | bytes 9547200 | tf_op jit(solution)/shard_map/concatenate | solution.py:30
  57.9 9.9 %slice_multiply_fusion.2 = (f32[24,10,34,130]{3,2,1,0:T(8,128)}, f32[24,10,34,130]{3,2,1,0:T(8,128)}, f32[24,10,34,130]{3,2,1,0:T(8,128)}) fusion(f32[27,10,34,130]{3,2,1,0:T(8,128)S(1)} %pad_maximum_fusion, f32[10,34,130]{2,1,0:T(8,128)S(1)} %get-tuple-element.128, f32[10,34,130]{2,1,0:T(8,128)S(1)} %get-tuple-element.129, ...), kind=kLoop, calls=%fused_computation.35 | loop fusion | flops 3182400 | bytes 17503200 | tf_op jit(solution)/shard_map/mul | solution.py:80
  67.9 23.1 %fusion.71 = f32[24,8,32,128]{3,2,1,0:T(8,128)} fusion(f32[24,8,32,128]{3,2,1,0:T(8,128)} %param.15, f32[24,10,34,130]{3,2,1,0:T(8,128)} %get-tuple-element.136, f32[24,10,34,130]{3,2,1,0:T(8,128)} %get-tuple-element.135, f32[24,10,34,130]{3,2,1,0:T(8,128)} %get-tuple-element.134, f32[27,10,34,1]{3,2,1,0:T(8,128)} %copy-done, ...), kind=kLoop, calls=%fused_computation.146 | loop fusion | flops 26738688 | bytes 29939424 | tf_op jit(solution)/shard_map/add | solution.py:119
  91.0 6.6 %fusion.116 = (f32[24,8,32,1]{3,2,1,0:T(8,128)}, f32[24,8,32,1]{3,2,1,0:T(8,128)}) fusion(f32[24,8,32,128]{3,2,1,0:T(8,128)} %fusion.71), kind=kLoop, calls=%fused_computation.234 | loop fusion | bytes 98304 | tf_op jit(solution)/shard_map/slice | solution.py:20
  98.6 2.7 copy.58
  101.3 1.8 collective-permute-start.10
  103.1 3.0 collective-permute-start.6
  106.9 2.7 copy.60
  109.6 2.8 collective-permute-start.8
  113.1 11.4 %all-to-all-start = ((s32[128,1,1,1]{3,2,1,0:T(1,128)}), s32[128,1,1,1]{3,2,1,0:T(1,128)}, u32[]{:S(2)}, u32[]{:S(2)}) async-start(s32[128,1,1,1]{3,2,1,0:T(1,128)} %copy.66), calls=%async_computation | async-start | bytes 131072 | tf_op jit(solution)/shard_map/all_to_all | solution.py:53
  124.5 2.5 copy.59
  127.0 4.6 %pad.58 = f32[24,10,34,1]{3,2,1,0:T(8,128)} pad(f32[24,8,32,1]{3,2,1,0:T(8,128)} %copy.59, f32[]{:T(128)} %constant.24.clone.1), padding=0_0x1_1x1_1x0_0 | pad | bytes 57220 | tf_op jit(solution)/shard_map/jit(_pad)/pad | solution.py:30
  131.6 2.4 copy.61
  134.1 2.6 pad.59
  137.9 13.0 %broadcast_multiply_fusion.5 = (f32[24,10,34,130]{3,2,1,0:T(8,128)}, f32[24,10,34,130]{3,2,1,0:T(8,128)}) fusion(f32[10,34,130]{2,1,0:T(8,128)S(1)} %copy-done.8, f32[24,10,34,1]{3,2,1,0:T(8,128)} %pad.58, f32[24,10,1,128]{3,2,1,0:T(1,128)S(1)} %pad.56, f32[24,1,32,128]{3,2,1,0:T(8,128)} %collective-permute-done.6, f32[24,8,32,128]{3,2,1,0:T(8,128)S(1)} %copy-done.1, ...), kind=kLoop, calls=%fused_computation.41 | loop fusion | flops 8486400 | bytes 13083200 | tf_op jit(solution)/shard_map/mul | solution.py:80
  151.0 10.9 %broadcast_multiply_fusion.1 = f32[24,10,34,130]{3,2,1,0:T(8,128)} fusion(f32[10,34,130]{2,1,0:T(8,128)S(1)} %copy-done.6, f32[24,10,34,1]{3,2,1,0:T(8,128)S(1)} %bitcast.166, f32[24,10,1,128]{3,2,1,0:T(1,128)S(1)} %pad.56, f32[24,1,32,128]{3,2,1,0:T(8,128)} %collective-permute-done.6, f32[24,8,32,128]{3,2,1,0:T(8,128)S(1)} %copy-done.1, ...), kind=kLoop, calls=%fused_computation.37 | loop fusion | flops 7425600 | bytes 8663200 | tf_op jit(solution)/shard_map/mul | solution.py:80
  161.9 21.5 %fusion.59 = f32[24,8,32,128]{3,2,1,0:T(8,128)} fusion(f32[24,8,32,128]{3,2,1,0:T(8,128)S(1)} %copy-done.1, f32[24,10,34,130]{3,2,1,0:T(8,128)} %broadcast_multiply_fusion.1, f32[24,10,34,130]{3,2,1,0:T(8,128)} %get-tuple-element.133, f32[24,10,34,130]{3,2,1,0:T(8,128)} %get-tuple-element.132, f32[24,10,34,1]{3,2,1,0:T(8,128)} %copy-done.3, ...), kind=kLoop, calls=%fused_computation.113 | loop fusion | flops 29097984 | bytes 29409024 | tf_op jit(solution)/shard_map/add | solution.py:120
  183.4 6.6 %fusion.113 = (f32[24,8,32,1]{3,2,1,0:T(8,128)}, f32[24,8,32,1]{3,2,1,0:T(8,128)}) fusion(f32[24,8,32,128]{3,2,1,0:T(8,128)} %fusion.59), kind=kLoop, calls=%fused_computation.231 | loop fusion | bytes 98304 | tf_op jit(solution)/shard_map/slice | solution.py:20
  191.0 3.3 copy.62
  198.0 3.3 copy.64
  203.0 3.1 collective-permute-start.14
  207.7 3.2 copy.63
  210.9 4.6 %pad.62 = f32[24,10,34,1]{3,2,1,0:T(8,128)} pad(f32[24,8,32,1]{3,2,1,0:T(8,128)} %copy.63, f32[]{:T(128)} %constant.24.clone.1), padding=0_0x1_1x1_1x0_0 | pad | bytes 57220 | tf_op jit(solution)/shard_map/jit(_pad)/pad | solution.py:30
  215.5 3.2 copy.65
  218.8 2.6 pad.63
  223.6 12.5 %broadcast_multiply_fusion.4 = (f32[24,10,34,130]{3,2,1,0:T(8,128)}, f32[24,10,34,130]{3,2,1,0:T(8,128)}) fusion(f32[10,34,130]{2,1,0:T(8,128)S(1)} %copy-done.9, f32[24,10,34,1]{3,2,1,0:T(8,128)} %pad.62, f32[24,10,1,128]{3,2,1,0:T(1,128)S(1)} %pad.60, f32[24,1,32,128]{3,2,1,0:T(8,128)} %collective-permute-done.12, f32[24,8,32,128]{3,2,1,0:T(8,128)S(1)} %copy-done.2, ...), kind=kLoop, calls=%fused_computation.40 | loop fusion | flops 8486400 | bytes 13083200 | tf_op jit(solution)/shard_map/mul | solution.py:80
  236.2 10.8 %broadcast_multiply_fusion = f32[24,10,34,130]{3,2,1,0:T(8,128)} fusion(f32[10,34,130]{2,1,0:T(8,128)S(1)} %copy-done.6, f32[24,10,34,1]{3,2,1,0:T(8,128)S(1)} %bitcast.168, f32[24,10,1,128]{3,2,1,0:T(1,128)S(1)} %pad.60, f32[24,1,32,128]{3,2,1,0:T(8,128)} %collective-permute-done.12, f32[24,8,32,128]{3,2,1,0:T(8,128)S(1)} %copy-done.2, ...), kind=kLoop, calls=%fused_computation.36 | loop fusion | flops 7425600 | bytes 8663200 | tf_op jit(solution)/shard_map/mul | solution.py:80
  247.1 22.0 %fusion.105 = (bf16[24,8,32,128]{3,2,1,0:T(8,128)(2,1)}, f32[24,8,32,128]{3,2,1,0:T(8,128)}) fusion(f32[24,8,32,128]{3,2,1,0:T(8,128)S(1)} %copy-done.2, f32[24,10,34,130]{3,2,1,0:T(8,128)} %broadcast_multiply_fusion, f32[24,10,34,130]{3,2,1,0:T(8,128)} %get-tuple-element.131, f32[24,10,34,130]{3,2,1,0:T(8,128)} %get-tuple-element.130, ...), kind=kLoop, calls=%fused_computation.224 | loop fusion | flops 29884416 | bytes 30981888 | tf_op jit(solution)/shard_map/convert_element_type | solution.py:148
  269.2 1.9 fusion.81
  272.5 10.1 %all-to-all-start.1 = ((bf16[128,1,1,1,24,128]{5,4,3,2,1,0:T(8,128)(2,1)}), bf16[128,1,1,1,24,128]{5,4,3,2,1,0:T(8,128)(2,1)S(1)}, u32[]{:S(2)}, u32[]{:S(2)}) async-start(bf16[128,1,1,1,24,128]{5,4,3,2,1,0:T(8,128)(2,1)} %copy.69), calls=%async_computation.1 | async-start | bytes 1572864 | tf_op jit(solution)/shard_map/all_to_all | solution.py:53
  282.6 3.2 reduce.1
  286.3 12.7 %all-to-all-done.1 = bf16[128,1,1,1,24,128]{5,4,3,2,1,0:T(8,128)(2,1)S(1)} async-done(((bf16[128,1,1,1,24,128]{5,4,3,2,1,0:T(8,128)(2,1)}), bf16[128,1,1,1,24,128]{5,4,3,2,1,0:T(8,128)(2,1)S(1)}, u32[]{:S(2)}, u32[]{:S(2)}) %all-to-all-start.1) | async-done | bytes 786464 | tf_op jit(solution)/shard_map/all_to_all | solution.py:53
  299.3 43.7 %while.10 = (s32[]{:T(128)}, f32[4,8,24,128]{3,2,1,0:T(8,128)S(1)}, bf16[4,8,24,128]{3,1,0,2:T(8,128)(2,1)S(1)}, bf16[24,1600]{1,0:T(8,128)(2,1)S(1)}, f32[1600]...) while((s32[]{:T(128)}, f32[4,8,24,128]{3,2,1,0:T(8,128)S(1)}, ...), condition=%wide.region_4.5_spmd, body=%wide.region_3.4_spmd.sunk | while | flops 3392331776 | bytes 11750973 | solution.py:203
  299.3 3.7 fusion.139
  303.0 7.0 %fusion.140 = bf16[8,400,128]{2,1,0:T(8,128)(2,1)S(1)} fusion(f32[800]{0:T(1024)S(1)} %get-tuple-element.258, bf16[8,1600,128]{2,1,0:T(8,128)(2,1)} %fusion.139, bf16[1600,800]{0,1:T(8,128)(2,1)} %get-tuple-element.257, f32[400]{0:T(512)S(1)} %get-tuple-element.260, bf16[800,400]{0,1:T(8,128)(2,1)S(1)} %get-tuple-element.259), kind=kOutput, calls=%fused_computation.19.clone.1 | convolution fusion | flops 3284172800 | bytes 7300800 | tf_op jit(solution)/shard_map/while/body/eval_jaxpr/bkz,kl->blz/dot_general | solution.py:95
  310.3 3.7 fusion.139
  314.0 7.0 %fusion.140 = bf16[8,400,128]{2,1,0:T(8,128)(2,1)S(1)} fusion(f32[800]{0:T(1024)S(1)} %get-tuple-element.258, bf16[8,1600,128]{2,1,0:T(8,128)(2,1)} %fusion.139, bf16[1600,800]{0,1:T(8,128)(2,1)} %get-tuple-element.257, f32[400]{0:T(512)S(1)} %get-tuple-element.260, bf16[800,400]{0,1:T(8,128)(2,1)S(1)} %get-tuple-element.259), kind=kOutput, calls=%fused_computation.19.clone.1 | convolution fusion | flops 3284172800 | bytes 7300800 | tf_op jit(solution)/shard_map/while/body/eval_jaxpr/bkz,kl->blz/dot_general | solution.py:95
  321.2 3.7 fusion.139
  324.9 7.0 %fusion.140 = bf16[8,400,128]{2,1,0:T(8,128)(2,1)S(1)} fusion(f32[800]{0:T(1024)S(1)} %get-tuple-element.258, bf16[8,1600,128]{2,1,0:T(8,128)(2,1)} %fusion.139, bf16[1600,800]{0,1:T(8,128)(2,1)} %get-tuple-element.257, f32[400]{0:T(512)S(1)} %get-tuple-element.260, bf16[800,400]{0,1:T(8,128)(2,1)S(1)} %get-tuple-element.259), kind=kOutput, calls=%fused_computation.19.clone.1 | convolution fusion | flops 3284172800 | bytes 7300800 | tf_op jit(solution)/shard_map/while/body/eval_jaxpr/bkz,kl->blz/dot_general | solution.py:95
  332.1 3.7 fusion.139
  335.8 7.0 %fusion.140 = bf16[8,400,128]{2,1,0:T(8,128)(2,1)S(1)} fusion(f32[800]{0:T(1024)S(1)} %get-tuple-element.258, bf16[8,1600,128]{2,1,0:T(8,128)(2,1)} %fusion.139, bf16[1600,800]{0,1:T(8,128)(2,1)} %get-tuple-element.257, f32[400]{0:T(512)S(1)} %get-tuple-element.260, bf16[800,400]{0,1:T(8,128)(2,1)S(1)} %get-tuple-element.259), kind=kOutput, calls=%fused_computation.19.clone.1 | convolution fusion | flops 3284172800 | bytes 7300800 | tf_op jit(solution)/shard_map/while/body/eval_jaxpr/bkz,kl->blz/dot_general | solution.py:95
  343.8 2.1 copy.73
  345.9 5.0 %all-to-all-start.2 = ((f32[128,1,1,1,24,128]{5,4,3,2,1,0:T(8,128)}), f32[128,1,1,1,24,128]{5,4,3,2,1,0:T(8,128)S(1)}, u32[]{:S(2)}, u32[]{:S(2)}) async-start(f32[128,1,1,1,24,128]{5,4,3,2,1,0:T(8,128)} %copy.73), calls=%async_computation.2 | async-start | bytes 3145728 | tf_op jit(solution)/shard_map/all_to_all | solution.py:53
  351.3 24.3 %all-to-all-done.2 = f32[128,1,1,1,24,128]{5,4,3,2,1,0:T(8,128)S(1)} async-done(((f32[128,1,1,1,24,128]{5,4,3,2,1,0:T(8,128)}), f32[128,1,1,1,24,128]{5,4,3,2,1,0:T(8,128)S(1)}, u32[]{:S(2)}, u32[]{:S(2)}) %all-to-all-start.2) | async-done | bytes 1572896 | tf_op jit(solution)/shard_map/all_to_all | solution.py:53
  376.7 4.1 convolution_bitcast_fusion
  380.8 2.3 copy.75
  383.1 3.7 add.247
  389.0 3.9 fusion.110
  392.9 3.3 copy.76
  398.7 3.3 copy.78
  404.8 3.2 copy.77
  408.0 3.2 copy.79
  413.3 8.1 %fusion.33 = f32[24,8,32,128]{3,2,1,0:T(8,128)} fusion(f32[24,8,32,128]{3,2,1,0:T(8,128)S(1)} %add.247, f32[24,8,32,1]{3,2,1,0:T(8,128)} %copy.79, f32[24,10,1,128]{3,2,1,0:T(1,128)S(1)} %pad.64, f32[24,10,1,128]{3,2,1,0:T(1,128)S(1)} %pad.65, f32[24,1,32,128]{3,2,1,0:T(8,128)} %collective-permute-done.18, f32[24,1,32,128]{3,2,1,0:T(8,128)} %collective-permute-done.19, ...), kind=kLoop, calls=%fused_computation.46 | loop fusion | flops 25952256 | bytes 7372896 | tf_op jit(solution)/shard_map/add | solution.py:224
  (170 shorter events, 37.7 us)
Async XLA Ops:
  0.6 2.4 copy-start.22
  10.8 14.4 %copy-start.25 = (s32[1,96]{1,0:T(1,128)S(1)}, s32[1,96]{1,0:T(1,128)}, u32[]{:S(2)}) copy-start(s32[1,96]{1,0:T(1,128)} %param.26) | copy-start | bytes 1156
  10.8 14.4 %copy-start.24 = (s32[1,96]{1,0:T(1,128)S(1)}, s32[1,96]{1,0:T(1,128)}, u32[]{:S(2)}) copy-start(s32[1,96]{1,0:T(1,128)} %param.27) | copy-start | bytes 1156
  10.8 14.6 %collective-permute-start.4 = (f32[27,8,32,1]{2,1,3,0:T(8,128)}, f32[27,8,32,1]{2,1,3,0:T(8,128)}, u32[]{:S(2)}, u32[]{:S(2)}) collective-permute-start(f32[27,8,32,1]{2,1,3,0:T(8,128)} %copy.54), channel_id=1, source_target_pairs={{1,0},{2,1},{3,2},{4,3},{5,4},{6,5},{7,6},{0,7},{9,8},{10,9},{11,1... | collective-permute-start | bytes 82952 | tf_op jit(solution)/shard_map/ppermute | solution.py:24
  15.8 18.7 %collective-permute-start.5 = (f32[27,8,32,1]{2,1,3,0:T(8,128)}, f32[27,8,32,1]{2,1,3,0:T(8,128)}, u32[]{:S(2)}, u32[]{:S(2)}) collective-permute-start(f32[27,8,32,1]{2,1,3,0:T(8,128)} %copy.56), channel_id=1, source_target_pairs={{0,1},{1,2},{2,3},{3,4},{4,5},{5,6},{6,7},{7,0},{8,9},{9,10},{10,1... | collective-permute-start | bytes 82952 | tf_op jit(solution)/shard_map/ppermute | solution.py:23
  18.1 26.8 %collective-permute-start = (f32[27,1,32,128]{3,2,1,0:T(8,128)}, f32[27,1,32,128]{3,2,1,0:T(8,128)}, u32[]{:S(2)}, u32[]{:S(2)}) collective-permute-start(f32[27,1,32,128]{3,2,1,0:T(8,128)} %get-tuple-element.142), channel_id=1, source_target_pairs={{32,0},{64,32},{96,64},{0,96},{33,1},{65,33},{97,65},{1,97},{34,2}... | collective-permute-start | bytes 1327112 | tf_op jit(solution)/shard_map/ppermute | solution.py:24
  20.6 24.3 %collective-permute-start.1 = (f32[27,1,32,128]{3,2,1,0:T(8,128)}, f32[27,1,32,128]{3,2,1,0:T(8,128)}, u32[]{:S(2)}, u32[]{:S(2)}) collective-permute-start(f32[27,1,32,128]{3,2,1,0:T(8,128)} %get-tuple-element.141), channel_id=1, source_target_pairs={{0,32},{32,64},{64,96},{96,0},{1,33},{33,65},{65,97},{97,1},{2,34}... | collective-permute-start | bytes 1327112 | tf_op jit(solution)/shard_map/ppermute | solution.py:23
  21.4 19.2 %collective-permute-start.2 = (f32[27,8,1,128]{3,2,1,0:T(1,128)}, f32[27,8,1,128]{3,2,1,0:T(1,128)}, u32[]{:S(2)}, u32[]{:S(2)}) collective-permute-start(f32[27,8,1,128]{3,2,1,0:T(1,128)} %get-tuple-element.140), channel_id=1, source_target_pairs={{8,0},{16,8},{24,16},{0,24},{9,1},{17,9},{25,17},{1,25},{10,2},{18... | collective-permute-start | bytes 331784 | tf_op jit(solution)/shard_map/ppermute | solution.py:24
  25.4 16.5 %collective-permute-start.3 = (f32[27,8,1,128]{3,2,1,0:T(1,128)}, f32[27,8,1,128]{3,2,1,0:T(1,128)}, u32[]{:S(2)}, u32[]{:S(2)}) collective-permute-start(f32[27,8,1,128]{3,2,1,0:T(1,128)} %get-tuple-element.139), channel_id=1, source_target_pairs={{0,8},{8,16},{16,24},{24,0},{1,9},{9,17},{17,25},{25,1},{2,10},{10... | collective-permute-start | bytes 331784 | tf_op jit(solution)/shard_map/ppermute | solution.py:23
  40.6 7.0 %copy-start = (f32[27,10,34,1]{3,2,1,0:T(8,128)}, f32[27,10,34,1]{3,2,1,0:T(8,128)S(1)}, u32[]{:S(2)}) copy-start(f32[27,10,34,1]{3,2,1,0:T(8,128)S(1)} %pad.55) | copy-start | bytes 110164
  40.6 5.9 %slice-start = ((s8[5529600]{0:T(1024)(128)(4,1)}), s8[4194304]{0:T(1024)(128)(4,1)S(1)}, s32[]{:S(2)}) async-start(s8[5529600]{0:T(1024)(128)(4,1)} %bitcast.163), calls=%async_computation.3 | async-start | bytes 8388608
  41.9 5.7 %copy-start.14 = (f32[27,10,1,128]{3,2,1,0:T(1,128)}, f32[27,10,1,128]{3,2,1,0:T(1,128)S(1)}, u32[]{:S(2)}) copy-start(f32[27,10,1,128]{3,2,1,0:T(1,128)S(1)} %pad.52) | copy-start | bytes 414724
  44.8 2.8 copy-start.15
  44.8 1.7 slice-start.1
  46.5 11.4 %copy-start.7 = (f32[10,34,130]{2,1,0:T(8,128)}, f32[10,34,130]{2,1,0:T(8,128)S(1)}, u32[]{:S(2)}) copy-start(f32[10,34,130]{2,1,0:T(8,128)S(1)} %get-tuple-element.128) | copy-start | bytes 530404
  46.5 11.4 %copy-start.10 = (f32[10,34,130]{2,1,0:T(8,128)}, f32[10,34,130]{2,1,0:T(8,128)S(1)}, u32[]{:S(2)}) copy-start(f32[10,34,130]{2,1,0:T(8,128)S(1)} %get-tuple-element.129) | copy-start | bytes 530404
  47.7 10.3 %copy-start.5 = (f32[10,34,130]{2,1,0:T(8,128)}, f32[10,34,130]{2,1,0:T(8,128)S(1)}, u32[]{:S(2)}) copy-start(f32[10,34,130]{2,1,0:T(8,128)S(1)} %maximum_bitcast_fusion) | copy-start | bytes 530404
  91.0 6.6 %copy-start.1 = (f32[24,8,32,128]{3,2,1,0:T(8,128)S(1)}, f32[24,8,32,128]{3,2,1,0:T(8,128)}, u32[]{:S(2)}) copy-start(f32[24,8,32,128]{3,2,1,0:T(8,128)} %fusion.71) | copy-start | bytes 9437188
  101.3 11.1 %collective-permute-start.10 = (f32[24,8,32,1]{2,1,3,0:T(8,128)S(1)}, f32[24,8,32,1]{2,1,3,0:T(8,128)S(1)}, u32[]{:S(2)}, u32[]{:S(2)}) collective-permute-start(f32[24,8,32,1]{2,1,3,0:T(8,128)S(1)} %copy.58), channel_id=1, source_target_pairs={{1,0},{2,1},{3,2},{4,3},{5,4},{6,5},{7,6},{0,7},{9,8},{10,9},{11,1... | collective-permute-start | bytes 73736 | tf_op jit(solution)/shard_map/ppermute | solution.py:24
  103.1 34.8 %collective-permute-start.6 = (f32[24,1,32,128]{3,2,1,0:T(8,128)}, f32[24,1,32,128]{3,2,1,0:T(8,128)}, u32[]{:S(2)}, u32[]{:S(2)}) collective-permute-start(f32[24,1,32,128]{3,2,1,0:T(8,128)} %get-tuple-element.160), channel_id=1, source_target_pairs={{32,0},{64,32},{96,64},{0,96},{33,1},{65,33},{97,65},{1,97},{34,2}... | collective-permute-start | bytes 1179656 | tf_op jit(solution)/shard_map/ppermute | solution.py:24
  106.1 31.9 %collective-permute-start.7 = (f32[24,1,32,128]{3,2,1,0:T(8,128)}, f32[24,1,32,128]{3,2,1,0:T(8,128)}, u32[]{:S(2)}, u32[]{:S(2)}) collective-permute-start(f32[24,1,32,128]{3,2,1,0:T(8,128)} %get-tuple-element.159), channel_id=1, source_target_pairs={{0,32},{32,64},{64,96},{96,0},{1,33},{33,65},{65,97},{97,1},{2,34}... | collective-permute-start | bytes 1179656 | tf_op jit(solution)/shard_map/ppermute | solution.py:23
  109.5 22.1 %collective-permute-start.11 = (f32[24,8,32,1]{2,1,3,0:T(8,128)S(1)}, f32[24,8,32,1]{2,1,3,0:T(8,128)S(1)}, u32[]{:S(2)}, u32[]{:S(2)}) collective-permute-start(f32[24,8,32,1]{2,1,3,0:T(8,128)S(1)} %copy.60), channel_id=1, source_target_pairs={{0,1},{1,2},{2,3},{3,4},{4,5},{5,6},{6,7},{7,0},{8,9},{9,10},{10,1... | collective-permute-start | bytes 73736 | tf_op jit(solution)/shard_map/ppermute | solution.py:23
  109.6 27.1 %collective-permute-start.8 = (f32[24,8,1,128]{3,2,1,0:T(1,128)}, f32[24,8,1,128]{3,2,1,0:T(1,128)}, u32[]{:S(2)}, u32[]{:S(2)}) collective-permute-start(f32[24,8,1,128]{3,2,1,0:T(1,128)} %get-tuple-element.158), channel_id=1, source_target_pairs={{8,0},{16,8},{24,16},{0,24},{9,1},{17,9},{25,17},{1,25},{10,2},{18... | collective-permute-start | bytes 294920 | tf_op jit(solution)/shard_map/ppermute | solution.py:24
  112.4 25.4 %collective-permute-start.9 = (f32[24,8,1,128]{3,2,1,0:T(1,128)}, f32[24,8,1,128]{3,2,1,0:T(1,128)S(1)}, u32[]{:S(2)}, u32[]{:S(2)}) collective-permute-start(f32[24,8,1,128]{3,2,1,0:T(1,128)} %get-tuple-element.157), channel_id=1, source_target_pairs={{0,8},{8,16},{16,24},{24,0},{1,9},{9,17},{17,25},{25,1},{2,10},{10... | collective-permute-start | bytes 294920 | tf_op jit(solution)/shard_map/ppermute | solution.py:23
  113.1 159.3 %all-to-all-start = ((s32[128,1,1,1]{3,2,1,0:T(1,128)}), s32[128,1,1,1]{3,2,1,0:T(1,128)}, u32[]{:S(2)}, u32[]{:S(2)}) async-start(s32[128,1,1,1]{3,2,1,0:T(1,128)} %copy.66), calls=%async_computation | async-start | bytes 131072 | tf_op jit(solution)/shard_map/all_to_all | solution.py:53
  134.1 3.9 copy-start.8
  134.1 3.9 copy-start.11
  134.1 16.9 %slice-start.2 = ((s8[4915200]{0:T(1024)(128)(4,1)}), s8[4194304]{0:T(1024)(128)(4,1)S(1)}, s32[]{:S(2)}) async-start(s8[4915200]{0:T(1024)(128)(4,1)} %bitcast.165), calls=%async_computation.5 | async-start | bytes 8388608
  136.6 14.3 %copy-start.3 = (f32[24,10,34,1]{3,2,1,0:T(8,128)}, f32[24,10,34,1]{3,2,1,0:T(8,128)S(1)}, u32[]{:S(2)}) copy-start(f32[24,10,34,1]{3,2,1,0:T(8,128)S(1)} %pad.59) | copy-start | bytes 97924
  137.8 13.2 %copy-start.16 = (f32[24,10,1,128]{3,2,1,0:T(1,128)}, f32[24,10,1,128]{3,2,1,0:T(1,128)S(1)}, u32[]{:S(2)}) copy-start(f32[24,10,1,128]{3,2,1,0:T(1,128)S(1)} %pad.56) | copy-start | bytes 368644
  137.9 13.1 %copy-start.17 = (f32[24,10,1,128]{3,2,1,0:T(1,128)}, f32[24,10,1,128]{3,2,1,0:T(1,128)S(1)}, u32[]{:S(2)}) copy-start(f32[24,10,1,128]{3,2,1,0:T(1,128)S(1)} %pad.57) | copy-start | bytes 368644
  137.9 13.1 %slice-start.3 = ((s8[4915200]{0:T(1024)(128)(4,1)}), s8[720896]{0:T(1024)(128)(4,1)S(1)}, s32[]{:S(2)}) async-start(s8[4915200]{0:T(1024)(128)(4,1)} %bitcast.165), calls=%async_computation.6 | async-start | bytes 1441792
  137.9 13.1 %copy-start.6 = (f32[10,34,130]{2,1,0:T(8,128)S(1)}, f32[10,34,130]{2,1,0:T(8,128)}, u32[]{:S(2)}) copy-start(f32[10,34,130]{2,1,0:T(8,128)} %copy-done.5) | copy-start | bytes 530404
  183.4 6.6 %copy-start.2 = (f32[24,8,32,128]{3,2,1,0:T(8,128)S(1)}, f32[24,8,32,128]{3,2,1,0:T(8,128)}, u32[]{:S(2)}) copy-start(f32[24,8,32,128]{3,2,1,0:T(8,128)} %fusion.59) | copy-start | bytes 9437188
  194.3 11.8 %collective-permute-start.16 = (f32[24,8,32,1]{2,1,3,0:T(8,128)}, f32[24,8,32,1]{2,1,3,0:T(8,128)}, u32[]{:S(2)}, u32[]{:S(2)}) collective-permute-start(f32[24,8,32,1]{2,1,3,0:T(8,128)} %copy.62), channel_id=1, source_target_pairs={{1,0},{2,1},{3,2},{4,3},{5,4},{6,5},{7,6},{0,7},{9,8},{10,9},{11,1... | collective-permute-start | bytes 73736 | tf_op jit(solution)/shard_map/ppermute | solution.py:24
  195.4 28.2 %collective-permute-start.12 = (f32[24,1,32,128]{3,2,1,0:T(8,128)}, f32[24,1,32,128]{3,2,1,0:T(8,128)}, u32[]{:S(2)}, u32[]{:S(2)}) collective-permute-start(f32[24,1,32,128]{3,2,1,0:T(8,128)} %get-tuple-element.154), channel_id=1, source_target_pairs={{32,0},{64,32},{96,64},{0,96},{33,1},{65,33},{97,65},{1,97},{34,2}... | collective-permute-start | bytes 1179656 | tf_op jit(solution)/shard_map/ppermute | solution.py:24
  197.2 26.4 %collective-permute-start.13 = (f32[24,1,32,128]{3,2,1,0:T(8,128)}, f32[24,1,32,128]{3,2,1,0:T(8,128)}, u32[]{:S(2)}, u32[]{:S(2)}) collective-permute-start(f32[24,1,32,128]{3,2,1,0:T(8,128)} %get-tuple-element.153), channel_id=1, source_target_pairs={{0,32},{32,64},{64,96},{96,0},{1,33},{33,65},{65,97},{97,1},{2,34}... | collective-permute-start | bytes 1179656 | tf_op jit(solution)/shard_map/ppermute | solution.py:23
  201.3 14.2 %collective-permute-start.17 = (f32[24,8,32,1]{2,1,3,0:T(8,128)}, f32[24,8,32,1]{2,1,3,0:T(8,128)}, u32[]{:S(2)}, u32[]{:S(2)}) collective-permute-start(f32[24,8,32,1]{2,1,3,0:T(8,128)} %copy.64), channel_id=1, source_target_pairs={{0,1},{1,2},{2,3},{3,4},{4,5},{5,6},{6,7},{7,0},{8,9},{9,10},{10,1... | collective-permute-start | bytes 73736 | tf_op jit(solution)/shard_map/ppermute | solution.py:23
  203.0 18.4 %collective-permute-start.14 = (f32[24,8,1,128]{3,2,1,0:T(1,128)}, f32[24,8,1,128]{3,2,1,0:T(1,128)}, u32[]{:S(2)}, u32[]{:S(2)}) collective-permute-start(f32[24,8,1,128]{3,2,1,0:T(1,128)} %get-tuple-element.152), channel_id=1, source_target_pairs={{8,0},{16,8},{24,16},{0,24},{9,1},{17,9},{25,17},{1,25},{10,2},{18... | collective-permute-start | bytes 294920 | tf_op jit(solution)/shard_map/ppermute | solution.py:24
  206.1 16.4 %collective-permute-start.15 = (f32[24,8,1,128]{3,2,1,0:T(1,128)}, f32[24,8,1,128]{3,2,1,0:T(1,128)}, u32[]{:S(2)}, u32[]{:S(2)}) collective-permute-start(f32[24,8,1,128]{3,2,1,0:T(1,128)} %get-tuple-element.151), channel_id=1, source_target_pairs={{0,8},{8,16},{16,24},{24,0},{1,9},{9,17},{17,25},{25,1},{2,10},{10... | collective-permute-start | bytes 294920 | tf_op jit(solution)/shard_map/ppermute | solution.py:23
  218.8 4.9 %copy-start.9 = (f32[10,34,130]{2,1,0:T(8,128)S(1)}, f32[10,34,130]{2,1,0:T(8,128)}, u32[]{:S(2)}) copy-start(f32[10,34,130]{2,1,0:T(8,128)} %copy-done.7) | copy-start | bytes 530404
  218.8 4.9 %copy-start.12 = (f32[10,34,130]{2,1,0:T(8,128)S(1)}, f32[10,34,130]{2,1,0:T(8,128)}, u32[]{:S(2)}) copy-start(f32[10,34,130]{2,1,0:T(8,128)} %copy-done.10) | copy-start | bytes 530404
  218.8 17.4 %slice-start.4 = ((s8[4915200]{0:T(1024)(128)(4,1)}), s8[4194304]{0:T(1024)(128)(4,1)S(1)}, s32[]{:S(2)}) async-start(s8[4915200]{0:T(1024)(128)(4,1)} %bitcast.167), calls=%async_computation.7 | async-start | bytes 8388608
  221.4 14.8 %copy-start.4 = (f32[24,10,34,1]{3,2,1,0:T(8,128)}, f32[24,10,34,1]{3,2,1,0:T(8,128)S(1)}, u32[]{:S(2)}) copy-start(f32[24,10,34,1]{3,2,1,0:T(8,128)S(1)} %pad.63) | copy-start | bytes 97924
  222.5 13.7 %copy-start.18 = (f32[24,10,1,128]{3,2,1,0:T(1,128)}, f32[24,10,1,128]{3,2,1,0:T(1,128)S(1)}, u32[]{:S(2)}) copy-start(f32[24,10,1,128]{3,2,1,0:T(1,128)S(1)} %pad.60) | copy-start | bytes 368644
  223.6 12.6 %copy-start.19 = (f32[24,10,1,128]{3,2,1,0:T(1,128)}, f32[24,10,1,128]{3,2,1,0:T(1,128)S(1)}, u32[]{:S(2)}) copy-start(f32[24,10,1,128]{3,2,1,0:T(1,128)S(1)} %pad.61) | copy-start | bytes 368644
  223.6 12.6 %slice-start.5 = ((s8[4915200]{0:T(1024)(128)(4,1)}), s8[720896]{0:T(1024)(128)(4,1)S(1)}, s32[]{:S(2)}) async-start(s8[4915200]{0:T(1024)(128)(4,1)} %bitcast.167), calls=%async_computation.8 | async-start | bytes 1441792
  247.1 22.0 %copy-start.20 = (f32[128,256]{1,0:T(8,128)S(1)}, f32[128,256]{1,0:T(8,128)}, u32[]{:S(2)}) copy-start(f32[128,256]{1,0:T(8,128)} %fusion.87) | copy-start | bytes 393220
  269.1 30.1 %copy-start.21 = (bf16[400,24]{0,1:T(8,128)(2,1)S(1)}, bf16[400,24]{0,1:T(8,128)(2,1)}, u32[]{:S(2)}) copy-start(bf16[400,24]{0,1:T(8,128)(2,1)} %param.24) | copy-start | bytes 57604
  269.1 30.1 %copy-start.23 = (f32[24]{0:T(128)S(1)}, f32[24]{0:T(128)}, u32[]{:S(2)}) copy-start(f32[24]{0:T(128)} %param.25) | copy-start | bytes 292
  269.1 30.1 %copy-start.28 = (bf16[800,400]{0,1:T(8,128)(2,1)S(1)}, bf16[800,400]{0,1:T(8,128)(2,1)}, u32[]{:S(2)}) copy-start(bf16[800,400]{0,1:T(8,128)(2,1)} %param.22) | copy-start | bytes 1920004
  269.1 30.1 %copy-start.29 = (bf16[24,1600]{1,0:T(8,128)(2,1)S(1)}, bf16[24,1600]{1,0:T(8,128)(2,1)}, u32[]{:S(2)}) copy-start(bf16[24,1600]{1,0:T(8,128)(2,1)} %param.18) | copy-start | bytes 230404
  269.2 30.1 %copy-start.30 = (f32[1600]{0:T(1024)S(1)}, f32[1600]{0:T(1024)}, u32[]{:S(2)}) copy-start(f32[1600]{0:T(1024)} %param.19) | copy-start | bytes 19204
  269.2 30.1 %copy-start.31 = (f32[800]{0:T(1024)S(1)}, f32[800]{0:T(1024)}, u32[]{:S(2)}) copy-start(f32[800]{0:T(1024)} %param.21) | copy-start | bytes 9604
  269.2 30.1 %copy-start.32 = (f32[400]{0:T(512)S(1)}, f32[400]{0:T(512)}, u32[]{:S(2)}) copy-start(f32[400]{0:T(512)} %param.23) | copy-start | bytes 4804
  272.5 26.5 %all-to-all-start.1 = ((bf16[128,1,1,1,24,128]{5,4,3,2,1,0:T(8,128)(2,1)}), bf16[128,1,1,1,24,128]{5,4,3,2,1,0:T(8,128)(2,1)S(1)}, u32[]{:S(2)}, u32[]{:S(2)}) async-start(bf16[128,1,1,1,24,128]{5,4,3,2,1,0:T(8,128)(2,1)} %copy.69), calls=%async_computation.1 | async-start | bytes 1572864 | tf_op jit(solution)/shard_map/all_to_all | solution.py:53
  345.9 29.6 %all-to-all-start.2 = ((f32[128,1,1,1,24,128]{5,4,3,2,1,0:T(8,128)}), f32[128,1,1,1,24,128]{5,4,3,2,1,0:T(8,128)S(1)}, u32[]{:S(2)}, u32[]{:S(2)}) async-start(f32[128,1,1,1,24,128]{5,4,3,2,1,0:T(8,128)} %copy.73), calls=%async_computation.2 | async-start | bytes 3145728 | tf_op jit(solution)/shard_map/all_to_all | solution.py:53
  387.6 25.7 %collective-permute-start.18 = (f32[24,1,32,128]{3,2,1,0:T(8,128)}, f32[24,1,32,128]{3,2,1,0:T(8,128)}, u32[]{:S(2)}, u32[]{:S(2)}) collective-permute-start(f32[24,1,32,128]{3,2,1,0:T(8,128)} %get-tuple-element.146), channel_id=1, source_target_pairs={{32,0},{64,32},{96,64},{0,96},{33,1},{65,33},{97,65},{1,97},{34,2}... | collective-permute-start | bytes 1179656 | tf_op jit(solution)/shard_map/ppermute | solution.py:24
  388.5 24.7 %collective-permute-start.19 = (f32[24,1,32,128]{3,2,1,0:T(8,128)S(1)}, f32[24,1,32,128]{3,2,1,0:T(8,128)}, u32[]{:S(2)}, u32[]{:S(2)}) collective-permute-start(f32[24,1,32,128]{3,2,1,0:T(8,128)S(1)} %get-tuple-element.145), channel_id=1, source_target_pairs={{0,32},{32,64},{64,96},{96,0},{1,33},{33,65},{65,97},{97,1},{2,34}... | collective-permute-start | bytes 1179656 | tf_op jit(solution)/shard_map/ppermute | solution.py:23
  396.2 6.6 %collective-permute-start.22 = (f32[24,8,32,1]{2,1,3,0:T(8,128)}, f32[24,8,32,1]{2,1,3,0:T(8,128)}, u32[]{:S(2)}, u32[]{:S(2)}) collective-permute-start(f32[24,8,32,1]{2,1,3,0:T(8,128)} %copy.76), channel_id=1, source_target_pairs={{1,0},{2,1},{3,2},{4,3},{5,4},{6,5},{7,6},{0,7},{9,8},{10,9},{11,1... | collective-permute-start | bytes 73736 | tf_op jit(solution)/shard_map/ppermute | solution.py:24
  402.0 6.0 %collective-permute-start.23 = (f32[24,8,32,1]{2,1,3,0:T(8,128)}, f32[24,8,32,1]{2,1,3,0:T(8,128)}, u32[]{:S(2)}, u32[]{:S(2)}) collective-permute-start(f32[24,8,32,1]{2,1,3,0:T(8,128)} %copy.78), channel_id=1, source_target_pairs={{0,1},{1,2},{2,3},{3,4},{4,5},{5,6},{6,7},{7,0},{8,9},{9,10},{10,1... | collective-permute-start | bytes 73736 | tf_op jit(solution)/shard_map/ppermute | solution.py:23
  402.1 9.2 %collective-permute-start.20 = (f32[24,8,1,128]{3,2,1,0:T(1,128)}, f32[24,8,1,128]{3,2,1,0:T(1,128)}, u32[]{:S(2)}, u32[]{:S(2)}) collective-permute-start(f32[24,8,1,128]{3,2,1,0:T(1,128)} %get-tuple-element.148), channel_id=1, source_target_pairs={{8,0},{16,8},{24,16},{0,24},{9,1},{17,9},{25,17},{1,25},{10,2},{18... | collective-permute-start | bytes 294920 | tf_op jit(solution)/shard_map/ppermute | solution.py:24
  402.8 9.4 %collective-permute-start.21 = (f32[24,8,1,128]{3,2,1,0:T(1,128)}, f32[24,8,1,128]{3,2,1,0:T(1,128)}, u32[]{:S(2)}, u32[]{:S(2)}) collective-permute-start(f32[24,8,1,128]{3,2,1,0:T(1,128)} %get-tuple-element.147), channel_id=1, source_target_pairs={{0,8},{8,16},{16,24},{24,0},{1,9},{9,17},{17,25},{25,1},{2,10},{10... | collective-permute-start | bytes 294920 | tf_op jit(solution)/shard_map/ppermute | solution.py:23
  404.8 8.5 %copy-start.27 = (f32[24]{0:T(128)S(1)}, f32[24]{0:T(128)}, u32[]{:S(2)}) copy-start(f32[24]{0:T(128)} %param.17) | copy-start | bytes 292
  (2 other events, 1.7 us)

commit v2 on v0

v2 whole, which is shorter than its diff:
```python
import functools

import jax
import jax.numpy as jnp
from jax import lax
from jax.experimental import pallas as pl
from jax.experimental.pallas import tpu as pltpu
from jax.sharding import PartitionSpec as P

OWNED = 32
GROUP = 4
ALL = ("gx", "gy", "gz")
F32, BF16 = jnp.float32, jnp.bfloat16
TN = (((0,), (0,)), ((), ()))
NT = (((1,), (1,)), ((), ()))


def one_hot_ends():
    rows = lax.broadcasted_iota(jnp.int32, (16, 128), 0)
    lanes = lax.broadcasted_iota(jnp.int32, (16, 128), 1)
    return (((rows == 0) & (lanes == 0)) | ((rows == 1) & (lanes == 127))).astype(F32).astype(BF16)


def z_columns(low, high):
    rows = lax.broadcasted_iota(jnp.int32, (16, 256), 0)
    pair = jnp.where(rows == 0, low, jnp.where(rows == 1, high, 0.0)).astype(BF16)
    return lax.dot_general(pair, one_hot_ends(), TN, preferred_element_type=F32)


def z_ends(cells):
    return lax.dot_general(one_hot_ends(), cells.astype(BF16), NT, preferred_element_type=F32)


def shifted(centre, y_low, y_high, z_col):
    rows = lax.broadcasted_iota(jnp.int32, (32, 128), 0)
    lanes = lax.broadcasted_iota(jnp.int32, (32, 128), 1)
    y_next = jnp.where(rows == 31, y_high, pltpu.roll(centre, 31, 0))
    y_prev = jnp.where(rows == 0, y_low, pltpu.roll(centre, 1, 0))
    z_next = jnp.where(lanes == 127, z_col, pltpu.roll(centre, 127, 1))
    z_prev = jnp.where(lanes == 0, z_col, pltpu.roll(centre, 1, 1))
    return y_next, y_prev, z_next, z_prev


def put_faces(new, f, x, xf, xl, yf, yl):
    if x == 0:
        xf[f] = new.astype(BF16)
    if x == 7:
        xl[f] = new.astype(BF16)
    yf[f, x : x + 1] = new[0:1]
    yl[f, x : x + 1] = new[31:32]


def put_z_faces(out, f, zf, zl):
    ends = z_ends(out[f].reshape(256, 128))
    zf[f] = ends[0:1]
    zl[f] = ends[1:2]


CODE_UNIT = 32.0
CODE_SCALE = 32767.0 / 38.0 / 0.6931471805599453


def coded(value):
    level = (jnp.log(1.0 + CODE_UNIT * jnp.abs(value)) * CODE_SCALE + 0.5).astype(jnp.int32)
    return jnp.where(value < 0.0, -level, level).astype(jnp.int16)


def decoded(code):
    level = code.astype(jnp.int32).astype(F32)
    size = (jnp.exp(jnp.abs(level) * (1.0 / CODE_SCALE)) - 1.0) * (1.0 / CODE_UNIT)
    return jnp.where(level < 0.0, -size, size)


def prep_kernel(fields, velocity, xf, xl, yf, yl, zf, zl):
    def put(ref, i, f):
        xf[f] = ref[i, 0].astype(BF16)
        xl[f] = ref[i, 7].astype(BF16)
        for x in range(8):
            yf[f, x : x + 1] = ref[i, x, 0:1]
            yl[f, x : x + 1] = ref[i, x, 31:32]
        ends = z_ends(ref[i].reshape(256, 128))
        zf[f] = ends[0:1]
        zl[f] = ends[1:2]

    for f in range(24):
        put(fields, f, f)
    xf[24] = velocity[0, 0].astype(BF16)
    xl[24] = velocity[0, 7].astype(BF16)
    for x in range(8):
        yf[24, x : x + 1] = velocity[1, x, 0:1]
        yl[24, x : x + 1] = velocity[1, x, 31:32]
    ends = z_ends(velocity[2].reshape(256, 128))
    zf[24] = ends[0:1]
    zl[24] = ends[1:2]


def section_kernel(kind, *refs):
    refs = list(refs)
    q = refs.pop(0)
    start = q if kind == 1 else refs.pop(0)
    xlo, xhi, ylo, yhi, zlo, zhi = refs[:6]
    del refs[:6]
    if kind == 1:
        velocity, vxlo, vxhi, vylo, vyhi, vzlo, vzhi = refs[:7]
        del refs[:7]
    else:
        coef = refs.pop(0)
    if kind == 3:
        routing = refs.pop(0)
    out = refs.pop(0)
    if kind == 1:
        coef = refs.pop(0)
    if kind < 3:
        xf, xl, yf, yl, zf, zl = refs[:6]
        del refs[:6]
    else:
        outgoing = refs.pop(0)
    zcol = refs.pop(0)

    if kind == 1:

        @pl.when(pl.program_id(0) == 0)
        def _():
            zcol[0] = z_columns(vzlo[0], vzhi[0])
            for x in range(8):
                before = vxlo[0].astype(F32) if x == 0 else velocity[0, x - 1]
                after = vxhi[0].astype(F32) if x == 7 else velocity[0, x + 1]
                y_next, y_prev, _, _ = shifted(
                    velocity[1, x], vylo[0, x : x + 1], vyhi[0, x : x + 1], velocity[1, x]
                )
                _, _, z_next, z_prev = shifted(
                    velocity[2, x], vylo[0, x : x + 1], vyhi[0, x : x + 1], zcol[0, 32 * x : 32 * x + 32]
                )
                coef[0, x] = 0.05 - 0.5 * after
                coef[1, x] = 0.05 + 0.5 * before
                coef[2, x] = 0.05 - 0.5 * y_next
                coef[3, x] = 0.05 + 0.5 * y_prev
                coef[4, x] = 0.05 - 0.5 * z_next
                coef[5, x] = 0.05 + 0.5 * z_prev

    for f in range(GROUP):
        zcol[f] = z_columns(zlo[f], zhi[f])
    for x in range(8):
        ce = [coef[i, x] for i in range(6)]
        for f in range(GROUP):
            centre = q[f, x]
            before = xlo[f].astype(F32) if x == 0 else q[f, x - 1]
            after = xhi[f].astype(F32) if x == 7 else q[f, x + 1]
            y_next, y_prev, z_next, z_prev = shifted(
                centre, ylo[f, x : x + 1], yhi[f, x : x + 1], zcol[f, 32 * x : 32 * x + 32]
            )
            moved = (
                0.7 * centre
                + (ce[0] * after + ce[1] * before)
                + (ce[2] * y_next + ce[3] * y_prev)
                + (ce[4] * z_next + ce[5] * z_prev)
            )
            if kind == 1:
                new = moved
            elif kind == 2:
                new = 0.75 * start[f, x] + 0.25 * moved
            else:
                new = (1.0 / 3.0) * start[f, x] + (2.0 / 3.0) * moved
            out[f, x] = new
            if kind < 3:
                put_faces(new, f, x, xf, xl, yf, yl)
    for f in range(GROUP):
        if kind < 3:
            put_z_faces(out, f, zf, zl)
        else:
            blocks = out[f].reshape(256, 128).astype(BF16)
            outgoing[:, 128 * f : 128 * f + 128] = jnp.dot(
                routing[...], blocks, preferred_element_type=F32
            ).astype(BF16)


def react_kernel(flowed, back, table, out, xf, xl, yf, yl, zf, zl):
    for f in range(GROUP):
        value = decoded(back[:, 128 * f : 128 * f + 128])
        coarse = value.astype(BF16)
        rest = (value - coarse.astype(F32)).astype(BF16)
        added = jnp.dot(table[...], coarse, preferred_element_type=F32)
        added += jnp.dot(table[...], rest, preferred_element_type=F32)
        for x in range(8):
            new = flowed[f, x] + added[32 * x : 32 * x + 32]
            out[f, x] = new
            put_faces(new, f, x, xf, xl, yf, yl)
        put_z_faces(out, f, zf, zl)


def diffuse_kernel(rates, q, xlo, xhi, ylo, yhi, zlo, zhi, out, zcol):
    base = pl.program_id(0) * GROUP
    for f in range(GROUP):
        zcol[f] = z_columns(zlo[f], zhi[f])
        rate = rates[base + f]
        for x in range(8):
            centre = q[f, x]
            before = xlo[f].astype(F32) if x == 0 else q[f, x - 1]
            after = xhi[f].astype(F32) if x == 7 else q[f, x + 1]
            y_next, y_prev, z_next, z_prev = shifted(
                centre, ylo[f, x : x + 1], yhi[f, x : x + 1], zcol[f, 32 * x : 32 * x + 32]
            )
            spread = (after + before) + (y_next + y_prev) + (z_next + z_prev) - 6.0 * centre
            out[f, x] = centre + rate * spread


def network_kernel(slots, arrived, w1, b1, w2, b2, w3, b3, w4, b4, out, heat):
    step = pl.program_id(0)

    @pl.when(step == 0)
    def _():
        out[...] = jnp.zeros_like(out)
        heat[...] = jnp.zeros_like(heat)

    def activated(weights, bias, cells):
        half = jnp.dot(weights[...], cells, preferred_element_type=F32)
        half = half + jnp.concatenate([bias[...], bias[...]], axis=1)
        return (half + half * jnp.tanh(half)).astype(BF16)

    first, second = slots[2 * step], slots[2 * step + 1]
    cells = jnp.concatenate([arrived[first], arrived[second]], axis=1)
    hidden = activated(w1, b1, cells)
    hidden = activated(w2, b2, hidden)
    hidden = activated(w3, b3, hidden)
    result = jnp.dot(w4[...], hidden, preferred_element_type=F32)
    result = result + jnp.concatenate([b4[...], b4[...]], axis=1)
    codes = coded(result)
    out[first] = codes[:, :128]
    out[second] = codes[:, 128:]
    squares = result[0:8] * result[0:8]
    heat[...] += squares[:, :128] + squares[:, 128:]


def params(mib):
    return pltpu.CompilerParams(vmem_limit_bytes=mib * 1024 * 1024)


def sds(shape, dtype):
    return jax.ShapeDtypeStruct(shape, dtype)


def whole(shape):
    return pl.BlockSpec(shape, lambda *_: (0,) * len(shape))


def at(shape, place):
    return pl.BlockSpec(shape, lambda *_: place)


BRICK = pl.BlockSpec((GROUP, 8, 32, 128), lambda g, *_: (g, 0, 0, 0))
X_FACE = pl.BlockSpec((GROUP, 32, 128), lambda g, *_: (g, 0, 0))
Y_FACE = pl.BlockSpec((GROUP, 8, 128), lambda g, *_: (g, 0, 0))
Z_FACE = pl.BlockSpec((GROUP, 1, 256), lambda g, *_: (g, 0, 0))
FACES = [X_FACE, X_FACE, Y_FACE, Y_FACE, Z_FACE, Z_FACE]
SLOTS = pl.BlockSpec((128, GROUP * 128), lambda g, *_: (0, g))


def face_shapes(count):
    return [
        sds((count, 32, 128), BF16),
        sds((count, 32, 128), BF16),
        sds((count, 8, 128), F32),
        sds((count, 8, 128), F32),
        sds((count, 1, 256), F32),
        sds((count, 1, 256), F32),
    ]


def exchange(faces):
    got = []
    for axis, first, last in zip(ALL, faces[0::2], faces[1::2]):
        n = lax.axis_size(axis)
        got.append(lax.ppermute(last, axis, [(i, (i + 1) % n) for i in range(n)]))
        got.append(lax.ppermute(first, axis, [((i + 1) % n, i) for i in range(n)]))
    return got


def section(kind, args, in_specs, out_shapes, out_specs):
    return pl.pallas_call(
        functools.partial(section_kernel, kind),
        grid=(24 // GROUP,),
        in_specs=in_specs,
        out_specs=out_specs,
        out_shape=out_shapes,
        scratch_shapes=[pltpu.VMEM((GROUP, 256, 128), F32)],
        compiler_params=params(24),
    )(*args)


def swap(tiles):
    return lax.all_to_all(tiles, ALL, split_axis=0, concat_axis=0, tiled=True)


def local(
    fields,
    velocity,
    diffusivity,
    weight_in,
    bias_in,
    weight_mid,
    bias_mid,
    weight_low,
    bias_low,
    weight_out,
    bias_out,
    react_list,
    owner_table,
):
    brick = sds(fields.shape, F32)
    ids, owners = react_list[0], owner_table[0]
    everyone = lax.all_gather(owner_table, ALL, axis=0, tiled=True)
    me = lax.axis_index(ALL)
    sends = jnp.any(everyone == me, axis=1)
    numbers = jnp.arange(128, dtype=jnp.int32)
    rank = jnp.sum(jnp.where((numbers[None, :] < numbers[:, None]) & sends[None, :], 1, 0), axis=1)
    slots = jnp.sum(
        jnp.where((rank[None, :] == numbers[:OWNED, None]) & sends[None, :], numbers[None, :], 0), axis=1
    ).astype(jnp.int32)
    slot_hot = (owners[None, :] == numbers[:, None]).astype(BF16)
    block_hot = (ids[:, None] == jnp.arange(256, dtype=jnp.int32)[None, :]).astype(BF16)
    routing = jnp.dot(slot_hot, block_hot, preferred_element_type=F32).astype(BF16)
    table = lax.dot_general(block_hot, slot_hot, (((0,), (1,)), ((), ())), preferred_element_type=F32).astype(BF16)

    half = jnp.asarray(0.5, BF16)
    w1, w2, w3, w4 = (weight_in * half).T, (weight_mid * half).T, (weight_low * half).T, weight_out.T
    b1, b2, b3, b4 = (
        jnp.broadcast_to((s * b)[:, None], (b.shape[0], 128))
        for s, b in ((0.5, bias_in), (0.5, bias_mid), (0.5, bias_low), (1.0, bias_out))
    )

    faces = pl.pallas_call(
        prep_kernel, out_shape=face_shapes(25), compiler_params=params(24)
    )(fields, velocity)
    halo = exchange(faces)
    own_halo = [
        at((1, 32, 128), (24, 0, 0)),
        at((1, 32, 128), (24, 0, 0)),
        at((1, 8, 128), (24, 0, 0)),
        at((1, 8, 128), (24, 0, 0)),
        at((1, 1, 256), (24, 0, 0)),
        at((1, 1, 256), (24, 0, 0)),
    ]
    one, coef, *faces = section(
        1,
        (fields, *halo, velocity, *halo),
        [BRICK, *FACES, whole((3, 8, 32, 128)), *own_halo],
        [brick, sds((6, 8, 32, 128), F32), *face_shapes(24)],
        [BRICK, whole((6, 8, 32, 128)), *FACES],
    )
    two, *faces = section(
        2,
        (one, fields, *exchange(faces), coef),
        [BRICK, BRICK, *FACES, whole((6, 8, 32, 128))],
        [brick, *face_shapes(24)],
        [BRICK, *FACES],
    )
    flowed, outgoing = section(
        3,
        (two, fields, *exchange(faces), coef, routing),
        [BRICK, BRICK, *FACES, whole((6, 8, 32, 128)), whole((128, 256))],
        [brick, sds((128, 24 * 128), BF16)],
        [BRICK, SLOTS],
    )
    arrived = swap(outgoing.reshape(128, 24, 128))
    returning, heat = pl.pallas_call(
        network_kernel,
        grid_spec=pltpu.PrefetchScalarGridSpec(
            num_scalar_prefetch=1,
            grid=(OWNED // 2,),
            in_specs=[
                whole(a.shape) for a in (arrived, w1, b1, w2, b2, w3, b3, w4, b4)
            ],
            out_specs=[whole((128, 24, 128)), whole((8, 128))],
        ),
        out_shape=[sds((128, 24, 128), jnp.int16), sds((8, 128), F32)],
        compiler_params=params(40),
    )(slots, arrived, w1, b1, w2, b2, w3, b3, w4, b4)
    owner_activity = (jnp.sum(heat[0]) / (8.0 * 128.0)).reshape(1)
    back = swap(returning).reshape(128, 24 * 128)
    reacted, *faces = pl.pallas_call(
        react_kernel,
        grid=(24 // GROUP,),
        in_specs=[BRICK, SLOTS, whole((256, 128))],
        out_specs=[BRICK, *FACES],
        out_shape=[brick, *face_shapes(24)],
        compiler_params=params(24),
    )(flowed, back, table)
    updated = pl.pallas_call(
        diffuse_kernel,
        grid=(24 // GROUP,),
        in_specs=[pl.BlockSpec(memory_space=pltpu.SMEM), BRICK, *FACES],
        out_specs=BRICK,
        out_shape=brick,
        scratch_shapes=[pltpu.VMEM((GROUP, 256, 128), F32)],
        compiler_params=params(24),
    )(diffusivity, reacted, *exchange(faces))
    return (updated, owner_activity)


def solution(mesh):
    return jax.shard_map(
        local,
        mesh=mesh,
        in_specs=(
            P(None, *ALL),
            P(None, *ALL),
            *(P(),) * 9,
            P(ALL, None),
            P(ALL, None),
        ),
        out_specs=(P(None, *ALL), P(ALL)),
        check_vma=False,
    )
```

time: 428 us -> 212 us (0.50)
  other arithmetic: 153 us -> 9.66 us
  local copies, waits for them, and re-layouts: 121 us -> 22.4 us
  Pallas kernels: 0 us -> 63.2 us
  matrix products: 52.1 us -> 1.11 us
  blocking collectives: 0 us -> 30.2 us
  starting transfers between devices: 55.8 us -> 45.1 us
    pallas_call x0 -> x7, Pallas kernels: none -> 63.2 us  [the longest x1 34.9 us: local(): pl.pallas_call(network_kernel, grid_spec=pltpu.PrefetchScalarGridSpec(num...]
    mul x7 -> x3, other arithmetic: 59.9 us -> 0.01 us  [local(): s * b]
    add x4 -> x0, other arithmetic: 56.4 us -> none  [the longest x1 23.1 us: local(): section_one = fields + transport(padded[:field_count], speeds)]
    slice x20 -> x0, local copies, waits for them, and re-layouts: 53.9 us -> none  [the longest x15 37.2 us: extended(): last = lax.slice_in_dim(value, length - width, length, axis=dim)]
    dot_general x17 -> x2, matrix products: 52.1 us -> 1.11 us  [the longest x1 0.85 us: local(): jnp.dot(slot_hot, block_hot, preferred_element_type=F32).astype(BF16)]
    pad x14 -> x0, local copies, waits for them, and re-layouts: 31.5 us -> none  [the longest x7 18.7 us: extended(): jnp.pad(high, around)]
    all_gather x0 -> x1, blocking collectives: none -> 30.2 us  [local(): everyone = lax.all_gather(owner_table, ALL, axis=0, tiled=True)]
    ppermute x8 -> x0, local copies, waits for them, and re-layouts: 24.8 us -> none  [the longest x4 12.4 us: extended(): lax.ppermute(last, axis, up)]
  transfers between devices with their start and end apart: 27 -> 26, of which waited for: 2 -> 5; matrix products, arithmetic and copies ran while one was open for 46% -> 6% of each run, Pallas kernels for 0% -> 0%
where the time goes in v2:
time: 212 us; the launch traced here: 210 us
  Pallas kernels  63.2 us (30%)
  starting transfers between devices  45.1 us (21%)
  waiting for transfers between devices  35.9 us (17%)
  blocking collectives  30.2 us (14%)
  local copies, waits for them, and re-layouts  22.4 us (11%)
  other arithmetic  9.66 us (5%)
  between operations  2.79 us (1%)
    pallas_call x1, Pallas kernels, local(): pl.pallas_call(network_kernel, grid_spec=pltpu.PrefetchScalarGridSpec(num...  34.9 us
    all_gather x1, blocking collectives, local(): everyone = lax.all_gather(owner_table, ALL, axis=0, tiled=True)  30.2 us
    all_to_all x2, waiting for transfers between devices, swap(): return lax.all_to_all(tiles, ALL, split_axis=0, concat_axis=0, tiled=True)  30.1 us
    ppermute x12, starting transfers between devices, exchange(): got.append(lax.ppermute(first, axis, [((i + 1) % n, i) for i in range(n)]))  22.6 us
    unnamed x67, local copies, waits for them, and re-layouts  21.8 us
    pallas_call x3, Pallas kernels, section(): pl.pallas_call(functools.partial(section_kernel, kind), grid=(24 // GROUP...  14.9 us
    all_to_all x2, starting transfers between devices, swap(): return lax.all_to_all(tiles, ALL, split_axis=0, concat_axis=0, tiled=True)  12.4 us
    ppermute x12, starting transfers between devices, exchange(): got.append(lax.ppermute(last, axis, [(i, (i + 1) % n) for i in range(n)]))  10.1 us
  transfers between devices with their start and end apart: 26, of which 5 were waited for; matrix products, arithmetic and copies ran while one was open for 6% of the time, Pallas kernels for 0%

profile of v2, /device:TPU:1, one launch (start us, length us, event | category | flops | bytes accessed | tf_op | source)
XLA Modules:
  0.0 210.4 jit_solution(7197256125074073200)
XLA Ops:
  0.6 1.9 copy-done
  2.5 1.0 copy-done.10
  3.5 1.4 shard_map.140
  4.9 0.6 copy-done.20
  5.5 2.0 collective-permute-start
  7.5 1.3 collective-permute-start.1
  8.8 1.8 collective-permute-start.2
  10.6 2.1 %collective-permute-start.3 = (f32[25,8,128]{2,1,0:T(8,128)}, f32[25,8,128]{2,1,0:T(8,128)}, u32[]{:S(2)}, u32[]{:S(2)}) collective-permute-start(f32[25,8,128]{2,1,0:T(8,128)} %get-tuple-element.37), channel_id=1, source_target_pairs={{8,0},{16,8},{24,16},{0,24},{9,1},{17,9},{25,17},{1,25},{10,2},{18... | collective-permute-start | bytes 307208 | tf_op jit(solution)/shard_map/ppermute | solution.py:274
  12.7 2.7 %collective-permute-start.4 = (f32[25,1,256]{2,1,0:T(1,128)}, f32[25,1,256]{2,1,0:T(1,128)}, u32[]{:S(2)}, u32[]{:S(2)}) collective-permute-start(f32[25,1,256]{2,1,0:T(1,128)} %get-tuple-element.38), channel_id=1, source_target_pairs={{0,1},{1,2},{2,3},{3,4},{4,5},{5,6},{6,7},{7,0},{8,9},{9,10},{10,1... | collective-permute-start | bytes 76808 | tf_op jit(solution)/shard_map/ppermute | solution.py:273
  15.4 1.8 copy.18
  17.3 1.8 multiply_bitcast_fusion.2.w1
  19.1 2.1 multiply_bitcast_fusion.1.w3
  21.2 0.8 convolution_convert_fusion.1.refs_9_
  22.0 2.6 %collective-permute-done.5.refs_6_.refs_13_ = f32[25,1,256]{2,1,0:T(1,128)S(1)} collective-permute-done((f32[25,1,256]{2,1,0:T(1,128)}, f32[25,1,256]{2,1,0:T(1,128)S(1)}, u32[]{:S(2)}, u32[]{:S(2)}) %collective-permute-start.5) | collective-permute-done | bytes 25632 | tf_op jit(solution)/shard_map/ppermute | solution.py:274
  24.7 5.2 %shard_map.141 = (f32[24,8,32,128]{3,2,1,0:T(8,128)S(1)}, f32[6,8,32,128]{3,2,1,0:T(8,128)S(1)}, bf16[24,32,128]{2,1,0:T(8,128)(2,1)S(1)}, bf16[24,32,128]{2,1,0...) custom-call(f32[24,8,32,128]{3,2,1,0:T(8,128)S(1)} %copy-done.1, ...), custom_call_target="tpu_custom_call" | custom-call | tf_op jit(solution)/shard_map/pallas_call | solution.py:279
  30.0 2.7 %collective-permute-start.7 = (bf16[24,32,128]{2,1,0:T(8,128)(2,1)S(1)}, bf16[24,32,128]{2,1,0:T(8,128)(2,1)S(1)}, u32[]{:S(2)}, u32[]{:S(2)}) collective-permute-start(bf16[24,32,128]{2,1,0:T(8,128)(2,1)S(1)} %get-tuple-element.42), channel_id=1, source_target_pairs={{32,0},{64,32},{96,64},{0,96},{33,1},{65,33},{97,65},{1,97},{34,2}... | collective-permute-start | bytes 589832 | tf_op jit(solution)/shard_map/ppermute | solution.py:274
  32.7 2.7 %collective-permute-start.9 = (f32[24,8,128]{2,1,0:T(8,128)S(1)}, f32[24,8,128]{2,1,0:T(8,128)S(1)}, u32[]{:S(2)}, u32[]{:S(2)}) collective-permute-start(f32[24,8,128]{2,1,0:T(8,128)S(1)} %get-tuple-element.44), channel_id=1, source_target_pairs={{8,0},{16,8},{24,16},{0,24},{9,1},{17,9},{25,17},{1,25},{10,2},{18... | collective-permute-start | bytes 294920 | tf_op jit(solution)/shard_map/ppermute | solution.py:274
  35.3 1.5 collective-permute-start.11
  36.9 2.7 %collective-permute-done.11.refs_7_ = f32[24,1,256]{2,1,0:T(1,128)S(1)} collective-permute-done((f32[24,1,256]{2,1,0:T(1,128)S(1)}, f32[24,1,256]{2,1,0:T(1,128)S(1)}, u32[]{:S(2)}, u32[]{:S(2)}) %collective-permute-start.11) | collective-permute-done | bytes 24608 | tf_op jit(solution)/shard_map/ppermute | solution.py:274
  39.6 4.9 %shard_map.142 = (f32[24,8,32,128]{3,2,1,0:T(8,128)S(1)}, bf16[24,32,128]{2,1,0:T(8,128)(2,1)}, bf16[24,32,128]{2,1,0:T(8,128)(2,1)}, f32[24,8,128]{2,1,0:T(8,12...) custom-call(f32[24,8,32,128]{3,2,1,0:T(8,128)S(1)} %get-tuple-element.40.refs_0_, ...), custom_call_target="tpu_custom_call" | custom-call | tf_op jit(solution)/shard_map/pallas_call | solution.py:279
  44.5 1.7 copy-done.6
  46.2 0.6 copy-done.21
  46.8 0.6 copy-done.22
  47.4 0.6 copy-done.18
  48.1 2.0 collective-permute-start.13
  50.1 1.6 collective-permute-start.16
  51.7 30.2 %all-gather = s32[128,1,96]{2,1,0:T(1,128)S(1)} all-gather(s32[1,1,96]{2,1,0:T(1,128)} %bitcast.22), channel_id=1, replica_groups=mesh['gx'=4,'gy'=4,'gz'=8] {'gx','gy','gz'}, dimensions={0}, use_global_device_ids=true | all-gather | bytes 49536 | tf_op jit(solution)/shard_map/all_gather | solution.py:311
  81.9 2.7 %collective-permute-start.15 = (f32[24,8,128]{2,1,0:T(8,128)}, f32[24,8,128]{2,1,0:T(8,128)S(1)}, u32[]{:S(2)}, u32[]{:S(2)}) collective-permute-start(f32[24,8,128]{2,1,0:T(8,128)} %copy-done.18), channel_id=1, source_target_pairs={{8,0},{16,8},{24,16},{0,24},{9,1},{17,9},{25,17},{1,25},{10,2},{18... | collective-permute-start | bytes 294920 | tf_op jit(solution)/shard_map/ppermute | solution.py:274
  84.6 0.7 collective-permute-start.17
  85.3 2.9 %compare_reduce_fusion = pred[128]{0:T(512)(128)(4,1)} fusion(s32[128,1,96]{2,1,0:T(1,128)S(1)} %all-gather, s32[]{:T(128)S(6)} %add.7), kind=kLoop, calls=%fused_computation.6 | loop fusion | flops 24448 | bytes 49284 | tf_op jit(solution)/shard_map/reduce_or | solution.py:313
  88.2 1.1 copy-done.3
  89.3 1.9 copy-done.7
  91.2 0.8 copy-done.13
  92.0 4.8 %shard_map.143 = (f32[24,8,32,128]{3,2,1,0:T(8,128)S(1)}, bf16[128,3072]{1,0:T(8,128)(2,1)S(1)}) custom-call(f32[24,8,32,128]{3,2,1,0:T(8,128)S(1)} %copy-done.7, f32[24,8,32,128]{3,2,1,0:T(8,128)S(1)} %copy-done.1, bf16[24,32,128]{2,1,0:T(8,128)(2,1)S(1)} %collective-permute-done.12.refs_2_, bf16[24,32,128]{2,1,0:T(8,128)(2,1)S(1)} %collective-permute-done.13.refs_3_, ...), custom_call_target="tpu_custom_call" | custom-call | tf_op jit(solution)/shard_map/pallas_call | solution.py:279
  96.8 1.7 copy-done.4
  98.5 1.0 copy.20
  99.5 7.7 %all-to-all-start = ((bf16[128,24,128]{2,1,0:T(8,128)(2,1)}), bf16[128,24,128]{2,1,0:T(8,128)(2,1)S(1)}, u32[]{:S(2)}, u32[]{:S(2)}) async-start(bf16[128,24,128]{2,1,0:T(8,128)(2,1)} %bitcast.9), calls=%async_computation | async-start | bytes 1572864 | tf_op jit(solution)/shard_map/all_to_all | solution.py:291
  107.3 0.1 select_reduce_fusion
  107.4 0.2 select_reduce_fusion.1.slots
  107.6 2.0 multiply_bitcast_fusion.w2
  109.6 14.0 %all-to-all-done.arrived = bf16[128,24,128]{2,1,0:T(8,128)(2,1)S(1)} async-done(((bf16[128,24,128]{2,1,0:T(8,128)(2,1)}), bf16[128,24,128]{2,1,0:T(8,128)(2,1)S(1)}, u32[]{:S(2)}, u32[]{:S(2)}) %all-to-all-start) | async-done | bytes 786464 | tf_op jit(solution)/shard_map/all_to_all | solution.py:291
  123.6 0.3 broadcast_in_dim.32.b1
  123.9 0.2 broadcast_in_dim.33.b2
  124.1 0.1 broadcast_in_dim.34.b3
  124.3 1.1 copy-done.8
  125.4 1.0 copy-done.9
  126.4 34.9 %shard_map.144 = (s16[128,24,128]{2,1,0:T(8,128)(2,1)S(1)}, f32[8,128]{1,0:T(8,128)S(1)}) custom-call(s32[32]{0:T(128)S(1)} %select_reduce_fusion.1.slots, bf16[128,24,128]{2,1,0:T(8,128)(2,1)S(1)} %all-to-all-done.arrived, bf16[1600,24]{1,0:T(8,128)(2,1)S(1)} %copy-done.9, f32[1600,128]{1,0:T(8,128)S(1)} %broadcast_in_dim.32.b1, ...), custom_call_target="tpu_custom_call" | custom-call | tf_op jit(solution)/shard_map/pallas_call | solution.py:365
  161.3 0.9 copy-done.12
  162.2 4.6 %all-to-all-start.1 = ((s16[128,24,128]{2,1,0:T(8,128)(2,1)}), s16[128,24,128]{2,1,0:T(8,128)(2,1)S(1)}, u32[]{:S(2)}, u32[]{:S(2)}) async-start(s16[128,24,128]{2,1,0:T(8,128)(2,1)} %copy-done.12), calls=%async_computation.1 | async-start | bytes 1572864 | tf_op jit(solution)/shard_map/all_to_all | solution.py:291
  166.8 0.3 convolution_convert_fusion.table
  167.1 16.1 %all-to-all-done.1 = s16[128,24,128]{2,1,0:T(8,128)(2,1)S(1)} async-done(((s16[128,24,128]{2,1,0:T(8,128)(2,1)}), s16[128,24,128]{2,1,0:T(8,128)(2,1)S(1)}, u32[]{:S(2)}, u32[]{:S(2)}) %all-to-all-start.1) | async-done | bytes 786464 | tf_op jit(solution)/shard_map/all_to_all | solution.py:291
  183.2 0.2 copy.23
  183.4 1.9 copy-done.5
  185.2 6.8 %shard_map.145 = (f32[24,8,32,128]{3,2,1,0:T(8,128)S(1)}, bf16[24,32,128]{2,1,0:T(8,128)(2,1)}, bf16[24,32,128]{2,1,0:T(8,128)(2,1)}, f32[24,8,128]{2,1,0:T(8,12...) custom-call(f32[24,8,32,128]{3,2,1,0:T(8,128)S(1)} %copy-done.5, ...), custom_call_target="tpu_custom_call" | custom-call | tf_op jit(solution)/shard_map/pallas_call | solution.py:380
  192.1 0.2 collective-permute-start.18
  192.3 2.5 %collective-permute-start.19 = (bf16[24,32,128]{2,1,0:T(8,128)(2,1)}, bf16[24,32,128]{2,1,0:T(8,128)(2,1)S(1)}, u32[]{:S(2)}, u32[]{:S(2)}) collective-permute-start(bf16[24,32,128]{2,1,0:T(8,128)(2,1)} %get-tuple-element.60), channel_id=1, source_target_pairs={{32,0},{64,32},{96,64},{0,96},{33,1},{65,33},{97,65},{1,97},{34,2}... | collective-permute-start | bytes 589832 | tf_op jit(solution)/shard_map/ppermute | solution.py:274
  194.7 1.6 collective-permute-start.22
  196.3 2.7 %collective-permute-start.21 = (f32[24,8,128]{2,1,0:T(8,128)}, f32[24,8,128]{2,1,0:T(8,128)}, u32[]{:S(2)}, u32[]{:S(2)}) collective-permute-start(f32[24,8,128]{2,1,0:T(8,128)} %get-tuple-element.62), channel_id=1, source_target_pairs={{8,0},{16,8},{24,16},{0,24},{9,1},{17,9},{25,17},{1,25},{10,2},{18... | collective-permute-start | bytes 294920 | tf_op jit(solution)/shard_map/ppermute | solution.py:274
  199.0 0.6 copy-done.15
  199.6 1.8 collective-permute-start.23
  201.4 0.6 slice_reduce_fusion
  202.7 0.5 collective-permute-done.23.zhi
  203.2 0.7 copy-done.16
  204.0 5.3 %shard_map.146 = f32[24,8,32,128]{3,2,1,0:T(8,128)} custom-call(f32[24]{0:T(128)S(1)} %copy-done.17, f32[24,8,32,128]{3,2,1,0:T(8,128)S(1)} %get-tuple-element.58.q, bf16[24,32,128]{2,1,0:T(8,128)(2,1)S(1)} %collective-permute-done.18.xlo, bf16[24,32,128]{2,1,0:T(8,128)(2,1)S(1)} %collective-permute-done.19.xhi, f32[24,8,128]{2,1,0:T(8,128)} %collective-permute-done.20.ylo, ...), custom_call_target="tpu_custom_call" | custom-call | tf_op jit(solution)/shard_map/pallas_call | solution.py:388
  (80 shorter events, 0.4 us)
Async XLA Ops:
  0.6 1.9 copy-start
  2.5 1.0 copy-start.10
  3.5 17.6 %copy-start.27 = (s32[1,96]{1,0:T(1,128)S(1)}, s32[1,96]{1,0:T(1,128)}, u32[]{:S(2)}) copy-start(s32[1,96]{1,0:T(1,128)} %param.25) | copy-start | bytes 1156
  3.5 17.6 %copy-start.30 = (s32[1,96]{1,0:T(1,128)S(1)}, s32[1,96]{1,0:T(1,128)}, u32[]{:S(2)}) copy-start(s32[1,96]{1,0:T(1,128)} %param.24) | copy-start | bytes 1156
  3.5 21.1 %copy-start.1 = (f32[24,8,32,128]{3,2,1,0:T(8,128)S(1)}, f32[24,8,32,128]{3,2,1,0:T(8,128)}, u32[]{:S(2)}) copy-start(f32[24,8,32,128]{3,2,1,0:T(8,128)} %refs_1_.3) | copy-start | bytes 9437188
  3.5 21.1 %copy-start.11 = (f32[3,8,32,128]{3,2,1,0:T(8,128)S(1)}, f32[3,8,32,128]{3,2,1,0:T(8,128)}, u32[]{:S(2)}) copy-start(f32[3,8,32,128]{3,2,1,0:T(8,128)} %refs_7_.1) | copy-start | bytes 1179652
  4.9 0.6 copy-start.20
  5.5 19.2 %collective-permute-start = (bf16[25,32,128]{2,1,0:T(8,128)(2,1)}, bf16[25,32,128]{2,1,0:T(8,128)(2,1)}, u32[]{:S(2)}, u32[]{:S(2)}) collective-permute-start(bf16[25,32,128]{2,1,0:T(8,128)(2,1)} %get-tuple-element.34), channel_id=1, source_target_pairs={{0,32},{32,64},{64,96},{96,0},{1,33},{33,65},{65,97},{97,1},{2,34}... | collective-permute-start | bytes 614408 | tf_op jit(solution)/shard_map/ppermute | solution.py:273
  7.5 17.1 %collective-permute-start.1 = (bf16[25,32,128]{2,1,0:T(8,128)(2,1)}, bf16[25,32,128]{2,1,0:T(8,128)(2,1)}, u32[]{:S(2)}, u32[]{:S(2)}) collective-permute-start(bf16[25,32,128]{2,1,0:T(8,128)(2,1)} %get-tuple-element.35), channel_id=1, source_target_pairs={{32,0},{64,32},{96,64},{0,96},{33,1},{65,33},{97,65},{1,97},{34,2}... | collective-permute-start | bytes 614408 | tf_op jit(solution)/shard_map/ppermute | solution.py:274
  8.8 15.8 %collective-permute-start.2 = (f32[25,8,128]{2,1,0:T(8,128)}, f32[25,8,128]{2,1,0:T(8,128)}, u32[]{:S(2)}, u32[]{:S(2)}) collective-permute-start(f32[25,8,128]{2,1,0:T(8,128)} %get-tuple-element.36), channel_id=1, source_target_pairs={{0,8},{8,16},{16,24},{24,0},{1,9},{9,17},{17,25},{25,1},{2,10},{10... | collective-permute-start | bytes 307208 | tf_op jit(solution)/shard_map/ppermute | solution.py:273
  10.6 14.0 %collective-permute-start.3 = (f32[25,8,128]{2,1,0:T(8,128)}, f32[25,8,128]{2,1,0:T(8,128)}, u32[]{:S(2)}, u32[]{:S(2)}) collective-permute-start(f32[25,8,128]{2,1,0:T(8,128)} %get-tuple-element.37), channel_id=1, source_target_pairs={{8,0},{16,8},{24,16},{0,24},{9,1},{17,9},{25,17},{1,25},{10,2},{18... | collective-permute-start | bytes 307208 | tf_op jit(solution)/shard_map/ppermute | solution.py:274
  12.7 8.4 %collective-permute-start.4 = (f32[25,1,256]{2,1,0:T(1,128)}, f32[25,1,256]{2,1,0:T(1,128)}, u32[]{:S(2)}, u32[]{:S(2)}) collective-permute-start(f32[25,1,256]{2,1,0:T(1,128)} %get-tuple-element.38), channel_id=1, source_target_pairs={{0,1},{1,2},{2,3},{3,4},{4,5},{5,6},{6,7},{7,0},{8,9},{9,10},{10,1... | collective-permute-start | bytes 76808 | tf_op jit(solution)/shard_map/ppermute | solution.py:273
  19.1 10.8 %copy-start.23 = (f32[1600]{0:T(1024)S(1)}, f32[1600]{0:T(1024)}, u32[]{:S(2)}) copy-start(f32[1600]{0:T(1024)} %param.17) | copy-start | bytes 19204
  19.1 17.8 %copy-start.24 = (f32[800]{0:T(1024)S(1)}, f32[800]{0:T(1024)}, u32[]{:S(2)}) copy-start(f32[800]{0:T(1024)} %param.19) | copy-start | bytes 9604
  21.1 3.5 %collective-permute-start.5 = (f32[25,1,256]{2,1,0:T(1,128)}, f32[25,1,256]{2,1,0:T(1,128)S(1)}, u32[]{:S(2)}, u32[]{:S(2)}) collective-permute-start(f32[25,1,256]{2,1,0:T(1,128)} %copy-done.20), channel_id=1, source_target_pairs={{1,0},{2,1},{3,2},{4,3},{5,4},{6,5},{7,6},{0,7},{9,8},{10,9},{11,1... | collective-permute-start | bytes 76808 | tf_op jit(solution)/shard_map/ppermute | solution.py:274
  29.9 14.7 %copy-start.2 = (f32[6,8,32,128]{3,2,1,0:T(8,128)}, f32[6,8,32,128]{3,2,1,0:T(8,128)S(1)}, u32[]{:S(2)}) copy-start(f32[6,8,32,128]{3,2,1,0:T(8,128)S(1)} %get-tuple-element.47.refs_8_) | copy-start | bytes 2359300
  29.9 5.5 %collective-permute-start.10 = (f32[24,1,256]{2,1,0:T(1,128)S(1)}, f32[24,1,256]{2,1,0:T(1,128)S(1)}, u32[]{:S(2)}, u32[]{:S(2)}) collective-permute-start(f32[24,1,256]{2,1,0:T(1,128)S(1)} %get-tuple-element.45), channel_id=1, source_target_pairs={{0,1},{1,2},{2,3},{3,4},{4,5},{5,6},{6,7},{7,0},{8,9},{9,10},{10,1... | collective-permute-start | bytes 73736 | tf_op jit(solution)/shard_map/ppermute | solution.py:273
  29.9 9.7 %collective-permute-start.6 = (bf16[24,32,128]{2,1,0:T(8,128)(2,1)S(1)}, bf16[24,32,128]{2,1,0:T(8,128)(2,1)S(1)}, u32[]{:S(2)}, u32[]{:S(2)}) collective-permute-start(bf16[24,32,128]{2,1,0:T(8,128)(2,1)S(1)} %get-tuple-element.41), channel_id=1, source_target_pairs={{0,32},{32,64},{64,96},{96,0},{1,33},{33,65},{65,97},{97,1},{2,34}... | collective-permute-start | bytes 589832 | tf_op jit(solution)/shard_map/ppermute | solution.py:273
  30.0 9.6 %collective-permute-start.7 = (bf16[24,32,128]{2,1,0:T(8,128)(2,1)S(1)}, bf16[24,32,128]{2,1,0:T(8,128)(2,1)S(1)}, u32[]{:S(2)}, u32[]{:S(2)}) collective-permute-start(bf16[24,32,128]{2,1,0:T(8,128)(2,1)S(1)} %get-tuple-element.42), channel_id=1, source_target_pairs={{32,0},{64,32},{96,64},{0,96},{33,1},{65,33},{97,65},{1,97},{34,2}... | collective-permute-start | bytes 589832 | tf_op jit(solution)/shard_map/ppermute | solution.py:274
  32.7 6.9 %collective-permute-start.8 = (f32[24,8,128]{2,1,0:T(8,128)S(1)}, f32[24,8,128]{2,1,0:T(8,128)S(1)}, u32[]{:S(2)}, u32[]{:S(2)}) collective-permute-start(f32[24,8,128]{2,1,0:T(8,128)S(1)} %get-tuple-element.43), channel_id=1, source_target_pairs={{0,8},{8,16},{16,24},{24,0},{1,9},{9,17},{17,25},{25,1},{2,10},{10... | collective-permute-start | bytes 294920 | tf_op jit(solution)/shard_map/ppermute | solution.py:273
  32.7 6.9 %collective-permute-start.9 = (f32[24,8,128]{2,1,0:T(8,128)S(1)}, f32[24,8,128]{2,1,0:T(8,128)S(1)}, u32[]{:S(2)}, u32[]{:S(2)}) collective-permute-start(f32[24,8,128]{2,1,0:T(8,128)S(1)} %get-tuple-element.44), channel_id=1, source_target_pairs={{8,0},{16,8},{24,16},{0,24},{9,1},{17,9},{25,17},{1,25},{10,2},{18... | collective-permute-start | bytes 294920 | tf_op jit(solution)/shard_map/ppermute | solution.py:274
  35.3 4.2 %collective-permute-start.11 = (f32[24,1,256]{2,1,0:T(1,128)S(1)}, f32[24,1,256]{2,1,0:T(1,128)S(1)}, u32[]{:S(2)}, u32[]{:S(2)}) collective-permute-start(f32[24,1,256]{2,1,0:T(1,128)S(1)} %get-tuple-element.46), channel_id=1, source_target_pairs={{1,0},{2,1},{3,2},{4,3},{5,4},{6,5},{7,6},{0,7},{9,8},{10,9},{11,1... | collective-permute-start | bytes 73736 | tf_op jit(solution)/shard_map/ppermute | solution.py:274
  39.6 10.5 %copy-start.26 = (f32[400]{0:T(512)S(1)}, f32[400]{0:T(512)}, u32[]{:S(2)}) copy-start(f32[400]{0:T(512)} %param.21) | copy-start | bytes 4804
  44.5 1.7 copy-start.6
  46.2 0.6 copy-start.21
  46.8 0.6 copy-start.22
  47.4 0.6 copy-start.18
  47.4 0.7 copy-start.19
  47.4 40.8 %collective-permute-start.12 = (bf16[24,32,128]{2,1,0:T(8,128)(2,1)}, bf16[24,32,128]{2,1,0:T(8,128)(2,1)S(1)}, u32[]{:S(2)}, u32[]{:S(2)}) collective-permute-start(bf16[24,32,128]{2,1,0:T(8,128)(2,1)} %get-tuple-element.49), channel_id=1, source_target_pairs={{0,32},{32,64},{64,96},{96,0},{1,33},{33,65},{65,97},{97,1},{2,34}... | collective-permute-start | bytes 589832 | tf_op jit(solution)/shard_map/ppermute | solution.py:273
  48.1 40.1 %collective-permute-start.13 = (bf16[24,32,128]{2,1,0:T(8,128)(2,1)}, bf16[24,32,128]{2,1,0:T(8,128)(2,1)S(1)}, u32[]{:S(2)}, u32[]{:S(2)}) collective-permute-start(bf16[24,32,128]{2,1,0:T(8,128)(2,1)} %get-tuple-element.50), channel_id=1, source_target_pairs={{32,0},{64,32},{96,64},{0,96},{33,1},{65,33},{97,65},{1,97},{34,2}... | collective-permute-start | bytes 589832 | tf_op jit(solution)/shard_map/ppermute | solution.py:274
  50.1 34.5 %collective-permute-start.16 = (f32[24,1,256]{2,1,0:T(1,128)}, f32[24,1,256]{2,1,0:T(1,128)S(1)}, u32[]{:S(2)}, u32[]{:S(2)}) collective-permute-start(f32[24,1,256]{2,1,0:T(1,128)} %copy-done.22), channel_id=1, source_target_pairs={{0,1},{1,2},{2,3},{3,4},{4,5},{5,6},{6,7},{7,0},{8,9},{9,10},{10,1... | collective-permute-start | bytes 73736 | tf_op jit(solution)/shard_map/ppermute | solution.py:273
  81.9 6.3 %collective-permute-start.14 = (f32[24,8,128]{2,1,0:T(8,128)}, f32[24,8,128]{2,1,0:T(8,128)S(1)}, u32[]{:S(2)}, u32[]{:S(2)}) collective-permute-start(f32[24,8,128]{2,1,0:T(8,128)} %copy-done.19), channel_id=1, source_target_pairs={{0,8},{8,16},{16,24},{24,0},{1,9},{9,17},{17,25},{25,1},{2,10},{10... | collective-permute-start | bytes 294920 | tf_op jit(solution)/shard_map/ppermute | solution.py:273
  81.9 6.3 %collective-permute-start.15 = (f32[24,8,128]{2,1,0:T(8,128)}, f32[24,8,128]{2,1,0:T(8,128)S(1)}, u32[]{:S(2)}, u32[]{:S(2)}) collective-permute-start(f32[24,8,128]{2,1,0:T(8,128)} %copy-done.18), channel_id=1, source_target_pairs={{8,0},{16,8},{24,16},{0,24},{9,1},{17,9},{25,17},{1,25},{10,2},{18... | collective-permute-start | bytes 294920 | tf_op jit(solution)/shard_map/ppermute | solution.py:274
  84.6 3.6 %collective-permute-start.17 = (f32[24,1,256]{2,1,0:T(1,128)}, f32[24,1,256]{2,1,0:T(1,128)S(1)}, u32[]{:S(2)}, u32[]{:S(2)}) collective-permute-start(f32[24,1,256]{2,1,0:T(1,128)} %copy-done.21), channel_id=1, source_target_pairs={{1,0},{2,1},{3,2},{4,3},{5,4},{6,5},{7,6},{0,7},{9,8},{10,9},{11,1... | collective-permute-start | bytes 73736 | tf_op jit(solution)/shard_map/ppermute | solution.py:274
  88.2 1.1 copy-start.3
  89.3 1.9 copy-start.7
  91.2 0.8 copy-start.13
  96.8 1.7 copy-start.4
  98.5 8.8 %copy-start.25 = (pred[128]{0:T(512)(128)(4,1)S(1)}, pred[128]{0:T(512)(128)(4,1)}, u32[]{:S(2)}) copy-start(pred[128]{0:T(512)(128)(4,1)} %compare_reduce_fusion) | copy-start | bytes 388
  99.5 24.1 %all-to-all-start = ((bf16[128,24,128]{2,1,0:T(8,128)(2,1)}), bf16[128,24,128]{2,1,0:T(8,128)(2,1)S(1)}, u32[]{:S(2)}, u32[]{:S(2)}) async-start(bf16[128,24,128]{2,1,0:T(8,128)(2,1)} %bitcast.9), calls=%async_computation | async-start | bytes 1572864 | tf_op jit(solution)/shard_map/all_to_all | solution.py:291
  107.6 16.6 %copy-start.29 = (f32[24]{0:T(128)S(1)}, f32[24]{0:T(128)}, u32[]{:S(2)}) copy-start(f32[24]{0:T(128)} %param.23) | copy-start | bytes 292
  107.6 16.7 %copy-start.14 = (bf16[400,24]{0,1:T(8,128)(2,1)S(1)}, bf16[400,24]{0,1:T(8,128)(2,1)}, u32[]{:S(2)}) copy-start(bf16[400,24]{0,1:T(8,128)(2,1)} %param.22) | copy-start | bytes 57604
  124.3 1.1 copy-start.8
  125.4 1.0 copy-start.9
  126.4 40.4 %copy-start.28 = (s32[1,96]{1,0:T(1,128)S(1)}, s32[1,96]{1,0:T(1,128)}, u32[]{:S(2)}) copy-start(s32[1,96]{1,0:T(1,128)} %param.25) | copy-start | bytes 1156
  126.4 40.4 %copy-start.31 = (s32[1,96]{1,0:T(1,128)S(1)}, s32[1,96]{1,0:T(1,128)}, u32[]{:S(2)}) copy-start(s32[1,96]{1,0:T(1,128)} %param.24) | copy-start | bytes 1156
  161.3 0.9 copy-start.12
  162.2 21.0 %all-to-all-start.1 = ((s16[128,24,128]{2,1,0:T(8,128)(2,1)}), s16[128,24,128]{2,1,0:T(8,128)(2,1)S(1)}, u32[]{:S(2)}, u32[]{:S(2)}) async-start(s16[128,24,128]{2,1,0:T(8,128)(2,1)} %copy-done.12), calls=%async_computation.1 | async-start | bytes 1572864 | tf_op jit(solution)/shard_map/all_to_all | solution.py:291
  166.8 36.4 %copy-start.17 = (f32[24]{0:T(128)S(1)}, f32[24]{0:T(128)}, u32[]{:S(2)}) copy-start(f32[24]{0:T(128)} %rates.1) | copy-start | bytes 292
  183.3 1.9 copy-start.5
  192.1 11.1 %collective-permute-start.18 = (bf16[24,32,128]{2,1,0:T(8,128)(2,1)}, bf16[24,32,128]{2,1,0:T(8,128)(2,1)S(1)}, u32[]{:S(2)}, u32[]{:S(2)}) collective-permute-start(bf16[24,32,128]{2,1,0:T(8,128)(2,1)} %get-tuple-element.59), channel_id=1, source_target_pairs={{0,32},{32,64},{64,96},{96,0},{1,33},{33,65},{65,97},{97,1},{2,34}... | collective-permute-start | bytes 589832 | tf_op jit(solution)/shard_map/ppermute | solution.py:273
  192.3 10.9 %collective-permute-start.19 = (bf16[24,32,128]{2,1,0:T(8,128)(2,1)}, bf16[24,32,128]{2,1,0:T(8,128)(2,1)S(1)}, u32[]{:S(2)}, u32[]{:S(2)}) collective-permute-start(bf16[24,32,128]{2,1,0:T(8,128)(2,1)} %get-tuple-element.60), channel_id=1, source_target_pairs={{32,0},{64,32},{96,64},{0,96},{33,1},{65,33},{97,65},{1,97},{34,2}... | collective-permute-start | bytes 589832 | tf_op jit(solution)/shard_map/ppermute | solution.py:274
  194.7 4.3 %collective-permute-start.22 = (f32[24,1,256]{2,1,0:T(1,128)S(1)}, f32[24,1,256]{2,1,0:T(1,128)S(1)}, u32[]{:S(2)}, u32[]{:S(2)}) collective-permute-start(f32[24,1,256]{2,1,0:T(1,128)S(1)} %get-tuple-element.63), channel_id=1, source_target_pairs={{0,1},{1,2},{2,3},{3,4},{4,5},{5,6},{6,7},{7,0},{8,9},{9,10},{10,1... | collective-permute-start | bytes 73736 | tf_op jit(solution)/shard_map/ppermute | solution.py:273
  196.3 6.9 %collective-permute-start.20 = (f32[24,8,128]{2,1,0:T(8,128)}, f32[24,8,128]{2,1,0:T(8,128)}, u32[]{:S(2)}, u32[]{:S(2)}) collective-permute-start(f32[24,8,128]{2,1,0:T(8,128)} %get-tuple-element.61), channel_id=1, source_target_pairs={{0,8},{8,16},{16,24},{24,0},{1,9},{9,17},{17,25},{25,1},{2,10},{10... | collective-permute-start | bytes 294920 | tf_op jit(solution)/shard_map/ppermute | solution.py:273
  196.3 6.9 %collective-permute-start.21 = (f32[24,8,128]{2,1,0:T(8,128)}, f32[24,8,128]{2,1,0:T(8,128)}, u32[]{:S(2)}, u32[]{:S(2)}) collective-permute-start(f32[24,8,128]{2,1,0:T(8,128)} %get-tuple-element.62), channel_id=1, source_target_pairs={{8,0},{16,8},{24,16},{0,24},{9,1},{17,9},{25,17},{1,25},{10,2},{18... | collective-permute-start | bytes 294920 | tf_op jit(solution)/shard_map/ppermute | solution.py:274
  199.0 0.6 copy-start.15
  199.6 3.6 %collective-permute-start.23 = (f32[24,1,256]{2,1,0:T(1,128)}, f32[24,1,256]{2,1,0:T(1,128)}, u32[]{:S(2)}, u32[]{:S(2)}) collective-permute-start(f32[24,1,256]{2,1,0:T(1,128)} %get-tuple-element.64), channel_id=1, source_target_pairs={{1,0},{2,1},{3,2},{4,3},{5,4},{6,5},{7,6},{0,7},{9,8},{10,9},{11,1... | collective-permute-start | bytes 73736 | tf_op jit(solution)/shard_map/ppermute | solution.py:274
  203.2 0.7 copy-start.16

commit v3 on v2

--- a/solution.py
+++ b/solution.py
@@ -7,8 +7,9 @@
 from jax.experimental.pallas import tpu as pltpu
 from jax.sharding import PartitionSpec as P
 
-OWNED = 32
 GROUP = 4
+TOGETHER = 8
+LISTED = 96
 ALL = ("gx", "gy", "gz")
 F32, BF16 = jnp.float32, jnp.bfloat16
 TN = (((0,), (0,)), ((), ()))
@@ -54,21 +55,6 @@
     ends = z_ends(out[f].reshape(256, 128))
     zf[f] = ends[0:1]
     zl[f] = ends[1:2]
-
-
-CODE_UNIT = 32.0
-CODE_SCALE = 32767.0 / 38.0 / 0.6931471805599453
-
-
-def coded(value):
-    level = (jnp.log(1.0 + CODE_UNIT * jnp.abs(value)) * CODE_SCALE + 0.5).astype(jnp.int32)
-    return jnp.where(value < 0.0, -level, level).astype(jnp.int16)
-
-
-def decoded(code):
-    level = code.astype(jnp.int32).astype(F32)
-    size = (jnp.exp(jnp.abs(level) * (1.0 / CODE_SCALE)) - 1.0) * (1.0 / CODE_UNIT)
-    return jnp.where(level < 0.0, -size, size)
 
 
 def prep_kernel(fields, velocity, xf, xl, yf, yl, zf, zl):
@@ -105,16 +91,12 @@
         del refs[:7]
     else:
         coef = refs.pop(0)
-    if kind == 3:
-        routing = refs.pop(0)
     out = refs.pop(0)
     if kind == 1:
         coef = refs.pop(0)
     if kind < 3:
         xf, xl, yf, yl, zf, zl = refs[:6]
         del refs[:6]
-    else:
-        outgoing = refs.pop(0)
     zcol = refs.pop(0)
 
     if kind == 1:
@@ -164,28 +146,9 @@
             out[f, x] = new
             if kind < 3:
                 put_faces(new, f, x, xf, xl, yf, yl)
-    for f in range(GROUP):
-        if kind < 3:
+    if kind < 3:
+        for f in range(GROUP):
             put_z_faces(out, f, zf, zl)
-        else:
-            blocks = out[f].reshape(256, 128).astype(BF16)
-            outgoing[:, 128 * f : 128 * f + 128] = jnp.dot(
-                routing[...], blocks, preferred_element_type=F32
-            ).astype(BF16)
-
-
-def react_kernel(flowed, back, table, out, xf, xl, yf, yl, zf, zl):
-    for f in range(GROUP):
-        value = decoded(back[:, 128 * f : 128 * f + 128])
-        coarse = value.astype(BF16)
-        rest = (value - coarse.astype(F32)).astype(BF16)
-        added = jnp.dot(table[...], coarse, preferred_element_type=F32)
-        added += jnp.dot(table[...], rest, preferred_element_type=F32)
-        for x in range(8):
-            new = flowed[f, x] + added[32 * x : 32 * x + 32]
-            out[f, x] = new
-            put_faces(new, f, x, xf, xl, yf, yl)
-        put_z_faces(out, f, zf, zl)
 
 
 def diffuse_kernel(rates, q, xlo, xhi, ylo, yhi, zlo, zhi, out, zcol):
@@ -204,31 +167,46 @@
             out[f, x] = centre + rate * spread
 
 
-def network_kernel(slots, arrived, w1, b1, w2, b2, w3, b3, w4, b4, out, heat):
-    step = pl.program_id(0)
-
-    @pl.when(step == 0)
-    def _():
-        out[...] = jnp.zeros_like(out)
-        heat[...] = jnp.zeros_like(heat)
+def network_kernel(listed, flowed, w1, b1, w2, b2, w3, b3, w4, b4, out, heat, xf, xl, yf, yl, zf, zl):
+    def copy(f, carry):
+        rows = pl.ds(pl.multiple_of(256 * f, 256), 256)
+        out[rows, :] = flowed[rows, :]
+        return carry
 
     def activated(weights, bias, cells):
         half = jnp.dot(weights[...], cells, preferred_element_type=F32)
-        half = half + jnp.concatenate([bias[...], bias[...]], axis=1)
+        half = half + jnp.concatenate([bias[...]] * TOGETHER, axis=1)
         return (half + half * jnp.tanh(half)).astype(BF16)
 
-    first, second = slots[2 * step], slots[2 * step + 1]
-    cells = jnp.concatenate([arrived[first], arrived[second]], axis=1)
-    hidden = activated(w1, b1, cells)
-    hidden = activated(w2, b2, hidden)
-    hidden = activated(w3, b3, hidden)
-    result = jnp.dot(w4[...], hidden, preferred_element_type=F32)
-    result = result + jnp.concatenate([b4[...], b4[...]], axis=1)
-    codes = coded(result)
-    out[first] = codes[:, :128]
-    out[second] = codes[:, 128:]
-    squares = result[0:8] * result[0:8]
-    heat[...] += squares[:, :128] + squares[:, 128:]
+    def react(step, carry):
+        first = step * TOGETHER
+        rows = [pl.ds(listed[1 + first + j], 24, stride=256) for j in range(TOGETHER)]
+        before = [flowed[r, :] for r in rows]
+        hidden = activated(w1, b1, jnp.concatenate(before, axis=1).astype(BF16))
+        hidden = activated(w2, b2, hidden)
+        hidden = activated(w3, b3, hidden)
+        result = jnp.dot(w4[...], hidden, preferred_element_type=F32)
+        result = result + jnp.concatenate([b4[...]] * TOGETHER, axis=1)
+        for j in range(TOGETHER):
+            increment = result[:, 128 * j : 128 * j + 128]
+            out[rows[j], :] = before[j] + increment
+            heat[pl.ds(first + j, 1), :] = increment[0:1] * increment[0:1]
+        return carry
+
+    def faces(f, carry):
+        base = pl.multiple_of(256 * f, 256)
+        xf[f] = out[pl.ds(base, 32), :].astype(BF16)
+        xl[f] = out[pl.ds(base + 224, 32), :].astype(BF16)
+        yf[f] = out[pl.ds(base, 8, stride=32), :]
+        yl[f] = out[pl.ds(base + 31, 8, stride=32), :]
+        ends = z_ends(out[pl.ds(base, 256), :])
+        zf[f] = ends[0:1]
+        zl[f] = ends[1:2]
+        return carry
+
+    lax.fori_loop(0, 24, copy, 0)
+    lax.fori_loop(0, (listed[0] + TOGETHER - 1) // TOGETHER, react, 0)
+    lax.fori_loop(0, 24, faces, 0)
 
 
 def params(mib):
@@ -252,7 +230,6 @@
 Y_FACE = pl.BlockSpec((GROUP, 8, 128), lambda g, *_: (g, 0, 0))
 Z_FACE = pl.BlockSpec((GROUP, 1, 256), lambda g, *_: (g, 0, 0))
 FACES = [X_FACE, X_FACE, Y_FACE, Y_FACE, Z_FACE, Z_FACE]
-SLOTS = pl.BlockSpec((128, GROUP * 128), lambda g, *_: (0, g))
 
 
 def face_shapes(count):
@@ -308,19 +285,8 @@
 ):
     brick = sds(fields.shape, F32)
     ids, owners = react_list[0], owner_table[0]
-    everyone = lax.all_gather(owner_table, ALL, axis=0, tiled=True)
-    me = lax.axis_index(ALL)
-    sends = jnp.any(everyone == me, axis=1)
-    numbers = jnp.arange(128, dtype=jnp.int32)
-    rank = jnp.sum(jnp.where((numbers[None, :] < numbers[:, None]) & sends[None, :], 1, 0), axis=1)
-    slots = jnp.sum(
-        jnp.where((rank[None, :] == numbers[:OWNED, None]) & sends[None, :], numbers[None, :], 0), axis=1
-    ).astype(jnp.int32)
-    slot_hot = (owners[None, :] == numbers[:, None]).astype(BF16)
-    block_hot = (ids[:, None] == jnp.arange(256, dtype=jnp.int32)[None, :]).astype(BF16)
-    routing = jnp.dot(slot_hot, block_hot, preferred_element_type=F32).astype(BF16)
-    table = lax.dot_general(block_hot, slot_hot, (((0,), (1,)), ((), ())), preferred_element_type=F32).astype(BF16)
-
+    count = jnp.sum((ids >= 0).astype(jnp.int32))
+    listed = jnp.concatenate([count[None], jnp.where(ids >= 0, ids, ids[0])])
     half = jnp.asarray(0.5, BF16)
     w1, w2, w3, w4 = (weight_in * half).T, (weight_mid * half).T, (weight_low * half).T, weight_out.T
     b1, b2, b3, b4 = (
@@ -354,37 +320,28 @@
         [brick, *face_shapes(24)],
         [BRICK, *FACES],
     )
-    flowed, outgoing = section(
+    (flowed,) = section(
         3,
-        (two, fields, *exchange(faces), coef, routing),
-        [BRICK, BRICK, *FACES, whole((6, 8, 32, 128)), whole((128, 256))],
-        [brick, sds((128, 24 * 128), BF16)],
-        [BRICK, SLOTS],
-    )
-    arrived = swap(outgoing.reshape(128, 24, 128))
-    returning, heat = pl.pallas_call(
+        (two, fields, *exchange(faces), coef),
+        [BRICK, BRICK, *FACES, whole((6, 8, 32, 128))],
+        [brick],
+        [BRICK],
+    )
+    in_vmem = pl.BlockSpec(memory_space=pltpu.VMEM)
+    reacted, heat, *faces = pl.pallas_call(
         network_kernel,
-        grid_spec=pltpu.PrefetchScalarGridSpec(
-            num_scalar_prefetch=1,
-            grid=(OWNED // 2,),
-            in_specs=[
-                whole(a.shape) for a in (arrived, w1, b1, w2, b2, w3, b3, w4, b4)
-            ],
-            out_specs=[whole((128, 24, 128)), whole((8, 128))],
-        ),
-        out_shape=[sds((128, 24, 128), jnp.int16), sds((8, 128), F32)],
-        compiler_params=params(40),
-    )(slots, arrived, w1, b1, w2, b2, w3, b3, w4, b4)
-    owner_activity = (jnp.sum(heat[0]) / (8.0 * 128.0)).reshape(1)
-    back = swap(returning).reshape(128, 24 * 128)
-    reacted, *faces = pl.pallas_call(
-        react_kernel,
-        grid=(24 // GROUP,),
-        in_specs=[BRICK, SLOTS, whole((256, 128))],
-        out_specs=[BRICK, *FACES],
-        out_shape=[brick, *face_shapes(24)],
-        compiler_params=params(24),
-    )(flowed, back, table)
+        in_specs=[pl.BlockSpec(memory_space=pltpu.SMEM)] + [in_vmem] * 9,
+        out_specs=[in_vmem] * 8,
+        out_shape=[sds((24 * 256, 128), F32), sds((LISTED, 128), F32), *face_shapes(24)],
+        compiler_params=params(56),
+    )(listed, flowed.reshape(24 * 256, 128), w1, b1, w2, b2, w3, b3, w4, b4)
+    reacted = reacted.reshape(fields.shape)
+    mean_heat = jnp.mean(heat, axis=1)
+    owned_by = owners[None, :] == jnp.arange(128, dtype=jnp.int32)[:, None]
+    by_owner = jnp.sum(jnp.where(owned_by, mean_heat[None, :], 0.0), axis=1)
+    around = exchange(faces)
+    sent = jnp.broadcast_to(by_owner[:, None, None], (128, 1, 128))
+    owner_activity = (jnp.sum(swap(sent)[:, 0, 0]) / 8.0).reshape(1)
     updated = pl.pallas_call(
         diffuse_kernel,
         grid=(24 // GROUP,),
@@ -393,7 +350,7 @@
         out_shape=brick,
         scratch_shapes=[pltpu.VMEM((GROUP, 256, 128), F32)],
         compiler_params=params(24),
-    )(diffusivity, reacted, *exchange(faces))
+    )(diffusivity, reacted, *around)
     return (updated, owner_activity)
 
 

time: 212 us -> 170 us (0.80)
  Pallas kernels: 63.2 us -> 93.6 us
  blocking collectives: 30.2 us -> 0 us
  waiting for transfers between devices: 35.9 us -> 11.8 us
  local copies, waits for them, and re-layouts: 22.4 us -> 13.3 us
  starting transfers between devices: 45.1 us -> 39.2 us
    pallas_call x2 -> x1, Pallas kernels: 41.7 us -> 74.1 us  [local(): pl.pallas_call(network_kernel, in_specs=[pl.BlockSpec(memory_space=pltpu....]
    all_gather x1 -> x0, blocking collectives: 30.2 us -> none  [local(): everyone = lax.all_gather(owner_table, ALL, axis=0, tiled=True)]
    all_to_all x2 -> x1, waiting for transfers between devices: 30.1 us -> 3.63 us  [swap(): return lax.all_to_all(tiles, ALL, split_axis=0, concat_axis=0, tiled=True)]
    unnamed x67 -> x31, local copies, waits for them, and re-layouts: 21.8 us -> 8.89 us
    all_to_all x2 -> x1, starting transfers between devices: 12.4 us -> 6.41 us  [swap(): return lax.all_to_all(tiles, ALL, split_axis=0, concat_axis=0, tiled=True)]
    broadcast_in_dim x4, local copies, waits for them, and re-layouts: 0.61 us -> 3.6 us  [local(): jnp.broadcast_to((s * b)[:, None], (b.shape[0], 128))]
    reduce_or x1 -> x0, other arithmetic: 2.87 us -> none  [local(): sends = jnp.any(everyone == me, axis=1)]
    ppermute x12, waiting for transfers between devices: 5.82 us -> 8.09 us  [exchange(): got.append(lax.ppermute(first, axis, [((i + 1) % n, i) for i in range(n)]))]
  transfers between devices with their start and end apart: 26 -> 25, of which waited for: 5 -> 4; matrix products, arithmetic and copies ran while one was open for 6% -> 7% of each run, Pallas kernels for 0% -> 0%
where the time goes in v3:
time: 170 us
  Pallas kernels  93.6 us (55%)
  starting transfers between devices  39.2 us (23%)
  local copies, waits for them, and re-layouts  13.3 us (8%)
  waiting for transfers between devices  11.8 us (7%)
  other arithmetic  9.31 us (5%)
  between operations  2.68 us (2%)
    pallas_call x1, Pallas kernels, local(): pl.pallas_call(network_kernel, in_specs=[pl.BlockSpec(memory_space=pltpu....  74.1 us
    ppermute x12, starting transfers between devices, exchange(): got.append(lax.ppermute(first, axis, [((i + 1) % n, i) for i in range(n)]))  21.1 us
    pallas_call x3, Pallas kernels, section(): pl.pallas_call(functools.partial(section_kernel, kind), grid=(24 // GROUP...  13.3 us
    ppermute x12, starting transfers between devices, exchange(): got.append(lax.ppermute(last, axis, [(i, (i + 1) % n) for i in range(n)]))  11.7 us
    unnamed x31, local copies, waits for them, and re-layouts  8.89 us
    ppermute x12, waiting for transfers between devices, exchange(): got.append(lax.ppermute(first, axis, [((i + 1) % n, i) for i in range(n)]))  8.09 us
    all_to_all x1, starting transfers between devices, swap(): return lax.all_to_all(tiles, ALL, split_axis=0, concat_axis=0, tiled=True)  6.41 us
    transpose x3, other arithmetic, local(): w1, w2, w3, w4 = ((weight_in * half).T, (weight_mid * half).T, (weight_lo...  5.63 us
  transfers between devices with their start and end apart: 25, of which 4 were waited for; matrix products, arithmetic and copies ran while one was open for 7% of the time, Pallas kernels for 0%

profile of v3, /device:TPU:1, one launch (start us, length us, event | category | flops | bytes accessed | tf_op | source)
XLA Modules:
  0.0 169.8 jit_solution(1137491965795859474)
XLA Ops:
  0.6 0.0 copy-start
  0.6 1.9 %copy-done = f32[24,8,32,128]{3,2,1,0:T(8,128)S(1)} copy-done((f32[24,8,32,128]{3,2,1,0:T(8,128)S(1)}, f32[24,8,32,128]{3,2,1,0:T(8,128)}, u32[]{:S(2)}) %copy-start) | copy-done | bytes 3145752
  2.5 1.0 copy-done.4
  3.5 1.3 shard_map.140
  4.9 0.6 copy-done.7
  5.5 2.0 %collective-permute-start = (bf16[25,32,128]{2,1,0:T(8,128)(2,1)}, bf16[25,32,128]{2,1,0:T(8,128)(2,1)}, u32[]{:S(2)}, u32[]{:S(2)}) collective-permute-start(bf16[25,32,128]{2,1,0:T(8,128)(2,1)} %get-tuple-element.31), channel_id=1, source_target_pairs={{0,32},{32,64},{64,96},{96,0},{1,33},{33,65},{65,97},{97,1},{2,34}... | collective-permute-start | bytes 614408 | tf_op jit(solution)/shard_map/ppermute | solution.py:250
  7.5 1.3 collective-permute-start.1
  8.8 1.8 %collective-permute-start.2 = (f32[25,8,128]{2,1,0:T(8,128)}, f32[25,8,128]{2,1,0:T(8,128)}, u32[]{:S(2)}, u32[]{:S(2)}) collective-permute-start(f32[25,8,128]{2,1,0:T(8,128)} %get-tuple-element.33), channel_id=1, source_target_pairs={{0,8},{8,16},{16,24},{24,0},{1,9},{9,17},{17,25},{25,1},{2,10},{10... | collective-permute-start | bytes 307208 | tf_op jit(solution)/shard_map/ppermute | solution.py:250
  10.6 2.1 %collective-permute-start.3 = (f32[25,8,128]{2,1,0:T(8,128)}, f32[25,8,128]{2,1,0:T(8,128)}, u32[]{:S(2)}, u32[]{:S(2)}) collective-permute-start(f32[25,8,128]{2,1,0:T(8,128)} %get-tuple-element.34), channel_id=1, source_target_pairs={{8,0},{16,8},{24,16},{0,24},{9,1},{17,9},{25,17},{1,25},{10,2},{18... | collective-permute-start | bytes 307208 | tf_op jit(solution)/shard_map/ppermute | solution.py:251
  12.7 2.7 %collective-permute-start.4 = (f32[25,1,256]{2,1,0:T(1,128)}, f32[25,1,256]{2,1,0:T(1,128)}, u32[]{:S(2)}, u32[]{:S(2)}) collective-permute-start(f32[25,1,256]{2,1,0:T(1,128)} %get-tuple-element.35), channel_id=1, source_target_pairs={{0,1},{1,2},{2,3},{3,4},{4,5},{5,6},{6,7},{7,0},{8,9},{9,10},{10,1... | collective-permute-start | bytes 76808 | tf_op jit(solution)/shard_map/ppermute | solution.py:250
  15.4 1.8 %multiply_bitcast_fusion.w2 = bf16[800,1600]{1,0:T(8,128)(2,1)} fusion(bf16[1600,800]{0,1:T(8,128)(2,1)S(1)} %copy-done.8), kind=kLoop, calls=%fused_computation | loop fusion | flops 1280000 | bytes 5120000 | tf_op jit(solution)/shard_map/transpose | solution.py:291
  17.2 1.8 %copy.19 = bf16[24,1600]{0,1:T(8,128)(2,1)} copy(bf16[24,1600]{1,0:T(8,128)(2,1)} %param.16) | data formatting | bytes 153600 | tf_op args[3]
  19.0 1.8 %multiply_bitcast_fusion.2.w1 = bf16[1600,24]{1,0:T(8,128)(2,1)} fusion(bf16[24,1600]{0,1:T(8,128)(2,1)} %copy.19), kind=kLoop, calls=%fused_computation.2 | loop fusion | flops 38400 | bytes 153600 | tf_op jit(solution)/shard_map/transpose | solution.py:291
  20.8 2.1 %multiply_bitcast_fusion.1.w3 = bf16[400,800]{1,0:T(8,128)(2,1)} fusion(bf16[800,400]{0,1:T(8,128)(2,1)} %param.20), kind=kLoop, calls=%fused_computation.1 | loop fusion | flops 320000 | bytes 1280000 | tf_op jit(solution)/shard_map/transpose | solution.py:291
  22.9 3.5 %collective-permute-done.5.refs_6_.refs_13_ = f32[25,1,256]{2,1,0:T(1,128)S(1)} collective-permute-done((f32[25,1,256]{2,1,0:T(1,128)}, f32[25,1,256]{2,1,0:T(1,128)S(1)}, u32[]{:S(2)}, u32[]{:S(2)}) %collective-permute-start.5) | collective-permute-done | bytes 25632 | tf_op jit(solution)/shard_map/ppermute | solution.py:251
  26.4 0.0 collective-permute-done.2.refs_3_.refs_10_
  26.4 0.0 collective-permute-done.3.refs_4_.refs_11_
  26.4 0.0 collective-permute-done.refs_1_.refs_8_
  26.4 0.0 collective-permute-done.1.refs_2_.refs_9_
  26.4 5.2 %shard_map.141 = (f32[24,8,32,128]{3,2,1,0:T(8,128)S(1)}, f32[6,8,32,128]{3,2,1,0:T(8,128)S(1)}, bf16[24,32,128]{2,1,0:T(8,128)(2,1)S(1)}, bf16[24,32,128]{2,1,0...) custom-call(f32[24,8,32,128]{3,2,1,0:T(8,128)S(1)} %copy-done.1, ...), custom_call_target="tpu_custom_call" | custom-call | tf_op jit(solution)/shard_map/pallas_call | solution.py:256
  31.6 0.0 collective-permute-start.10
  31.7 0.1 collective-permute-start.6
  31.7 2.7 %collective-permute-start.7 = (bf16[24,32,128]{2,1,0:T(8,128)(2,1)S(1)}, bf16[24,32,128]{2,1,0:T(8,128)(2,1)S(1)}, u32[]{:S(2)}, u32[]{:S(2)}) collective-permute-start(bf16[24,32,128]{2,1,0:T(8,128)(2,1)S(1)} %get-tuple-element.39), channel_id=1, source_target_pairs={{32,0},{64,32},{96,64},{0,96},{33,1},{65,33},{97,65},{1,97},{34,2}... | collective-permute-start | bytes 589832 | tf_op jit(solution)/shard_map/ppermute | solution.py:251
  34.4 2.7 %collective-permute-start.9 = (f32[24,8,128]{2,1,0:T(8,128)S(1)}, f32[24,8,128]{2,1,0:T(8,128)S(1)}, u32[]{:S(2)}, u32[]{:S(2)}) collective-permute-start(f32[24,8,128]{2,1,0:T(8,128)S(1)} %get-tuple-element.41), channel_id=1, source_target_pairs={{8,0},{16,8},{24,16},{0,24},{9,1},{17,9},{25,17},{1,25},{10,2},{18... | collective-permute-start | bytes 294920 | tf_op jit(solution)/shard_map/ppermute | solution.py:251
  37.1 0.0 collective-permute-done.10.refs_6_
  37.1 1.5 collective-permute-start.11
  38.6 2.7 %collective-permute-done.11.refs_7_ = f32[24,1,256]{2,1,0:T(1,128)S(1)} collective-permute-done((f32[24,1,256]{2,1,0:T(1,128)S(1)}, f32[24,1,256]{2,1,0:T(1,128)S(1)}, u32[]{:S(2)}, u32[]{:S(2)}) %collective-permute-start.11) | collective-permute-done | bytes 24608 | tf_op jit(solution)/shard_map/ppermute | solution.py:251
  41.3 0.0 collective-permute-done.7.refs_3_
  41.3 0.0 copy-start.12
  41.4 4.4 %shard_map.142 = (f32[24,8,32,128]{3,2,1,0:T(8,128)S(1)}, bf16[24,32,128]{2,1,0:T(8,128)(2,1)S(1)}, bf16[24,32,128]{2,1,0:T(8,128)(2,1)S(1)}, f32[24,8,128]{2,1,...) custom-call(f32[24,8,32,128]{3,2,1,0:T(8,128)S(1)} %get-tuple-element.37.refs_0_, ...), custom_call_target="tpu_custom_call" | custom-call | tf_op jit(solution)/shard_map/pallas_call | solution.py:256
  45.8 0.0 collective-permute-start.12
  45.8 2.7 %collective-permute-start.13 = (bf16[24,32,128]{2,1,0:T(8,128)(2,1)S(1)}, bf16[24,32,128]{2,1,0:T(8,128)(2,1)S(1)}, u32[]{:S(2)}, u32[]{:S(2)}) collective-permute-start(bf16[24,32,128]{2,1,0:T(8,128)(2,1)S(1)} %get-tuple-element.47), channel_id=1, source_target_pairs={{32,0},{64,32},{96,64},{0,96},{33,1},{65,33},{97,65},{1,97},{34,2}... | collective-permute-start | bytes 589832 | tf_op jit(solution)/shard_map/ppermute | solution.py:251
  48.5 1.6 collective-permute-start.16
  50.1 0.7 fusion
  50.8 0.3 collective-permute-start.14
  51.1 2.6 %collective-permute-start.15 = (f32[24,8,128]{2,1,0:T(8,128)S(1)}, f32[24,8,128]{2,1,0:T(8,128)S(1)}, u32[]{:S(2)}, u32[]{:S(2)}) collective-permute-start(f32[24,8,128]{2,1,0:T(8,128)S(1)} %get-tuple-element.49), channel_id=1, source_target_pairs={{8,0},{16,8},{24,16},{0,24},{9,1},{17,9},{25,17},{1,25},{10,2},{18... | collective-permute-start | bytes 294920 | tf_op jit(solution)/shard_map/ppermute | solution.py:251
  53.7 0.0 collective-permute-done.16.refs_6_
  53.7 0.1 collective-permute-start.17
  53.8 1.3 pad_add_fusion.listed
  55.1 1.9 %collective-permute-done.17.refs_7_ = f32[24,1,256]{2,1,0:T(1,128)S(1)} collective-permute-done((f32[24,1,256]{2,1,0:T(1,128)S(1)}, f32[24,1,256]{2,1,0:T(1,128)S(1)}, u32[]{:S(2)}, u32[]{:S(2)}) %collective-permute-start.17) | collective-permute-done | bytes 24608 | tf_op jit(solution)/shard_map/ppermute | solution.py:251
  57.0 0.0 collective-permute-done.14.refs_4_
  57.0 0.0 copy-start.13
  57.0 3.7 %shard_map.143 = f32[24,8,32,128]{3,2,1,0:T(8,128)S(1)} custom-call(f32[24,8,32,128]{3,2,1,0:T(8,128)S(1)} %get-tuple-element.45.refs_0_, f32[24,8,32,128]{3,2,1,0:T(8,128)S(1)} %copy-done.1, bf16[24,32,128]{2,1,0:T(8,128)(2,1)S(1)} %collective-permute-done.12.refs_2_, bf16[24,32,128]{2,1,0:T(8,128)(2,1)S(1)} %collective-permute-done.13.refs_3_, ...), custom_call_target="tpu_custom_call" | custom-call | tf_op jit(solution)/shard_map/pallas_call | solution.py:256
  60.7 0.0 copy-start.2
  60.7 1.7 copy-done.2
  62.4 1.2 broadcast_in_dim.30.b1
  63.6 1.0 broadcast_in_dim.31.b2
  64.5 0.8 broadcast_in_dim.32.b3
  65.3 0.7 broadcast_in_dim.56.b4
  66.0 74.1 %shard_map.144 = (f32[6144,128]{1,0:T(8,128)}, f32[96,128]{1,0:T(8,128)}, bf16[24,32,128]{2,1,0:T(8,128)(2,1)}, bf16[24,32,128]{2,1,0:T(8,128)(2,1)}, f32[24,8,1...) custom-call(s32[97]{0:T(128)} %pad_add_fusion.listed, ...), custom_call_target="tpu_custom_call" | custom-call | tf_op jit(solution)/shard_map/pallas_call | solution.py:331
  140.1 0.1 collective-permute-start.18
  140.2 2.7 %collective-permute-start.19 = (bf16[24,32,128]{2,1,0:T(8,128)(2,1)}, bf16[24,32,128]{2,1,0:T(8,128)(2,1)S(1)}, u32[]{:S(2)}, u32[]{:S(2)}) collective-permute-start(bf16[24,32,128]{2,1,0:T(8,128)(2,1)} %get-tuple-element.54), channel_id=1, source_target_pairs={{32,0},{64,32},{96,64},{0,96},{33,1},{65,33},{97,65},{1,97},{34,2}... | collective-permute-start | bytes 589832 | tf_op jit(solution)/shard_map/ppermute | solution.py:251
  142.8 0.9 reduce_sum.37
  143.8 0.1 select_reduce_fusion
  143.9 0.8 broadcast_in_dim.59
  144.7 6.4 %all-to-all-start = ((f32[128,1,128]{2,1,0:T(1,128)}), f32[128,1,128]{2,1,0:T(1,128)S(1)}, u32[]{:S(2)}, u32[]{:S(2)}) async-start(f32[128,1,128]{2,1,0:T(1,128)} %broadcast_in_dim.59), calls=%async_computation | async-start | bytes 131072 | tf_op jit(solution)/shard_map/all_to_all | solution.py:268
  151.1 1.6 collective-permute-start.22
  152.8 1.4 collective-permute-start.20
  154.1 1.8 %collective-permute-start.21 = (f32[24,8,128]{2,1,0:T(8,128)}, f32[24,8,128]{2,1,0:T(8,128)S(1)}, u32[]{:S(2)}, u32[]{:S(2)}) collective-permute-start(f32[24,8,128]{2,1,0:T(8,128)} %get-tuple-element.56), channel_id=1, source_target_pairs={{8,0},{16,8},{24,16},{0,24},{9,1},{17,9},{25,17},{1,25},{10,2},{18... | collective-permute-start | bytes 294920 | tf_op jit(solution)/shard_map/ppermute | solution.py:251
  155.9 1.0 collective-permute-start.23
  156.9 3.6 %all-to-all-done = f32[128,1,128]{2,1,0:T(1,128)S(1)} async-done(((f32[128,1,128]{2,1,0:T(1,128)}), f32[128,1,128]{2,1,0:T(1,128)S(1)}, u32[]{:S(2)}, u32[]{:S(2)}) %all-to-all-start) | async-done | bytes 65568 | tf_op jit(solution)/shard_map/all_to_all | solution.py:268
  160.6 0.7 slice_reduce_fusion
  162.0 1.9 %copy-done.3 = f32[6144,128]{1,0:T(8,128)S(1)} copy-done((f32[6144,128]{1,0:T(8,128)S(1)}, f32[6144,128]{1,0:T(8,128)}, u32[]{:S(2)}) %copy-start.3) | copy-done | bytes 3145752
  163.9 4.8 %shard_map.145 = f32[24,8,32,128]{3,2,1,0:T(8,128)} custom-call(f32[24]{0:T(128)S(1)} %copy-done.6, f32[24,8,32,128]{3,2,1,0:T(8,128)S(1)} %bitcast.18, bf16[24,32,128]{2,1,0:T(8,128)(2,1)S(1)} %collective-permute-done.18.xlo, bf16[24,32,128]{2,1,0:T(8,128)(2,1)S(1)} %collective-permute-done.19.xhi, f32[24,8,128]{2,1,0:T(8,128)S(1)} %collective-permute-done.20.ylo, ...), custom_call_target="tpu_custom_call" | custom-call | tf_op jit(solution)/shard_map/pallas_call | solution.py:345
  (40 shorter events, 0.1 us)
Async XLA Ops:
  0.6 1.9 %copy-start = (f32[24,8,32,128]{3,2,1,0:T(8,128)S(1)}, f32[24,8,32,128]{3,2,1,0:T(8,128)}, u32[]{:S(2)}) copy-start(f32[24,8,32,128]{3,2,1,0:T(8,128)} %refs_1_.3) | copy-start | bytes 9437188
  2.5 1.0 copy-start.4
  3.5 11.9 %copy-start.8 = (bf16[1600,800]{0,1:T(8,128)(2,1)S(1)}, bf16[1600,800]{0,1:T(8,128)(2,1)}, u32[]{:S(2)}) copy-start(bf16[1600,800]{0,1:T(8,128)(2,1)} %param.18) | copy-start | bytes 7680004
  4.9 0.6 copy-start.7
  5.5 20.9 %collective-permute-start = (bf16[25,32,128]{2,1,0:T(8,128)(2,1)}, bf16[25,32,128]{2,1,0:T(8,128)(2,1)}, u32[]{:S(2)}, u32[]{:S(2)}) collective-permute-start(bf16[25,32,128]{2,1,0:T(8,128)(2,1)} %get-tuple-element.31), channel_id=1, source_target_pairs={{0,32},{32,64},{64,96},{96,0},{1,33},{33,65},{65,97},{97,1},{2,34}... | collective-permute-start | bytes 614408 | tf_op jit(solution)/shard_map/ppermute | solution.py:250
  7.5 18.9 %collective-permute-start.1 = (bf16[25,32,128]{2,1,0:T(8,128)(2,1)}, bf16[25,32,128]{2,1,0:T(8,128)(2,1)}, u32[]{:S(2)}, u32[]{:S(2)}) collective-permute-start(bf16[25,32,128]{2,1,0:T(8,128)(2,1)} %get-tuple-element.32), channel_id=1, source_target_pairs={{32,0},{64,32},{96,64},{0,96},{33,1},{65,33},{97,65},{1,97},{34,2}... | collective-permute-start | bytes 614408 | tf_op jit(solution)/shard_map/ppermute | solution.py:251
  8.8 17.6 %collective-permute-start.2 = (f32[25,8,128]{2,1,0:T(8,128)}, f32[25,8,128]{2,1,0:T(8,128)}, u32[]{:S(2)}, u32[]{:S(2)}) collective-permute-start(f32[25,8,128]{2,1,0:T(8,128)} %get-tuple-element.33), channel_id=1, source_target_pairs={{0,8},{8,16},{16,24},{24,0},{1,9},{9,17},{17,25},{25,1},{2,10},{10... | collective-permute-start | bytes 307208 | tf_op jit(solution)/shard_map/ppermute | solution.py:250
  10.6 15.8 %collective-permute-start.3 = (f32[25,8,128]{2,1,0:T(8,128)}, f32[25,8,128]{2,1,0:T(8,128)}, u32[]{:S(2)}, u32[]{:S(2)}) collective-permute-start(f32[25,8,128]{2,1,0:T(8,128)} %get-tuple-element.34), channel_id=1, source_target_pairs={{8,0},{16,8},{24,16},{0,24},{9,1},{17,9},{25,17},{1,25},{10,2},{18... | collective-permute-start | bytes 307208 | tf_op jit(solution)/shard_map/ppermute | solution.py:251
  12.7 10.2 %copy-start.9 = (f32[1600]{0:T(1024)S(1)}, f32[1600]{0:T(1024)}, u32[]{:S(2)}) copy-start(f32[1600]{0:T(1024)} %param.17) | copy-start | bytes 19204
  12.7 13.7 %copy-start.1 = (f32[24,8,32,128]{3,2,1,0:T(8,128)S(1)}, f32[24,8,32,128]{3,2,1,0:T(8,128)}, u32[]{:S(2)}) copy-start(f32[24,8,32,128]{3,2,1,0:T(8,128)} %refs_1_.3) | copy-start | bytes 9437188
  12.7 13.7 %copy-start.5 = (f32[3,8,32,128]{3,2,1,0:T(8,128)S(1)}, f32[3,8,32,128]{3,2,1,0:T(8,128)}, u32[]{:S(2)}) copy-start(f32[3,8,32,128]{3,2,1,0:T(8,128)} %refs_7_.1) | copy-start | bytes 1179652
  12.7 10.2 %collective-permute-start.4 = (f32[25,1,256]{2,1,0:T(1,128)}, f32[25,1,256]{2,1,0:T(1,128)}, u32[]{:S(2)}, u32[]{:S(2)}) collective-permute-start(f32[25,1,256]{2,1,0:T(1,128)} %get-tuple-element.35), channel_id=1, source_target_pairs={{0,1},{1,2},{2,3},{3,4},{4,5},{5,6},{6,7},{7,0},{8,9},{9,10},{10,1... | collective-permute-start | bytes 76808 | tf_op jit(solution)/shard_map/ppermute | solution.py:250
  20.8 10.8 %copy-start.10 = (f32[800]{0:T(1024)S(1)}, f32[800]{0:T(1024)}, u32[]{:S(2)}) copy-start(f32[800]{0:T(1024)} %param.19) | copy-start | bytes 9604
  20.8 17.8 %copy-start.11 = (f32[400]{0:T(512)S(1)}, f32[400]{0:T(512)}, u32[]{:S(2)}) copy-start(f32[400]{0:T(512)} %param.21) | copy-start | bytes 4804
  22.9 3.5 %collective-permute-start.5 = (f32[25,1,256]{2,1,0:T(1,128)}, f32[25,1,256]{2,1,0:T(1,128)S(1)}, u32[]{:S(2)}, u32[]{:S(2)}) collective-permute-start(f32[25,1,256]{2,1,0:T(1,128)} %copy-done.7), channel_id=1, source_target_pairs={{1,0},{2,1},{3,2},{4,3},{5,4},{6,5},{7,6},{0,7},{9,8},{10,9},{11,1... | collective-permute-start | bytes 76808 | tf_op jit(solution)/shard_map/ppermute | solution.py:251
  31.6 5.5 %collective-permute-start.10 = (f32[24,1,256]{2,1,0:T(1,128)S(1)}, f32[24,1,256]{2,1,0:T(1,128)S(1)}, u32[]{:S(2)}, u32[]{:S(2)}) collective-permute-start(f32[24,1,256]{2,1,0:T(1,128)S(1)} %get-tuple-element.42), channel_id=1, source_target_pairs={{0,1},{1,2},{2,3},{3,4},{4,5},{5,6},{6,7},{7,0},{8,9},{9,10},{10,1... | collective-permute-start | bytes 73736 | tf_op jit(solution)/shard_map/ppermute | solution.py:250
  31.7 9.7 %collective-permute-start.6 = (bf16[24,32,128]{2,1,0:T(8,128)(2,1)S(1)}, bf16[24,32,128]{2,1,0:T(8,128)(2,1)S(1)}, u32[]{:S(2)}, u32[]{:S(2)}) collective-permute-start(bf16[24,32,128]{2,1,0:T(8,128)(2,1)S(1)} %get-tuple-element.38), channel_id=1, source_target_pairs={{0,32},{32,64},{64,96},{96,0},{1,33},{33,65},{65,97},{97,1},{2,34}... | collective-permute-start | bytes 589832 | tf_op jit(solution)/shard_map/ppermute | solution.py:250
  31.7 9.6 %collective-permute-start.7 = (bf16[24,32,128]{2,1,0:T(8,128)(2,1)S(1)}, bf16[24,32,128]{2,1,0:T(8,128)(2,1)S(1)}, u32[]{:S(2)}, u32[]{:S(2)}) collective-permute-start(bf16[24,32,128]{2,1,0:T(8,128)(2,1)S(1)} %get-tuple-element.39), channel_id=1, source_target_pairs={{32,0},{64,32},{96,64},{0,96},{33,1},{65,33},{97,65},{1,97},{34,2}... | collective-permute-start | bytes 589832 | tf_op jit(solution)/shard_map/ppermute | solution.py:251
  34.4 6.9 %collective-permute-start.8 = (f32[24,8,128]{2,1,0:T(8,128)S(1)}, f32[24,8,128]{2,1,0:T(8,128)S(1)}, u32[]{:S(2)}, u32[]{:S(2)}) collective-permute-start(f32[24,8,128]{2,1,0:T(8,128)S(1)} %get-tuple-element.40), channel_id=1, source_target_pairs={{0,8},{8,16},{16,24},{24,0},{1,9},{9,17},{17,25},{25,1},{2,10},{10... | collective-permute-start | bytes 294920 | tf_op jit(solution)/shard_map/ppermute | solution.py:250
  34.4 6.9 %collective-permute-start.9 = (f32[24,8,128]{2,1,0:T(8,128)S(1)}, f32[24,8,128]{2,1,0:T(8,128)S(1)}, u32[]{:S(2)}, u32[]{:S(2)}) collective-permute-start(f32[24,8,128]{2,1,0:T(8,128)S(1)} %get-tuple-element.41), channel_id=1, source_target_pairs={{8,0},{16,8},{24,16},{0,24},{9,1},{17,9},{25,17},{1,25},{10,2},{18... | collective-permute-start | bytes 294920 | tf_op jit(solution)/shard_map/ppermute | solution.py:251
  37.1 4.2 %collective-permute-start.11 = (f32[24,1,256]{2,1,0:T(1,128)S(1)}, f32[24,1,256]{2,1,0:T(1,128)S(1)}, u32[]{:S(2)}, u32[]{:S(2)}) collective-permute-start(f32[24,1,256]{2,1,0:T(1,128)S(1)} %get-tuple-element.43), channel_id=1, source_target_pairs={{1,0},{2,1},{3,2},{4,3},{5,4},{6,5},{7,6},{0,7},{9,8},{10,9},{11,1... | collective-permute-start | bytes 73736 | tf_op jit(solution)/shard_map/ppermute | solution.py:251
  41.3 8.8 %copy-start.12 = (s32[1,96]{1,0:T(1,128)S(1)}, s32[1,96]{1,0:T(1,128)}, u32[]{:S(2)}) copy-start(s32[1,96]{1,0:T(1,128)} %param.24) | copy-start | bytes 1156
  45.8 11.2 %collective-permute-start.12 = (bf16[24,32,128]{2,1,0:T(8,128)(2,1)S(1)}, bf16[24,32,128]{2,1,0:T(8,128)(2,1)S(1)}, u32[]{:S(2)}, u32[]{:S(2)}) collective-permute-start(bf16[24,32,128]{2,1,0:T(8,128)(2,1)S(1)} %get-tuple-element.46), channel_id=1, source_target_pairs={{0,32},{32,64},{64,96},{96,0},{1,33},{33,65},{65,97},{97,1},{2,34}... | collective-permute-start | bytes 589832 | tf_op jit(solution)/shard_map/ppermute | solution.py:250
  45.8 11.2 %collective-permute-start.13 = (bf16[24,32,128]{2,1,0:T(8,128)(2,1)S(1)}, bf16[24,32,128]{2,1,0:T(8,128)(2,1)S(1)}, u32[]{:S(2)}, u32[]{:S(2)}) collective-permute-start(bf16[24,32,128]{2,1,0:T(8,128)(2,1)S(1)} %get-tuple-element.47), channel_id=1, source_target_pairs={{32,0},{64,32},{96,64},{0,96},{33,1},{65,33},{97,65},{1,97},{34,2}... | collective-permute-start | bytes 589832 | tf_op jit(solution)/shard_map/ppermute | solution.py:251
  48.5 5.2 %collective-permute-start.16 = (f32[24,1,256]{2,1,0:T(1,128)S(1)}, f32[24,1,256]{2,1,0:T(1,128)S(1)}, u32[]{:S(2)}, u32[]{:S(2)}) collective-permute-start(f32[24,1,256]{2,1,0:T(1,128)S(1)} %get-tuple-element.50), channel_id=1, source_target_pairs={{0,1},{1,2},{2,3},{3,4},{4,5},{5,6},{6,7},{7,0},{8,9},{9,10},{10,1... | collective-permute-start | bytes 73736 | tf_op jit(solution)/shard_map/ppermute | solution.py:250
  50.8 6.2 %collective-permute-start.14 = (f32[24,8,128]{2,1,0:T(8,128)S(1)}, f32[24,8,128]{2,1,0:T(8,128)S(1)}, u32[]{:S(2)}, u32[]{:S(2)}) collective-permute-start(f32[24,8,128]{2,1,0:T(8,128)S(1)} %get-tuple-element.48), channel_id=1, source_target_pairs={{0,8},{8,16},{16,24},{24,0},{1,9},{9,17},{17,25},{25,1},{2,10},{10... | collective-permute-start | bytes 294920 | tf_op jit(solution)/shard_map/ppermute | solution.py:250
  51.1 5.9 %collective-permute-start.15 = (f32[24,8,128]{2,1,0:T(8,128)S(1)}, f32[24,8,128]{2,1,0:T(8,128)S(1)}, u32[]{:S(2)}, u32[]{:S(2)}) collective-permute-start(f32[24,8,128]{2,1,0:T(8,128)S(1)} %get-tuple-element.49), channel_id=1, source_target_pairs={{8,0},{16,8},{24,16},{0,24},{9,1},{17,9},{25,17},{1,25},{10,2},{18... | collective-permute-start | bytes 294920 | tf_op jit(solution)/shard_map/ppermute | solution.py:251
  53.7 3.3 %collective-permute-start.17 = (f32[24,1,256]{2,1,0:T(1,128)S(1)}, f32[24,1,256]{2,1,0:T(1,128)S(1)}, u32[]{:S(2)}, u32[]{:S(2)}) collective-permute-start(f32[24,1,256]{2,1,0:T(1,128)S(1)} %get-tuple-element.51), channel_id=1, source_target_pairs={{1,0},{2,1},{3,2},{4,3},{5,4},{6,5},{7,6},{0,7},{9,8},{10,9},{11,1... | collective-permute-start | bytes 73736 | tf_op jit(solution)/shard_map/ppermute | solution.py:251
  57.0 8.3 %copy-start.13 = (f32[24]{0:T(128)S(1)}, f32[24]{0:T(128)}, u32[]{:S(2)}) copy-start(f32[24]{0:T(128)} %param.23) | copy-start | bytes 292
  60.7 1.7 copy-start.2
  66.0 77.8 %copy-start.14 = (s32[1,96]{1,0:T(1,128)S(1)}, s32[1,96]{1,0:T(1,128)}, u32[]{:S(2)}) copy-start(s32[1,96]{1,0:T(1,128)} %param.25) | copy-start | bytes 1156
  66.0 96.0 %copy-start.6 = (f32[24]{0:T(128)S(1)}, f32[24]{0:T(128)}, u32[]{:S(2)}) copy-start(f32[24]{0:T(128)} %rates.1) | copy-start | bytes 292
  140.1 21.9 %collective-permute-start.18 = (bf16[24,32,128]{2,1,0:T(8,128)(2,1)}, bf16[24,32,128]{2,1,0:T(8,128)(2,1)S(1)}, u32[]{:S(2)}, u32[]{:S(2)}) collective-permute-start(bf16[24,32,128]{2,1,0:T(8,128)(2,1)} %get-tuple-element.53), channel_id=1, source_target_pairs={{0,32},{32,64},{64,96},{96,0},{1,33},{33,65},{65,97},{97,1},{2,34}... | collective-permute-start | bytes 589832 | tf_op jit(solution)/shard_map/ppermute | solution.py:250
  140.2 21.8 %collective-permute-start.19 = (bf16[24,32,128]{2,1,0:T(8,128)(2,1)}, bf16[24,32,128]{2,1,0:T(8,128)(2,1)S(1)}, u32[]{:S(2)}, u32[]{:S(2)}) collective-permute-start(bf16[24,32,128]{2,1,0:T(8,128)(2,1)} %get-tuple-element.54), channel_id=1, source_target_pairs={{32,0},{64,32},{96,64},{0,96},{33,1},{65,33},{97,65},{1,97},{34,2}... | collective-permute-start | bytes 589832 | tf_op jit(solution)/shard_map/ppermute | solution.py:251
  144.7 15.8 %all-to-all-start = ((f32[128,1,128]{2,1,0:T(1,128)}), f32[128,1,128]{2,1,0:T(1,128)S(1)}, u32[]{:S(2)}, u32[]{:S(2)}) async-start(f32[128,1,128]{2,1,0:T(1,128)} %broadcast_in_dim.59), calls=%async_computation | async-start | bytes 131072 | tf_op jit(solution)/shard_map/all_to_all | solution.py:268
  151.1 4.8 %collective-permute-start.22 = (f32[24,1,256]{2,1,0:T(1,128)}, f32[24,1,256]{2,1,0:T(1,128)S(1)}, u32[]{:S(2)}, u32[]{:S(2)}) collective-permute-start(f32[24,1,256]{2,1,0:T(1,128)} %get-tuple-element.57), channel_id=1, source_target_pairs={{0,1},{1,2},{2,3},{3,4},{4,5},{5,6},{6,7},{7,0},{8,9},{9,10},{10,1... | collective-permute-start | bytes 73736 | tf_op jit(solution)/shard_map/ppermute | solution.py:250
  152.8 9.2 %collective-permute-start.20 = (f32[24,8,128]{2,1,0:T(8,128)}, f32[24,8,128]{2,1,0:T(8,128)S(1)}, u32[]{:S(2)}, u32[]{:S(2)}) collective-permute-start(f32[24,8,128]{2,1,0:T(8,128)} %get-tuple-element.55), channel_id=1, source_target_pairs={{0,8},{8,16},{16,24},{24,0},{1,9},{9,17},{17,25},{25,1},{2,10},{10... | collective-permute-start | bytes 294920 | tf_op jit(solution)/shard_map/ppermute | solution.py:250
  154.1 7.8 %collective-permute-start.21 = (f32[24,8,128]{2,1,0:T(8,128)}, f32[24,8,128]{2,1,0:T(8,128)S(1)}, u32[]{:S(2)}, u32[]{:S(2)}) collective-permute-start(f32[24,8,128]{2,1,0:T(8,128)} %get-tuple-element.56), channel_id=1, source_target_pairs={{8,0},{16,8},{24,16},{0,24},{9,1},{17,9},{25,17},{1,25},{10,2},{18... | collective-permute-start | bytes 294920 | tf_op jit(solution)/shard_map/ppermute | solution.py:251
  155.9 6.0 %collective-permute-start.23 = (f32[24,1,256]{2,1,0:T(1,128)}, f32[24,1,256]{2,1,0:T(1,128)S(1)}, u32[]{:S(2)}, u32[]{:S(2)}) collective-permute-start(f32[24,1,256]{2,1,0:T(1,128)} %get-tuple-element.58), channel_id=1, source_target_pairs={{1,0},{2,1},{3,2},{4,3},{5,4},{6,5},{7,6},{0,7},{9,8},{10,9},{11,1... | collective-permute-start | bytes 73736 | tf_op jit(solution)/shard_map/ppermute | solution.py:251
  162.0 1.9 %copy-start.3 = (f32[6144,128]{1,0:T(8,128)S(1)}, f32[6144,128]{1,0:T(8,128)}, u32[]{:S(2)}) copy-start(f32[6144,128]{1,0:T(8,128)} %get-tuple-element.52) | copy-start | bytes 9437188

commit v4 on v3

--- a/solution.py
+++ b/solution.py
@@ -10,6 +10,7 @@
 GROUP = 4
 TOGETHER = 8
 LISTED = 96
+NETWORK_MIB = 30
 ALL = ("gx", "gy", "gz")
 F32, BF16 = jnp.float32, jnp.bfloat16
 TN = (((0,), (0,)), ((), ()))
@@ -167,7 +168,13 @@
             out[f, x] = centre + rate * spread
 
 
-def network_kernel(listed, flowed, w1, b1, w2, b2, w3, b3, w4, b4, out, heat, xf, xl, yf, yl, zf, zl):
+def columns_kernel(weights, *refs):
+    refs[4][...] = weights[...].astype(F32).T.astype(BF16)
+    for row, out in zip(refs[:4], refs[5:]):
+        out[...] = jnp.broadcast_to(row[...], (128, row.shape[1])).T
+
+
+def network_kernel(listed, flowed, owned_by, w1, b1, b2, b3, b4, w2, w3, w4, out, sent, xf, xl, yf, yl, zf, zl, heat):
     def copy(f, carry):
         rows = pl.ds(pl.multiple_of(256 * f, 256), 256)
         out[rows, :] = flowed[rows, :]
@@ -175,7 +182,7 @@
 
     def activated(weights, bias, cells):
         half = jnp.dot(weights[...], cells, preferred_element_type=F32)
-        half = half + jnp.concatenate([bias[...]] * TOGETHER, axis=1)
+        half = 0.5 * (half + jnp.concatenate([bias[...]] * TOGETHER, axis=1))
         return (half + half * jnp.tanh(half)).astype(BF16)
 
     def react(step, carry):
@@ -204,9 +211,13 @@
         zl[f] = ends[1:2]
         return carry
 
+    heat[...] = jnp.zeros_like(heat)
     lax.fori_loop(0, 24, copy, 0)
     lax.fori_loop(0, (listed[0] + TOGETHER - 1) // TOGETHER, react, 0)
     lax.fori_loop(0, 24, faces, 0)
+    sent[...] = jnp.dot(
+        owned_by[...], heat[...], preferred_element_type=F32, precision=lax.Precision.HIGHEST
+    )
 
 
 def params(mib):
@@ -287,12 +298,7 @@
     ids, owners = react_list[0], owner_table[0]
     count = jnp.sum((ids >= 0).astype(jnp.int32))
     listed = jnp.concatenate([count[None], jnp.where(ids >= 0, ids, ids[0])])
-    half = jnp.asarray(0.5, BF16)
-    w1, w2, w3, w4 = (weight_in * half).T, (weight_mid * half).T, (weight_low * half).T, weight_out.T
-    b1, b2, b3, b4 = (
-        jnp.broadcast_to((s * b)[:, None], (b.shape[0], 128))
-        for s, b in ((0.5, bias_in), (0.5, bias_mid), (0.5, bias_low), (1.0, bias_out))
-    )
+    owned_by = (owners[None, :] == jnp.arange(128, dtype=jnp.int32)[:, None]).astype(F32)
 
     faces = pl.pallas_call(
         prep_kernel, out_shape=face_shapes(25), compiler_params=params(24)
@@ -313,6 +319,14 @@
         [brick, sds((6, 8, 32, 128), F32), *face_shapes(24)],
         [BRICK, whole((6, 8, 32, 128)), *FACES],
     )
+    biases = (bias_in, bias_mid, bias_low, bias_out)
+    one, *given = lax.optimization_barrier((one, weight_in, *(b.reshape(1, -1) for b in biases)))
+    columns = pl.pallas_call(
+        columns_kernel,
+        out_shape=[sds(weight_in.shape[::-1], BF16), *(sds((b.shape[0], 128), F32) for b in biases)],
+        compiler_params=params(16),
+        cost_estimate=pl.CostEstimate(flops=0, bytes_accessed=4 * 2**20, transcendentals=0),
+    )(*given)
     two, *faces = section(
         2,
         (one, fields, *exchange(faces), coef),
@@ -328,20 +342,17 @@
         [BRICK],
     )
     in_vmem = pl.BlockSpec(memory_space=pltpu.VMEM)
-    reacted, heat, *faces = pl.pallas_call(
+    reacted, sent, *faces = pl.pallas_call(
         network_kernel,
-        in_specs=[pl.BlockSpec(memory_space=pltpu.SMEM)] + [in_vmem] * 9,
+        in_specs=[pl.BlockSpec(memory_space=pltpu.SMEM)] + [in_vmem] * 10,
         out_specs=[in_vmem] * 8,
-        out_shape=[sds((24 * 256, 128), F32), sds((LISTED, 128), F32), *face_shapes(24)],
-        compiler_params=params(56),
-    )(listed, flowed.reshape(24 * 256, 128), w1, b1, w2, b2, w3, b3, w4, b4)
+        out_shape=[sds((24 * 256, 128), F32), sds((128, 128), F32), *face_shapes(24)],
+        scratch_shapes=[pltpu.VMEM((LISTED, 128), F32)],
+        compiler_params=params(NETWORK_MIB),
+    )(listed, flowed.reshape(24 * 256, 128), owned_by, *columns, weight_mid.T, weight_low.T, weight_out.T)
     reacted = reacted.reshape(fields.shape)
-    mean_heat = jnp.mean(heat, axis=1)
-    owned_by = owners[None, :] == jnp.arange(128, dtype=jnp.int32)[:, None]
-    by_owner = jnp.sum(jnp.where(owned_by, mean_heat[None, :], 0.0), axis=1)
     around = exchange(faces)
-    sent = jnp.broadcast_to(by_owner[:, None, None], (128, 1, 128))
-    owner_activity = (jnp.sum(swap(sent)[:, 0, 0]) / 8.0).reshape(1)
+    heats = swap(sent.reshape(128, 1, 128))
     updated = pl.pallas_call(
         diffuse_kernel,
         grid=(24 // GROUP,),
@@ -350,7 +361,10 @@
         out_shape=brick,
         scratch_shapes=[pltpu.VMEM((GROUP, 256, 128), F32)],
         compiler_params=params(24),
+        cost_estimate=pl.CostEstimate(flops=10**9, bytes_accessed=24 * 2**20, transcendentals=0),
     )(diffusivity, reacted, *around)
+    heats, updated = lax.optimization_barrier((heats, updated))
+    owner_activity = (jnp.sum(heats) / (8.0 * 128.0)).reshape(1)
     return (updated, owner_activity)
 
 

time: 170 us -> 162 us (0.953)
  starting transfers between devices: 39.2 us -> 104 us
  Pallas kernels: 93.6 us -> 36.1 us
  local copies, waits for them, and re-layouts: 13.3 us -> 4.91 us
  other arithmetic: 9.31 us -> 2.97 us
    pallas_call x1, Pallas kernels: 74.1 us -> 17.6 us  [local(): pl.pallas_call(network_kernel, in_specs=[pl.BlockSpec(memory_space=pltpu....]
    ppermute x12, starting transfers between devices: 11.7 us -> 67.7 us  [exchange(): got.append(lax.ppermute(last, axis, [(i, (i + 1) % n) for i in range(n)]))]
    ppermute x12, starting transfers between devices: 21.1 us -> 30.9 us  [exchange(): got.append(lax.ppermute(first, axis, [((i + 1) % n, i) for i in range(n)]))]
    ppermute x12, waiting for transfers between devices: 8.09 us -> 1.52 us  [exchange(): got.append(lax.ppermute(first, axis, [((i + 1) % n, i) for i in range(n)]))]
    transpose x3 -> x0, other arithmetic: 5.63 us -> none  [local(): w1, w2, w3, w4 = ((weight_in * half).T, (weight_mid * half).T, (weight_lo...]
    ppermute x12, waiting for transfers between devices: 0.03 us -> 5.56 us  [exchange(): got.append(lax.ppermute(last, axis, [(i, (i + 1) % n) for i in range(n)]))]
    broadcast_in_dim x5 -> x0, local copies, waits for them, and re-layouts: 4.44 us -> none  [the longest x4 3.6 us: local(): jnp.broadcast_to((s * b)[:, None], (b.shape[0], 128))]
    unnamed x31 -> x32, local copies, waits for them, and re-layouts: 8.89 us -> 4.9 us
  transfers between devices with their start and end apart: 25 -> 25, of which waited for: 4 -> 6; matrix products, arithmetic and copies ran while one was open for 7% -> 1% of each run, Pallas kernels for 0% -> 4%
where the time goes in v4:
time: 162 us; the launch traced here: 161 us
  starting transfers between devices  104 us (64%)
  Pallas kernels  36.1 us (22%)
  waiting for transfers between devices  10.2 us (6%)
  local copies, waits for them, and re-layouts  4.91 us (3%)
  other arithmetic  2.97 us (2%)
  between operations  2.7 us (2%)
    ppermute x12, starting transfers between devices, exchange(): got.append(lax.ppermute(last, axis, [(i, (i + 1) % n) for i in range(n)]))  67.7 us
    ppermute x12, starting transfers between devices, exchange(): got.append(lax.ppermute(first, axis, [((i + 1) % n, i) for i in range(n)]))  30.9 us
    pallas_call x1, Pallas kernels, local(): pl.pallas_call(network_kernel, in_specs=[pl.BlockSpec(memory_space=pltpu....  17.6 us
    pallas_call x3, Pallas kernels, section(): pl.pallas_call(functools.partial(section_kernel, kind), grid=(24 // GROUP...  12 us
    all_to_all x1, starting transfers between devices, swap(): return lax.all_to_all(tiles, ALL, split_axis=0, concat_axis=0, tiled=True)  5.75 us
    ppermute x12, waiting for transfers between devices, exchange(): got.append(lax.ppermute(last, axis, [(i, (i + 1) % n) for i in range(n)]))  5.56 us
    pallas_call x1, Pallas kernels, local(): pl.pallas_call(diffuse_kernel, grid=(24 // GROUP,), in_specs=[pl.BlockSpe...  5.33 us
    unnamed x32, local copies, waits for them, and re-layouts  4.9 us
  transfers between devices with their start and end apart: 25, of which 6 were waited for; matrix products, arithmetic and copies ran while one was open for 1% of the time, Pallas kernels for 4%

profile of v4, /device:TPU:1, one launch (start us, length us, event | category | flops | bytes accessed | tf_op | source)
XLA Modules:
  0.0 161.2 jit_solution(7055786463923312673)
XLA Ops:
  0.6 1.9 %copy-done = f32[24,8,32,128]{3,2,1,0:T(8,128)S(1)} copy-done((f32[24,8,32,128]{3,2,1,0:T(8,128)S(1)}, f32[24,8,32,128]{3,2,1,0:T(8,128)}, u32[]{:S(2)}) %copy-start) | copy-done | bytes 3145752
  2.5 1.0 copy-done.2
  3.5 0.5 shard_map.140
  4.1 0.0 copy-start.15
  4.1 0.0 copy-start.13
  4.1 0.0 copy-start.12
  4.1 2.1 %collective-permute-start = (bf16[25,32,128]{2,1,0:T(8,128)(2,1)S(1)}, bf16[25,32,128]{2,1,0:T(8,128)(2,1)S(1)}, u32[]{:S(2)}, u32[]{:S(2)}) collective-permute-start(bf16[25,32,128]{2,1,0:T(8,128)(2,1)S(1)} %get-tuple-element.44), channel_id=1, source_target_pairs={{0,32},{32,64},{64,96},{96,0},{1,33},{33,65},{65,97},{97,1},{2,34}... | collective-permute-start | bytes 614408 | tf_op jit(solution)/shard_map/ppermute | solution.py:261
  6.2 1.3 collective-permute-start.1
  7.6 1.8 %collective-permute-start.2 = (f32[25,8,128]{2,1,0:T(8,128)S(1)}, f32[25,8,128]{2,1,0:T(8,128)S(1)}, u32[]{:S(2)}, u32[]{:S(2)}) collective-permute-start(f32[25,8,128]{2,1,0:T(8,128)S(1)} %get-tuple-element.46), channel_id=1, source_target_pairs={{0,8},{8,16},{16,24},{24,0},{1,9},{9,17},{17,25},{25,1},{2,10},{10... | collective-permute-start | bytes 307208 | tf_op jit(solution)/shard_map/ppermute | solution.py:261
  9.3 2.1 %collective-permute-start.3 = (f32[25,8,128]{2,1,0:T(8,128)S(1)}, f32[25,8,128]{2,1,0:T(8,128)S(1)}, u32[]{:S(2)}, u32[]{:S(2)}) collective-permute-start(f32[25,8,128]{2,1,0:T(8,128)S(1)} %get-tuple-element.47), channel_id=1, source_target_pairs={{8,0},{16,8},{24,16},{0,24},{9,1},{17,9},{25,17},{1,25},{10,2},{18... | collective-permute-start | bytes 307208 | tf_op jit(solution)/shard_map/ppermute | solution.py:262
  11.4 2.7 %collective-permute-start.4 = (f32[25,1,256]{2,1,0:T(1,128)S(1)}, f32[25,1,256]{2,1,0:T(1,128)S(1)}, u32[]{:S(2)}, u32[]{:S(2)}) collective-permute-start(f32[25,1,256]{2,1,0:T(1,128)S(1)} %get-tuple-element.48), channel_id=1, source_target_pairs={{0,1},{1,2},{2,3},{3,4},{4,5},{5,6},{6,7},{7,0},{8,9},{9,10},{10,1... | collective-permute-start | bytes 76808 | tf_op jit(solution)/shard_map/ppermute | solution.py:261
  14.1 1.0 collective-permute-done.4.refs_5_.refs_12_
  15.1 2.3 %collective-permute-start.5 = (f32[25,1,256]{2,1,0:T(1,128)S(1)}, f32[25,1,256]{2,1,0:T(1,128)S(1)}, u32[]{:S(2)}, u32[]{:S(2)}) collective-permute-start(f32[25,1,256]{2,1,0:T(1,128)S(1)} %get-tuple-element.49), channel_id=1, source_target_pairs={{1,0},{2,1},{3,2},{4,3},{5,4},{6,5},{7,6},{0,7},{9,8},{10,9},{11,1... | collective-permute-start | bytes 76808 | tf_op jit(solution)/shard_map/ppermute | solution.py:262
  17.4 1.5 collective-permute-done.5.refs_6_.refs_13_
  18.9 0.0 collective-permute-done.2.refs_3_.refs_10_
  18.9 0.0 collective-permute-done.3.refs_4_.refs_11_
  18.9 0.0 collective-permute-done.refs_1_.refs_8_
  18.9 0.0 collective-permute-done.1.refs_2_.refs_9_
  18.9 4.0 %shard_map.141 = (f32[24,8,32,128]{3,2,1,0:T(8,128)S(1)}, f32[6,8,32,128]{3,2,1,0:T(8,128)S(1)}, bf16[24,32,128]{2,1,0:T(8,128)(2,1)S(1)}, bf16[24,32,128]{2,1,0...) custom-call(f32[24,8,32,128]{3,2,1,0:T(8,128)S(1)} %copy-done, ...), custom_call_target="tpu_custom_call" | custom-call | tf_op jit(solution)/shard_map/pallas_call | solution.py:267
  23.0 0.0 collective-permute-start.10
  23.0 0.5 collective-permute-start.11
  23.5 0.0 collective-permute-start.8
  23.5 2.7 %collective-permute-start.9 = (f32[24,8,128]{2,1,0:T(8,128)S(1)}, f32[24,8,128]{2,1,0:T(8,128)S(1)}, u32[]{:S(2)}, u32[]{:S(2)}) collective-permute-start(f32[24,8,128]{2,1,0:T(8,128)S(1)} %get-tuple-element.55), channel_id=1, source_target_pairs={{8,0},{16,8},{24,16},{0,24},{9,1},{17,9},{25,17},{1,25},{10,2},{18... | collective-permute-start | bytes 294920 | tf_op jit(solution)/shard_map/ppermute | solution.py:262
  26.2 0.0 collective-permute-start.6
  26.2 0.0 collective-permute-done.10.refs_6_
  26.2 2.7 %collective-permute-start.7 = (bf16[24,32,128]{2,1,0:T(8,128)(2,1)S(1)}, bf16[24,32,128]{2,1,0:T(8,128)(2,1)S(1)}, u32[]{:S(2)}, u32[]{:S(2)}) collective-permute-start(bf16[24,32,128]{2,1,0:T(8,128)(2,1)S(1)} %get-tuple-element.53), channel_id=1, source_target_pairs={{32,0},{64,32},{96,64},{0,96},{33,1},{65,33},{97,65},{1,97},{34,2}... | collective-permute-start | bytes 589832 | tf_op jit(solution)/shard_map/ppermute | solution.py:262
  28.9 0.0 collective-permute-done.9.refs_5_
  28.9 3.0 %collective-permute-done.6.refs_2_ = bf16[24,32,128]{2,1,0:T(8,128)(2,1)S(1)} collective-permute-done((bf16[24,32,128]{2,1,0:T(8,128)(2,1)S(1)}, bf16[24,32,128]{2,1,0:T(8,128)(2,1)S(1)}, u32[]{:S(2)}, u32[]{:S(2)}) %collective-permute-start.6) | collective-permute-done | bytes 196640 | tf_op jit(solution)/shard_map/ppermute | solution.py:261
  31.9 0.0 copy-start.10
  31.9 4.4 %shard_map.142 = (f32[24,8,32,128]{3,2,1,0:T(8,128)S(1)}, bf16[24,32,128]{2,1,0:T(8,128)(2,1)S(1)}, bf16[24,32,128]{2,1,0:T(8,128)(2,1)S(1)}, f32[24,8,128]{2,1,...) custom-call(f32[24,8,32,128]{3,2,1,0:T(8,128)S(1)} %get-tuple-element.51.refs_0_, ...), custom_call_target="tpu_custom_call" | custom-call | tf_op jit(solution)/shard_map/pallas_call | solution.py:267
  36.3 4.0 %collective-permute-start.16 = (f32[24,1,256]{2,1,0:T(1,128)S(1)}, f32[24,1,256]{2,1,0:T(1,128)S(1)}, u32[]{:S(2)}, u32[]{:S(2)}) collective-permute-start(f32[24,1,256]{2,1,0:T(1,128)S(1)} %get-tuple-element.64), channel_id=1, source_target_pairs={{0,1},{1,2},{2,3},{3,4},{4,5},{5,6},{6,7},{7,0},{8,9},{9,10},{10,1... | collective-permute-start | bytes 73736 | tf_op jit(solution)/shard_map/ppermute | solution.py:261
  40.3 0.0 collective-permute-start.12
  40.3 2.7 %collective-permute-start.13 = (bf16[24,32,128]{2,1,0:T(8,128)(2,1)S(1)}, bf16[24,32,128]{2,1,0:T(8,128)(2,1)S(1)}, u32[]{:S(2)}, u32[]{:S(2)}) collective-permute-start(bf16[24,32,128]{2,1,0:T(8,128)(2,1)S(1)} %get-tuple-element.61), channel_id=1, source_target_pairs={{32,0},{64,32},{96,64},{0,96},{33,1},{65,33},{97,65},{1,97},{34,2}... | collective-permute-start | bytes 589832 | tf_op jit(solution)/shard_map/ppermute | solution.py:262
  43.0 0.7 fusion.1
  43.6 0.9 collective-permute-start.17
  44.5 0.0 collective-permute-start.14
  44.6 2.7 %collective-permute-start.15 = (f32[24,8,128]{2,1,0:T(8,128)S(1)}, f32[24,8,128]{2,1,0:T(8,128)S(1)}, u32[]{:S(2)}, u32[]{:S(2)}) collective-permute-start(f32[24,8,128]{2,1,0:T(8,128)S(1)} %get-tuple-element.63), channel_id=1, source_target_pairs={{8,0},{16,8},{24,16},{0,24},{9,1},{17,9},{25,17},{1,25},{10,2},{18... | collective-permute-start | bytes 294920 | tf_op jit(solution)/shard_map/ppermute | solution.py:262
  47.2 0.7 pad_add_fusion.listed
  48.0 0.6 shard_map.144
  48.5 0.7 collective-permute-done.14.refs_4_
  49.2 0.0 collective-permute-done.15.refs_5_
  49.2 0.0 collective-permute-done.12.refs_2_
  49.2 0.0 copy-start.1
  49.3 0.0 copy-start.3
  49.3 0.0 copy-start.8
  49.3 3.6 %shard_map.143 = f32[24,8,32,128]{3,2,1,0:T(8,128)S(1)} custom-call(f32[24,8,32,128]{3,2,1,0:T(8,128)S(1)} %get-tuple-element.59.refs_0_, f32[24,8,32,128]{3,2,1,0:T(8,128)S(1)} %copy-done, bf16[24,32,128]{2,1,0:T(8,128)(2,1)S(1)} %collective-permute-done.12.refs_2_, bf16[24,32,128]{2,1,0:T(8,128)(2,1)S(1)} %collective-permute-done.13.refs_3_, ...), custom_call_target="tpu_custom_call" | custom-call | tf_op jit(solution)/shard_map/pallas_call | solution.py:267
  52.9 0.0 copy-start.11
  53.0 17.6 %shard_map.145 = (f32[6144,128]{1,0:T(8,128)S(1)}, f32[128,128]{1,0:T(8,128)S(1)}, bf16[24,32,128]{2,1,0:T(8,128)(2,1)}, bf16[24,32,128]{2,1,0:T(8,128)(2,1)}, f...) custom-call(s32[97]{0:T(128)S(1)} %pad_add_fusion.listed, ...), custom_call_target="tpu_custom_call" | custom-call | tf_op jit(solution)/shard_map/pallas_call | solution.py:345
  70.6 0.6 copy-done.5
  71.2 7.9 %collective-permute-start.19 = (bf16[24,32,128]{2,1,0:T(8,128)(2,1)}, bf16[24,32,128]{2,1,0:T(8,128)(2,1)S(1)}, u32[]{:S(2)}, u32[]{:S(2)}) collective-permute-start(bf16[24,32,128]{2,1,0:T(8,128)(2,1)} %get-tuple-element.79), channel_id=1, source_target_pairs={{32,0},{64,32},{96,64},{0,96},{33,1},{65,33},{97,65},{1,97},{34,2}... | collective-permute-start | bytes 589832 | tf_op jit(solution)/shard_map/ppermute | solution.py:262
  79.1 53.0 %collective-permute-start.20 = (f32[24,8,128]{2,1,0:T(8,128)}, f32[24,8,128]{2,1,0:T(8,128)}, u32[]{:S(2)}, u32[]{:S(2)}) collective-permute-start(f32[24,8,128]{2,1,0:T(8,128)} %get-tuple-element.80), channel_id=1, source_target_pairs={{0,8},{8,16},{16,24},{24,0},{1,9},{9,17},{17,25},{25,1},{2,10},{10... | collective-permute-start | bytes 294920 | tf_op jit(solution)/shard_map/ppermute | solution.py:261
  132.1 3.7 %collective-permute-start.21 = (f32[24,8,128]{2,1,0:T(8,128)}, f32[24,8,128]{2,1,0:T(8,128)}, u32[]{:S(2)}, u32[]{:S(2)}) collective-permute-start(f32[24,8,128]{2,1,0:T(8,128)} %get-tuple-element.81), channel_id=1, source_target_pairs={{8,0},{16,8},{24,16},{0,24},{9,1},{17,9},{25,17},{1,25},{10,2},{18... | collective-permute-start | bytes 294920 | tf_op jit(solution)/shard_map/ppermute | solution.py:262
  135.8 4.1 %collective-permute-start.22 = (f32[24,1,256]{2,1,0:T(1,128)S(1)}, f32[24,1,256]{2,1,0:T(1,128)S(1)}, u32[]{:S(2)}, u32[]{:S(2)}) collective-permute-start(f32[24,1,256]{2,1,0:T(1,128)S(1)} %get-tuple-element.82), channel_id=1, source_target_pairs={{0,1},{1,2},{2,3},{3,4},{4,5},{5,6},{6,7},{7,0},{8,9},{9,10},{10,1... | collective-permute-start | bytes 73736 | tf_op jit(solution)/shard_map/ppermute | solution.py:261
  139.9 0.9 collective-permute-done.22.zlo
  140.9 0.6 copy-done.6
  141.5 1.3 collective-permute-start.23
  142.9 5.7 %all-to-all-start = ((f32[128,1,128]{2,1,0:T(1,128)}), f32[128,1,128]{2,1,0:T(1,128)}, u32[]{:S(2)}, u32[]{:S(2)}) async-start(f32[128,1,128]{2,1,0:T(1,128)} %bitcast.22), calls=%async_computation | async-start | bytes 131072 | tf_op jit(solution)/shard_map/all_to_all | solution.py:279
  148.6 0.0 collective-permute-done.20.ylo
  148.6 0.0 collective-permute-done.21.yhi
  148.7 0.0 collective-permute-done.19.xhi
  148.7 0.7 copy-done.7
  149.4 5.3 %shard_map.146 = f32[24,8,32,128]{3,2,1,0:T(8,128)} custom-call(f32[24]{0:T(128)S(1)} %copy-done.11, f32[24,8,32,128]{3,2,1,0:T(8,128)S(1)} %bitcast.19, bf16[24,32,128]{2,1,0:T(8,128)(2,1)S(1)} %collective-permute-done.18.xlo, bf16[24,32,128]{2,1,0:T(8,128)(2,1)S(1)} %collective-permute-done.19.xhi, f32[24,8,128]{2,1,0:T(8,128)} %collective-permute-done.20.ylo, ...), custom_call_target="tpu_custom_call" | custom-call | flops 1000000000 | bytes 25165824 | tf_op jit(solution)/shard_map/pallas_call | solution.py:356
  154.7 3.1 %all-to-all-done = f32[128,1,128]{2,1,0:T(1,128)} async-done(((f32[128,1,128]{2,1,0:T(1,128)}), f32[128,1,128]{2,1,0:T(1,128)}, u32[]{:S(2)}, u32[]{:S(2)}) %all-to-all-start) | async-done | bytes 65568 | tf_op jit(solution)/shard_map/all_to_all | solution.py:279
  157.8 1.6 reduce_sum.19
  (31 shorter events, 0.1 us)
Async XLA Ops:
  0.6 1.9 %copy-start = (f32[24,8,32,128]{3,2,1,0:T(8,128)S(1)}, f32[24,8,32,128]{3,2,1,0:T(8,128)}, u32[]{:S(2)}) copy-start(f32[24,8,32,128]{3,2,1,0:T(8,128)} %refs_1_.3) | copy-start | bytes 9437188
  2.5 1.0 copy-start.2
  4.1 24.8 %copy-start.15 = (s32[1,96]{1,0:T(1,128)S(1)}, s32[1,96]{1,0:T(1,128)}, u32[]{:S(2)}) copy-start(s32[1,96]{1,0:T(1,128)} %param.25) | copy-start | bytes 1156
  4.1 24.8 %copy-start.13 = (f32[800]{0:T(1024)S(1)}, f32[800]{0:T(1024)}, u32[]{:S(2)}) copy-start(f32[800]{0:T(1024)} %param.19) | copy-start | bytes 9604
  4.1 24.8 %copy-start.12 = (f32[1600]{0:T(1024)S(1)}, f32[1600]{0:T(1024)}, u32[]{:S(2)}) copy-start(f32[1600]{0:T(1024)} %param.17) | copy-start | bytes 19204
  4.1 14.8 %collective-permute-start = (bf16[25,32,128]{2,1,0:T(8,128)(2,1)S(1)}, bf16[25,32,128]{2,1,0:T(8,128)(2,1)S(1)}, u32[]{:S(2)}, u32[]{:S(2)}) collective-permute-start(bf16[25,32,128]{2,1,0:T(8,128)(2,1)S(1)} %get-tuple-element.44), channel_id=1, source_target_pairs={{0,32},{32,64},{64,96},{96,0},{1,33},{33,65},{65,97},{97,1},{2,34}... | collective-permute-start | bytes 614408 | tf_op jit(solution)/shard_map/ppermute | solution.py:261
  6.2 12.7 %collective-permute-start.1 = (bf16[25,32,128]{2,1,0:T(8,128)(2,1)S(1)}, bf16[25,32,128]{2,1,0:T(8,128)(2,1)S(1)}, u32[]{:S(2)}, u32[]{:S(2)}) collective-permute-start(bf16[25,32,128]{2,1,0:T(8,128)(2,1)S(1)} %get-tuple-element.45), channel_id=1, source_target_pairs={{32,0},{64,32},{96,64},{0,96},{33,1},{65,33},{97,65},{1,97},{34,2}... | collective-permute-start | bytes 614408 | tf_op jit(solution)/shard_map/ppermute | solution.py:262
  7.6 11.4 %collective-permute-start.2 = (f32[25,8,128]{2,1,0:T(8,128)S(1)}, f32[25,8,128]{2,1,0:T(8,128)S(1)}, u32[]{:S(2)}, u32[]{:S(2)}) collective-permute-start(f32[25,8,128]{2,1,0:T(8,128)S(1)} %get-tuple-element.46), channel_id=1, source_target_pairs={{0,8},{8,16},{16,24},{24,0},{1,9},{9,17},{17,25},{25,1},{2,10},{10... | collective-permute-start | bytes 307208 | tf_op jit(solution)/shard_map/ppermute | solution.py:261
  9.3 9.6 %collective-permute-start.3 = (f32[25,8,128]{2,1,0:T(8,128)S(1)}, f32[25,8,128]{2,1,0:T(8,128)S(1)}, u32[]{:S(2)}, u32[]{:S(2)}) collective-permute-start(f32[25,8,128]{2,1,0:T(8,128)S(1)} %get-tuple-element.47), channel_id=1, source_target_pairs={{8,0},{16,8},{24,16},{0,24},{9,1},{17,9},{25,17},{1,25},{10,2},{18... | collective-permute-start | bytes 307208 | tf_op jit(solution)/shard_map/ppermute | solution.py:262
  11.4 3.7 %collective-permute-start.4 = (f32[25,1,256]{2,1,0:T(1,128)S(1)}, f32[25,1,256]{2,1,0:T(1,128)S(1)}, u32[]{:S(2)}, u32[]{:S(2)}) collective-permute-start(f32[25,1,256]{2,1,0:T(1,128)S(1)} %get-tuple-element.48), channel_id=1, source_target_pairs={{0,1},{1,2},{2,3},{3,4},{4,5},{5,6},{6,7},{7,0},{8,9},{9,10},{10,1... | collective-permute-start | bytes 76808 | tf_op jit(solution)/shard_map/ppermute | solution.py:261
  15.1 3.8 %collective-permute-start.5 = (f32[25,1,256]{2,1,0:T(1,128)S(1)}, f32[25,1,256]{2,1,0:T(1,128)S(1)}, u32[]{:S(2)}, u32[]{:S(2)}) collective-permute-start(f32[25,1,256]{2,1,0:T(1,128)S(1)} %get-tuple-element.49), channel_id=1, source_target_pairs={{1,0},{2,1},{3,2},{4,3},{5,4},{6,5},{7,6},{0,7},{9,8},{10,9},{11,1... | collective-permute-start | bytes 76808 | tf_op jit(solution)/shard_map/ppermute | solution.py:262
  23.0 3.2 %collective-permute-start.10 = (f32[24,1,256]{2,1,0:T(1,128)S(1)}, f32[24,1,256]{2,1,0:T(1,128)S(1)}, u32[]{:S(2)}, u32[]{:S(2)}) collective-permute-start(f32[24,1,256]{2,1,0:T(1,128)S(1)} %get-tuple-element.56), channel_id=1, source_target_pairs={{0,1},{1,2},{2,3},{3,4},{4,5},{5,6},{6,7},{7,0},{8,9},{9,10},{10,1... | collective-permute-start | bytes 73736 | tf_op jit(solution)/shard_map/ppermute | solution.py:261
  23.0 5.9 %collective-permute-start.11 = (f32[24,1,256]{2,1,0:T(1,128)S(1)}, f32[24,1,256]{2,1,0:T(1,128)S(1)}, u32[]{:S(2)}, u32[]{:S(2)}) collective-permute-start(f32[24,1,256]{2,1,0:T(1,128)S(1)} %get-tuple-element.57), channel_id=1, source_target_pairs={{1,0},{2,1},{3,2},{4,3},{5,4},{6,5},{7,6},{0,7},{9,8},{10,9},{11,1... | collective-permute-start | bytes 73736 | tf_op jit(solution)/shard_map/ppermute | solution.py:262
  23.5 5.4 %collective-permute-start.8 = (f32[24,8,128]{2,1,0:T(8,128)S(1)}, f32[24,8,128]{2,1,0:T(8,128)S(1)}, u32[]{:S(2)}, u32[]{:S(2)}) collective-permute-start(f32[24,8,128]{2,1,0:T(8,128)S(1)} %get-tuple-element.54), channel_id=1, source_target_pairs={{0,8},{8,16},{16,24},{24,0},{1,9},{9,17},{17,25},{25,1},{2,10},{10... | collective-permute-start | bytes 294920 | tf_op jit(solution)/shard_map/ppermute | solution.py:261
  23.5 5.4 %collective-permute-start.9 = (f32[24,8,128]{2,1,0:T(8,128)S(1)}, f32[24,8,128]{2,1,0:T(8,128)S(1)}, u32[]{:S(2)}, u32[]{:S(2)}) collective-permute-start(f32[24,8,128]{2,1,0:T(8,128)S(1)} %get-tuple-element.55), channel_id=1, source_target_pairs={{8,0},{16,8},{24,16},{0,24},{9,1},{17,9},{25,17},{1,25},{10,2},{18... | collective-permute-start | bytes 294920 | tf_op jit(solution)/shard_map/ppermute | solution.py:262
  26.2 5.7 %collective-permute-start.6 = (bf16[24,32,128]{2,1,0:T(8,128)(2,1)S(1)}, bf16[24,32,128]{2,1,0:T(8,128)(2,1)S(1)}, u32[]{:S(2)}, u32[]{:S(2)}) collective-permute-start(bf16[24,32,128]{2,1,0:T(8,128)(2,1)S(1)} %get-tuple-element.52), channel_id=1, source_target_pairs={{0,32},{32,64},{64,96},{96,0},{1,33},{33,65},{65,97},{97,1},{2,34}... | collective-permute-start | bytes 589832 | tf_op jit(solution)/shard_map/ppermute | solution.py:261
  26.2 5.7 %collective-permute-start.7 = (bf16[24,32,128]{2,1,0:T(8,128)(2,1)S(1)}, bf16[24,32,128]{2,1,0:T(8,128)(2,1)S(1)}, u32[]{:S(2)}, u32[]{:S(2)}) collective-permute-start(bf16[24,32,128]{2,1,0:T(8,128)(2,1)S(1)} %get-tuple-element.53), channel_id=1, source_target_pairs={{32,0},{64,32},{96,64},{0,96},{33,1},{65,33},{97,65},{1,97},{34,2}... | collective-permute-start | bytes 589832 | tf_op jit(solution)/shard_map/ppermute | solution.py:262
  31.9 11.1 %copy-start.14 = (s32[1,96]{1,0:T(1,128)S(1)}, s32[1,96]{1,0:T(1,128)}, u32[]{:S(2)}) copy-start(s32[1,96]{1,0:T(1,128)} %param.24) | copy-start | bytes 1156
  31.9 16.0 %copy-start.4 = (bf16[24,1600]{1,0:T(8,128)(2,1)S(1)}, bf16[24,1600]{1,0:T(8,128)(2,1)}, u32[]{:S(2)}) copy-start(bf16[24,1600]{1,0:T(8,128)(2,1)} %weights) | copy-start | bytes 230404
  31.9 16.0 %copy-start.9 = (f32[400]{0:T(512)S(1)}, f32[400]{0:T(512)}, u32[]{:S(2)}) copy-start(f32[400]{0:T(512)} %param.21) | copy-start | bytes 4804
  31.9 16.0 %copy-start.10 = (f32[24]{0:T(128)S(1)}, f32[24]{0:T(128)}, u32[]{:S(2)}) copy-start(f32[24]{0:T(128)} %param.23) | copy-start | bytes 292
  36.3 8.3 %collective-permute-start.16 = (f32[24,1,256]{2,1,0:T(1,128)S(1)}, f32[24,1,256]{2,1,0:T(1,128)S(1)}, u32[]{:S(2)}, u32[]{:S(2)}) collective-permute-start(f32[24,1,256]{2,1,0:T(1,128)S(1)} %get-tuple-element.64), channel_id=1, source_target_pairs={{0,1},{1,2},{2,3},{3,4},{4,5},{5,6},{6,7},{7,0},{8,9},{9,10},{10,1... | collective-permute-start | bytes 73736 | tf_op jit(solution)/shard_map/ppermute | solution.py:261
  40.3 9.0 %collective-permute-start.12 = (bf16[24,32,128]{2,1,0:T(8,128)(2,1)S(1)}, bf16[24,32,128]{2,1,0:T(8,128)(2,1)S(1)}, u32[]{:S(2)}, u32[]{:S(2)}) collective-permute-start(bf16[24,32,128]{2,1,0:T(8,128)(2,1)S(1)} %get-tuple-element.60), channel_id=1, source_target_pairs={{0,32},{32,64},{64,96},{96,0},{1,33},{33,65},{65,97},{97,1},{2,34}... | collective-permute-start | bytes 589832 | tf_op jit(solution)/shard_map/ppermute | solution.py:261
  40.3 9.0 %collective-permute-start.13 = (bf16[24,32,128]{2,1,0:T(8,128)(2,1)S(1)}, bf16[24,32,128]{2,1,0:T(8,128)(2,1)S(1)}, u32[]{:S(2)}, u32[]{:S(2)}) collective-permute-start(bf16[24,32,128]{2,1,0:T(8,128)(2,1)S(1)} %get-tuple-element.61), channel_id=1, source_target_pairs={{32,0},{64,32},{96,64},{0,96},{33,1},{65,33},{97,65},{1,97},{34,2}... | collective-permute-start | bytes 589832 | tf_op jit(solution)/shard_map/ppermute | solution.py:262
  43.6 4.9 %collective-permute-start.17 = (f32[24,1,256]{2,1,0:T(1,128)S(1)}, f32[24,1,256]{2,1,0:T(1,128)S(1)}, u32[]{:S(2)}, u32[]{:S(2)}) collective-permute-start(f32[24,1,256]{2,1,0:T(1,128)S(1)} %get-tuple-element.65), channel_id=1, source_target_pairs={{1,0},{2,1},{3,2},{4,3},{5,4},{6,5},{7,6},{0,7},{9,8},{10,9},{11,1... | collective-permute-start | bytes 73736 | tf_op jit(solution)/shard_map/ppermute | solution.py:262
  44.5 4.7 %collective-permute-start.14 = (f32[24,8,128]{2,1,0:T(8,128)S(1)}, f32[24,8,128]{2,1,0:T(8,128)S(1)}, u32[]{:S(2)}, u32[]{:S(2)}) collective-permute-start(f32[24,8,128]{2,1,0:T(8,128)S(1)} %get-tuple-element.62), channel_id=1, source_target_pairs={{0,8},{8,16},{16,24},{24,0},{1,9},{9,17},{17,25},{25,1},{2,10},{10... | collective-permute-start | bytes 294920 | tf_op jit(solution)/shard_map/ppermute | solution.py:261
  44.6 4.7 %collective-permute-start.15 = (f32[24,8,128]{2,1,0:T(8,128)S(1)}, f32[24,8,128]{2,1,0:T(8,128)S(1)}, u32[]{:S(2)}, u32[]{:S(2)}) collective-permute-start(f32[24,8,128]{2,1,0:T(8,128)S(1)} %get-tuple-element.63), channel_id=1, source_target_pairs={{8,0},{16,8},{24,16},{0,24},{9,1},{17,9},{25,17},{1,25},{10,2},{18... | collective-permute-start | bytes 294920 | tf_op jit(solution)/shard_map/ppermute | solution.py:262
  49.2 3.7 %copy-start.1 = (bf16[1600,800]{0,1:T(8,128)(2,1)S(1)}, bf16[1600,800]{0,1:T(8,128)(2,1)}, u32[]{:S(2)}) copy-start(bf16[1600,800]{0,1:T(8,128)(2,1)} %param.18) | copy-start | bytes 7680004
  49.3 3.7 %copy-start.3 = (bf16[800,400]{0,1:T(8,128)(2,1)S(1)}, bf16[800,400]{0,1:T(8,128)(2,1)}, u32[]{:S(2)}) copy-start(bf16[800,400]{0,1:T(8,128)(2,1)} %param.20) | copy-start | bytes 1920004
  49.3 3.7 %copy-start.8 = (bf16[400,24]{0,1:T(8,128)(2,1)S(1)}, bf16[400,24]{0,1:T(8,128)(2,1)}, u32[]{:S(2)}) copy-start(bf16[400,24]{0,1:T(8,128)(2,1)} %param.22) | copy-start | bytes 57604
  52.9 95.7 %copy-start.11 = (f32[24]{0:T(128)S(1)}, f32[24]{0:T(128)}, u32[]{:S(2)}) copy-start(f32[24]{0:T(128)} %rates.1) | copy-start | bytes 292
  70.6 0.6 copy-start.5
  71.2 77.4 %collective-permute-start.18 = (bf16[24,32,128]{2,1,0:T(8,128)(2,1)}, bf16[24,32,128]{2,1,0:T(8,128)(2,1)S(1)}, u32[]{:S(2)}, u32[]{:S(2)}) collective-permute-start(bf16[24,32,128]{2,1,0:T(8,128)(2,1)} %get-tuple-element.78), channel_id=1, source_target_pairs={{0,32},{32,64},{64,96},{96,0},{1,33},{33,65},{65,97},{97,1},{2,34}... | collective-permute-start | bytes 589832 | tf_op jit(solution)/shard_map/ppermute | solution.py:261
  71.2 77.4 %collective-permute-start.19 = (bf16[24,32,128]{2,1,0:T(8,128)(2,1)}, bf16[24,32,128]{2,1,0:T(8,128)(2,1)S(1)}, u32[]{:S(2)}, u32[]{:S(2)}) collective-permute-start(bf16[24,32,128]{2,1,0:T(8,128)(2,1)} %get-tuple-element.79), channel_id=1, source_target_pairs={{32,0},{64,32},{96,64},{0,96},{33,1},{65,33},{97,65},{1,97},{34,2}... | collective-permute-start | bytes 589832 | tf_op jit(solution)/shard_map/ppermute | solution.py:262
  79.1 69.5 %collective-permute-start.20 = (f32[24,8,128]{2,1,0:T(8,128)}, f32[24,8,128]{2,1,0:T(8,128)}, u32[]{:S(2)}, u32[]{:S(2)}) collective-permute-start(f32[24,8,128]{2,1,0:T(8,128)} %get-tuple-element.80), channel_id=1, source_target_pairs={{0,8},{8,16},{16,24},{24,0},{1,9},{9,17},{17,25},{25,1},{2,10},{10... | collective-permute-start | bytes 294920 | tf_op jit(solution)/shard_map/ppermute | solution.py:261
  132.1 16.5 %collective-permute-start.21 = (f32[24,8,128]{2,1,0:T(8,128)}, f32[24,8,128]{2,1,0:T(8,128)}, u32[]{:S(2)}, u32[]{:S(2)}) collective-permute-start(f32[24,8,128]{2,1,0:T(8,128)} %get-tuple-element.81), channel_id=1, source_target_pairs={{8,0},{16,8},{24,16},{0,24},{9,1},{17,9},{25,17},{1,25},{10,2},{18... | collective-permute-start | bytes 294920 | tf_op jit(solution)/shard_map/ppermute | solution.py:262
  135.8 5.1 %collective-permute-start.22 = (f32[24,1,256]{2,1,0:T(1,128)S(1)}, f32[24,1,256]{2,1,0:T(1,128)S(1)}, u32[]{:S(2)}, u32[]{:S(2)}) collective-permute-start(f32[24,1,256]{2,1,0:T(1,128)S(1)} %get-tuple-element.82), channel_id=1, source_target_pairs={{0,1},{1,2},{2,3},{3,4},{4,5},{5,6},{6,7},{7,0},{8,9},{9,10},{10,1... | collective-permute-start | bytes 73736 | tf_op jit(solution)/shard_map/ppermute | solution.py:261
  140.9 0.6 copy-start.6
  141.5 7.1 %collective-permute-start.23 = (f32[24,1,256]{2,1,0:T(1,128)}, f32[24,1,256]{2,1,0:T(1,128)}, u32[]{:S(2)}, u32[]{:S(2)}) collective-permute-start(f32[24,1,256]{2,1,0:T(1,128)} %get-tuple-element.83), channel_id=1, source_target_pairs={{1,0},{2,1},{3,2},{4,3},{5,4},{6,5},{7,6},{0,7},{9,8},{10,9},{11,1... | collective-permute-start | bytes 73736 | tf_op jit(solution)/shard_map/ppermute | solution.py:262
  142.9 15.0 %all-to-all-start = ((f32[128,1,128]{2,1,0:T(1,128)}), f32[128,1,128]{2,1,0:T(1,128)}, u32[]{:S(2)}, u32[]{:S(2)}) async-start(f32[128,1,128]{2,1,0:T(1,128)} %bitcast.22), calls=%async_computation | async-start | bytes 131072 | tf_op jit(solution)/shard_map/all_to_all | solution.py:279
  148.7 0.7 copy-start.7

commit v5 on v4

--- a/solution.py
+++ b/solution.py
@@ -7,10 +7,11 @@
 from jax.experimental.pallas import tpu as pltpu
 from jax.sharding import PartitionSpec as P
 
-GROUP = 4
-TOGETHER = 8
+GROUP = 12
+TOGETHER = 12
+SPREAD = 8
 LISTED = 96
-NETWORK_MIB = 30
+NETWORK_MIB = 38
 ALL = ("gx", "gy", "gz")
 F32, BF16 = jnp.float32, jnp.bfloat16
 TN = (((0,), (0,)), ((), ()))
@@ -168,32 +169,45 @@
             out[f, x] = centre + rate * spread
 
 
-def columns_kernel(weights, *refs):
-    refs[4][...] = weights[...].astype(F32).T.astype(BF16)
-    for row, out in zip(refs[:4], refs[5:]):
-        out[...] = jnp.broadcast_to(row[...], (128, row.shape[1])).T
-
-
-def network_kernel(listed, flowed, owned_by, w1, b1, b2, b3, b4, w2, w3, w4, out, sent, xf, xl, yf, yl, zf, zl, heat):
+def columns_kernel(w_in, b_in, w_mid, w_low, b_mid, b_low, b_out, w1, w2, w3, b2, b3, b4):
+    bias = 0.5 * b_in[...]
+    parts = []
+    for _ in range(3):
+        parts.append(bias.astype(BF16).astype(F32))
+        bias = bias - parts[-1]
+    zeros = jnp.zeros((5, bias.shape[1]), F32)
+    w1[...] = jnp.concatenate([0.5 * w_in[...].astype(F32), *parts, zeros], axis=0).T.astype(BF16)
+    w2[...] = (0.5 * w_mid[...].astype(F32)).astype(BF16)
+    w3[...] = (0.5 * w_low[...].astype(F32)).astype(BF16)
+    for row, out, factor in ((b_mid, b2, 0.5), (b_low, b3, 0.5), (b_out, b4, 1.0)):
+        out[...] = jnp.broadcast_to(factor * row[...], (128, row.shape[1])).T
+
+
+def network_kernel(listed, flowed, owned_by, w1, w2, w3, b2, b3, b4, w4, out, sent, xf, xl, yf, yl, zf, zl, heat):
     def copy(f, carry):
         rows = pl.ds(pl.multiple_of(256 * f, 256), 256)
         out[rows, :] = flowed[rows, :]
         return carry
 
-    def activated(weights, bias, cells):
-        half = jnp.dot(weights[...], cells, preferred_element_type=F32)
-        half = 0.5 * (half + jnp.concatenate([bias[...]] * TOGETHER, axis=1))
+    def product(weights, cells):
+        return jnp.dot(weights[...], cells, preferred_element_type=F32)
+
+    def beside(bias):
+        return jnp.concatenate([bias[...]] * TOGETHER, axis=1)
+
+    def silu(half):
         return (half + half * jnp.tanh(half)).astype(BF16)
 
     def react(step, carry):
         first = step * TOGETHER
         rows = [pl.ds(listed[1 + first + j], 24, stride=256) for j in range(TOGETHER)]
         before = [flowed[r, :] for r in rows]
-        hidden = activated(w1, b1, jnp.concatenate(before, axis=1).astype(BF16))
-        hidden = activated(w2, b2, hidden)
-        hidden = activated(w3, b3, hidden)
-        result = jnp.dot(w4[...], hidden, preferred_element_type=F32)
-        result = result + jnp.concatenate([b4[...]] * TOGETHER, axis=1)
+        ones = jnp.ones((8, TOGETHER * 128), F32)
+        cells = jnp.concatenate([jnp.concatenate(before, axis=1), ones], axis=0).astype(BF16)
+        hidden = silu(product(w1, cells))
+        hidden = silu(product(w2, hidden) + beside(b2))
+        hidden = silu(product(w3, hidden) + beside(b3))
+        result = product(w4, hidden) + beside(b4)
         for j in range(TOGETHER):
             increment = result[:, 128 * j : 128 * j + 128]
             out[rows[j], :] = before[j] + increment
@@ -271,7 +285,7 @@
         out_specs=out_specs,
         out_shape=out_shapes,
         scratch_shapes=[pltpu.VMEM((GROUP, 256, 128), F32)],
-        compiler_params=params(24),
+        compiler_params=params(32),
     )(*args)
 
 
@@ -298,10 +312,11 @@
     ids, owners = react_list[0], owner_table[0]
     count = jnp.sum((ids >= 0).astype(jnp.int32))
     listed = jnp.concatenate([count[None], jnp.where(ids >= 0, ids, ids[0])])
-    owned_by = (owners[None, :] == jnp.arange(128, dtype=jnp.int32)[:, None]).astype(F32)
+    rows = jnp.arange(128 * SPREAD, dtype=jnp.int32)[:, None]
+    owned_by = (owners[None, :] * SPREAD == rows).astype(F32)
 
     faces = pl.pallas_call(
-        prep_kernel, out_shape=face_shapes(25), compiler_params=params(24)
+        prep_kernel, out_shape=face_shapes(25), compiler_params=params(32)
     )(fields, velocity)
     halo = exchange(faces)
     own_halo = [
@@ -319,13 +334,26 @@
         [brick, sds((6, 8, 32, 128), F32), *face_shapes(24)],
         [BRICK, whole((6, 8, 32, 128)), *FACES],
     )
-    biases = (bias_in, bias_mid, bias_low, bias_out)
-    one, *given = lax.optimization_barrier((one, weight_in, *(b.reshape(1, -1) for b in biases)))
+    one, *given = lax.optimization_barrier(
+        (
+            one,
+            weight_in,
+            bias_in.reshape(1, -1),
+            weight_mid.T,
+            weight_low.T,
+            *(b.reshape(1, -1) for b in (bias_mid, bias_low, bias_out)),
+        )
+    )
     columns = pl.pallas_call(
         columns_kernel,
-        out_shape=[sds(weight_in.shape[::-1], BF16), *(sds((b.shape[0], 128), F32) for b in biases)],
-        compiler_params=params(16),
-        cost_estimate=pl.CostEstimate(flops=0, bytes_accessed=4 * 2**20, transcendentals=0),
+        out_shape=[
+            sds((weight_in.shape[1], 32), BF16),
+            sds(weight_mid.shape[::-1], BF16),
+            sds(weight_low.shape[::-1], BF16),
+            *(sds((b.shape[0], 128), F32) for b in (bias_mid, bias_low, bias_out)),
+        ],
+        compiler_params=params(20),
+        cost_estimate=pl.CostEstimate(flops=0, bytes_accessed=8 * 2**20, transcendentals=0),
     )(*given)
     two, *faces = section(
         2,
@@ -344,15 +372,15 @@
     in_vmem = pl.BlockSpec(memory_space=pltpu.VMEM)
     reacted, sent, *faces = pl.pallas_call(
         network_kernel,
-        in_specs=[pl.BlockSpec(memory_space=pltpu.SMEM)] + [in_vmem] * 10,
+        in_specs=[pl.BlockSpec(memory_space=pltpu.SMEM)] + [in_vmem] * 9,
         out_specs=[in_vmem] * 8,
-        out_shape=[sds((24 * 256, 128), F32), sds((128, 128), F32), *face_shapes(24)],
+        out_shape=[sds((24 * 256, 128), F32), sds((128 * SPREAD, 128), F32), *face_shapes(24)],
         scratch_shapes=[pltpu.VMEM((LISTED, 128), F32)],
         compiler_params=params(NETWORK_MIB),
-    )(listed, flowed.reshape(24 * 256, 128), owned_by, *columns, weight_mid.T, weight_low.T, weight_out.T)
+    )(listed, flowed.reshape(24 * 256, 128), owned_by, *columns, weight_out.T)
     reacted = reacted.reshape(fields.shape)
     around = exchange(faces)
-    heats = swap(sent.reshape(128, 1, 128))
+    heats = swap(sent.reshape(128, SPREAD, 128))
     updated = pl.pallas_call(
         diffuse_kernel,
         grid=(24 // GROUP,),
@@ -360,7 +388,7 @@
         out_specs=BRICK,
         out_shape=brick,
         scratch_shapes=[pltpu.VMEM((GROUP, 256, 128), F32)],
-        compiler_params=params(24),
+        compiler_params=params(32),
         cost_estimate=pl.CostEstimate(flops=10**9, bytes_accessed=24 * 2**20, transcendentals=0),
     )(diffusivity, reacted, *around)
     heats, updated = lax.optimization_barrier((heats, updated))

time: 162 us -> 153 us (0.944)
  Pallas kernels: 36.1 us -> 29.9 us
  waiting for transfers between devices: 10.2 us -> 8.14 us
    all_to_all x1, starting transfers between devices: 5.75 us -> 62.9 us  [swap(): return lax.all_to_all(tiles, ALL, split_axis=0, concat_axis=0, tiled=True)]
    ppermute x12, starting transfers between devices: 67.7 us -> 15.9 us  [exchange(): got.append(lax.ppermute(last, axis, [(i, (i + 1) % n) for i in range(n)]))]
    ppermute x12, starting transfers between devices: 30.9 us -> 23.8 us  [exchange(): got.append(lax.ppermute(first, axis, [((i + 1) % n, i) for i in range(n)]))]
    pallas_call x1, Pallas kernels: 17.6 us -> 13.1 us  [local(): pl.pallas_call(network_kernel, in_specs=[pl.BlockSpec(memory_space=pltpu....]
    all_to_all x1, waiting for transfers between devices: 3.11 us -> 0.01 us  [swap(): return lax.all_to_all(tiles, ALL, split_axis=0, concat_axis=0, tiled=True)]
    unnamed x32 -> x36, local copies, waits for them, and re-layouts: 4.9 us -> 6.22 us
  transfers between devices with their start and end apart: 25 -> 25, of which waited for: 6 -> 5; matrix products, arithmetic and copies ran while one was open for 1% -> 1% of each run, Pallas kernels for 4% -> 4%
where the time goes in v5:
time: 153 us
  starting transfers between devices  103 us (67%)
  Pallas kernels  29.9 us (20%)
  waiting for transfers between devices  8.14 us (5%)
  local copies, waits for them, and re-layouts  6.24 us (4%)
  other arithmetic  3.22 us (2%)
  between operations  2.71 us (2%)
    all_to_all x1, starting transfers between devices, swap(): return lax.all_to_all(tiles, ALL, split_axis=0, concat_axis=0, tiled=True)  62.9 us
    ppermute x12, starting transfers between devices, exchange(): got.append(lax.ppermute(first, axis, [((i + 1) % n, i) for i in range(n)]))  23.8 us
    ppermute x12, starting transfers between devices, exchange(): got.append(lax.ppermute(last, axis, [(i, (i + 1) % n) for i in range(n)]))  15.9 us
    pallas_call x1, Pallas kernels, local(): pl.pallas_call(network_kernel, in_specs=[pl.BlockSpec(memory_space=pltpu....  13.1 us
    pallas_call x3, Pallas kernels, section(): pl.pallas_call(functools.partial(section_kernel, kind), grid=(24 // GROUP...  10.6 us
    unnamed x36, local copies, waits for them, and re-layouts  6.22 us
    ppermute x12, waiting for transfers between devices, exchange(): got.append(lax.ppermute(last, axis, [(i, (i + 1) % n) for i in range(n)]))  5.05 us
    pallas_call x1, Pallas kernels, local(): pl.pallas_call(diffuse_kernel, grid=(24 // GROUP,), in_specs=[pl.BlockSpe...  4.18 us
  transfers between devices with their start and end apart: 25, of which 5 were waited for; matrix products, arithmetic and copies ran while one was open for 1% of the time, Pallas kernels for 4%

profile of v5, /device:TPU:1, one launch (start us, length us, event | category | flops | bytes accessed | tf_op | source)
XLA Modules:
  0.0 152.8 jit_solution(2330709591743770692)
XLA Ops:
  0.6 1.9 %copy-done = f32[24,8,32,128]{3,2,1,0:T(8,128)S(1)} copy-done((f32[24,8,32,128]{3,2,1,0:T(8,128)S(1)}, f32[24,8,32,128]{3,2,1,0:T(8,128)}, u32[]{:S(2)}) %copy-start) | copy-done | bytes 3145752
  2.5 1.0 copy-done.2
  3.5 0.5 shard_map.140
  4.1 0.0 copy-start.17
  4.1 0.0 copy-start.15
  4.1 0.0 copy-start.14
  4.1 2.1 %collective-permute-start = (bf16[25,32,128]{2,1,0:T(8,128)(2,1)S(1)}, bf16[25,32,128]{2,1,0:T(8,128)(2,1)S(1)}, u32[]{:S(2)}, u32[]{:S(2)}) collective-permute-start(bf16[25,32,128]{2,1,0:T(8,128)(2,1)S(1)} %get-tuple-element.47), channel_id=1, source_target_pairs={{0,32},{32,64},{64,96},{96,0},{1,33},{33,65},{65,97},{97,1},{2,34}... | collective-permute-start | bytes 614408 | tf_op jit(solution)/shard_map/ppermute | solution.py:275
  6.2 1.3 collective-permute-start.1
  7.6 1.8 %collective-permute-start.2 = (f32[25,8,128]{2,1,0:T(8,128)S(1)}, f32[25,8,128]{2,1,0:T(8,128)S(1)}, u32[]{:S(2)}, u32[]{:S(2)}) collective-permute-start(f32[25,8,128]{2,1,0:T(8,128)S(1)} %get-tuple-element.49), channel_id=1, source_target_pairs={{0,8},{8,16},{16,24},{24,0},{1,9},{9,17},{17,25},{25,1},{2,10},{10... | collective-permute-start | bytes 307208 | tf_op jit(solution)/shard_map/ppermute | solution.py:275
  9.3 2.1 %collective-permute-start.3 = (f32[25,8,128]{2,1,0:T(8,128)S(1)}, f32[25,8,128]{2,1,0:T(8,128)S(1)}, u32[]{:S(2)}, u32[]{:S(2)}) collective-permute-start(f32[25,8,128]{2,1,0:T(8,128)S(1)} %get-tuple-element.50), channel_id=1, source_target_pairs={{8,0},{16,8},{24,16},{0,24},{9,1},{17,9},{25,17},{1,25},{10,2},{18... | collective-permute-start | bytes 307208 | tf_op jit(solution)/shard_map/ppermute | solution.py:276
  11.4 2.7 %collective-permute-start.4 = (f32[25,1,256]{2,1,0:T(1,128)S(1)}, f32[25,1,256]{2,1,0:T(1,128)S(1)}, u32[]{:S(2)}, u32[]{:S(2)}) collective-permute-start(f32[25,1,256]{2,1,0:T(1,128)S(1)} %get-tuple-element.51), channel_id=1, source_target_pairs={{0,1},{1,2},{2,3},{3,4},{4,5},{5,6},{6,7},{7,0},{8,9},{9,10},{10,1... | collective-permute-start | bytes 76808 | tf_op jit(solution)/shard_map/ppermute | solution.py:275
  14.1 1.0 collective-permute-done.4.refs_5_.refs_12_
  15.1 2.3 %collective-permute-start.5 = (f32[25,1,256]{2,1,0:T(1,128)S(1)}, f32[25,1,256]{2,1,0:T(1,128)S(1)}, u32[]{:S(2)}, u32[]{:S(2)}) collective-permute-start(f32[25,1,256]{2,1,0:T(1,128)S(1)} %get-tuple-element.52), channel_id=1, source_target_pairs={{1,0},{2,1},{3,2},{4,3},{5,4},{6,5},{7,6},{0,7},{9,8},{10,9},{11,1... | collective-permute-start | bytes 76808 | tf_op jit(solution)/shard_map/ppermute | solution.py:276
  17.4 1.5 collective-permute-done.5.refs_6_.refs_13_
  18.9 0.0 collective-permute-done.2.refs_3_.refs_10_
  18.9 0.0 collective-permute-done.3.refs_4_.refs_11_
  18.9 0.0 collective-permute-done.refs_1_.refs_8_
  18.9 3.6 %shard_map.141 = (f32[24,8,32,128]{3,2,1,0:T(8,128)S(1)}, f32[6,8,32,128]{3,2,1,0:T(8,128)S(1)}, bf16[24,32,128]{2,1,0:T(8,128)(2,1)S(1)}, bf16[24,32,128]{2,1,0...) custom-call(f32[24,8,32,128]{3,2,1,0:T(8,128)S(1)} %copy-done, ...), custom_call_target="tpu_custom_call" | custom-call | tf_op jit(solution)/shard_map/pallas_call | solution.py:281
  22.5 0.0 collective-permute-start.10
  22.6 0.5 collective-permute-start.11
  23.1 2.7 %collective-permute-start.9 = (f32[24,8,128]{2,1,0:T(8,128)S(1)}, f32[24,8,128]{2,1,0:T(8,128)S(1)}, u32[]{:S(2)}, u32[]{:S(2)}) collective-permute-start(f32[24,8,128]{2,1,0:T(8,128)S(1)} %get-tuple-element.58), channel_id=1, source_target_pairs={{8,0},{16,8},{24,16},{0,24},{9,1},{17,9},{25,17},{1,25},{10,2},{18... | collective-permute-start | bytes 294920 | tf_op jit(solution)/shard_map/ppermute | solution.py:276
  25.7 0.0 collective-permute-start.6
  25.7 0.0 collective-permute-done.10.refs_6_
  25.7 2.7 %collective-permute-start.7 = (bf16[24,32,128]{2,1,0:T(8,128)(2,1)S(1)}, bf16[24,32,128]{2,1,0:T(8,128)(2,1)S(1)}, u32[]{:S(2)}, u32[]{:S(2)}) collective-permute-start(bf16[24,32,128]{2,1,0:T(8,128)(2,1)S(1)} %get-tuple-element.56), channel_id=1, source_target_pairs={{32,0},{64,32},{96,64},{0,96},{33,1},{65,33},{97,65},{1,97},{34,2}... | collective-permute-start | bytes 589832 | tf_op jit(solution)/shard_map/ppermute | solution.py:276
  28.4 0.1 fusion.owned_by
  28.5 0.0 collective-permute-done.11.refs_7_
  28.5 0.0 collective-permute-done.8.refs_4_
  28.6 2.9 %collective-permute-done.6.refs_2_ = bf16[24,32,128]{2,1,0:T(8,128)(2,1)S(1)} collective-permute-done((bf16[24,32,128]{2,1,0:T(8,128)(2,1)S(1)}, bf16[24,32,128]{2,1,0:T(8,128)(2,1)S(1)}, u32[]{:S(2)}, u32[]{:S(2)}) %collective-permute-start.6) | collective-permute-done | bytes 196640 | tf_op jit(solution)/shard_map/ppermute | solution.py:275
  31.5 0.0 collective-permute-done.7.refs_3_
  31.5 0.0 copy-start.5
  31.5 0.0 copy-start.7
  31.5 0.0 copy-start.8
  31.5 3.6 %shard_map.142 = (f32[24,8,32,128]{3,2,1,0:T(8,128)S(1)}, bf16[24,32,128]{2,1,0:T(8,128)(2,1)S(1)}, bf16[24,32,128]{2,1,0:T(8,128)(2,1)S(1)}, f32[24,8,128]{2,1,...) custom-call(f32[24,8,32,128]{3,2,1,0:T(8,128)S(1)} %get-tuple-element.54.refs_0_, ...), custom_call_target="tpu_custom_call" | custom-call | tf_op jit(solution)/shard_map/pallas_call | solution.py:281
  35.1 4.0 %collective-permute-start.16 = (f32[24,1,256]{2,1,0:T(1,128)S(1)}, f32[24,1,256]{2,1,0:T(1,128)S(1)}, u32[]{:S(2)}, u32[]{:S(2)}) collective-permute-start(f32[24,1,256]{2,1,0:T(1,128)S(1)} %get-tuple-element.67), channel_id=1, source_target_pairs={{0,1},{1,2},{2,3},{3,4},{4,5},{5,6},{6,7},{7,0},{8,9},{9,10},{10,1... | collective-permute-start | bytes 73736 | tf_op jit(solution)/shard_map/ppermute | solution.py:275
  39.1 0.0 collective-permute-start.12
  39.1 2.7 %collective-permute-start.13 = (bf16[24,32,128]{2,1,0:T(8,128)(2,1)S(1)}, bf16[24,32,128]{2,1,0:T(8,128)(2,1)S(1)}, u32[]{:S(2)}, u32[]{:S(2)}) collective-permute-start(bf16[24,32,128]{2,1,0:T(8,128)(2,1)S(1)} %get-tuple-element.64), channel_id=1, source_target_pairs={{32,0},{64,32},{96,64},{0,96},{33,1},{65,33},{97,65},{1,97},{34,2}... | collective-permute-start | bytes 589832 | tf_op jit(solution)/shard_map/ppermute | solution.py:276
  41.8 0.7 fusion.1
  42.5 0.9 collective-permute-start.17
  43.4 0.0 collective-permute-start.14
  43.4 0.0 collective-permute-done.16.refs_6_
  43.4 2.7 %collective-permute-start.15 = (f32[24,8,128]{2,1,0:T(8,128)S(1)}, f32[24,8,128]{2,1,0:T(8,128)S(1)}, u32[]{:S(2)}, u32[]{:S(2)}) collective-permute-start(f32[24,8,128]{2,1,0:T(8,128)S(1)} %get-tuple-element.66), channel_id=1, source_target_pairs={{8,0},{16,8},{24,16},{0,24},{9,1},{17,9},{25,17},{1,25},{10,2},{18... | collective-permute-start | bytes 294920 | tf_op jit(solution)/shard_map/ppermute | solution.py:276
  46.1 0.7 pad_add_fusion.listed
  46.8 1.5 shard_map.144
  48.3 0.0 collective-permute-done.17.refs_7_
  48.4 0.0 copy-start.6
  48.4 3.4 %shard_map.143 = f32[24,8,32,128]{3,2,1,0:T(8,128)S(1)} custom-call(f32[24,8,32,128]{3,2,1,0:T(8,128)S(1)} %get-tuple-element.62.refs_0_, f32[24,8,32,128]{3,2,1,0:T(8,128)S(1)} %copy-done, bf16[24,32,128]{2,1,0:T(8,128)(2,1)S(1)} %collective-permute-done.12.refs_2_, bf16[24,32,128]{2,1,0:T(8,128)(2,1)S(1)} %collective-permute-done.13.refs_3_, ...), custom_call_target="tpu_custom_call" | custom-call | tf_op jit(solution)/shard_map/pallas_call | solution.py:281
  51.8 0.0 copy-start.9
  51.8 13.1 %shard_map.145 = (f32[6144,128]{1,0:T(8,128)S(1)}, f32[1024,128]{1,0:T(8,128)S(1)}, bf16[24,32,128]{2,1,0:T(8,128)(2,1)S(1)}, bf16[24,32,128]{2,1,0:T(8,128)(2,1...) custom-call(s32[97]{0:T(128)S(1)} %pad_add_fusion.listed, ...), custom_call_target="tpu_custom_call" | custom-call | tf_op jit(solution)/shard_map/pallas_call | solution.py:373
  64.9 0.8 copy-done.4
  65.7 0.6 copy-done.10
  66.3 0.6 copy-done.11
  67.0 0.6 copy-done.12
  67.6 0.6 copy-done.13
  68.2 62.9 %all-to-all-start = ((f32[128,8,128]{2,1,0:T(8,128)}), f32[128,8,128]{2,1,0:T(8,128)}, u32[]{:S(2)}, u32[]{:S(2)}) async-start(f32[128,8,128]{2,1,0:T(8,128)} %bitcast.21), calls=%async_computation | async-start | bytes 1048576 | tf_op jit(solution)/shard_map/all_to_all | solution.py:293
  131.1 1.5 collective-permute-start.18
  132.5 1.3 collective-permute-start.19
  133.8 1.5 collective-permute-start.20
  135.3 1.8 %collective-permute-start.21 = (f32[24,8,128]{2,1,0:T(8,128)}, f32[24,8,128]{2,1,0:T(8,128)S(1)}, u32[]{:S(2)}, u32[]{:S(2)}) collective-permute-start(f32[24,8,128]{2,1,0:T(8,128)} %copy-done.10), channel_id=1, source_target_pairs={{8,0},{16,8},{24,16},{0,24},{9,1},{17,9},{25,17},{1,25},{10,2},{18... | collective-permute-start | bytes 294920 | tf_op jit(solution)/shard_map/ppermute | solution.py:276
  137.1 2.3 %collective-permute-start.22 = (f32[24,1,256]{2,1,0:T(1,128)}, f32[24,1,256]{2,1,0:T(1,128)S(1)}, u32[]{:S(2)}, u32[]{:S(2)}) collective-permute-start(f32[24,1,256]{2,1,0:T(1,128)} %copy-done.13), channel_id=1, source_target_pairs={{0,1},{1,2},{2,3},{3,4},{4,5},{5,6},{6,7},{7,0},{8,9},{9,10},{10,1... | collective-permute-start | bytes 73736 | tf_op jit(solution)/shard_map/ppermute | solution.py:275
  139.4 1.2 collective-permute-done.22.zlo
  140.6 2.9 %collective-permute-start.23 = (f32[24,1,256]{2,1,0:T(1,128)}, f32[24,1,256]{2,1,0:T(1,128)S(1)}, u32[]{:S(2)}, u32[]{:S(2)}) collective-permute-start(f32[24,1,256]{2,1,0:T(1,128)} %copy-done.12), channel_id=1, source_target_pairs={{1,0},{2,1},{3,2},{4,3},{5,4},{6,5},{7,6},{0,7},{9,8},{10,9},{11,1... | collective-permute-start | bytes 73736 | tf_op jit(solution)/shard_map/ppermute | solution.py:276
  143.4 1.6 %collective-permute-done.23.zhi = f32[24,1,256]{2,1,0:T(1,128)S(1)} collective-permute-done((f32[24,1,256]{2,1,0:T(1,128)}, f32[24,1,256]{2,1,0:T(1,128)S(1)}, u32[]{:S(2)}, u32[]{:S(2)}) %collective-permute-start.23) | collective-permute-done | bytes 24608 | tf_op jit(solution)/shard_map/ppermute | solution.py:276
  145.0 4.2 %shard_map.146 = f32[24,8,32,128]{3,2,1,0:T(8,128)} custom-call(f32[24]{0:T(128)S(1)} %copy-done.9, f32[24,8,32,128]{3,2,1,0:T(8,128)S(1)} %bitcast.18, bf16[24,32,128]{2,1,0:T(8,128)(2,1)S(1)} %collective-permute-done.18.xlo, bf16[24,32,128]{2,1,0:T(8,128)(2,1)S(1)} %collective-permute-done.19.xhi, f32[24,8,128]{2,1,0:T(8,128)S(1)} %collective-permute-done.20.ylo, ...), custom_call_target="tpu_custom_call" | custom-call | flops 1000000000 | bytes 25165824 | tf_op jit(solution)/shard_map/pallas_call | solution.py:384
  149.2 1.8 %reduce_sum.19 = f32[]{:T(128)} reduce(f32[128,8,128]{2,1,0:T(8,128)} %all-to-all-done, f32[]{:T(128)} %constant.2.clone.1), dimensions={0,1,2}, to_apply=%region_1.2 | reduce | flops 131071 | bytes 524296 | tf_op jit(solution)/shard_map/reduce_sum | solution.py:395
  (36 shorter events, 0.1 us)
Async XLA Ops:
  0.6 1.9 %copy-start = (f32[24,8,32,128]{3,2,1,0:T(8,128)S(1)}, f32[24,8,32,128]{3,2,1,0:T(8,128)}, u32[]{:S(2)}) copy-start(f32[24,8,32,128]{3,2,1,0:T(8,128)} %refs_1_.3) | copy-start | bytes 9437188
  2.5 1.0 copy-start.2
  4.1 18.5 %copy-start.17 = (s32[1,96]{1,0:T(1,128)S(1)}, s32[1,96]{1,0:T(1,128)}, u32[]{:S(2)}) copy-start(s32[1,96]{1,0:T(1,128)} %param.25) | copy-start | bytes 1156
  4.1 24.4 %copy-start.15 = (f32[800]{0:T(1024)S(1)}, f32[800]{0:T(1024)}, u32[]{:S(2)}) copy-start(f32[800]{0:T(1024)} %param.19) | copy-start | bytes 9604
  4.1 24.4 %copy-start.14 = (f32[1600]{0:T(1024)S(1)}, f32[1600]{0:T(1024)}, u32[]{:S(2)}) copy-start(f32[1600]{0:T(1024)} %param.17) | copy-start | bytes 19204
  4.1 14.8 %collective-permute-start = (bf16[25,32,128]{2,1,0:T(8,128)(2,1)S(1)}, bf16[25,32,128]{2,1,0:T(8,128)(2,1)S(1)}, u32[]{:S(2)}, u32[]{:S(2)}) collective-permute-start(bf16[25,32,128]{2,1,0:T(8,128)(2,1)S(1)} %get-tuple-element.47), channel_id=1, source_target_pairs={{0,32},{32,64},{64,96},{96,0},{1,33},{33,65},{65,97},{97,1},{2,34}... | collective-permute-start | bytes 614408 | tf_op jit(solution)/shard_map/ppermute | solution.py:275
  6.2 12.7 %collective-permute-start.1 = (bf16[25,32,128]{2,1,0:T(8,128)(2,1)S(1)}, bf16[25,32,128]{2,1,0:T(8,128)(2,1)S(1)}, u32[]{:S(2)}, u32[]{:S(2)}) collective-permute-start(bf16[25,32,128]{2,1,0:T(8,128)(2,1)S(1)} %get-tuple-element.48), channel_id=1, source_target_pairs={{32,0},{64,32},{96,64},{0,96},{33,1},{65,33},{97,65},{1,97},{34,2}... | collective-permute-start | bytes 614408 | tf_op jit(solution)/shard_map/ppermute | solution.py:276
  7.6 11.4 %collective-permute-start.2 = (f32[25,8,128]{2,1,0:T(8,128)S(1)}, f32[25,8,128]{2,1,0:T(8,128)S(1)}, u32[]{:S(2)}, u32[]{:S(2)}) collective-permute-start(f32[25,8,128]{2,1,0:T(8,128)S(1)} %get-tuple-element.49), channel_id=1, source_target_pairs={{0,8},{8,16},{16,24},{24,0},{1,9},{9,17},{17,25},{25,1},{2,10},{10... | collective-permute-start | bytes 307208 | tf_op jit(solution)/shard_map/ppermute | solution.py:275
  9.3 9.6 %collective-permute-start.3 = (f32[25,8,128]{2,1,0:T(8,128)S(1)}, f32[25,8,128]{2,1,0:T(8,128)S(1)}, u32[]{:S(2)}, u32[]{:S(2)}) collective-permute-start(f32[25,8,128]{2,1,0:T(8,128)S(1)} %get-tuple-element.50), channel_id=1, source_target_pairs={{8,0},{16,8},{24,16},{0,24},{9,1},{17,9},{25,17},{1,25},{10,2},{18... | collective-permute-start | bytes 307208 | tf_op jit(solution)/shard_map/ppermute | solution.py:276
  11.4 3.7 %collective-permute-start.4 = (f32[25,1,256]{2,1,0:T(1,128)S(1)}, f32[25,1,256]{2,1,0:T(1,128)S(1)}, u32[]{:S(2)}, u32[]{:S(2)}) collective-permute-start(f32[25,1,256]{2,1,0:T(1,128)S(1)} %get-tuple-element.51), channel_id=1, source_target_pairs={{0,1},{1,2},{2,3},{3,4},{4,5},{5,6},{6,7},{7,0},{8,9},{9,10},{10,1... | collective-permute-start | bytes 76808 | tf_op jit(solution)/shard_map/ppermute | solution.py:275
  15.1 3.8 %collective-permute-start.5 = (f32[25,1,256]{2,1,0:T(1,128)S(1)}, f32[25,1,256]{2,1,0:T(1,128)S(1)}, u32[]{:S(2)}, u32[]{:S(2)}) collective-permute-start(f32[25,1,256]{2,1,0:T(1,128)S(1)} %get-tuple-element.52), channel_id=1, source_target_pairs={{1,0},{2,1},{3,2},{4,3},{5,4},{6,5},{7,6},{0,7},{9,8},{10,9},{11,1... | collective-permute-start | bytes 76808 | tf_op jit(solution)/shard_map/ppermute | solution.py:276
  22.5 3.2 %collective-permute-start.10 = (f32[24,1,256]{2,1,0:T(1,128)S(1)}, f32[24,1,256]{2,1,0:T(1,128)S(1)}, u32[]{:S(2)}, u32[]{:S(2)}) collective-permute-start(f32[24,1,256]{2,1,0:T(1,128)S(1)} %get-tuple-element.59), channel_id=1, source_target_pairs={{0,1},{1,2},{2,3},{3,4},{4,5},{5,6},{6,7},{7,0},{8,9},{9,10},{10,1... | collective-permute-start | bytes 73736 | tf_op jit(solution)/shard_map/ppermute | solution.py:275
  22.6 6.0 %collective-permute-start.11 = (f32[24,1,256]{2,1,0:T(1,128)S(1)}, f32[24,1,256]{2,1,0:T(1,128)S(1)}, u32[]{:S(2)}, u32[]{:S(2)}) collective-permute-start(f32[24,1,256]{2,1,0:T(1,128)S(1)} %get-tuple-element.60), channel_id=1, source_target_pairs={{1,0},{2,1},{3,2},{4,3},{5,4},{6,5},{7,6},{0,7},{9,8},{10,9},{11,1... | collective-permute-start | bytes 73736 | tf_op jit(solution)/shard_map/ppermute | solution.py:276
  23.1 5.5 %collective-permute-start.8 = (f32[24,8,128]{2,1,0:T(8,128)S(1)}, f32[24,8,128]{2,1,0:T(8,128)S(1)}, u32[]{:S(2)}, u32[]{:S(2)}) collective-permute-start(f32[24,8,128]{2,1,0:T(8,128)S(1)} %get-tuple-element.57), channel_id=1, source_target_pairs={{0,8},{8,16},{16,24},{24,0},{1,9},{9,17},{17,25},{25,1},{2,10},{10... | collective-permute-start | bytes 294920 | tf_op jit(solution)/shard_map/ppermute | solution.py:275
  23.1 5.5 %collective-permute-start.9 = (f32[24,8,128]{2,1,0:T(8,128)S(1)}, f32[24,8,128]{2,1,0:T(8,128)S(1)}, u32[]{:S(2)}, u32[]{:S(2)}) collective-permute-start(f32[24,8,128]{2,1,0:T(8,128)S(1)} %get-tuple-element.58), channel_id=1, source_target_pairs={{8,0},{16,8},{24,16},{0,24},{9,1},{17,9},{25,17},{1,25},{10,2},{18... | collective-permute-start | bytes 294920 | tf_op jit(solution)/shard_map/ppermute | solution.py:276
  25.7 5.7 %collective-permute-start.6 = (bf16[24,32,128]{2,1,0:T(8,128)(2,1)S(1)}, bf16[24,32,128]{2,1,0:T(8,128)(2,1)S(1)}, u32[]{:S(2)}, u32[]{:S(2)}) collective-permute-start(bf16[24,32,128]{2,1,0:T(8,128)(2,1)S(1)} %get-tuple-element.55), channel_id=1, source_target_pairs={{0,32},{32,64},{64,96},{96,0},{1,33},{33,65},{65,97},{97,1},{2,34}... | collective-permute-start | bytes 589832 | tf_op jit(solution)/shard_map/ppermute | solution.py:275
  25.7 5.7 %collective-permute-start.7 = (bf16[24,32,128]{2,1,0:T(8,128)(2,1)S(1)}, bf16[24,32,128]{2,1,0:T(8,128)(2,1)S(1)}, u32[]{:S(2)}, u32[]{:S(2)}) collective-permute-start(bf16[24,32,128]{2,1,0:T(8,128)(2,1)S(1)} %get-tuple-element.56), channel_id=1, source_target_pairs={{32,0},{64,32},{96,64},{0,96},{33,1},{65,33},{97,65},{1,97},{34,2}... | collective-permute-start | bytes 589832 | tf_op jit(solution)/shard_map/ppermute | solution.py:276
  31.5 10.3 %copy-start.16 = (s32[1,96]{1,0:T(1,128)S(1)}, s32[1,96]{1,0:T(1,128)}, u32[]{:S(2)}) copy-start(s32[1,96]{1,0:T(1,128)} %param.24) | copy-start | bytes 1156
  31.5 15.3 %copy-start.1 = (bf16[1600,800]{0,1:T(8,128)(2,1)S(1)}, bf16[1600,800]{0,1:T(8,128)(2,1)}, u32[]{:S(2)}) copy-start(bf16[1600,800]{0,1:T(8,128)(2,1)} %param.18) | copy-start | bytes 7680004
  31.5 15.3 %copy-start.3 = (bf16[800,400]{0,1:T(8,128)(2,1)S(1)}, bf16[800,400]{0,1:T(8,128)(2,1)}, u32[]{:S(2)}) copy-start(bf16[800,400]{0,1:T(8,128)(2,1)} %param.20) | copy-start | bytes 1920004
  31.5 15.3 %copy-start.5 = (bf16[24,1600]{1,0:T(8,128)(2,1)S(1)}, bf16[24,1600]{1,0:T(8,128)(2,1)}, u32[]{:S(2)}) copy-start(bf16[24,1600]{1,0:T(8,128)(2,1)} %w_in) | copy-start | bytes 230404
  31.5 15.3 %copy-start.7 = (f32[400]{0:T(512)S(1)}, f32[400]{0:T(512)}, u32[]{:S(2)}) copy-start(f32[400]{0:T(512)} %param.21) | copy-start | bytes 4804
  31.5 15.3 %copy-start.8 = (f32[24]{0:T(128)S(1)}, f32[24]{0:T(128)}, u32[]{:S(2)}) copy-start(f32[24]{0:T(128)} %param.23) | copy-start | bytes 292
  35.1 8.3 %collective-permute-start.16 = (f32[24,1,256]{2,1,0:T(1,128)S(1)}, f32[24,1,256]{2,1,0:T(1,128)S(1)}, u32[]{:S(2)}, u32[]{:S(2)}) collective-permute-start(f32[24,1,256]{2,1,0:T(1,128)S(1)} %get-tuple-element.67), channel_id=1, source_target_pairs={{0,1},{1,2},{2,3},{3,4},{4,5},{5,6},{6,7},{7,0},{8,9},{9,10},{10,1... | collective-permute-start | bytes 73736 | tf_op jit(solution)/shard_map/ppermute | solution.py:275
  39.1 9.2 %collective-permute-start.12 = (bf16[24,32,128]{2,1,0:T(8,128)(2,1)S(1)}, bf16[24,32,128]{2,1,0:T(8,128)(2,1)S(1)}, u32[]{:S(2)}, u32[]{:S(2)}) collective-permute-start(bf16[24,32,128]{2,1,0:T(8,128)(2,1)S(1)} %get-tuple-element.63), channel_id=1, source_target_pairs={{0,32},{32,64},{64,96},{96,0},{1,33},{33,65},{65,97},{97,1},{2,34}... | collective-permute-start | bytes 589832 | tf_op jit(solution)/shard_map/ppermute | solution.py:275
  39.1 9.2 %collective-permute-start.13 = (bf16[24,32,128]{2,1,0:T(8,128)(2,1)S(1)}, bf16[24,32,128]{2,1,0:T(8,128)(2,1)S(1)}, u32[]{:S(2)}, u32[]{:S(2)}) collective-permute-start(bf16[24,32,128]{2,1,0:T(8,128)(2,1)S(1)} %get-tuple-element.64), channel_id=1, source_target_pairs={{32,0},{64,32},{96,64},{0,96},{33,1},{65,33},{97,65},{1,97},{34,2}... | collective-permute-start | bytes 589832 | tf_op jit(solution)/shard_map/ppermute | solution.py:276
  42.5 5.8 %collective-permute-start.17 = (f32[24,1,256]{2,1,0:T(1,128)S(1)}, f32[24,1,256]{2,1,0:T(1,128)S(1)}, u32[]{:S(2)}, u32[]{:S(2)}) collective-permute-start(f32[24,1,256]{2,1,0:T(1,128)S(1)} %get-tuple-element.68), channel_id=1, source_target_pairs={{1,0},{2,1},{3,2},{4,3},{5,4},{6,5},{7,6},{0,7},{9,8},{10,9},{11,1... | collective-permute-start | bytes 73736 | tf_op jit(solution)/shard_map/ppermute | solution.py:276
  43.4 4.9 %collective-permute-start.14 = (f32[24,8,128]{2,1,0:T(8,128)S(1)}, f32[24,8,128]{2,1,0:T(8,128)S(1)}, u32[]{:S(2)}, u32[]{:S(2)}) collective-permute-start(f32[24,8,128]{2,1,0:T(8,128)S(1)} %get-tuple-element.65), channel_id=1, source_target_pairs={{0,8},{8,16},{16,24},{24,0},{1,9},{9,17},{17,25},{25,1},{2,10},{10... | collective-permute-start | bytes 294920 | tf_op jit(solution)/shard_map/ppermute | solution.py:275
  43.4 4.9 %collective-permute-start.15 = (f32[24,8,128]{2,1,0:T(8,128)S(1)}, f32[24,8,128]{2,1,0:T(8,128)S(1)}, u32[]{:S(2)}, u32[]{:S(2)}) collective-permute-start(f32[24,8,128]{2,1,0:T(8,128)S(1)} %get-tuple-element.66), channel_id=1, source_target_pairs={{8,0},{16,8},{24,16},{0,24},{9,1},{17,9},{25,17},{1,25},{10,2},{18... | collective-permute-start | bytes 294920 | tf_op jit(solution)/shard_map/ppermute | solution.py:276
  48.4 3.4 %copy-start.6 = (bf16[400,24]{0,1:T(8,128)(2,1)S(1)}, bf16[400,24]{0,1:T(8,128)(2,1)}, u32[]{:S(2)}) copy-start(bf16[400,24]{0,1:T(8,128)(2,1)} %param.22) | copy-start | bytes 57604
  51.8 93.3 %copy-start.9 = (f32[24]{0:T(128)S(1)}, f32[24]{0:T(128)}, u32[]{:S(2)}) copy-start(f32[24]{0:T(128)} %rates.1) | copy-start | bytes 292
  64.9 0.8 copy-start.4
  65.7 0.6 copy-start.10
  66.3 0.6 copy-start.11
  67.0 0.6 copy-start.12
  67.6 0.6 copy-start.13
  68.2 81.0 %all-to-all-start = ((f32[128,8,128]{2,1,0:T(8,128)}), f32[128,8,128]{2,1,0:T(8,128)}, u32[]{:S(2)}, u32[]{:S(2)}) async-start(f32[128,8,128]{2,1,0:T(8,128)} %bitcast.21), calls=%async_computation | async-start | bytes 1048576 | tf_op jit(solution)/shard_map/all_to_all | solution.py:293
  131.1 13.9 %collective-permute-start.18 = (bf16[24,32,128]{2,1,0:T(8,128)(2,1)S(1)}, bf16[24,32,128]{2,1,0:T(8,128)(2,1)S(1)}, u32[]{:S(2)}, u32[]{:S(2)}) collective-permute-start(bf16[24,32,128]{2,1,0:T(8,128)(2,1)S(1)} %get-tuple-element.84), channel_id=1, source_target_pairs={{0,32},{32,64},{64,96},{96,0},{1,33},{33,65},{65,97},{97,1},{2,34}... | collective-permute-start | bytes 589832 | tf_op jit(solution)/shard_map/ppermute | solution.py:275
  132.5 12.5 %collective-permute-start.19 = (bf16[24,32,128]{2,1,0:T(8,128)(2,1)S(1)}, bf16[24,32,128]{2,1,0:T(8,128)(2,1)S(1)}, u32[]{:S(2)}, u32[]{:S(2)}) collective-permute-start(bf16[24,32,128]{2,1,0:T(8,128)(2,1)S(1)} %get-tuple-element.85), channel_id=1, source_target_pairs={{32,0},{64,32},{96,64},{0,96},{33,1},{65,33},{97,65},{1,97},{34,2}... | collective-permute-start | bytes 589832 | tf_op jit(solution)/shard_map/ppermute | solution.py:276
  133.8 11.2 %collective-permute-start.20 = (f32[24,8,128]{2,1,0:T(8,128)}, f32[24,8,128]{2,1,0:T(8,128)S(1)}, u32[]{:S(2)}, u32[]{:S(2)}) collective-permute-start(f32[24,8,128]{2,1,0:T(8,128)} %copy-done.11), channel_id=1, source_target_pairs={{0,8},{8,16},{16,24},{24,0},{1,9},{9,17},{17,25},{25,1},{2,10},{10... | collective-permute-start | bytes 294920 | tf_op jit(solution)/shard_map/ppermute | solution.py:275
  135.3 9.7 %collective-permute-start.21 = (f32[24,8,128]{2,1,0:T(8,128)}, f32[24,8,128]{2,1,0:T(8,128)S(1)}, u32[]{:S(2)}, u32[]{:S(2)}) collective-permute-start(f32[24,8,128]{2,1,0:T(8,128)} %copy-done.10), channel_id=1, source_target_pairs={{8,0},{16,8},{24,16},{0,24},{9,1},{17,9},{25,17},{1,25},{10,2},{18... | collective-permute-start | bytes 294920 | tf_op jit(solution)/shard_map/ppermute | solution.py:276
  137.1 3.5 %collective-permute-start.22 = (f32[24,1,256]{2,1,0:T(1,128)}, f32[24,1,256]{2,1,0:T(1,128)S(1)}, u32[]{:S(2)}, u32[]{:S(2)}) collective-permute-start(f32[24,1,256]{2,1,0:T(1,128)} %copy-done.13), channel_id=1, source_target_pairs={{0,1},{1,2},{2,3},{3,4},{4,5},{5,6},{6,7},{7,0},{8,9},{9,10},{10,1... | collective-permute-start | bytes 73736 | tf_op jit(solution)/shard_map/ppermute | solution.py:275
  140.6 4.4 %collective-permute-start.23 = (f32[24,1,256]{2,1,0:T(1,128)}, f32[24,1,256]{2,1,0:T(1,128)S(1)}, u32[]{:S(2)}, u32[]{:S(2)}) collective-permute-start(f32[24,1,256]{2,1,0:T(1,128)} %copy-done.12), channel_id=1, source_target_pairs={{1,0},{2,1},{3,2},{4,3},{5,4},{6,5},{7,6},{0,7},{9,8},{10,9},{11,1... | collective-permute-start | bytes 73736 | tf_op jit(solution)/shard_map/ppermute | solution.py:276

commit v6 on v5

--- a/solution.py
+++ b/solution.py
@@ -9,7 +9,6 @@
 
 GROUP = 12
 TOGETHER = 12
-SPREAD = 8
 LISTED = 96
 NETWORK_MIB = 38
 ALL = ("gx", "gy", "gz")
@@ -153,7 +152,11 @@
             put_z_faces(out, f, zf, zl)
 
 
-def diffuse_kernel(rates, q, xlo, xhi, ylo, yhi, zlo, zhi, out, zcol):
+def diffuse_kernel(rates, q, xlo, xhi, ylo, yhi, zlo, zhi, heats, out, activity, zcol):
+    @pl.when(pl.program_id(0) == 0)
+    def _():
+        activity[0, 0] = jnp.sum(heats[...]) * (1.0 / (8.0 * 128.0))
+
     base = pl.program_id(0) * GROUP
     for f in range(GROUP):
         zcol[f] = z_columns(zlo[f], zhi[f])
@@ -312,8 +315,7 @@
     ids, owners = react_list[0], owner_table[0]
     count = jnp.sum((ids >= 0).astype(jnp.int32))
     listed = jnp.concatenate([count[None], jnp.where(ids >= 0, ids, ids[0])])
-    rows = jnp.arange(128 * SPREAD, dtype=jnp.int32)[:, None]
-    owned_by = (owners[None, :] * SPREAD == rows).astype(F32)
+    owned_by = (owners[None, :] == jnp.arange(128, dtype=jnp.int32)[:, None]).astype(F32)
 
     faces = pl.pallas_call(
         prep_kernel, out_shape=face_shapes(25), compiler_params=params(32)
@@ -374,26 +376,24 @@
         network_kernel,
         in_specs=[pl.BlockSpec(memory_space=pltpu.SMEM)] + [in_vmem] * 9,
         out_specs=[in_vmem] * 8,
-        out_shape=[sds((24 * 256, 128), F32), sds((128 * SPREAD, 128), F32), *face_shapes(24)],
+        out_shape=[sds((24 * 256, 128), F32), sds((128, 128), F32), *face_shapes(24)],
         scratch_shapes=[pltpu.VMEM((LISTED, 128), F32)],
         compiler_params=params(NETWORK_MIB),
     )(listed, flowed.reshape(24 * 256, 128), owned_by, *columns, weight_out.T)
     reacted = reacted.reshape(fields.shape)
     around = exchange(faces)
-    heats = swap(sent.reshape(128, SPREAD, 128))
-    updated = pl.pallas_call(
+    heats = swap(sent.reshape(128, 1, 128)).reshape(128, 128)
+    updated, activity = pl.pallas_call(
         diffuse_kernel,
         grid=(24 // GROUP,),
-        in_specs=[pl.BlockSpec(memory_space=pltpu.SMEM), BRICK, *FACES],
-        out_specs=BRICK,
-        out_shape=brick,
+        in_specs=[pl.BlockSpec(memory_space=pltpu.SMEM), BRICK, *FACES, whole((128, 128))],
+        out_specs=[BRICK, pl.BlockSpec(memory_space=pltpu.SMEM)],
+        out_shape=[brick, sds((1, 1), F32)],
         scratch_shapes=[pltpu.VMEM((GROUP, 256, 128), F32)],
         compiler_params=params(32),
         cost_estimate=pl.CostEstimate(flops=10**9, bytes_accessed=24 * 2**20, transcendentals=0),
-    )(diffusivity, reacted, *around)
-    heats, updated = lax.optimization_barrier((heats, updated))
-    owner_activity = (jnp.sum(heats) / (8.0 * 128.0)).reshape(1)
-    return (updated, owner_activity)
+    )(diffusivity, reacted, *around, heats)
+    return (updated, activity.reshape(1))
 
 
 def solution(mesh):

time: 153 us -> 147 us (0.961)
  starting transfers between devices: 103 us -> 45.5 us
  Pallas kernels: 29.9 us -> 84.3 us
  waiting for transfers between devices: 8.14 us -> 10.3 us
  other arithmetic: 3.22 us -> 1.39 us
  between operations: 2.71 us -> 0.91 us
    all_to_all x1, starting transfers between devices: 62.9 us -> 7.01 us  [swap(): return lax.all_to_all(tiles, ALL, split_axis=0, concat_axis=0, tiled=True)]
    pallas_call x1, Pallas kernels: 13.1 us -> 66.8 us  [local(): pl.pallas_call(network_kernel, in_specs=[pl.BlockSpec(memory_space=pltpu....]
    ppermute x12, starting transfers between devices: 15.9 us -> 12.2 us  [exchange(): got.append(lax.ppermute(last, axis, [(i, (i + 1) % n) for i in range(n)]))]
    all_to_all x1, waiting for transfers between devices: 0.01 us -> 2.49 us  [swap(): return lax.all_to_all(tiles, ALL, split_axis=0, concat_axis=0, tiled=True)]
    ppermute x12, starting transfers between devices: 23.8 us -> 26.3 us  [exchange(): got.append(lax.ppermute(first, axis, [((i + 1) % n, i) for i in range(n)]))]
    reduce_sum x1 -> x0, other arithmetic: 1.78 us -> none  [local(): owner_activity = (jnp.sum(heats) / (8.0 * 128.0)).reshape(1)]
    unnamed x36 -> x30, local copies, waits for them, and re-layouts: 6.22 us -> 4.8 us
  transfers between devices with their start and end apart: 25 -> 25, of which waited for: 5 -> 6; matrix products, arithmetic and copies ran while one was open for 1% -> 1% of each run, Pallas kernels for 4% -> 1%
where the time goes in v6:
time: 147 us
  Pallas kernels  84.3 us (57%)
  starting transfers between devices  45.5 us (31%)
  waiting for transfers between devices  10.3 us (7%)
  local copies, waits for them, and re-layouts  4.81 us (3%)
    pallas_call x1, Pallas kernels, local(): pl.pallas_call(network_kernel, in_specs=[pl.BlockSpec(memory_space=pltpu....  66.8 us
    ppermute x12, starting transfers between devices, exchange(): got.append(lax.ppermute(first, axis, [((i + 1) % n, i) for i in range(n)]))  26.3 us
    ppermute x12, starting transfers between devices, exchange(): got.append(lax.ppermute(last, axis, [(i, (i + 1) % n) for i in range(n)]))  12.2 us
    pallas_call x3, Pallas kernels, section(): pl.pallas_call(functools.partial(section_kernel, kind), grid=(24 // GROUP...  10.8 us
    all_to_all x1, starting transfers between devices, swap(): return lax.all_to_all(tiles, ALL, split_axis=0, concat_axis=0, tiled=True)  7.01 us
    ppermute x12, waiting for transfers between devices, exchange(): got.append(lax.ppermute(last, axis, [(i, (i + 1) % n) for i in range(n)]))  4.88 us
    unnamed x30, local copies, waits for them, and re-layouts  4.8 us
    pallas_call x1, Pallas kernels, local(): pl.pallas_call(diffuse_kernel, grid=(24 // GROUP,), in_specs=[pl.BlockSpe...  4.69 us
  transfers between devices with their start and end apart: 25, of which 6 were waited for; matrix products, arithmetic and copies ran while one was open for 1% of the time, Pallas kernels for 1%

profile of v6, /device:TPU:1, one launch (start us, length us, event | category | flops | bytes accessed | tf_op | source)
XLA Modules:
  0.0 147.2 jit_solution(14322376831661614103)
XLA Ops:
  0.6 1.9 %copy-done = f32[24,8,32,128]{3,2,1,0:T(8,128)S(1)} copy-done((f32[24,8,32,128]{3,2,1,0:T(8,128)S(1)}, f32[24,8,32,128]{3,2,1,0:T(8,128)}, u32[]{:S(2)}) %copy-start) | copy-done | bytes 3145752
  2.5 1.0 copy-done.2
  3.5 0.5 shard_map.140
  4.1 0.0 copy-start.14
  4.1 0.0 copy-start.12
  4.1 0.0 copy-start.11
  4.1 2.1 %collective-permute-start = (bf16[25,32,128]{2,1,0:T(8,128)(2,1)S(1)}, bf16[25,32,128]{2,1,0:T(8,128)(2,1)S(1)}, u32[]{:S(2)}, u32[]{:S(2)}) collective-permute-start(bf16[25,32,128]{2,1,0:T(8,128)(2,1)S(1)} %get-tuple-element.47), channel_id=1, source_target_pairs={{0,32},{32,64},{64,96},{96,0},{1,33},{33,65},{65,97},{97,1},{2,34}... | collective-permute-start | bytes 614408 | tf_op jit(solution)/shard_map/ppermute | solution.py:278
  6.2 1.3 collective-permute-start.1
  7.6 1.8 %collective-permute-start.2 = (f32[25,8,128]{2,1,0:T(8,128)S(1)}, f32[25,8,128]{2,1,0:T(8,128)S(1)}, u32[]{:S(2)}, u32[]{:S(2)}) collective-permute-start(f32[25,8,128]{2,1,0:T(8,128)S(1)} %get-tuple-element.49), channel_id=1, source_target_pairs={{0,8},{8,16},{16,24},{24,0},{1,9},{9,17},{17,25},{25,1},{2,10},{10... | collective-permute-start | bytes 307208 | tf_op jit(solution)/shard_map/ppermute | solution.py:278
  9.3 2.1 %collective-permute-start.3 = (f32[25,8,128]{2,1,0:T(8,128)S(1)}, f32[25,8,128]{2,1,0:T(8,128)S(1)}, u32[]{:S(2)}, u32[]{:S(2)}) collective-permute-start(f32[25,8,128]{2,1,0:T(8,128)S(1)} %get-tuple-element.50), channel_id=1, source_target_pairs={{8,0},{16,8},{24,16},{0,24},{9,1},{17,9},{25,17},{1,25},{10,2},{18... | collective-permute-start | bytes 307208 | tf_op jit(solution)/shard_map/ppermute | solution.py:279
  11.4 2.7 %collective-permute-start.4 = (f32[25,1,256]{2,1,0:T(1,128)S(1)}, f32[25,1,256]{2,1,0:T(1,128)S(1)}, u32[]{:S(2)}, u32[]{:S(2)}) collective-permute-start(f32[25,1,256]{2,1,0:T(1,128)S(1)} %get-tuple-element.51), channel_id=1, source_target_pairs={{0,1},{1,2},{2,3},{3,4},{4,5},{5,6},{6,7},{7,0},{8,9},{9,10},{10,1... | collective-permute-start | bytes 76808 | tf_op jit(solution)/shard_map/ppermute | solution.py:278
  14.1 1.0 collective-permute-done.4.refs_5_.refs_12_
  15.1 2.3 %collective-permute-start.5 = (f32[25,1,256]{2,1,0:T(1,128)S(1)}, f32[25,1,256]{2,1,0:T(1,128)S(1)}, u32[]{:S(2)}, u32[]{:S(2)}) collective-permute-start(f32[25,1,256]{2,1,0:T(1,128)S(1)} %get-tuple-element.52), channel_id=1, source_target_pairs={{1,0},{2,1},{3,2},{4,3},{5,4},{6,5},{7,6},{0,7},{9,8},{10,9},{11,1... | collective-permute-start | bytes 76808 | tf_op jit(solution)/shard_map/ppermute | solution.py:279
  17.4 1.5 %collective-permute-done.5.refs_6_.refs_13_ = f32[25,1,256]{2,1,0:T(1,128)S(1)} collective-permute-done((f32[25,1,256]{2,1,0:T(1,128)S(1)}, f32[25,1,256]{2,1,0:T(1,128)S(1)}, u32[]{:S(2)}, u32[]{:S(2)}) %collective-permute-start.5) | collective-permute-done | bytes 25632 | tf_op jit(solution)/shard_map/ppermute | solution.py:279
  18.9 0.0 collective-permute-done.2.refs_3_.refs_10_
  18.9 0.0 collective-permute-done.3.refs_4_.refs_11_
  18.9 0.0 collective-permute-done.refs_1_.refs_8_
  18.9 0.0 collective-permute-done.1.refs_2_.refs_9_
  18.9 3.6 %shard_map.141 = (f32[24,8,32,128]{3,2,1,0:T(8,128)S(1)}, f32[6,8,32,128]{3,2,1,0:T(8,128)S(1)}, bf16[24,32,128]{2,1,0:T(8,128)(2,1)S(1)}, bf16[24,32,128]{2,1,0...) custom-call(f32[24,8,32,128]{3,2,1,0:T(8,128)S(1)} %copy-done, ...), custom_call_target="tpu_custom_call" | custom-call | tf_op jit(solution)/shard_map/pallas_call | solution.py:284
  22.6 0.0 collective-permute-start.10
  22.6 0.5 collective-permute-start.11
  23.1 0.0 collective-permute-start.8
  23.1 2.7 %collective-permute-start.9 = (f32[24,8,128]{2,1,0:T(8,128)S(1)}, f32[24,8,128]{2,1,0:T(8,128)S(1)}, u32[]{:S(2)}, u32[]{:S(2)}) collective-permute-start(f32[24,8,128]{2,1,0:T(8,128)S(1)} %get-tuple-element.58), channel_id=1, source_target_pairs={{8,0},{16,8},{24,16},{0,24},{9,1},{17,9},{25,17},{1,25},{10,2},{18... | collective-permute-start | bytes 294920 | tf_op jit(solution)/shard_map/ppermute | solution.py:279
  25.8 0.0 collective-permute-start.6
  25.8 2.7 %collective-permute-start.7 = (bf16[24,32,128]{2,1,0:T(8,128)(2,1)S(1)}, bf16[24,32,128]{2,1,0:T(8,128)(2,1)S(1)}, u32[]{:S(2)}, u32[]{:S(2)}) collective-permute-start(bf16[24,32,128]{2,1,0:T(8,128)(2,1)S(1)} %get-tuple-element.56), channel_id=1, source_target_pairs={{32,0},{64,32},{96,64},{0,96},{33,1},{65,33},{97,65},{1,97},{34,2}... | collective-permute-start | bytes 589832 | tf_op jit(solution)/shard_map/ppermute | solution.py:279
  28.5 0.0 collective-permute-done.8.refs_4_
  28.5 0.0 collective-permute-done.9.refs_5_
  28.5 3.0 %collective-permute-done.6.refs_2_ = bf16[24,32,128]{2,1,0:T(8,128)(2,1)S(1)} collective-permute-done((bf16[24,32,128]{2,1,0:T(8,128)(2,1)S(1)}, bf16[24,32,128]{2,1,0:T(8,128)(2,1)S(1)}, u32[]{:S(2)}, u32[]{:S(2)}) %collective-permute-start.6) | collective-permute-done | bytes 196640 | tf_op jit(solution)/shard_map/ppermute | solution.py:278
  31.5 0.0 copy-start.4
  31.5 0.0 copy-start.7
  31.5 0.0 copy-start.8
  31.5 3.9 %shard_map.142 = (f32[24,8,32,128]{3,2,1,0:T(8,128)S(1)}, bf16[24,32,128]{2,1,0:T(8,128)(2,1)S(1)}, bf16[24,32,128]{2,1,0:T(8,128)(2,1)S(1)}, f32[24,8,128]{2,1,...) custom-call(f32[24,8,32,128]{3,2,1,0:T(8,128)S(1)} %get-tuple-element.54.refs_0_, ...), custom_call_target="tpu_custom_call" | custom-call | tf_op jit(solution)/shard_map/pallas_call | solution.py:284
  35.4 4.0 %collective-permute-start.16 = (f32[24,1,256]{2,1,0:T(1,128)S(1)}, f32[24,1,256]{2,1,0:T(1,128)S(1)}, u32[]{:S(2)}, u32[]{:S(2)}) collective-permute-start(f32[24,1,256]{2,1,0:T(1,128)S(1)} %get-tuple-element.67), channel_id=1, source_target_pairs={{0,1},{1,2},{2,3},{3,4},{4,5},{5,6},{6,7},{7,0},{8,9},{9,10},{10,1... | collective-permute-start | bytes 73736 | tf_op jit(solution)/shard_map/ppermute | solution.py:278
  39.4 0.0 collective-permute-start.12
  39.4 2.7 %collective-permute-start.13 = (bf16[24,32,128]{2,1,0:T(8,128)(2,1)S(1)}, bf16[24,32,128]{2,1,0:T(8,128)(2,1)S(1)}, u32[]{:S(2)}, u32[]{:S(2)}) collective-permute-start(bf16[24,32,128]{2,1,0:T(8,128)(2,1)S(1)} %get-tuple-element.64), channel_id=1, source_target_pairs={{32,0},{64,32},{96,64},{0,96},{33,1},{65,33},{97,65},{1,97},{34,2}... | collective-permute-start | bytes 589832 | tf_op jit(solution)/shard_map/ppermute | solution.py:279
  42.1 0.7 fusion.1
  42.8 0.9 collective-permute-start.17
  43.7 0.0 collective-permute-start.14
  43.7 0.0 collective-permute-done.16.refs_6_
  43.7 2.7 %collective-permute-start.15 = (f32[24,8,128]{2,1,0:T(8,128)S(1)}, f32[24,8,128]{2,1,0:T(8,128)S(1)}, u32[]{:S(2)}, u32[]{:S(2)}) collective-permute-start(f32[24,8,128]{2,1,0:T(8,128)S(1)} %get-tuple-element.66), channel_id=1, source_target_pairs={{8,0},{16,8},{24,16},{0,24},{9,1},{17,9},{25,17},{1,25},{10,2},{18... | collective-permute-start | bytes 294920 | tf_op jit(solution)/shard_map/ppermute | solution.py:279
  46.4 0.7 pad_add_fusion.listed
  47.1 1.5 %shard_map.144 = (bf16[1600,32]{1,0:T(8,128)(2,1)S(1)}, bf16[800,1600]{1,0:T(8,128)(2,1)S(1)}, bf16[400,800]{1,0:T(8,128)(2,1)S(1)}, f32[800,128]{1,0:T(8,128)S(...) custom-call(bf16[24,1600]{1,0:T(8,128)(2,1)S(1)} %copy-done.4, f32[1,1600]{1,0:T(1,128)S(1)} %reshape.33.b_in, ...), custom_call_target="tpu_custom_call" | custom-call | bytes 8388608 | tf_op jit(solution)/shard_map/pallas_call | solution.py:349
  48.6 0.0 collective-permute-done.17.refs_7_
  48.6 0.0 collective-permute-done.15.refs_5_
  48.6 0.0 collective-permute-done.12.refs_2_
  48.7 0.0 copy-start.6
  48.7 3.3 %shard_map.143 = f32[24,8,32,128]{3,2,1,0:T(8,128)S(1)} custom-call(f32[24,8,32,128]{3,2,1,0:T(8,128)S(1)} %get-tuple-element.62.refs_0_, f32[24,8,32,128]{3,2,1,0:T(8,128)S(1)} %copy-done, bf16[24,32,128]{2,1,0:T(8,128)(2,1)S(1)} %collective-permute-done.12.refs_2_, bf16[24,32,128]{2,1,0:T(8,128)(2,1)S(1)} %collective-permute-done.13.refs_3_, ...), custom_call_target="tpu_custom_call" | custom-call | tf_op jit(solution)/shard_map/pallas_call | solution.py:284
  52.0 66.8 %shard_map.145 = (f32[6144,128]{1,0:T(8,128)S(1)}, f32[128,128]{1,0:T(8,128)S(1)}, bf16[24,32,128]{2,1,0:T(8,128)(2,1)}, bf16[24,32,128]{2,1,0:T(8,128)(2,1)}, f...) custom-call(s32[97]{0:T(128)S(1)} %pad_add_fusion.listed, ...), custom_call_target="tpu_custom_call" | custom-call | tf_op jit(solution)/shard_map/pallas_call | solution.py:375
  118.8 0.6 copy-done.5
  119.4 0.6 copy-done.10
  120.0 2.7 %collective-permute-start.19 = (bf16[24,32,128]{2,1,0:T(8,128)(2,1)}, bf16[24,32,128]{2,1,0:T(8,128)(2,1)}, u32[]{:S(2)}, u32[]{:S(2)}) collective-permute-start(bf16[24,32,128]{2,1,0:T(8,128)(2,1)} %get-tuple-element.84), channel_id=1, source_target_pairs={{32,0},{64,32},{96,64},{0,96},{33,1},{65,33},{97,65},{1,97},{34,2}... | collective-permute-start | bytes 589832 | tf_op jit(solution)/shard_map/ppermute | solution.py:279
  122.7 0.0 collective-permute-start.20
  122.7 2.7 %collective-permute-start.21 = (f32[24,8,128]{2,1,0:T(8,128)}, f32[24,8,128]{2,1,0:T(8,128)}, u32[]{:S(2)}, u32[]{:S(2)}) collective-permute-start(f32[24,8,128]{2,1,0:T(8,128)} %get-tuple-element.86), channel_id=1, source_target_pairs={{8,0},{16,8},{24,16},{0,24},{9,1},{17,9},{25,17},{1,25},{10,2},{18... | collective-permute-start | bytes 294920 | tf_op jit(solution)/shard_map/ppermute | solution.py:279
  125.3 7.0 %all-to-all-start = ((f32[128,1,128]{2,1,0:T(1,128)}), f32[128,1,128]{2,1,0:T(1,128)S(1)}, u32[]{:S(2)}, u32[]{:S(2)}) async-start(f32[128,1,128]{2,1,0:T(1,128)} %bitcast.24), calls=%async_computation | async-start | bytes 131072 | tf_op jit(solution)/shard_map/all_to_all | solution.py:296
  132.4 1.6 %collective-permute-start.22 = (f32[24,1,256]{2,1,0:T(1,128)S(1)}, f32[24,1,256]{2,1,0:T(1,128)S(1)}, u32[]{:S(2)}, u32[]{:S(2)}) collective-permute-start(f32[24,1,256]{2,1,0:T(1,128)S(1)} %get-tuple-element.87), channel_id=1, source_target_pairs={{0,1},{1,2},{2,3},{3,4},{4,5},{5,6},{6,7},{7,0},{8,9},{9,10},{10,1... | collective-permute-start | bytes 73736 | tf_op jit(solution)/shard_map/ppermute | solution.py:278
  134.0 0.9 collective-permute-done.22.zlo
  135.0 3.0 %collective-permute-start.23 = (f32[24,1,256]{2,1,0:T(1,128)}, f32[24,1,256]{2,1,0:T(1,128)S(1)}, u32[]{:S(2)}, u32[]{:S(2)}) collective-permute-start(f32[24,1,256]{2,1,0:T(1,128)} %copy-done.10), channel_id=1, source_target_pairs={{1,0},{2,1},{3,2},{4,3},{5,4},{6,5},{7,6},{0,7},{9,8},{10,9},{11,1... | collective-permute-start | bytes 73736 | tf_op jit(solution)/shard_map/ppermute | solution.py:279
  138.0 1.4 collective-permute-done.23.zhi
  139.3 2.5 %all-to-all-done = f32[128,1,128]{2,1,0:T(1,128)S(1)} async-done(((f32[128,1,128]{2,1,0:T(1,128)}), f32[128,1,128]{2,1,0:T(1,128)S(1)}, u32[]{:S(2)}, u32[]{:S(2)}) %all-to-all-start) | async-done | bytes 65568 | tf_op jit(solution)/shard_map/all_to_all | solution.py:296
  141.8 0.0 collective-permute-done.20.ylo
  141.8 0.0 collective-permute-done.21.yhi
  141.9 0.0 copy-start.9
  141.9 0.6 copy-done.9
  142.5 4.7 %shard_map.146 = (f32[24,8,32,128]{3,2,1,0:T(8,128)}, f32[1,1]{1,0:T(1,128)}) custom-call(f32[24]{0:T(128)S(1)} %copy-done.9, f32[24,8,32,128]{3,2,1,0:T(8,128)S(1)} %bitcast.20, bf16[24,32,128]{2,1,0:T(8,128)(2,1)S(1)} %collective-permute-done.18.xlo, bf16[24,32,128]{2,1,0:T(8,128)(2,1)} %collective-permute-done.19.xhi, ...), custom_call_target="tpu_custom_call" | custom-call | flops 1000000000 | bytes 25165824 | tf_op jit(solution)/shard_map/pallas_call | solution.py:386
  (28 shorter events, 0.1 us)
Async XLA Ops:
  0.6 1.9 %copy-start = (f32[24,8,32,128]{3,2,1,0:T(8,128)S(1)}, f32[24,8,32,128]{3,2,1,0:T(8,128)}, u32[]{:S(2)}) copy-start(f32[24,8,32,128]{3,2,1,0:T(8,128)} %refs_1_.3) | copy-start | bytes 9437188
  2.5 1.0 copy-start.2
  4.1 24.4 %copy-start.14 = (s32[1,96]{1,0:T(1,128)S(1)}, s32[1,96]{1,0:T(1,128)}, u32[]{:S(2)}) copy-start(s32[1,96]{1,0:T(1,128)} %param.25) | copy-start | bytes 1156
  4.1 24.4 %copy-start.12 = (f32[800]{0:T(1024)S(1)}, f32[800]{0:T(1024)}, u32[]{:S(2)}) copy-start(f32[800]{0:T(1024)} %param.19) | copy-start | bytes 9604
  4.1 24.4 %copy-start.11 = (f32[1600]{0:T(1024)S(1)}, f32[1600]{0:T(1024)}, u32[]{:S(2)}) copy-start(f32[1600]{0:T(1024)} %param.17) | copy-start | bytes 19204
  4.1 14.8 %collective-permute-start = (bf16[25,32,128]{2,1,0:T(8,128)(2,1)S(1)}, bf16[25,32,128]{2,1,0:T(8,128)(2,1)S(1)}, u32[]{:S(2)}, u32[]{:S(2)}) collective-permute-start(bf16[25,32,128]{2,1,0:T(8,128)(2,1)S(1)} %get-tuple-element.47), channel_id=1, source_target_pairs={{0,32},{32,64},{64,96},{96,0},{1,33},{33,65},{65,97},{97,1},{2,34}... | collective-permute-start | bytes 614408 | tf_op jit(solution)/shard_map/ppermute | solution.py:278
  6.2 12.7 %collective-permute-start.1 = (bf16[25,32,128]{2,1,0:T(8,128)(2,1)S(1)}, bf16[25,32,128]{2,1,0:T(8,128)(2,1)S(1)}, u32[]{:S(2)}, u32[]{:S(2)}) collective-permute-start(bf16[25,32,128]{2,1,0:T(8,128)(2,1)S(1)} %get-tuple-element.48), channel_id=1, source_target_pairs={{32,0},{64,32},{96,64},{0,96},{33,1},{65,33},{97,65},{1,97},{34,2}... | collective-permute-start | bytes 614408 | tf_op jit(solution)/shard_map/ppermute | solution.py:279
  7.6 11.4 %collective-permute-start.2 = (f32[25,8,128]{2,1,0:T(8,128)S(1)}, f32[25,8,128]{2,1,0:T(8,128)S(1)}, u32[]{:S(2)}, u32[]{:S(2)}) collective-permute-start(f32[25,8,128]{2,1,0:T(8,128)S(1)} %get-tuple-element.49), channel_id=1, source_target_pairs={{0,8},{8,16},{16,24},{24,0},{1,9},{9,17},{17,25},{25,1},{2,10},{10... | collective-permute-start | bytes 307208 | tf_op jit(solution)/shard_map/ppermute | solution.py:278
  9.3 9.6 %collective-permute-start.3 = (f32[25,8,128]{2,1,0:T(8,128)S(1)}, f32[25,8,128]{2,1,0:T(8,128)S(1)}, u32[]{:S(2)}, u32[]{:S(2)}) collective-permute-start(f32[25,8,128]{2,1,0:T(8,128)S(1)} %get-tuple-element.50), channel_id=1, source_target_pairs={{8,0},{16,8},{24,16},{0,24},{9,1},{17,9},{25,17},{1,25},{10,2},{18... | collective-permute-start | bytes 307208 | tf_op jit(solution)/shard_map/ppermute | solution.py:279
  11.4 3.7 %collective-permute-start.4 = (f32[25,1,256]{2,1,0:T(1,128)S(1)}, f32[25,1,256]{2,1,0:T(1,128)S(1)}, u32[]{:S(2)}, u32[]{:S(2)}) collective-permute-start(f32[25,1,256]{2,1,0:T(1,128)S(1)} %get-tuple-element.51), channel_id=1, source_target_pairs={{0,1},{1,2},{2,3},{3,4},{4,5},{5,6},{6,7},{7,0},{8,9},{9,10},{10,1... | collective-permute-start | bytes 76808 | tf_op jit(solution)/shard_map/ppermute | solution.py:278
  15.1 3.8 %collective-permute-start.5 = (f32[25,1,256]{2,1,0:T(1,128)S(1)}, f32[25,1,256]{2,1,0:T(1,128)S(1)}, u32[]{:S(2)}, u32[]{:S(2)}) collective-permute-start(f32[25,1,256]{2,1,0:T(1,128)S(1)} %get-tuple-element.52), channel_id=1, source_target_pairs={{1,0},{2,1},{3,2},{4,3},{5,4},{6,5},{7,6},{0,7},{9,8},{10,9},{11,1... | collective-permute-start | bytes 76808 | tf_op jit(solution)/shard_map/ppermute | solution.py:279
  22.6 3.2 %collective-permute-start.10 = (f32[24,1,256]{2,1,0:T(1,128)S(1)}, f32[24,1,256]{2,1,0:T(1,128)S(1)}, u32[]{:S(2)}, u32[]{:S(2)}) collective-permute-start(f32[24,1,256]{2,1,0:T(1,128)S(1)} %get-tuple-element.59), channel_id=1, source_target_pairs={{0,1},{1,2},{2,3},{3,4},{4,5},{5,6},{6,7},{7,0},{8,9},{9,10},{10,1... | collective-permute-start | bytes 73736 | tf_op jit(solution)/shard_map/ppermute | solution.py:278
  22.6 5.9 %collective-permute-start.11 = (f32[24,1,256]{2,1,0:T(1,128)S(1)}, f32[24,1,256]{2,1,0:T(1,128)S(1)}, u32[]{:S(2)}, u32[]{:S(2)}) collective-permute-start(f32[24,1,256]{2,1,0:T(1,128)S(1)} %get-tuple-element.60), channel_id=1, source_target_pairs={{1,0},{2,1},{3,2},{4,3},{5,4},{6,5},{7,6},{0,7},{9,8},{10,9},{11,1... | collective-permute-start | bytes 73736 | tf_op jit(solution)/shard_map/ppermute | solution.py:279
  23.1 5.4 %collective-permute-start.8 = (f32[24,8,128]{2,1,0:T(8,128)S(1)}, f32[24,8,128]{2,1,0:T(8,128)S(1)}, u32[]{:S(2)}, u32[]{:S(2)}) collective-permute-start(f32[24,8,128]{2,1,0:T(8,128)S(1)} %get-tuple-element.57), channel_id=1, source_target_pairs={{0,8},{8,16},{16,24},{24,0},{1,9},{9,17},{17,25},{25,1},{2,10},{10... | collective-permute-start | bytes 294920 | tf_op jit(solution)/shard_map/ppermute | solution.py:278
  23.1 5.4 %collective-permute-start.9 = (f32[24,8,128]{2,1,0:T(8,128)S(1)}, f32[24,8,128]{2,1,0:T(8,128)S(1)}, u32[]{:S(2)}, u32[]{:S(2)}) collective-permute-start(f32[24,8,128]{2,1,0:T(8,128)S(1)} %get-tuple-element.58), channel_id=1, source_target_pairs={{8,0},{16,8},{24,16},{0,24},{9,1},{17,9},{25,17},{1,25},{10,2},{18... | collective-permute-start | bytes 294920 | tf_op jit(solution)/shard_map/ppermute | solution.py:279
  25.8 5.7 %collective-permute-start.6 = (bf16[24,32,128]{2,1,0:T(8,128)(2,1)S(1)}, bf16[24,32,128]{2,1,0:T(8,128)(2,1)S(1)}, u32[]{:S(2)}, u32[]{:S(2)}) collective-permute-start(bf16[24,32,128]{2,1,0:T(8,128)(2,1)S(1)} %get-tuple-element.55), channel_id=1, source_target_pairs={{0,32},{32,64},{64,96},{96,0},{1,33},{33,65},{65,97},{97,1},{2,34}... | collective-permute-start | bytes 589832 | tf_op jit(solution)/shard_map/ppermute | solution.py:278
  25.8 5.7 %collective-permute-start.7 = (bf16[24,32,128]{2,1,0:T(8,128)(2,1)S(1)}, bf16[24,32,128]{2,1,0:T(8,128)(2,1)S(1)}, u32[]{:S(2)}, u32[]{:S(2)}) collective-permute-start(bf16[24,32,128]{2,1,0:T(8,128)(2,1)S(1)} %get-tuple-element.56), channel_id=1, source_target_pairs={{32,0},{64,32},{96,64},{0,96},{33,1},{65,33},{97,65},{1,97},{34,2}... | collective-permute-start | bytes 589832 | tf_op jit(solution)/shard_map/ppermute | solution.py:279
  31.5 10.6 %copy-start.13 = (s32[1,96]{1,0:T(1,128)S(1)}, s32[1,96]{1,0:T(1,128)}, u32[]{:S(2)}) copy-start(s32[1,96]{1,0:T(1,128)} %param.24) | copy-start | bytes 1156
  31.5 15.6 %copy-start.1 = (bf16[1600,800]{0,1:T(8,128)(2,1)S(1)}, bf16[1600,800]{0,1:T(8,128)(2,1)}, u32[]{:S(2)}) copy-start(bf16[1600,800]{0,1:T(8,128)(2,1)} %param.18) | copy-start | bytes 7680004
  31.5 15.6 %copy-start.3 = (bf16[800,400]{0,1:T(8,128)(2,1)S(1)}, bf16[800,400]{0,1:T(8,128)(2,1)}, u32[]{:S(2)}) copy-start(bf16[800,400]{0,1:T(8,128)(2,1)} %param.20) | copy-start | bytes 1920004
  31.5 15.6 %copy-start.4 = (bf16[24,1600]{1,0:T(8,128)(2,1)S(1)}, bf16[24,1600]{1,0:T(8,128)(2,1)}, u32[]{:S(2)}) copy-start(bf16[24,1600]{1,0:T(8,128)(2,1)} %w_in) | copy-start | bytes 230404
  31.5 15.6 %copy-start.7 = (f32[400]{0:T(512)S(1)}, f32[400]{0:T(512)}, u32[]{:S(2)}) copy-start(f32[400]{0:T(512)} %param.21) | copy-start | bytes 4804
  31.5 15.6 %copy-start.8 = (f32[24]{0:T(128)S(1)}, f32[24]{0:T(128)}, u32[]{:S(2)}) copy-start(f32[24]{0:T(128)} %param.23) | copy-start | bytes 292
  35.4 8.3 %collective-permute-start.16 = (f32[24,1,256]{2,1,0:T(1,128)S(1)}, f32[24,1,256]{2,1,0:T(1,128)S(1)}, u32[]{:S(2)}, u32[]{:S(2)}) collective-permute-start(f32[24,1,256]{2,1,0:T(1,128)S(1)} %get-tuple-element.67), channel_id=1, source_target_pairs={{0,1},{1,2},{2,3},{3,4},{4,5},{5,6},{6,7},{7,0},{8,9},{9,10},{10,1... | collective-permute-start | bytes 73736 | tf_op jit(solution)/shard_map/ppermute | solution.py:278
  39.4 9.2 %collective-permute-start.12 = (bf16[24,32,128]{2,1,0:T(8,128)(2,1)S(1)}, bf16[24,32,128]{2,1,0:T(8,128)(2,1)S(1)}, u32[]{:S(2)}, u32[]{:S(2)}) collective-permute-start(bf16[24,32,128]{2,1,0:T(8,128)(2,1)S(1)} %get-tuple-element.63), channel_id=1, source_target_pairs={{0,32},{32,64},{64,96},{96,0},{1,33},{33,65},{65,97},{97,1},{2,34}... | collective-permute-start | bytes 589832 | tf_op jit(solution)/shard_map/ppermute | solution.py:278
  39.4 9.2 %collective-permute-start.13 = (bf16[24,32,128]{2,1,0:T(8,128)(2,1)S(1)}, bf16[24,32,128]{2,1,0:T(8,128)(2,1)S(1)}, u32[]{:S(2)}, u32[]{:S(2)}) collective-permute-start(bf16[24,32,128]{2,1,0:T(8,128)(2,1)S(1)} %get-tuple-element.64), channel_id=1, source_target_pairs={{32,0},{64,32},{96,64},{0,96},{33,1},{65,33},{97,65},{1,97},{34,2}... | collective-permute-start | bytes 589832 | tf_op jit(solution)/shard_map/ppermute | solution.py:279
  42.8 5.8 %collective-permute-start.17 = (f32[24,1,256]{2,1,0:T(1,128)S(1)}, f32[24,1,256]{2,1,0:T(1,128)S(1)}, u32[]{:S(2)}, u32[]{:S(2)}) collective-permute-start(f32[24,1,256]{2,1,0:T(1,128)S(1)} %get-tuple-element.68), channel_id=1, source_target_pairs={{1,0},{2,1},{3,2},{4,3},{5,4},{6,5},{7,6},{0,7},{9,8},{10,9},{11,1... | collective-permute-start | bytes 73736 | tf_op jit(solution)/shard_map/ppermute | solution.py:279
  43.7 4.9 %collective-permute-start.14 = (f32[24,8,128]{2,1,0:T(8,128)S(1)}, f32[24,8,128]{2,1,0:T(8,128)S(1)}, u32[]{:S(2)}, u32[]{:S(2)}) collective-permute-start(f32[24,8,128]{2,1,0:T(8,128)S(1)} %get-tuple-element.65), channel_id=1, source_target_pairs={{0,8},{8,16},{16,24},{24,0},{1,9},{9,17},{17,25},{25,1},{2,10},{10... | collective-permute-start | bytes 294920 | tf_op jit(solution)/shard_map/ppermute | solution.py:278
  43.7 4.9 %collective-permute-start.15 = (f32[24,8,128]{2,1,0:T(8,128)S(1)}, f32[24,8,128]{2,1,0:T(8,128)S(1)}, u32[]{:S(2)}, u32[]{:S(2)}) collective-permute-start(f32[24,8,128]{2,1,0:T(8,128)S(1)} %get-tuple-element.66), channel_id=1, source_target_pairs={{8,0},{16,8},{24,16},{0,24},{9,1},{17,9},{25,17},{1,25},{10,2},{18... | collective-permute-start | bytes 294920 | tf_op jit(solution)/shard_map/ppermute | solution.py:279
  48.7 3.3 %copy-start.6 = (bf16[400,24]{0,1:T(8,128)(2,1)S(1)}, bf16[400,24]{0,1:T(8,128)(2,1)}, u32[]{:S(2)}) copy-start(bf16[400,24]{0,1:T(8,128)(2,1)} %param.22) | copy-start | bytes 57604
  118.8 0.6 copy-start.5
  119.4 0.6 copy-start.10
  120.0 21.9 %collective-permute-start.18 = (bf16[24,32,128]{2,1,0:T(8,128)(2,1)}, bf16[24,32,128]{2,1,0:T(8,128)(2,1)S(1)}, u32[]{:S(2)}, u32[]{:S(2)}) collective-permute-start(bf16[24,32,128]{2,1,0:T(8,128)(2,1)} %get-tuple-element.83), channel_id=1, source_target_pairs={{0,32},{32,64},{64,96},{96,0},{1,33},{33,65},{65,97},{97,1},{2,34}... | collective-permute-start | bytes 589832 | tf_op jit(solution)/shard_map/ppermute | solution.py:278
  120.0 21.9 %collective-permute-start.19 = (bf16[24,32,128]{2,1,0:T(8,128)(2,1)}, bf16[24,32,128]{2,1,0:T(8,128)(2,1)}, u32[]{:S(2)}, u32[]{:S(2)}) collective-permute-start(bf16[24,32,128]{2,1,0:T(8,128)(2,1)} %get-tuple-element.84), channel_id=1, source_target_pairs={{32,0},{64,32},{96,64},{0,96},{33,1},{65,33},{97,65},{1,97},{34,2}... | collective-permute-start | bytes 589832 | tf_op jit(solution)/shard_map/ppermute | solution.py:279
  122.7 19.2 %collective-permute-start.20 = (f32[24,8,128]{2,1,0:T(8,128)}, f32[24,8,128]{2,1,0:T(8,128)S(1)}, u32[]{:S(2)}, u32[]{:S(2)}) collective-permute-start(f32[24,8,128]{2,1,0:T(8,128)} %get-tuple-element.85), channel_id=1, source_target_pairs={{0,8},{8,16},{16,24},{24,0},{1,9},{9,17},{17,25},{25,1},{2,10},{10... | collective-permute-start | bytes 294920 | tf_op jit(solution)/shard_map/ppermute | solution.py:278
  122.7 19.2 %collective-permute-start.21 = (f32[24,8,128]{2,1,0:T(8,128)}, f32[24,8,128]{2,1,0:T(8,128)}, u32[]{:S(2)}, u32[]{:S(2)}) collective-permute-start(f32[24,8,128]{2,1,0:T(8,128)} %get-tuple-element.86), channel_id=1, source_target_pairs={{8,0},{16,8},{24,16},{0,24},{9,1},{17,9},{25,17},{1,25},{10,2},{18... | collective-permute-start | bytes 294920 | tf_op jit(solution)/shard_map/ppermute | solution.py:279
  125.3 16.5 %all-to-all-start = ((f32[128,1,128]{2,1,0:T(1,128)}), f32[128,1,128]{2,1,0:T(1,128)S(1)}, u32[]{:S(2)}, u32[]{:S(2)}) async-start(f32[128,1,128]{2,1,0:T(1,128)} %bitcast.24), calls=%async_computation | async-start | bytes 131072 | tf_op jit(solution)/shard_map/all_to_all | solution.py:296
  132.4 2.6 %collective-permute-start.22 = (f32[24,1,256]{2,1,0:T(1,128)S(1)}, f32[24,1,256]{2,1,0:T(1,128)S(1)}, u32[]{:S(2)}, u32[]{:S(2)}) collective-permute-start(f32[24,1,256]{2,1,0:T(1,128)S(1)} %get-tuple-element.87), channel_id=1, source_target_pairs={{0,1},{1,2},{2,3},{3,4},{4,5},{5,6},{6,7},{7,0},{8,9},{9,10},{10,1... | collective-permute-start | bytes 73736 | tf_op jit(solution)/shard_map/ppermute | solution.py:278
  135.0 4.4 %collective-permute-start.23 = (f32[24,1,256]{2,1,0:T(1,128)}, f32[24,1,256]{2,1,0:T(1,128)S(1)}, u32[]{:S(2)}, u32[]{:S(2)}) collective-permute-start(f32[24,1,256]{2,1,0:T(1,128)} %copy-done.10), channel_id=1, source_target_pairs={{1,0},{2,1},{3,2},{4,3},{5,4},{6,5},{7,6},{0,7},{9,8},{10,9},{11,1... | collective-permute-start | bytes 73736 | tf_op jit(solution)/shard_map/ppermute | solution.py:279
  141.9 0.7 copy-start.9

commit v7 on v6

--- a/solution.py
+++ b/solution.py
@@ -187,11 +187,14 @@
 
 
 def network_kernel(listed, flowed, owned_by, w1, w2, w3, b2, b3, b4, w4, out, sent, xf, xl, yf, yl, zf, zl, heat):
-    def copy(f, carry):
-        rows = pl.ds(pl.multiple_of(256 * f, 256), 256)
+    def copy(part, carry):
+        rows = pl.ds(pl.multiple_of(part * 1536, 1536), 1536)
         out[rows, :] = flowed[rows, :]
         return carry
 
+    def block(i):
+        return jnp.where(listed[0, i] < 0, listed[0, 0], listed[0, i])
+
     def product(weights, cells):
         return jnp.dot(weights[...], cells, preferred_element_type=F32)
 
@@ -203,7 +206,7 @@
 
     def react(step, carry):
         first = step * TOGETHER
-        rows = [pl.ds(listed[1 + first + j], 24, stride=256) for j in range(TOGETHER)]
+        rows = [pl.ds(block(first + j), 24, stride=256) for j in range(TOGETHER)]
         before = [flowed[r, :] for r in rows]
         ones = jnp.ones((8, TOGETHER * 128), F32)
         cells = jnp.concatenate([jnp.concatenate(before, axis=1), ones], axis=0).astype(BF16)
@@ -217,21 +220,24 @@
             heat[pl.ds(first + j, 1), :] = increment[0:1] * increment[0:1]
         return carry
 
-    def faces(f, carry):
-        base = pl.multiple_of(256 * f, 256)
-        xf[f] = out[pl.ds(base, 32), :].astype(BF16)
-        xl[f] = out[pl.ds(base + 224, 32), :].astype(BF16)
-        yf[f] = out[pl.ds(base, 8, stride=32), :]
-        yl[f] = out[pl.ds(base + 31, 8, stride=32), :]
-        ends = z_ends(out[pl.ds(base, 256), :])
-        zf[f] = ends[0:1]
-        zl[f] = ends[1:2]
+    def faces(part, carry):
+        ends = z_ends(out[pl.ds(pl.multiple_of(part * 1536, 1536), 1536), :])
+        for j in range(6):
+            f = 6 * part + j
+            base = pl.multiple_of(256 * f, 256)
+            xf[f] = out[pl.ds(base, 32), :].astype(BF16)
+            xl[f] = out[pl.ds(base + 224, 32), :].astype(BF16)
+            yf[f] = out[pl.ds(base, 8, stride=32), :]
+            yl[f] = out[pl.ds(base + 31, 8, stride=32), :]
+            zf[f] = ends[0:1, 256 * j : 256 * j + 256]
+            zl[f] = ends[1:2, 256 * j : 256 * j + 256]
         return carry
 
     heat[...] = jnp.zeros_like(heat)
-    lax.fori_loop(0, 24, copy, 0)
-    lax.fori_loop(0, (listed[0] + TOGETHER - 1) // TOGETHER, react, 0)
-    lax.fori_loop(0, 24, faces, 0)
+    lax.fori_loop(0, 4, copy, 0)
+    count = lax.fori_loop(0, LISTED, lambda i, n: n + jnp.where(listed[0, i] < 0, 0, 1), 0)
+    lax.fori_loop(0, (count + TOGETHER - 1) // TOGETHER, react, 0)
+    lax.fori_loop(0, 4, faces, 0)
     sent[...] = jnp.dot(
         owned_by[...], heat[...], preferred_element_type=F32, precision=lax.Precision.HIGHEST
     )
@@ -312,9 +318,7 @@
     owner_table,
 ):
     brick = sds(fields.shape, F32)
-    ids, owners = react_list[0], owner_table[0]
-    count = jnp.sum((ids >= 0).astype(jnp.int32))
-    listed = jnp.concatenate([count[None], jnp.where(ids >= 0, ids, ids[0])])
+    owners = owner_table[0]
     owned_by = (owners[None, :] == jnp.arange(128, dtype=jnp.int32)[:, None]).astype(F32)
 
     faces = pl.pallas_call(
@@ -379,7 +383,7 @@
         out_shape=[sds((24 * 256, 128), F32), sds((128, 128), F32), *face_shapes(24)],
         scratch_shapes=[pltpu.VMEM((LISTED, 128), F32)],
         compiler_params=params(NETWORK_MIB),
-    )(listed, flowed.reshape(24 * 256, 128), owned_by, *columns, weight_out.T)
+    )(react_list, flowed.reshape(24 * 256, 128), owned_by, *columns, weight_out.T)
     reacted = reacted.reshape(fields.shape)
     around = exchange(faces)
     heats = swap(sent.reshape(128, 1, 128)).reshape(128, 128)

time: 147 us -> 146 us (level)
  Pallas kernels: 84.3 us -> 36.4 us
  starting transfers between devices: 45.5 us -> 92.4 us
    pallas_call x1, Pallas kernels: 66.8 us -> 18.6 us  [local(): pl.pallas_call(network_kernel, in_specs=[pl.BlockSpec(memory_space=pltpu....]
    ppermute x12, starting transfers between devices: 12.2 us -> 56.8 us  [exchange(): got.append(lax.ppermute(last, axis, [(i, (i + 1) % n) for i in range(n)]))]
    all_to_all x1, starting transfers between devices: 7.01 us -> 10.8 us  [swap(): return lax.all_to_all(tiles, ALL, split_axis=0, concat_axis=0, tiled=True)]
  transfers between devices with their start and end apart: 25 -> 25, of which waited for: 6 -> 8; matrix products, arithmetic and copies ran while one was open for 1% -> 0% of each run, Pallas kernels for 1% -> 1%
where the time goes in v7:
time: 146 us; the launch traced here: 145 us
  starting transfers between devices  92.4 us (63%)
  Pallas kernels  36.4 us (25%)
  waiting for transfers between devices  10.6 us (7%)
  local copies, waits for them, and re-layouts  4.83 us (3%)
    ppermute x12, starting transfers between devices, exchange(): got.append(lax.ppermute(last, axis, [(i, (i + 1) % n) for i in range(n)]))  56.8 us
    ppermute x12, starting transfers between devices, exchange(): got.append(lax.ppermute(first, axis, [((i + 1) % n, i) for i in range(n)]))  24.9 us
    pallas_call x1, Pallas kernels, local(): pl.pallas_call(network_kernel, in_specs=[pl.BlockSpec(memory_space=pltpu....  18.6 us
    pallas_call x3, Pallas kernels, section(): pl.pallas_call(functools.partial(section_kernel, kind), grid=(24 // GROUP...  11 us
    all_to_all x1, starting transfers between devices, swap(): return lax.all_to_all(tiles, ALL, split_axis=0, concat_axis=0, tiled=True)  10.8 us
    unnamed x30, local copies, waits for them, and re-layouts  4.82 us
    pallas_call x1, Pallas kernels, local(): pl.pallas_call(diffuse_kernel, grid=(24 // GROUP,), in_specs=[pl.BlockSpe...  4.68 us
    ppermute x12, waiting for transfers between devices, exchange(): got.append(lax.ppermute(last, axis, [(i, (i + 1) % n) for i in range(n)]))  4.34 us
  transfers between devices with their start and end apart: 25, of which 8 were waited for; matrix products, arithmetic and copies ran while one was open for 0% of the time, Pallas kernels for 1%

profile of v7, /device:TPU:1, one launch (start us, length us, event | category | flops | bytes accessed | tf_op | source)
XLA Modules:
  0.0 145.1 jit_solution(204705365096359183)
XLA Ops:
  0.6 1.9 %copy-done = f32[24,8,32,128]{3,2,1,0:T(8,128)S(1)} copy-done((f32[24,8,32,128]{3,2,1,0:T(8,128)S(1)}, f32[24,8,32,128]{3,2,1,0:T(8,128)}, u32[]{:S(2)}) %copy-start) | copy-done | bytes 3145752
  2.5 1.0 copy-done.2
  3.5 0.5 shard_map.140
  4.1 0.0 copy-start.13
  4.1 0.0 copy-start.12
  4.1 2.1 %collective-permute-start = (bf16[25,32,128]{2,1,0:T(8,128)(2,1)S(1)}, bf16[25,32,128]{2,1,0:T(8,128)(2,1)S(1)}, u32[]{:S(2)}, u32[]{:S(2)}) collective-permute-start(bf16[25,32,128]{2,1,0:T(8,128)(2,1)S(1)} %get-tuple-element.47), channel_id=1, source_target_pairs={{0,32},{32,64},{64,96},{96,0},{1,33},{33,65},{65,97},{97,1},{2,34}... | collective-permute-start | bytes 614408 | tf_op jit(solution)/shard_map/ppermute | solution.py:284
  6.2 1.3 collective-permute-start.1
  7.6 1.8 %collective-permute-start.2 = (f32[25,8,128]{2,1,0:T(8,128)S(1)}, f32[25,8,128]{2,1,0:T(8,128)S(1)}, u32[]{:S(2)}, u32[]{:S(2)}) collective-permute-start(f32[25,8,128]{2,1,0:T(8,128)S(1)} %get-tuple-element.49), channel_id=1, source_target_pairs={{0,8},{8,16},{16,24},{24,0},{1,9},{9,17},{17,25},{25,1},{2,10},{10... | collective-permute-start | bytes 307208 | tf_op jit(solution)/shard_map/ppermute | solution.py:284
  9.3 2.1 %collective-permute-start.3 = (f32[25,8,128]{2,1,0:T(8,128)S(1)}, f32[25,8,128]{2,1,0:T(8,128)S(1)}, u32[]{:S(2)}, u32[]{:S(2)}) collective-permute-start(f32[25,8,128]{2,1,0:T(8,128)S(1)} %get-tuple-element.50), channel_id=1, source_target_pairs={{8,0},{16,8},{24,16},{0,24},{9,1},{17,9},{25,17},{1,25},{10,2},{18... | collective-permute-start | bytes 307208 | tf_op jit(solution)/shard_map/ppermute | solution.py:285
  11.4 2.7 %collective-permute-start.4 = (f32[25,1,256]{2,1,0:T(1,128)S(1)}, f32[25,1,256]{2,1,0:T(1,128)S(1)}, u32[]{:S(2)}, u32[]{:S(2)}) collective-permute-start(f32[25,1,256]{2,1,0:T(1,128)S(1)} %get-tuple-element.51), channel_id=1, source_target_pairs={{0,1},{1,2},{2,3},{3,4},{4,5},{5,6},{6,7},{7,0},{8,9},{9,10},{10,1... | collective-permute-start | bytes 76808 | tf_op jit(solution)/shard_map/ppermute | solution.py:284
  14.1 1.0 collective-permute-done.4.refs_5_.refs_12_
  15.1 2.3 %collective-permute-start.5 = (f32[25,1,256]{2,1,0:T(1,128)S(1)}, f32[25,1,256]{2,1,0:T(1,128)S(1)}, u32[]{:S(2)}, u32[]{:S(2)}) collective-permute-start(f32[25,1,256]{2,1,0:T(1,128)S(1)} %get-tuple-element.52), channel_id=1, source_target_pairs={{1,0},{2,1},{3,2},{4,3},{5,4},{6,5},{7,6},{0,7},{9,8},{10,9},{11,1... | collective-permute-start | bytes 76808 | tf_op jit(solution)/shard_map/ppermute | solution.py:285
  17.4 1.5 %collective-permute-done.5.refs_6_.refs_13_ = f32[25,1,256]{2,1,0:T(1,128)S(1)} collective-permute-done((f32[25,1,256]{2,1,0:T(1,128)S(1)}, f32[25,1,256]{2,1,0:T(1,128)S(1)}, u32[]{:S(2)}, u32[]{:S(2)}) %collective-permute-start.5) | collective-permute-done | bytes 25632 | tf_op jit(solution)/shard_map/ppermute | solution.py:285
  18.9 0.0 collective-permute-done.2.refs_3_.refs_10_
  18.9 0.0 collective-permute-done.3.refs_4_.refs_11_
  18.9 0.0 collective-permute-done.refs_1_.refs_8_
  18.9 0.0 collective-permute-done.1.refs_2_.refs_9_
  18.9 3.6 %shard_map.141 = (f32[24,8,32,128]{3,2,1,0:T(8,128)S(1)}, f32[6,8,32,128]{3,2,1,0:T(8,128)S(1)}, bf16[24,32,128]{2,1,0:T(8,128)(2,1)S(1)}, bf16[24,32,128]{2,1,0...) custom-call(f32[24,8,32,128]{3,2,1,0:T(8,128)S(1)} %copy-done, ...), custom_call_target="tpu_custom_call" | custom-call | tf_op jit(solution)/shard_map/pallas_call | solution.py:290
  22.6 0.0 collective-permute-start.6
  22.6 2.6 %collective-permute-start.7 = (bf16[24,32,128]{2,1,0:T(8,128)(2,1)S(1)}, bf16[24,32,128]{2,1,0:T(8,128)(2,1)S(1)}, u32[]{:S(2)}, u32[]{:S(2)}) collective-permute-start(bf16[24,32,128]{2,1,0:T(8,128)(2,1)S(1)} %get-tuple-element.56), channel_id=1, source_target_pairs={{32,0},{64,32},{96,64},{0,96},{33,1},{65,33},{97,65},{1,97},{34,2}... | collective-permute-start | bytes 589832 | tf_op jit(solution)/shard_map/ppermute | solution.py:285
  25.3 0.0 collective-permute-start.8
  25.3 2.7 %collective-permute-start.9 = (f32[24,8,128]{2,1,0:T(8,128)S(1)}, f32[24,8,128]{2,1,0:T(8,128)S(1)}, u32[]{:S(2)}, u32[]{:S(2)}) collective-permute-start(f32[24,8,128]{2,1,0:T(8,128)S(1)} %get-tuple-element.58), channel_id=1, source_target_pairs={{8,0},{16,8},{24,16},{0,24},{9,1},{17,9},{25,17},{1,25},{10,2},{18... | collective-permute-start | bytes 294920 | tf_op jit(solution)/shard_map/ppermute | solution.py:285
  27.9 1.2 collective-permute-start.10
  29.1 0.9 collective-permute-done.10.refs_6_
  30.0 3.5 %collective-permute-start.11 = (f32[24,1,256]{2,1,0:T(1,128)S(1)}, f32[24,1,256]{2,1,0:T(1,128)S(1)}, u32[]{:S(2)}, u32[]{:S(2)}) collective-permute-start(f32[24,1,256]{2,1,0:T(1,128)S(1)} %get-tuple-element.60), channel_id=1, source_target_pairs={{1,0},{2,1},{3,2},{4,3},{5,4},{6,5},{7,6},{0,7},{9,8},{10,9},{11,1... | collective-permute-start | bytes 73736 | tf_op jit(solution)/shard_map/ppermute | solution.py:285
  33.6 0.8 collective-permute-done.11.refs_7_
  34.4 0.0 collective-permute-done.8.refs_4_
  34.4 0.0 collective-permute-done.9.refs_5_
  34.4 0.0 collective-permute-done.6.refs_2_
  34.4 0.0 collective-permute-done.7.refs_3_
  34.4 0.0 copy-start.14
  34.5 0.0 copy-start.1
  34.5 0.0 copy-start.3
  34.5 0.0 copy-start.4
  34.5 0.0 copy-start.7
  34.5 0.0 copy-start.8
  34.5 3.9 %shard_map.142 = (f32[24,8,32,128]{3,2,1,0:T(8,128)S(1)}, bf16[24,32,128]{2,1,0:T(8,128)(2,1)S(1)}, bf16[24,32,128]{2,1,0:T(8,128)(2,1)S(1)}, f32[24,8,128]{2,1,...) custom-call(f32[24,8,32,128]{3,2,1,0:T(8,128)S(1)} %get-tuple-element.54.refs_0_, ...), custom_call_target="tpu_custom_call" | custom-call | tf_op jit(solution)/shard_map/pallas_call | solution.py:290
  38.4 0.0 collective-permute-start.16
  38.4 0.7 collective-permute-start.17
  39.1 0.0 collective-permute-start.14
  39.1 2.7 %collective-permute-start.15 = (f32[24,8,128]{2,1,0:T(8,128)S(1)}, f32[24,8,128]{2,1,0:T(8,128)S(1)}, u32[]{:S(2)}, u32[]{:S(2)}) collective-permute-start(f32[24,8,128]{2,1,0:T(8,128)S(1)} %get-tuple-element.66), channel_id=1, source_target_pairs={{8,0},{16,8},{24,16},{0,24},{9,1},{17,9},{25,17},{1,25},{10,2},{18... | collective-permute-start | bytes 294920 | tf_op jit(solution)/shard_map/ppermute | solution.py:285
  41.8 2.7 %collective-permute-start.13 = (bf16[24,32,128]{2,1,0:T(8,128)(2,1)S(1)}, bf16[24,32,128]{2,1,0:T(8,128)(2,1)S(1)}, u32[]{:S(2)}, u32[]{:S(2)}) collective-permute-start(bf16[24,32,128]{2,1,0:T(8,128)(2,1)S(1)} %get-tuple-element.64), channel_id=1, source_target_pairs={{32,0},{64,32},{96,64},{0,96},{33,1},{65,33},{97,65},{1,97},{34,2}... | collective-permute-start | bytes 589832 | tf_op jit(solution)/shard_map/ppermute | solution.py:285
  44.5 1.5 %shard_map.144 = (bf16[1600,32]{1,0:T(8,128)(2,1)S(1)}, bf16[800,1600]{1,0:T(8,128)(2,1)S(1)}, bf16[400,800]{1,0:T(8,128)(2,1)S(1)}, f32[800,128]{1,0:T(8,128)S(...) custom-call(bf16[24,1600]{1,0:T(8,128)(2,1)S(1)} %copy-done.4, f32[1,1600]{1,0:T(1,128)S(1)} %reshape.31.b_in, ...), custom_call_target="tpu_custom_call" | custom-call | bytes 8388608 | tf_op jit(solution)/shard_map/pallas_call | solution.py:353
  46.0 0.0 collective-permute-done.15.refs_5_
  46.1 1.5 %collective-permute-done.12.refs_2_ = bf16[24,32,128]{2,1,0:T(8,128)(2,1)S(1)} collective-permute-done((bf16[24,32,128]{2,1,0:T(8,128)(2,1)S(1)}, bf16[24,32,128]{2,1,0:T(8,128)(2,1)S(1)}, u32[]{:S(2)}, u32[]{:S(2)}) %collective-permute-start.12) | collective-permute-done | bytes 196640 | tf_op jit(solution)/shard_map/ppermute | solution.py:284
  47.5 3.5 %shard_map.143 = f32[24,8,32,128]{3,2,1,0:T(8,128)S(1)} custom-call(f32[24,8,32,128]{3,2,1,0:T(8,128)S(1)} %get-tuple-element.62.refs_0_, f32[24,8,32,128]{3,2,1,0:T(8,128)S(1)} %copy-done, bf16[24,32,128]{2,1,0:T(8,128)(2,1)S(1)} %collective-permute-done.12.refs_2_, bf16[24,32,128]{2,1,0:T(8,128)(2,1)S(1)} %collective-permute-done.13.refs_3_, ...), custom_call_target="tpu_custom_call" | custom-call | tf_op jit(solution)/shard_map/pallas_call | solution.py:290
  51.1 18.6 %shard_map.145 = (f32[6144,128]{1,0:T(8,128)S(1)}, f32[128,128]{1,0:T(8,128)S(1)}, bf16[24,32,128]{2,1,0:T(8,128)(2,1)}, bf16[24,32,128]{2,1,0:T(8,128)(2,1)}, f...) custom-call(s32[1,96]{1,0:T(1,128)S(1)} %copy-done.9, ...), custom_call_target="tpu_custom_call" | custom-call | tf_op jit(solution)/shard_map/pallas_call | solution.py:379
  69.7 0.6 copy-done.5
  70.3 0.6 copy-done.11
  70.9 44.7 %collective-permute-start.18 = (bf16[24,32,128]{2,1,0:T(8,128)(2,1)}, bf16[24,32,128]{2,1,0:T(8,128)(2,1)S(1)}, u32[]{:S(2)}, u32[]{:S(2)}) collective-permute-start(bf16[24,32,128]{2,1,0:T(8,128)(2,1)} %get-tuple-element.83), channel_id=1, source_target_pairs={{0,32},{32,64},{64,96},{96,0},{1,33},{33,65},{65,97},{97,1},{2,34}... | collective-permute-start | bytes 589832 | tf_op jit(solution)/shard_map/ppermute | solution.py:284
  115.6 0.0 collective-permute-start.19
  115.6 2.7 %collective-permute-start.20 = (f32[24,8,128]{2,1,0:T(8,128)}, f32[24,8,128]{2,1,0:T(8,128)S(1)}, u32[]{:S(2)}, u32[]{:S(2)}) collective-permute-start(f32[24,8,128]{2,1,0:T(8,128)} %get-tuple-element.85), channel_id=1, source_target_pairs={{0,8},{8,16},{16,24},{24,0},{1,9},{9,17},{17,25},{25,1},{2,10},{10... | collective-permute-start | bytes 294920 | tf_op jit(solution)/shard_map/ppermute | solution.py:284
  118.3 1.2 collective-permute-start.21
  119.5 10.8 %all-to-all-start = ((f32[128,1,128]{2,1,0:T(1,128)}), f32[128,1,128]{2,1,0:T(1,128)S(1)}, u32[]{:S(2)}, u32[]{:S(2)}) async-start(f32[128,1,128]{2,1,0:T(1,128)} %bitcast.18), calls=%async_computation | async-start | bytes 131072 | tf_op jit(solution)/shard_map/all_to_all | solution.py:302
  130.3 1.6 %collective-permute-start.22 = (f32[24,1,256]{2,1,0:T(1,128)S(1)}, f32[24,1,256]{2,1,0:T(1,128)S(1)}, u32[]{:S(2)}, u32[]{:S(2)}) collective-permute-start(f32[24,1,256]{2,1,0:T(1,128)S(1)} %get-tuple-element.87), channel_id=1, source_target_pairs={{0,1},{1,2},{2,3},{3,4},{4,5},{5,6},{6,7},{7,0},{8,9},{9,10},{10,1... | collective-permute-start | bytes 73736 | tf_op jit(solution)/shard_map/ppermute | solution.py:284
  131.9 0.9 collective-permute-done.22.zlo
  132.8 3.0 %collective-permute-start.23 = (f32[24,1,256]{2,1,0:T(1,128)}, f32[24,1,256]{2,1,0:T(1,128)S(1)}, u32[]{:S(2)}, u32[]{:S(2)}) collective-permute-start(f32[24,1,256]{2,1,0:T(1,128)} %copy-done.11), channel_id=1, source_target_pairs={{1,0},{2,1},{3,2},{4,3},{5,4},{6,5},{7,6},{0,7},{9,8},{10,9},{11,1... | collective-permute-start | bytes 73736 | tf_op jit(solution)/shard_map/ppermute | solution.py:285
  135.9 1.4 collective-permute-done.23.zhi
  137.2 2.5 %all-to-all-done = f32[128,1,128]{2,1,0:T(1,128)S(1)} async-done(((f32[128,1,128]{2,1,0:T(1,128)}), f32[128,1,128]{2,1,0:T(1,128)S(1)}, u32[]{:S(2)}, u32[]{:S(2)}) %all-to-all-start) | async-done | bytes 65568 | tf_op jit(solution)/shard_map/all_to_all | solution.py:302
  139.8 0.0 collective-permute-done.20.ylo
  139.8 0.0 collective-permute-done.21.yhi
  139.8 0.0 copy-start.10
  139.8 0.6 copy-done.10
  140.4 4.7 %shard_map.146 = (f32[24,8,32,128]{3,2,1,0:T(8,128)}, f32[1,1]{1,0:T(1,128)}) custom-call(f32[24]{0:T(128)S(1)} %copy-done.10, f32[24,8,32,128]{3,2,1,0:T(8,128)S(1)} %bitcast.14, bf16[24,32,128]{2,1,0:T(8,128)(2,1)S(1)} %collective-permute-done.18.xlo, bf16[24,32,128]{2,1,0:T(8,128)(2,1)} %collective-permute-done.19.xhi, ...), custom_call_target="tpu_custom_call" | custom-call | flops 1000000000 | bytes 25165824 | tf_op jit(solution)/shard_map/pallas_call | solution.py:390
  (26 shorter events, 0.1 us)
Async XLA Ops:
  0.6 1.9 %copy-start = (f32[24,8,32,128]{3,2,1,0:T(8,128)S(1)}, f32[24,8,32,128]{3,2,1,0:T(8,128)}, u32[]{:S(2)}) copy-start(f32[24,8,32,128]{3,2,1,0:T(8,128)} %refs_1_.3) | copy-start | bytes 9437188
  2.5 1.0 copy-start.2
  4.1 29.5 %copy-start.13 = (f32[800]{0:T(1024)S(1)}, f32[800]{0:T(1024)}, u32[]{:S(2)}) copy-start(f32[800]{0:T(1024)} %param.19) | copy-start | bytes 9604
  4.1 29.5 %copy-start.12 = (f32[1600]{0:T(1024)S(1)}, f32[1600]{0:T(1024)}, u32[]{:S(2)}) copy-start(f32[1600]{0:T(1024)} %param.17) | copy-start | bytes 19204
  4.1 14.8 %collective-permute-start = (bf16[25,32,128]{2,1,0:T(8,128)(2,1)S(1)}, bf16[25,32,128]{2,1,0:T(8,128)(2,1)S(1)}, u32[]{:S(2)}, u32[]{:S(2)}) collective-permute-start(bf16[25,32,128]{2,1,0:T(8,128)(2,1)S(1)} %get-tuple-element.47), channel_id=1, source_target_pairs={{0,32},{32,64},{64,96},{96,0},{1,33},{33,65},{65,97},{97,1},{2,34}... | collective-permute-start | bytes 614408 | tf_op jit(solution)/shard_map/ppermute | solution.py:284
  6.2 12.7 %collective-permute-start.1 = (bf16[25,32,128]{2,1,0:T(8,128)(2,1)S(1)}, bf16[25,32,128]{2,1,0:T(8,128)(2,1)S(1)}, u32[]{:S(2)}, u32[]{:S(2)}) collective-permute-start(bf16[25,32,128]{2,1,0:T(8,128)(2,1)S(1)} %get-tuple-element.48), channel_id=1, source_target_pairs={{32,0},{64,32},{96,64},{0,96},{33,1},{65,33},{97,65},{1,97},{34,2}... | collective-permute-start | bytes 614408 | tf_op jit(solution)/shard_map/ppermute | solution.py:285
  7.6 11.4 %collective-permute-start.2 = (f32[25,8,128]{2,1,0:T(8,128)S(1)}, f32[25,8,128]{2,1,0:T(8,128)S(1)}, u32[]{:S(2)}, u32[]{:S(2)}) collective-permute-start(f32[25,8,128]{2,1,0:T(8,128)S(1)} %get-tuple-element.49), channel_id=1, source_target_pairs={{0,8},{8,16},{16,24},{24,0},{1,9},{9,17},{17,25},{25,1},{2,10},{10... | collective-permute-start | bytes 307208 | tf_op jit(solution)/shard_map/ppermute | solution.py:284
  9.3 9.6 %collective-permute-start.3 = (f32[25,8,128]{2,1,0:T(8,128)S(1)}, f32[25,8,128]{2,1,0:T(8,128)S(1)}, u32[]{:S(2)}, u32[]{:S(2)}) collective-permute-start(f32[25,8,128]{2,1,0:T(8,128)S(1)} %get-tuple-element.50), channel_id=1, source_target_pairs={{8,0},{16,8},{24,16},{0,24},{9,1},{17,9},{25,17},{1,25},{10,2},{18... | collective-permute-start | bytes 307208 | tf_op jit(solution)/shard_map/ppermute | solution.py:285
  11.4 3.7 %collective-permute-start.4 = (f32[25,1,256]{2,1,0:T(1,128)S(1)}, f32[25,1,256]{2,1,0:T(1,128)S(1)}, u32[]{:S(2)}, u32[]{:S(2)}) collective-permute-start(f32[25,1,256]{2,1,0:T(1,128)S(1)} %get-tuple-element.51), channel_id=1, source_target_pairs={{0,1},{1,2},{2,3},{3,4},{4,5},{5,6},{6,7},{7,0},{8,9},{9,10},{10,1... | collective-permute-start | bytes 76808 | tf_op jit(solution)/shard_map/ppermute | solution.py:284
  15.1 3.8 %collective-permute-start.5 = (f32[25,1,256]{2,1,0:T(1,128)S(1)}, f32[25,1,256]{2,1,0:T(1,128)S(1)}, u32[]{:S(2)}, u32[]{:S(2)}) collective-permute-start(f32[25,1,256]{2,1,0:T(1,128)S(1)} %get-tuple-element.52), channel_id=1, source_target_pairs={{1,0},{2,1},{3,2},{4,3},{5,4},{6,5},{7,6},{0,7},{9,8},{10,9},{11,1... | collective-permute-start | bytes 76808 | tf_op jit(solution)/shard_map/ppermute | solution.py:285
  22.6 11.9 %collective-permute-start.6 = (bf16[24,32,128]{2,1,0:T(8,128)(2,1)S(1)}, bf16[24,32,128]{2,1,0:T(8,128)(2,1)S(1)}, u32[]{:S(2)}, u32[]{:S(2)}) collective-permute-start(bf16[24,32,128]{2,1,0:T(8,128)(2,1)S(1)} %get-tuple-element.55), channel_id=1, source_target_pairs={{0,32},{32,64},{64,96},{96,0},{1,33},{33,65},{65,97},{97,1},{2,34}... | collective-permute-start | bytes 589832 | tf_op jit(solution)/shard_map/ppermute | solution.py:284
  22.6 11.8 %collective-permute-start.7 = (bf16[24,32,128]{2,1,0:T(8,128)(2,1)S(1)}, bf16[24,32,128]{2,1,0:T(8,128)(2,1)S(1)}, u32[]{:S(2)}, u32[]{:S(2)}) collective-permute-start(bf16[24,32,128]{2,1,0:T(8,128)(2,1)S(1)} %get-tuple-element.56), channel_id=1, source_target_pairs={{32,0},{64,32},{96,64},{0,96},{33,1},{65,33},{97,65},{1,97},{34,2}... | collective-permute-start | bytes 589832 | tf_op jit(solution)/shard_map/ppermute | solution.py:285
  25.3 9.2 %collective-permute-start.8 = (f32[24,8,128]{2,1,0:T(8,128)S(1)}, f32[24,8,128]{2,1,0:T(8,128)S(1)}, u32[]{:S(2)}, u32[]{:S(2)}) collective-permute-start(f32[24,8,128]{2,1,0:T(8,128)S(1)} %get-tuple-element.57), channel_id=1, source_target_pairs={{0,8},{8,16},{16,24},{24,0},{1,9},{9,17},{17,25},{25,1},{2,10},{10... | collective-permute-start | bytes 294920 | tf_op jit(solution)/shard_map/ppermute | solution.py:284
  25.3 9.2 %collective-permute-start.9 = (f32[24,8,128]{2,1,0:T(8,128)S(1)}, f32[24,8,128]{2,1,0:T(8,128)S(1)}, u32[]{:S(2)}, u32[]{:S(2)}) collective-permute-start(f32[24,8,128]{2,1,0:T(8,128)S(1)} %get-tuple-element.58), channel_id=1, source_target_pairs={{8,0},{16,8},{24,16},{0,24},{9,1},{17,9},{25,17},{1,25},{10,2},{18... | collective-permute-start | bytes 294920 | tf_op jit(solution)/shard_map/ppermute | solution.py:285
  27.9 2.1 %collective-permute-start.10 = (f32[24,1,256]{2,1,0:T(1,128)S(1)}, f32[24,1,256]{2,1,0:T(1,128)S(1)}, u32[]{:S(2)}, u32[]{:S(2)}) collective-permute-start(f32[24,1,256]{2,1,0:T(1,128)S(1)} %get-tuple-element.59), channel_id=1, source_target_pairs={{0,1},{1,2},{2,3},{3,4},{4,5},{5,6},{6,7},{7,0},{8,9},{9,10},{10,1... | collective-permute-start | bytes 73736 | tf_op jit(solution)/shard_map/ppermute | solution.py:284
  30.0 4.4 %collective-permute-start.11 = (f32[24,1,256]{2,1,0:T(1,128)S(1)}, f32[24,1,256]{2,1,0:T(1,128)S(1)}, u32[]{:S(2)}, u32[]{:S(2)}) collective-permute-start(f32[24,1,256]{2,1,0:T(1,128)S(1)} %get-tuple-element.60), channel_id=1, source_target_pairs={{1,0},{2,1},{3,2},{4,3},{5,4},{6,5},{7,6},{0,7},{9,8},{10,9},{11,1... | collective-permute-start | bytes 73736 | tf_op jit(solution)/shard_map/ppermute | solution.py:285
  34.4 10.0 %copy-start.14 = (s32[1,96]{1,0:T(1,128)S(1)}, s32[1,96]{1,0:T(1,128)}, u32[]{:S(2)}) copy-start(s32[1,96]{1,0:T(1,128)} %param.25) | copy-start | bytes 1156
  34.5 10.0 %copy-start.1 = (bf16[1600,800]{0,1:T(8,128)(2,1)S(1)}, bf16[1600,800]{0,1:T(8,128)(2,1)}, u32[]{:S(2)}) copy-start(bf16[1600,800]{0,1:T(8,128)(2,1)} %param.18) | copy-start | bytes 7680004
  34.5 10.0 %copy-start.3 = (bf16[800,400]{0,1:T(8,128)(2,1)S(1)}, bf16[800,400]{0,1:T(8,128)(2,1)}, u32[]{:S(2)}) copy-start(bf16[800,400]{0,1:T(8,128)(2,1)} %param.20) | copy-start | bytes 1920004
  34.5 10.0 %copy-start.4 = (bf16[24,1600]{1,0:T(8,128)(2,1)S(1)}, bf16[24,1600]{1,0:T(8,128)(2,1)}, u32[]{:S(2)}) copy-start(bf16[24,1600]{1,0:T(8,128)(2,1)} %w_in) | copy-start | bytes 230404
  34.5 10.0 %copy-start.7 = (f32[400]{0:T(512)S(1)}, f32[400]{0:T(512)}, u32[]{:S(2)}) copy-start(f32[400]{0:T(512)} %param.21) | copy-start | bytes 4804
  34.5 10.0 %copy-start.8 = (f32[24]{0:T(128)S(1)}, f32[24]{0:T(128)}, u32[]{:S(2)}) copy-start(f32[24]{0:T(128)} %param.23) | copy-start | bytes 292
  38.4 3.4 %collective-permute-start.16 = (f32[24,1,256]{2,1,0:T(1,128)S(1)}, f32[24,1,256]{2,1,0:T(1,128)S(1)}, u32[]{:S(2)}, u32[]{:S(2)}) collective-permute-start(f32[24,1,256]{2,1,0:T(1,128)S(1)} %get-tuple-element.67), channel_id=1, source_target_pairs={{0,1},{1,2},{2,3},{3,4},{4,5},{5,6},{6,7},{7,0},{8,9},{9,10},{10,1... | collective-permute-start | bytes 73736 | tf_op jit(solution)/shard_map/ppermute | solution.py:284
  38.4 7.6 %collective-permute-start.17 = (f32[24,1,256]{2,1,0:T(1,128)S(1)}, f32[24,1,256]{2,1,0:T(1,128)S(1)}, u32[]{:S(2)}, u32[]{:S(2)}) collective-permute-start(f32[24,1,256]{2,1,0:T(1,128)S(1)} %get-tuple-element.68), channel_id=1, source_target_pairs={{1,0},{2,1},{3,2},{4,3},{5,4},{6,5},{7,6},{0,7},{9,8},{10,9},{11,1... | collective-permute-start | bytes 73736 | tf_op jit(solution)/shard_map/ppermute | solution.py:285
  39.1 6.9 %collective-permute-start.14 = (f32[24,8,128]{2,1,0:T(8,128)S(1)}, f32[24,8,128]{2,1,0:T(8,128)S(1)}, u32[]{:S(2)}, u32[]{:S(2)}) collective-permute-start(f32[24,8,128]{2,1,0:T(8,128)S(1)} %get-tuple-element.65), channel_id=1, source_target_pairs={{0,8},{8,16},{16,24},{24,0},{1,9},{9,17},{17,25},{25,1},{2,10},{10... | collective-permute-start | bytes 294920 | tf_op jit(solution)/shard_map/ppermute | solution.py:284
  39.1 6.9 %collective-permute-start.15 = (f32[24,8,128]{2,1,0:T(8,128)S(1)}, f32[24,8,128]{2,1,0:T(8,128)S(1)}, u32[]{:S(2)}, u32[]{:S(2)}) collective-permute-start(f32[24,8,128]{2,1,0:T(8,128)S(1)} %get-tuple-element.66), channel_id=1, source_target_pairs={{8,0},{16,8},{24,16},{0,24},{9,1},{17,9},{25,17},{1,25},{10,2},{18... | collective-permute-start | bytes 294920 | tf_op jit(solution)/shard_map/ppermute | solution.py:285
  41.8 5.7 %collective-permute-start.12 = (bf16[24,32,128]{2,1,0:T(8,128)(2,1)S(1)}, bf16[24,32,128]{2,1,0:T(8,128)(2,1)S(1)}, u32[]{:S(2)}, u32[]{:S(2)}) collective-permute-start(bf16[24,32,128]{2,1,0:T(8,128)(2,1)S(1)} %get-tuple-element.63), channel_id=1, source_target_pairs={{0,32},{32,64},{64,96},{96,0},{1,33},{33,65},{65,97},{97,1},{2,34}... | collective-permute-start | bytes 589832 | tf_op jit(solution)/shard_map/ppermute | solution.py:284
  41.8 5.7 %collective-permute-start.13 = (bf16[24,32,128]{2,1,0:T(8,128)(2,1)S(1)}, bf16[24,32,128]{2,1,0:T(8,128)(2,1)S(1)}, u32[]{:S(2)}, u32[]{:S(2)}) collective-permute-start(bf16[24,32,128]{2,1,0:T(8,128)(2,1)S(1)} %get-tuple-element.64), channel_id=1, source_target_pairs={{32,0},{64,32},{96,64},{0,96},{33,1},{65,33},{97,65},{1,97},{34,2}... | collective-permute-start | bytes 589832 | tf_op jit(solution)/shard_map/ppermute | solution.py:285
  47.5 3.5 %copy-start.6 = (bf16[400,24]{0,1:T(8,128)(2,1)S(1)}, bf16[400,24]{0,1:T(8,128)(2,1)}, u32[]{:S(2)}) copy-start(bf16[400,24]{0,1:T(8,128)(2,1)} %param.22) | copy-start | bytes 57604
  47.5 3.5 %copy-start.9 = (s32[1,96]{1,0:T(1,128)S(1)}, s32[1,96]{1,0:T(1,128)}, u32[]{:S(2)}) copy-start(s32[1,96]{1,0:T(1,128)} %listed.1) | copy-start | bytes 1156
  69.7 0.6 copy-start.5
  70.3 0.6 copy-start.11
  70.9 68.8 %collective-permute-start.18 = (bf16[24,32,128]{2,1,0:T(8,128)(2,1)}, bf16[24,32,128]{2,1,0:T(8,128)(2,1)S(1)}, u32[]{:S(2)}, u32[]{:S(2)}) collective-permute-start(bf16[24,32,128]{2,1,0:T(8,128)(2,1)} %get-tuple-element.83), channel_id=1, source_target_pairs={{0,32},{32,64},{64,96},{96,0},{1,33},{33,65},{65,97},{97,1},{2,34}... | collective-permute-start | bytes 589832 | tf_op jit(solution)/shard_map/ppermute | solution.py:284
  115.6 24.2 %collective-permute-start.19 = (bf16[24,32,128]{2,1,0:T(8,128)(2,1)}, bf16[24,32,128]{2,1,0:T(8,128)(2,1)}, u32[]{:S(2)}, u32[]{:S(2)}) collective-permute-start(bf16[24,32,128]{2,1,0:T(8,128)(2,1)} %get-tuple-element.84), channel_id=1, source_target_pairs={{32,0},{64,32},{96,64},{0,96},{33,1},{65,33},{97,65},{1,97},{34,2}... | collective-permute-start | bytes 589832 | tf_op jit(solution)/shard_map/ppermute | solution.py:285
  115.6 24.2 %collective-permute-start.20 = (f32[24,8,128]{2,1,0:T(8,128)}, f32[24,8,128]{2,1,0:T(8,128)S(1)}, u32[]{:S(2)}, u32[]{:S(2)}) collective-permute-start(f32[24,8,128]{2,1,0:T(8,128)} %get-tuple-element.85), channel_id=1, source_target_pairs={{0,8},{8,16},{16,24},{24,0},{1,9},{9,17},{17,25},{25,1},{2,10},{10... | collective-permute-start | bytes 294920 | tf_op jit(solution)/shard_map/ppermute | solution.py:284
  118.3 21.5 %collective-permute-start.21 = (f32[24,8,128]{2,1,0:T(8,128)}, f32[24,8,128]{2,1,0:T(8,128)}, u32[]{:S(2)}, u32[]{:S(2)}) collective-permute-start(f32[24,8,128]{2,1,0:T(8,128)} %get-tuple-element.86), channel_id=1, source_target_pairs={{8,0},{16,8},{24,16},{0,24},{9,1},{17,9},{25,17},{1,25},{10,2},{18... | collective-permute-start | bytes 294920 | tf_op jit(solution)/shard_map/ppermute | solution.py:285
  119.5 20.3 %all-to-all-start = ((f32[128,1,128]{2,1,0:T(1,128)}), f32[128,1,128]{2,1,0:T(1,128)S(1)}, u32[]{:S(2)}, u32[]{:S(2)}) async-start(f32[128,1,128]{2,1,0:T(1,128)} %bitcast.18), calls=%async_computation | async-start | bytes 131072 | tf_op jit(solution)/shard_map/all_to_all | solution.py:302
  130.3 2.6 %collective-permute-start.22 = (f32[24,1,256]{2,1,0:T(1,128)S(1)}, f32[24,1,256]{2,1,0:T(1,128)S(1)}, u32[]{:S(2)}, u32[]{:S(2)}) collective-permute-start(f32[24,1,256]{2,1,0:T(1,128)S(1)} %get-tuple-element.87), channel_id=1, source_target_pairs={{0,1},{1,2},{2,3},{3,4},{4,5},{5,6},{6,7},{7,0},{8,9},{9,10},{10,1... | collective-permute-start | bytes 73736 | tf_op jit(solution)/shard_map/ppermute | solution.py:284
  132.8 4.4 %collective-permute-start.23 = (f32[24,1,256]{2,1,0:T(1,128)}, f32[24,1,256]{2,1,0:T(1,128)S(1)}, u32[]{:S(2)}, u32[]{:S(2)}) collective-permute-start(f32[24,1,256]{2,1,0:T(1,128)} %copy-done.11), channel_id=1, source_target_pairs={{1,0},{2,1},{3,2},{4,3},{5,4},{6,5},{7,6},{0,7},{9,8},{10,9},{11,1... | collective-permute-start | bytes 73736 | tf_op jit(solution)/shard_map/ppermute | solution.py:285
  139.8 0.7 copy-start.10

commit v8 on v7

--- a/solution.py
+++ b/solution.py
@@ -101,78 +101,86 @@
     zcol = refs.pop(0)
 
     if kind == 1:
-
-        @pl.when(pl.program_id(0) == 0)
-        def _():
-            zcol[0] = z_columns(vzlo[0], vzhi[0])
+        zcol[0] = z_columns(vzlo[24], vzhi[24])
+        for x in range(8):
+            before = vxlo[24].astype(F32) if x == 0 else velocity[0, x - 1]
+            after = vxhi[24].astype(F32) if x == 7 else velocity[0, x + 1]
+            y_next, y_prev, _, _ = shifted(
+                velocity[1, x], vylo[24, x : x + 1], vyhi[24, x : x + 1], velocity[1, x]
+            )
+            _, _, z_next, z_prev = shifted(
+                velocity[2, x], vylo[24, x : x + 1], vyhi[24, x : x + 1], zcol[0, 32 * x : 32 * x + 32]
+            )
+            coef[0, x] = 0.05 - 0.5 * after
+            coef[1, x] = 0.05 + 0.5 * before
+            coef[2, x] = 0.05 - 0.5 * y_next
+            coef[3, x] = 0.05 + 0.5 * y_prev
+            coef[4, x] = 0.05 - 0.5 * z_next
+            coef[5, x] = 0.05 + 0.5 * z_prev
+
+    def part(p, carry):
+        fs = [p * GROUP + i for i in range(GROUP)]
+        for i, f in enumerate(fs):
+            zcol[i] = z_columns(zlo[f], zhi[f])
+        for x in range(8):
+            ce = [coef[i, x] for i in range(6)]
+            for i, f in enumerate(fs):
+                centre = q[f, x]
+                before = xlo[f].astype(F32) if x == 0 else q[f, x - 1]
+                after = xhi[f].astype(F32) if x == 7 else q[f, x + 1]
+                y_next, y_prev, z_next, z_prev = shifted(
+                    centre, ylo[f, x : x + 1], yhi[f, x : x + 1], zcol[i, 32 * x : 32 * x + 32]
+                )
+                moved = (
+                    0.7 * centre
+                    + (ce[0] * after + ce[1] * before)
+                    + (ce[2] * y_next + ce[3] * y_prev)
+                    + (ce[4] * z_next + ce[5] * z_prev)
+                )
+                if kind == 1:
+                    new = moved
+                elif kind == 2:
+                    new = 0.75 * start[f, x] + 0.25 * moved
+                else:
+                    new = (1.0 / 3.0) * start[f, x] + (2.0 / 3.0) * moved
+                out[f, x] = new
+                if kind < 3:
+                    put_faces(new, f, x, xf, xl, yf, yl)
+        if kind < 3:
+            for f in fs:
+                put_z_faces(out, f, zf, zl)
+        return carry
+
+    lax.fori_loop(0, 24 // GROUP, part, 0)
+
+
+def diffuse_kernel(rates, q, xlo, xhi, ylo, yhi, zlo, zhi, heats, out, activity, zcol):
+    activity[0, 0] = jnp.sum(heats[...]) * (1.0 / (8.0 * 128.0))
+
+    def part(p, carry):
+        for i in range(GROUP):
+            f = p * GROUP + i
+            zcol[i] = z_columns(zlo[f], zhi[f])
+        for i in range(GROUP):
+            f = p * GROUP + i
+            rate = rates[pl.ds(f, 1), :]
             for x in range(8):
-                before = vxlo[0].astype(F32) if x == 0 else velocity[0, x - 1]
-                after = vxhi[0].astype(F32) if x == 7 else velocity[0, x + 1]
-                y_next, y_prev, _, _ = shifted(
-                    velocity[1, x], vylo[0, x : x + 1], vyhi[0, x : x + 1], velocity[1, x]
+                centre = q[f, x]
+                before = xlo[f].astype(F32) if x == 0 else q[f, x - 1]
+                after = xhi[f].astype(F32) if x == 7 else q[f, x + 1]
+                y_next, y_prev, z_next, z_prev = shifted(
+                    centre, ylo[f, x : x + 1], yhi[f, x : x + 1], zcol[i, 32 * x : 32 * x + 32]
                 )
-                _, _, z_next, z_prev = shifted(
-                    velocity[2, x], vylo[0, x : x + 1], vyhi[0, x : x + 1], zcol[0, 32 * x : 32 * x + 32]
-                )
-                coef[0, x] = 0.05 - 0.5 * after
-                coef[1, x] = 0.05 + 0.5 * before
-                coef[2, x] = 0.05 - 0.5 * y_next
-                coef[3, x] = 0.05 + 0.5 * y_prev
-                coef[4, x] = 0.05 - 0.5 * z_next
-                coef[5, x] = 0.05 + 0.5 * z_prev
-
-    for f in range(GROUP):
-        zcol[f] = z_columns(zlo[f], zhi[f])
-    for x in range(8):
-        ce = [coef[i, x] for i in range(6)]
-        for f in range(GROUP):
-            centre = q[f, x]
-            before = xlo[f].astype(F32) if x == 0 else q[f, x - 1]
-            after = xhi[f].astype(F32) if x == 7 else q[f, x + 1]
-            y_next, y_prev, z_next, z_prev = shifted(
-                centre, ylo[f, x : x + 1], yhi[f, x : x + 1], zcol[f, 32 * x : 32 * x + 32]
-            )
-            moved = (
-                0.7 * centre
-                + (ce[0] * after + ce[1] * before)
-                + (ce[2] * y_next + ce[3] * y_prev)
-                + (ce[4] * z_next + ce[5] * z_prev)
-            )
-            if kind == 1:
-                new = moved
-            elif kind == 2:
-                new = 0.75 * start[f, x] + 0.25 * moved
-            else:
-                new = (1.0 / 3.0) * start[f, x] + (2.0 / 3.0) * moved
-            out[f, x] = new
-            if kind < 3:
-                put_faces(new, f, x, xf, xl, yf, yl)
-    if kind < 3:
-        for f in range(GROUP):
-            put_z_faces(out, f, zf, zl)
-
-
-def diffuse_kernel(rates, q, xlo, xhi, ylo, yhi, zlo, zhi, heats, out, activity, zcol):
-    @pl.when(pl.program_id(0) == 0)
-    def _():
-        activity[0, 0] = jnp.sum(heats[...]) * (1.0 / (8.0 * 128.0))
-
-    base = pl.program_id(0) * GROUP
-    for f in range(GROUP):
-        zcol[f] = z_columns(zlo[f], zhi[f])
-        rate = rates[base + f]
-        for x in range(8):
-            centre = q[f, x]
-            before = xlo[f].astype(F32) if x == 0 else q[f, x - 1]
-            after = xhi[f].astype(F32) if x == 7 else q[f, x + 1]
-            y_next, y_prev, z_next, z_prev = shifted(
-                centre, ylo[f, x : x + 1], yhi[f, x : x + 1], zcol[f, 32 * x : 32 * x + 32]
-            )
-            spread = (after + before) + (y_next + y_prev) + (z_next + z_prev) - 6.0 * centre
-            out[f, x] = centre + rate * spread
-
-
-def columns_kernel(w_in, b_in, w_mid, w_low, b_mid, b_low, b_out, w1, w2, w3, b2, b3, b4):
+                spread = (after + before) + (y_next + y_prev) + (z_next + z_prev) - 6.0 * centre
+                out[f, x] = centre + rate * spread
+        return carry
+
+    lax.fori_loop(0, 24 // GROUP, part, 0)
+
+
+def columns_kernel(
+    w_in, b_in, w_mid, w_low, b_mid, b_low, b_out, diffusivity, w1, w2, w3, b2, b3, b4, rates
+):
     bias = 0.5 * b_in[...]
     parts = []
     for _ in range(3):
@@ -182,7 +190,12 @@
     w1[...] = jnp.concatenate([0.5 * w_in[...].astype(F32), *parts, zeros], axis=0).T.astype(BF16)
     w2[...] = (0.5 * w_mid[...].astype(F32)).astype(BF16)
     w3[...] = (0.5 * w_low[...].astype(F32)).astype(BF16)
-    for row, out, factor in ((b_mid, b2, 0.5), (b_low, b3, 0.5), (b_out, b4, 1.0)):
+    for row, out, factor in (
+        (b_mid, b2, 0.5),
+        (b_low, b3, 0.5),
+        (b_out, b4, 1.0),
+        (diffusivity, rates, 1.0),
+    ):
         out[...] = jnp.broadcast_to(factor * row[...], (128, row.shape[1])).T
 
 
@@ -251,19 +264,7 @@
     return jax.ShapeDtypeStruct(shape, dtype)
 
 
-def whole(shape):
-    return pl.BlockSpec(shape, lambda *_: (0,) * len(shape))
-
-
-def at(shape, place):
-    return pl.BlockSpec(shape, lambda *_: place)
-
-
-BRICK = pl.BlockSpec((GROUP, 8, 32, 128), lambda g, *_: (g, 0, 0, 0))
-X_FACE = pl.BlockSpec((GROUP, 32, 128), lambda g, *_: (g, 0, 0))
-Y_FACE = pl.BlockSpec((GROUP, 8, 128), lambda g, *_: (g, 0, 0))
-Z_FACE = pl.BlockSpec((GROUP, 1, 256), lambda g, *_: (g, 0, 0))
-FACES = [X_FACE, X_FACE, Y_FACE, Y_FACE, Z_FACE, Z_FACE]
+IN_VMEM = pl.BlockSpec(memory_space=pltpu.VMEM)
 
 
 def face_shapes(count):
@@ -277,24 +278,23 @@
     ]
 
 
-def exchange(faces):
+def exchange(faces, axes=ALL):
     got = []
-    for axis, first, last in zip(ALL, faces[0::2], faces[1::2]):
+    for axis, first, last in zip(axes, faces[0::2], faces[1::2]):
         n = lax.axis_size(axis)
         got.append(lax.ppermute(last, axis, [(i, (i + 1) % n) for i in range(n)]))
         got.append(lax.ppermute(first, axis, [((i + 1) % n, i) for i in range(n)]))
     return got
 
 
-def section(kind, args, in_specs, out_shapes, out_specs):
+def section(kind, args, out_shapes):
     return pl.pallas_call(
         functools.partial(section_kernel, kind),
-        grid=(24 // GROUP,),
-        in_specs=in_specs,
-        out_specs=out_specs,
+        in_specs=[IN_VMEM] * len(args),
+        out_specs=[IN_VMEM] * len(out_shapes),
         out_shape=out_shapes,
         scratch_shapes=[pltpu.VMEM((GROUP, 256, 128), F32)],
-        compiler_params=params(32),
+        compiler_params=params(24),
     )(*args)
 
 
@@ -325,20 +325,8 @@
         prep_kernel, out_shape=face_shapes(25), compiler_params=params(32)
     )(fields, velocity)
     halo = exchange(faces)
-    own_halo = [
-        at((1, 32, 128), (24, 0, 0)),
-        at((1, 32, 128), (24, 0, 0)),
-        at((1, 8, 128), (24, 0, 0)),
-        at((1, 8, 128), (24, 0, 0)),
-        at((1, 1, 256), (24, 0, 0)),
-        at((1, 1, 256), (24, 0, 0)),
-    ]
     one, coef, *faces = section(
-        1,
-        (fields, *halo, velocity, *halo),
-        [BRICK, *FACES, whole((3, 8, 32, 128)), *own_halo],
-        [brick, sds((6, 8, 32, 128), F32), *face_shapes(24)],
-        [BRICK, whole((6, 8, 32, 128)), *FACES],
+        1, (fields, *halo, velocity, *halo), [brick, sds((6, 8, 32, 128), F32), *face_shapes(24)]
     )
     one, *given = lax.optimization_barrier(
         (
@@ -347,56 +335,44 @@
             bias_in.reshape(1, -1),
             weight_mid.T,
             weight_low.T,
-            *(b.reshape(1, -1) for b in (bias_mid, bias_low, bias_out)),
+            *(b.reshape(1, -1) for b in (bias_mid, bias_low, bias_out, diffusivity)),
         )
     )
-    columns = pl.pallas_call(
+    *columns, rates = pl.pallas_call(
         columns_kernel,
         out_shape=[
             sds((weight_in.shape[1], 32), BF16),
             sds(weight_mid.shape[::-1], BF16),
             sds(weight_low.shape[::-1], BF16),
-            *(sds((b.shape[0], 128), F32) for b in (bias_mid, bias_low, bias_out)),
+            *(sds((b.shape[0], 128), F32) for b in (bias_mid, bias_low, bias_out, diffusivity)),
         ],
         compiler_params=params(20),
         cost_estimate=pl.CostEstimate(flops=0, bytes_accessed=8 * 2**20, transcendentals=0),
     )(*given)
-    two, *faces = section(
-        2,
-        (one, fields, *exchange(faces), coef),
-        [BRICK, BRICK, *FACES, whole((6, 8, 32, 128))],
-        [brick, *face_shapes(24)],
-        [BRICK, *FACES],
-    )
-    (flowed,) = section(
-        3,
-        (two, fields, *exchange(faces), coef),
-        [BRICK, BRICK, *FACES, whole((6, 8, 32, 128))],
-        [brick],
-        [BRICK],
-    )
-    in_vmem = pl.BlockSpec(memory_space=pltpu.VMEM)
+    two, *faces = section(2, (one, fields, *exchange(faces), coef), [brick, *face_shapes(24)])
+    (flowed,) = section(3, (two, fields, *exchange(faces), coef), [brick])
     reacted, sent, *faces = pl.pallas_call(
         network_kernel,
-        in_specs=[pl.BlockSpec(memory_space=pltpu.SMEM)] + [in_vmem] * 9,
-        out_specs=[in_vmem] * 8,
+        in_specs=[pl.BlockSpec(memory_space=pltpu.SMEM)] + [IN_VMEM] * 9,
+        out_specs=[IN_VMEM] * 8,
         out_shape=[sds((24 * 256, 128), F32), sds((128, 128), F32), *face_shapes(24)],
         scratch_shapes=[pltpu.VMEM((LISTED, 128), F32)],
         compiler_params=params(NETWORK_MIB),
     )(react_list, flowed.reshape(24 * 256, 128), owned_by, *columns, weight_out.T)
     reacted = reacted.reshape(fields.shape)
-    around = exchange(faces)
+    x_and_y = exchange(faces[:4])
+    *z_faces, x_and_y[0], x_and_y[1] = lax.optimization_barrier((*faces[4:], *x_and_y[:2]))
+    around = x_and_y + exchange(z_faces, ALL[2:])
     heats = swap(sent.reshape(128, 1, 128)).reshape(128, 128)
     updated, activity = pl.pallas_call(
         diffuse_kernel,
-        grid=(24 // GROUP,),
-        in_specs=[pl.BlockSpec(memory_space=pltpu.SMEM), BRICK, *FACES, whole((128, 128))],
-        out_specs=[BRICK, pl.BlockSpec(memory_space=pltpu.SMEM)],
+        in_specs=[IN_VMEM] * 9,
+        out_specs=[IN_VMEM, pl.BlockSpec(memory_space=pltpu.SMEM)],
         out_shape=[brick, sds((1, 1), F32)],
         scratch_shapes=[pltpu.VMEM((GROUP, 256, 128), F32)],
-        compiler_params=params(32),
+        compiler_params=params(24),
         cost_estimate=pl.CostEstimate(flops=10**9, bytes_accessed=24 * 2**20, transcendentals=0),
-    )(diffusivity, reacted, *around, heats)
+    )(rates, reacted, *around, heats)
     return (updated, activity.reshape(1))
 
 

time: 146 us -> 146 us (level)
  Pallas kernels: 36.4 us -> 28.9 us
  starting transfers between devices: 92.4 us -> 97.5 us
  waiting for transfers between devices: 10.6 us -> 13.6 us
    pallas_call x1, Pallas kernels: 18.6 us -> 10.9 us  [local(): pl.pallas_call(network_kernel, in_specs=[pl.BlockSpec(memory_space=pltpu....]
    all_to_all x1, waiting for transfers between devices: 2.51 us -> 7.89 us  [swap(): return lax.all_to_all(tiles, ALL, split_axis=0, concat_axis=0, tiled=True)]
    ppermute x12, starting transfers between devices: 56.8 us -> 61 us  [exchange(): got.append(lax.ppermute(last, axis, [(i, (i + 1) % n) for i in range(n)]))]
    all_to_all x1, starting transfers between devices: 10.8 us -> 13 us  [swap(): return lax.all_to_all(tiles, ALL, split_axis=0, concat_axis=0, tiled=True)]
    ppermute x12, starting transfers between devices: 24.9 us -> 23.4 us  [exchange(): got.append(lax.ppermute(first, axis, [((i + 1) % n, i) for i in range(n)]))]
    unnamed x30 -> x38, local copies, waits for them, and re-layouts: 4.82 us -> 4.88 us
  transfers between devices with their start and end apart: 25 -> 25, of which waited for: 8 -> 6; matrix products, arithmetic and copies ran while one was open for 0% -> 0% of each run, Pallas kernels for 1% -> 1%
where the time goes in v8:
time: 146 us
  starting transfers between devices  97.5 us (67%)
  Pallas kernels  28.9 us (20%)
  waiting for transfers between devices  13.6 us (9%)
  local copies, waits for them, and re-layouts  4.89 us (3%)
    ppermute x12, starting transfers between devices, exchange(): got.append(lax.ppermute(last, axis, [(i, (i + 1) % n) for i in range(n)]))  61 us
    ppermute x12, starting transfers between devices, exchange(): got.append(lax.ppermute(first, axis, [((i + 1) % n, i) for i in range(n)]))  23.4 us
    all_to_all x1, starting transfers between devices, swap(): return lax.all_to_all(tiles, ALL, split_axis=0, concat_axis=0, tiled=True)  13 us
    pallas_call x3, Pallas kernels, section(): pl.pallas_call(functools.partial(section_kernel, kind), in_specs=[IN_VMEM...  10.9 us
    pallas_call x1, Pallas kernels, local(): pl.pallas_call(network_kernel, in_specs=[pl.BlockSpec(memory_space=pltpu....  10.9 us
    all_to_all x1, waiting for transfers between devices, swap(): return lax.all_to_all(tiles, ALL, split_axis=0, concat_axis=0, tiled=True)  7.89 us
    pallas_call x1, Pallas kernels, local(): pl.pallas_call(diffuse_kernel, in_specs=[IN_VMEM] * 9, out_specs=[IN_VMEM...  5.05 us
    unnamed x38, local copies, waits for them, and re-layouts  4.88 us
  transfers between devices with their start and end apart: 25, of which 6 were waited for; matrix products, arithmetic and copies ran while one was open for 0% of the time, Pallas kernels for 1%

profile of v8, /device:TPU:1, one launch (start us, length us, event | category | flops | bytes accessed | tf_op | source)
XLA Modules:
  0.0 146.0 jit_solution(8444783676700140485)
XLA Ops:
  0.6 1.9 %copy-done = f32[24,8,32,128]{3,2,1,0:T(8,128)S(1)} copy-done((f32[24,8,32,128]{3,2,1,0:T(8,128)S(1)}, f32[24,8,32,128]{3,2,1,0:T(8,128)}, u32[]{:S(2)}) %copy-start) | copy-done | bytes 3145752
  2.5 1.0 copy-done.3
  3.5 0.5 shard_map.140
  4.1 0.0 copy-start.17
  4.1 0.0 copy-start.16
  4.1 2.1 %collective-permute-start = (bf16[25,32,128]{2,1,0:T(8,128)(2,1)S(1)}, bf16[25,32,128]{2,1,0:T(8,128)(2,1)S(1)}, u32[]{:S(2)}, u32[]{:S(2)}) collective-permute-start(bf16[25,32,128]{2,1,0:T(8,128)(2,1)S(1)} %get-tuple-element.53), channel_id=1, source_target_pairs={{0,32},{32,64},{64,96},{96,0},{1,33},{33,65},{65,97},{97,1},{2,34}... | collective-permute-start | bytes 614408 | tf_op jit(solution)/shard_map/ppermute | solution.py:285
  6.2 1.3 collective-permute-start.1
  7.6 1.8 %collective-permute-start.2 = (f32[25,8,128]{2,1,0:T(8,128)S(1)}, f32[25,8,128]{2,1,0:T(8,128)S(1)}, u32[]{:S(2)}, u32[]{:S(2)}) collective-permute-start(f32[25,8,128]{2,1,0:T(8,128)S(1)} %get-tuple-element.55), channel_id=1, source_target_pairs={{0,8},{8,16},{16,24},{24,0},{1,9},{9,17},{17,25},{25,1},{2,10},{10... | collective-permute-start | bytes 307208 | tf_op jit(solution)/shard_map/ppermute | solution.py:285
  9.3 2.1 %collective-permute-start.3 = (f32[25,8,128]{2,1,0:T(8,128)S(1)}, f32[25,8,128]{2,1,0:T(8,128)S(1)}, u32[]{:S(2)}, u32[]{:S(2)}) collective-permute-start(f32[25,8,128]{2,1,0:T(8,128)S(1)} %get-tuple-element.56), channel_id=1, source_target_pairs={{8,0},{16,8},{24,16},{0,24},{9,1},{17,9},{25,17},{1,25},{10,2},{18... | collective-permute-start | bytes 307208 | tf_op jit(solution)/shard_map/ppermute | solution.py:286
  11.4 2.7 %collective-permute-start.4 = (f32[25,1,256]{2,1,0:T(1,128)S(1)}, f32[25,1,256]{2,1,0:T(1,128)S(1)}, u32[]{:S(2)}, u32[]{:S(2)}) collective-permute-start(f32[25,1,256]{2,1,0:T(1,128)S(1)} %get-tuple-element.57), channel_id=1, source_target_pairs={{0,1},{1,2},{2,3},{3,4},{4,5},{5,6},{6,7},{7,0},{8,9},{9,10},{10,1... | collective-permute-start | bytes 76808 | tf_op jit(solution)/shard_map/ppermute | solution.py:285
  14.1 1.0 collective-permute-done.4.refs_5_.refs_12_
  15.1 2.3 %collective-permute-start.5 = (f32[25,1,256]{2,1,0:T(1,128)S(1)}, f32[25,1,256]{2,1,0:T(1,128)S(1)}, u32[]{:S(2)}, u32[]{:S(2)}) collective-permute-start(f32[25,1,256]{2,1,0:T(1,128)S(1)} %get-tuple-element.58), channel_id=1, source_target_pairs={{1,0},{2,1},{3,2},{4,3},{5,4},{6,5},{7,6},{0,7},{9,8},{10,9},{11,1... | collective-permute-start | bytes 76808 | tf_op jit(solution)/shard_map/ppermute | solution.py:286
  17.4 1.5 %collective-permute-done.5.refs_6_.refs_13_ = f32[25,1,256]{2,1,0:T(1,128)S(1)} collective-permute-done((f32[25,1,256]{2,1,0:T(1,128)S(1)}, f32[25,1,256]{2,1,0:T(1,128)S(1)}, u32[]{:S(2)}, u32[]{:S(2)}) %collective-permute-start.5) | collective-permute-done | bytes 25632 | tf_op jit(solution)/shard_map/ppermute | solution.py:286
  18.9 0.0 collective-permute-done.2.refs_3_.refs_10_
  18.9 0.0 collective-permute-done.3.refs_4_.refs_11_
  18.9 0.0 collective-permute-done.refs_1_.refs_8_
  18.9 0.0 collective-permute-done.1.refs_2_.refs_9_
  19.0 3.6 %shard_map.141 = (f32[24,8,32,128]{3,2,1,0:T(8,128)S(1)}, f32[6,8,32,128]{3,2,1,0:T(8,128)S(1)}, bf16[24,32,128]{2,1,0:T(8,128)(2,1)S(1)}, bf16[24,32,128]{2,1,0...) custom-call(f32[24,8,32,128]{3,2,1,0:T(8,128)S(1)} %copy-done.1, ...), custom_call_target="tpu_custom_call" | custom-call | tf_op jit(solution)/shard_map/pallas_call | solution.py:291
  22.6 0.0 collective-permute-start.6
  22.6 2.7 %collective-permute-start.7 = (bf16[24,32,128]{2,1,0:T(8,128)(2,1)S(1)}, bf16[24,32,128]{2,1,0:T(8,128)(2,1)S(1)}, u32[]{:S(2)}, u32[]{:S(2)}) collective-permute-start(bf16[24,32,128]{2,1,0:T(8,128)(2,1)S(1)} %get-tuple-element.71), channel_id=1, source_target_pairs={{32,0},{64,32},{96,64},{0,96},{33,1},{65,33},{97,65},{1,97},{34,2}... | collective-permute-start | bytes 589832 | tf_op jit(solution)/shard_map/ppermute | solution.py:286
  25.3 0.0 collective-permute-start.8
  25.3 2.7 %collective-permute-start.9 = (f32[24,8,128]{2,1,0:T(8,128)S(1)}, f32[24,8,128]{2,1,0:T(8,128)S(1)}, u32[]{:S(2)}, u32[]{:S(2)}) collective-permute-start(f32[24,8,128]{2,1,0:T(8,128)S(1)} %get-tuple-element.73), channel_id=1, source_target_pairs={{8,0},{16,8},{24,16},{0,24},{9,1},{17,9},{25,17},{1,25},{10,2},{18... | collective-permute-start | bytes 294920 | tf_op jit(solution)/shard_map/ppermute | solution.py:286
  27.9 1.1 collective-permute-start.10
  29.1 0.9 collective-permute-done.10.refs_6_
  30.0 3.5 %collective-permute-start.11 = (f32[24,1,256]{2,1,0:T(1,128)S(1)}, f32[24,1,256]{2,1,0:T(1,128)S(1)}, u32[]{:S(2)}, u32[]{:S(2)}) collective-permute-start(f32[24,1,256]{2,1,0:T(1,128)S(1)} %get-tuple-element.75), channel_id=1, source_target_pairs={{1,0},{2,1},{3,2},{4,3},{5,4},{6,5},{7,6},{0,7},{9,8},{10,9},{11,1... | collective-permute-start | bytes 73736 | tf_op jit(solution)/shard_map/ppermute | solution.py:286
  33.6 0.8 collective-permute-done.11.refs_7_
  34.4 0.0 collective-permute-done.8.refs_4_
  34.4 0.0 collective-permute-done.9.refs_5_
  34.4 0.0 collective-permute-done.6.refs_2_
  34.4 0.0 copy-start.18
  34.4 0.0 copy-start.2
  34.5 0.0 copy-start.5
  34.5 0.0 copy-start.6
  34.5 0.0 copy-start.11
  34.5 0.0 copy-start.13
  34.5 0.0 copy-start.14
  34.5 3.9 %shard_map.143 = (f32[24,8,32,128]{3,2,1,0:T(8,128)S(1)}, bf16[24,32,128]{2,1,0:T(8,128)(2,1)S(1)}, bf16[24,32,128]{2,1,0:T(8,128)(2,1)S(1)}, f32[24,8,128]{2,1,...) custom-call(f32[24,8,32,128]{3,2,1,0:T(8,128)S(1)} %get-tuple-element.69.refs_0_, ...), custom_call_target="tpu_custom_call" | custom-call | tf_op jit(solution)/shard_map/pallas_call | solution.py:291
  38.4 0.0 collective-permute-start.16
  38.4 0.7 collective-permute-start.17
  39.1 0.0 collective-permute-start.14
  39.1 2.7 %collective-permute-start.15 = (f32[24,8,128]{2,1,0:T(8,128)S(1)}, f32[24,8,128]{2,1,0:T(8,128)S(1)}, u32[]{:S(2)}, u32[]{:S(2)}) collective-permute-start(f32[24,8,128]{2,1,0:T(8,128)S(1)} %get-tuple-element.81), channel_id=1, source_target_pairs={{8,0},{16,8},{24,16},{0,24},{9,1},{17,9},{25,17},{1,25},{10,2},{18... | collective-permute-start | bytes 294920 | tf_op jit(solution)/shard_map/ppermute | solution.py:286
  41.8 0.0 collective-permute-done.16.refs_6_
  41.8 2.7 %collective-permute-start.13 = (bf16[24,32,128]{2,1,0:T(8,128)(2,1)S(1)}, bf16[24,32,128]{2,1,0:T(8,128)(2,1)S(1)}, u32[]{:S(2)}, u32[]{:S(2)}) collective-permute-start(bf16[24,32,128]{2,1,0:T(8,128)(2,1)S(1)} %get-tuple-element.79), channel_id=1, source_target_pairs={{32,0},{64,32},{96,64},{0,96},{33,1},{65,33},{97,65},{1,97},{34,2}... | collective-permute-start | bytes 589832 | tf_op jit(solution)/shard_map/ppermute | solution.py:286
  44.5 1.5 %shard_map.142 = (bf16[1600,32]{1,0:T(8,128)(2,1)S(1)}, bf16[800,1600]{1,0:T(8,128)(2,1)S(1)}, bf16[400,800]{1,0:T(8,128)(2,1)S(1)}, f32[800,128]{1,0:T(8,128)S(...) custom-call(bf16[24,1600]{1,0:T(8,128)(2,1)S(1)} %copy-done.6, ...), custom_call_target="tpu_custom_call" | custom-call | bytes 8388608 | tf_op jit(solution)/shard_map/pallas_call | solution.py:341
  46.1 0.0 collective-permute-done.14.refs_4_
  46.1 0.0 collective-permute-done.15.refs_5_
  46.1 1.4 collective-permute-done.12.refs_2_
  47.5 0.0 collective-permute-done.13.refs_3_
  47.5 3.5 %shard_map.144 = f32[24,8,32,128]{3,2,1,0:T(8,128)S(1)} custom-call(f32[24,8,32,128]{3,2,1,0:T(8,128)S(1)} %get-tuple-element.77.refs_0_, f32[24,8,32,128]{3,2,1,0:T(8,128)S(1)} %copy-done.1, bf16[24,32,128]{2,1,0:T(8,128)(2,1)S(1)} %collective-permute-done.12.refs_2_, bf16[24,32,128]{2,1,0:T(8,128)(2,1)S(1)} %collective-permute-done.13.refs_3_, ...), custom_call_target="tpu_custom_call" | custom-call | tf_op jit(solution)/shard_map/pallas_call | solution.py:291
  51.0 10.9 %shard_map.145 = (f32[6144,128]{1,0:T(8,128)S(1)}, f32[128,128]{1,0:T(8,128)S(1)}, bf16[24,32,128]{2,1,0:T(8,128)(2,1)}, bf16[24,32,128]{2,1,0:T(8,128)(2,1)}, f...) custom-call(s32[1,96]{1,0:T(1,128)S(1)} %copy-done.12, ...), custom_call_target="tpu_custom_call" | custom-call | tf_op jit(solution)/shard_map/pallas_call | solution.py:354
  61.9 0.6 copy-done.7
  62.5 0.6 copy-done.15
  63.1 51.6 %collective-permute-start.18 = (bf16[24,32,128]{2,1,0:T(8,128)(2,1)}, bf16[24,32,128]{2,1,0:T(8,128)(2,1)S(1)}, u32[]{:S(2)}, u32[]{:S(2)}) collective-permute-start(bf16[24,32,128]{2,1,0:T(8,128)(2,1)} %get-tuple-element.93), channel_id=1, source_target_pairs={{0,32},{32,64},{64,96},{96,0},{1,33},{33,65},{65,97},{97,1},{2,34}... | collective-permute-start | bytes 589832 | tf_op jit(solution)/shard_map/ppermute | solution.py:285
  114.7 2.7 %collective-permute-start.21 = (f32[24,8,128]{2,1,0:T(8,128)}, f32[24,8,128]{2,1,0:T(8,128)}, u32[]{:S(2)}, u32[]{:S(2)}) collective-permute-start(f32[24,8,128]{2,1,0:T(8,128)} %get-tuple-element.98), channel_id=1, source_target_pairs={{8,0},{16,8},{24,16},{0,24},{9,1},{17,9},{25,17},{1,25},{10,2},{18... | collective-permute-start | bytes 294920 | tf_op jit(solution)/shard_map/ppermute | solution.py:286
  117.4 13.0 %all-to-all-start = ((f32[128,1,128]{2,1,0:T(1,128)}), f32[128,1,128]{2,1,0:T(1,128)S(1)}, u32[]{:S(2)}, u32[]{:S(2)}) async-start(f32[128,1,128]{2,1,0:T(1,128)} %bitcast.19), calls=%async_computation | async-start | bytes 131072 | tf_op jit(solution)/shard_map/all_to_all | solution.py:302
  130.4 0.0 collective-permute-done.18.xlo
  130.4 0.0 collective-permute-done.19.xhi
  130.4 1.7 %collective-permute-start.22 = (f32[24,1,256]{2,1,0:T(1,128)}, f32[24,1,256]{2,1,0:T(1,128)S(1)}, u32[]{:S(2)}, u32[]{:S(2)}) collective-permute-start(f32[24,1,256]{2,1,0:T(1,128)} %get-tuple-element.99), channel_id=1, source_target_pairs={{0,1},{1,2},{2,3},{3,4},{4,5},{5,6},{6,7},{7,0},{8,9},{9,10},{10,1... | collective-permute-start | bytes 73736 | tf_op jit(solution)/shard_map/ppermute | solution.py:285
  132.1 0.0 collective-permute-start.23
  132.1 7.9 %all-to-all-done = f32[128,1,128]{2,1,0:T(1,128)S(1)} async-done(((f32[128,1,128]{2,1,0:T(1,128)}), f32[128,1,128]{2,1,0:T(1,128)S(1)}, u32[]{:S(2)}, u32[]{:S(2)}) %all-to-all-start) | async-done | bytes 65568 | tf_op jit(solution)/shard_map/all_to_all | solution.py:302
  140.0 0.0 collective-permute-done.20.ylo
  140.0 0.0 collective-permute-done.21.yhi
  140.1 0.7 copy-done.10
  140.8 5.0 %shard_map.146 = (f32[24,8,32,128]{3,2,1,0:T(8,128)}, f32[1,1]{1,0:T(1,128)}) custom-call(f32[24,128]{1,0:T(8,128)S(1)} %copy-done.10, f32[24,8,32,128]{3,2,1,0:T(8,128)S(1)} %bitcast.15, bf16[24,32,128]{2,1,0:T(8,128)(2,1)S(1)} %collective-permute-done.18.xlo, bf16[24,32,128]{2,1,0:T(8,128)(2,1)} %collective-permute-done.19.xhi, ...), custom_call_target="tpu_custom_call" | custom-call | flops 1000000000 | bytes 25165824 | tf_op jit(solution)/shard_map/pallas_call | solution.py:367
  (34 shorter events, 0.1 us)
Async XLA Ops:
  0.6 1.9 %copy-start = (f32[24,8,32,128]{3,2,1,0:T(8,128)S(1)}, f32[24,8,32,128]{3,2,1,0:T(8,128)}, u32[]{:S(2)}) copy-start(f32[24,8,32,128]{3,2,1,0:T(8,128)} %refs_1_.3) | copy-start | bytes 9437188
  2.5 1.0 copy-start.3
  3.5 15.4 %copy-start.1 = (f32[24,8,32,128]{3,2,1,0:T(8,128)S(1)}, f32[24,8,32,128]{3,2,1,0:T(8,128)}, u32[]{:S(2)}) copy-start(f32[24,8,32,128]{3,2,1,0:T(8,128)} %refs_1_.3) | copy-start | bytes 9437188
  3.5 15.4 %copy-start.4 = (f32[3,8,32,128]{3,2,1,0:T(8,128)S(1)}, f32[3,8,32,128]{3,2,1,0:T(8,128)}, u32[]{:S(2)}) copy-start(f32[3,8,32,128]{3,2,1,0:T(8,128)} %refs_7_.1) | copy-start | bytes 1179652
  4.1 29.5 %copy-start.17 = (f32[800]{0:T(1024)S(1)}, f32[800]{0:T(1024)}, u32[]{:S(2)}) copy-start(f32[800]{0:T(1024)} %param.19) | copy-start | bytes 9604
  4.1 29.5 %copy-start.16 = (f32[1600]{0:T(1024)S(1)}, f32[1600]{0:T(1024)}, u32[]{:S(2)}) copy-start(f32[1600]{0:T(1024)} %param.17) | copy-start | bytes 19204
  4.1 14.8 %collective-permute-start = (bf16[25,32,128]{2,1,0:T(8,128)(2,1)S(1)}, bf16[25,32,128]{2,1,0:T(8,128)(2,1)S(1)}, u32[]{:S(2)}, u32[]{:S(2)}) collective-permute-start(bf16[25,32,128]{2,1,0:T(8,128)(2,1)S(1)} %get-tuple-element.53), channel_id=1, source_target_pairs={{0,32},{32,64},{64,96},{96,0},{1,33},{33,65},{65,97},{97,1},{2,34}... | collective-permute-start | bytes 614408 | tf_op jit(solution)/shard_map/ppermute | solution.py:285
  6.2 12.7 %collective-permute-start.1 = (bf16[25,32,128]{2,1,0:T(8,128)(2,1)S(1)}, bf16[25,32,128]{2,1,0:T(8,128)(2,1)S(1)}, u32[]{:S(2)}, u32[]{:S(2)}) collective-permute-start(bf16[25,32,128]{2,1,0:T(8,128)(2,1)S(1)} %get-tuple-element.54), channel_id=1, source_target_pairs={{32,0},{64,32},{96,64},{0,96},{33,1},{65,33},{97,65},{1,97},{34,2}... | collective-permute-start | bytes 614408 | tf_op jit(solution)/shard_map/ppermute | solution.py:286
  7.6 11.4 %collective-permute-start.2 = (f32[25,8,128]{2,1,0:T(8,128)S(1)}, f32[25,8,128]{2,1,0:T(8,128)S(1)}, u32[]{:S(2)}, u32[]{:S(2)}) collective-permute-start(f32[25,8,128]{2,1,0:T(8,128)S(1)} %get-tuple-element.55), channel_id=1, source_target_pairs={{0,8},{8,16},{16,24},{24,0},{1,9},{9,17},{17,25},{25,1},{2,10},{10... | collective-permute-start | bytes 307208 | tf_op jit(solution)/shard_map/ppermute | solution.py:285
  9.3 9.6 %collective-permute-start.3 = (f32[25,8,128]{2,1,0:T(8,128)S(1)}, f32[25,8,128]{2,1,0:T(8,128)S(1)}, u32[]{:S(2)}, u32[]{:S(2)}) collective-permute-start(f32[25,8,128]{2,1,0:T(8,128)S(1)} %get-tuple-element.56), channel_id=1, source_target_pairs={{8,0},{16,8},{24,16},{0,24},{9,1},{17,9},{25,17},{1,25},{10,2},{18... | collective-permute-start | bytes 307208 | tf_op jit(solution)/shard_map/ppermute | solution.py:286
  11.4 3.7 %collective-permute-start.4 = (f32[25,1,256]{2,1,0:T(1,128)S(1)}, f32[25,1,256]{2,1,0:T(1,128)S(1)}, u32[]{:S(2)}, u32[]{:S(2)}) collective-permute-start(f32[25,1,256]{2,1,0:T(1,128)S(1)} %get-tuple-element.57), channel_id=1, source_target_pairs={{0,1},{1,2},{2,3},{3,4},{4,5},{5,6},{6,7},{7,0},{8,9},{9,10},{10,1... | collective-permute-start | bytes 76808 | tf_op jit(solution)/shard_map/ppermute | solution.py:285
  15.1 3.8 %collective-permute-start.5 = (f32[25,1,256]{2,1,0:T(1,128)S(1)}, f32[25,1,256]{2,1,0:T(1,128)S(1)}, u32[]{:S(2)}, u32[]{:S(2)}) collective-permute-start(f32[25,1,256]{2,1,0:T(1,128)S(1)} %get-tuple-element.58), channel_id=1, source_target_pairs={{1,0},{2,1},{3,2},{4,3},{5,4},{6,5},{7,6},{0,7},{9,8},{10,9},{11,1... | collective-permute-start | bytes 76808 | tf_op jit(solution)/shard_map/ppermute | solution.py:286
  22.6 11.8 %collective-permute-start.6 = (bf16[24,32,128]{2,1,0:T(8,128)(2,1)S(1)}, bf16[24,32,128]{2,1,0:T(8,128)(2,1)S(1)}, u32[]{:S(2)}, u32[]{:S(2)}) collective-permute-start(bf16[24,32,128]{2,1,0:T(8,128)(2,1)S(1)} %get-tuple-element.70), channel_id=1, source_target_pairs={{0,32},{32,64},{64,96},{96,0},{1,33},{33,65},{65,97},{97,1},{2,34}... | collective-permute-start | bytes 589832 | tf_op jit(solution)/shard_map/ppermute | solution.py:285
  22.6 11.8 %collective-permute-start.7 = (bf16[24,32,128]{2,1,0:T(8,128)(2,1)S(1)}, bf16[24,32,128]{2,1,0:T(8,128)(2,1)S(1)}, u32[]{:S(2)}, u32[]{:S(2)}) collective-permute-start(bf16[24,32,128]{2,1,0:T(8,128)(2,1)S(1)} %get-tuple-element.71), channel_id=1, source_target_pairs={{32,0},{64,32},{96,64},{0,96},{33,1},{65,33},{97,65},{1,97},{34,2}... | collective-permute-start | bytes 589832 | tf_op jit(solution)/shard_map/ppermute | solution.py:286
  25.3 9.2 %collective-permute-start.8 = (f32[24,8,128]{2,1,0:T(8,128)S(1)}, f32[24,8,128]{2,1,0:T(8,128)S(1)}, u32[]{:S(2)}, u32[]{:S(2)}) collective-permute-start(f32[24,8,128]{2,1,0:T(8,128)S(1)} %get-tuple-element.72), channel_id=1, source_target_pairs={{0,8},{8,16},{16,24},{24,0},{1,9},{9,17},{17,25},{25,1},{2,10},{10... | collective-permute-start | bytes 294920 | tf_op jit(solution)/shard_map/ppermute | solution.py:285
  25.3 9.2 %collective-permute-start.9 = (f32[24,8,128]{2,1,0:T(8,128)S(1)}, f32[24,8,128]{2,1,0:T(8,128)S(1)}, u32[]{:S(2)}, u32[]{:S(2)}) collective-permute-start(f32[24,8,128]{2,1,0:T(8,128)S(1)} %get-tuple-element.73), channel_id=1, source_target_pairs={{8,0},{16,8},{24,16},{0,24},{9,1},{17,9},{25,17},{1,25},{10,2},{18... | collective-permute-start | bytes 294920 | tf_op jit(solution)/shard_map/ppermute | solution.py:286
  27.9 2.1 %collective-permute-start.10 = (f32[24,1,256]{2,1,0:T(1,128)S(1)}, f32[24,1,256]{2,1,0:T(1,128)S(1)}, u32[]{:S(2)}, u32[]{:S(2)}) collective-permute-start(f32[24,1,256]{2,1,0:T(1,128)S(1)} %get-tuple-element.74), channel_id=1, source_target_pairs={{0,1},{1,2},{2,3},{3,4},{4,5},{5,6},{6,7},{7,0},{8,9},{9,10},{10,1... | collective-permute-start | bytes 73736 | tf_op jit(solution)/shard_map/ppermute | solution.py:285
  30.0 4.4 %collective-permute-start.11 = (f32[24,1,256]{2,1,0:T(1,128)S(1)}, f32[24,1,256]{2,1,0:T(1,128)S(1)}, u32[]{:S(2)}, u32[]{:S(2)}) collective-permute-start(f32[24,1,256]{2,1,0:T(1,128)S(1)} %get-tuple-element.75), channel_id=1, source_target_pairs={{1,0},{2,1},{3,2},{4,3},{5,4},{6,5},{7,6},{0,7},{9,8},{10,9},{11,1... | collective-permute-start | bytes 73736 | tf_op jit(solution)/shard_map/ppermute | solution.py:286
  34.4 10.0 %copy-start.18 = (s32[1,96]{1,0:T(1,128)S(1)}, s32[1,96]{1,0:T(1,128)}, u32[]{:S(2)}) copy-start(s32[1,96]{1,0:T(1,128)} %param.25) | copy-start | bytes 1156
  34.4 10.0 %copy-start.2 = (bf16[1600,800]{0,1:T(8,128)(2,1)S(1)}, bf16[1600,800]{0,1:T(8,128)(2,1)}, u32[]{:S(2)}) copy-start(bf16[1600,800]{0,1:T(8,128)(2,1)} %param.18) | copy-start | bytes 7680004
  34.5 10.0 %copy-start.5 = (bf16[800,400]{0,1:T(8,128)(2,1)S(1)}, bf16[800,400]{0,1:T(8,128)(2,1)}, u32[]{:S(2)}) copy-start(bf16[800,400]{0,1:T(8,128)(2,1)} %param.20) | copy-start | bytes 1920004
  34.5 10.0 %copy-start.6 = (bf16[24,1600]{1,0:T(8,128)(2,1)S(1)}, bf16[24,1600]{1,0:T(8,128)(2,1)}, u32[]{:S(2)}) copy-start(bf16[24,1600]{1,0:T(8,128)(2,1)} %w_in) | copy-start | bytes 230404
  34.5 10.0 %copy-start.11 = (f32[400]{0:T(512)S(1)}, f32[400]{0:T(512)}, u32[]{:S(2)}) copy-start(f32[400]{0:T(512)} %param.21) | copy-start | bytes 4804
  34.5 10.0 %copy-start.13 = (f32[24]{0:T(128)S(1)}, f32[24]{0:T(128)}, u32[]{:S(2)}) copy-start(f32[24]{0:T(128)} %param.23) | copy-start | bytes 292
  34.5 10.0 %copy-start.14 = (f32[24]{0:T(128)S(1)}, f32[24]{0:T(128)}, u32[]{:S(2)}) copy-start(f32[24]{0:T(128)} %param.15) | copy-start | bytes 292
  38.4 3.4 %collective-permute-start.16 = (f32[24,1,256]{2,1,0:T(1,128)S(1)}, f32[24,1,256]{2,1,0:T(1,128)S(1)}, u32[]{:S(2)}, u32[]{:S(2)}) collective-permute-start(f32[24,1,256]{2,1,0:T(1,128)S(1)} %get-tuple-element.82), channel_id=1, source_target_pairs={{0,1},{1,2},{2,3},{3,4},{4,5},{5,6},{6,7},{7,0},{8,9},{9,10},{10,1... | collective-permute-start | bytes 73736 | tf_op jit(solution)/shard_map/ppermute | solution.py:285
  38.4 7.7 %collective-permute-start.17 = (f32[24,1,256]{2,1,0:T(1,128)S(1)}, f32[24,1,256]{2,1,0:T(1,128)S(1)}, u32[]{:S(2)}, u32[]{:S(2)}) collective-permute-start(f32[24,1,256]{2,1,0:T(1,128)S(1)} %get-tuple-element.83), channel_id=1, source_target_pairs={{1,0},{2,1},{3,2},{4,3},{5,4},{6,5},{7,6},{0,7},{9,8},{10,9},{11,1... | collective-permute-start | bytes 73736 | tf_op jit(solution)/shard_map/ppermute | solution.py:286
  39.1 7.0 %collective-permute-start.14 = (f32[24,8,128]{2,1,0:T(8,128)S(1)}, f32[24,8,128]{2,1,0:T(8,128)S(1)}, u32[]{:S(2)}, u32[]{:S(2)}) collective-permute-start(f32[24,8,128]{2,1,0:T(8,128)S(1)} %get-tuple-element.80), channel_id=1, source_target_pairs={{0,8},{8,16},{16,24},{24,0},{1,9},{9,17},{17,25},{25,1},{2,10},{10... | collective-permute-start | bytes 294920 | tf_op jit(solution)/shard_map/ppermute | solution.py:285
  39.1 7.0 %collective-permute-start.15 = (f32[24,8,128]{2,1,0:T(8,128)S(1)}, f32[24,8,128]{2,1,0:T(8,128)S(1)}, u32[]{:S(2)}, u32[]{:S(2)}) collective-permute-start(f32[24,8,128]{2,1,0:T(8,128)S(1)} %get-tuple-element.81), channel_id=1, source_target_pairs={{8,0},{16,8},{24,16},{0,24},{9,1},{17,9},{25,17},{1,25},{10,2},{18... | collective-permute-start | bytes 294920 | tf_op jit(solution)/shard_map/ppermute | solution.py:286
  41.8 5.7 %collective-permute-start.12 = (bf16[24,32,128]{2,1,0:T(8,128)(2,1)S(1)}, bf16[24,32,128]{2,1,0:T(8,128)(2,1)S(1)}, u32[]{:S(2)}, u32[]{:S(2)}) collective-permute-start(bf16[24,32,128]{2,1,0:T(8,128)(2,1)S(1)} %get-tuple-element.78), channel_id=1, source_target_pairs={{0,32},{32,64},{64,96},{96,0},{1,33},{33,65},{65,97},{97,1},{2,34}... | collective-permute-start | bytes 589832 | tf_op jit(solution)/shard_map/ppermute | solution.py:285
  41.8 5.7 %collective-permute-start.13 = (bf16[24,32,128]{2,1,0:T(8,128)(2,1)S(1)}, bf16[24,32,128]{2,1,0:T(8,128)(2,1)S(1)}, u32[]{:S(2)}, u32[]{:S(2)}) collective-permute-start(bf16[24,32,128]{2,1,0:T(8,128)(2,1)S(1)} %get-tuple-element.79), channel_id=1, source_target_pairs={{32,0},{64,32},{96,64},{0,96},{33,1},{65,33},{97,65},{1,97},{34,2}... | collective-permute-start | bytes 589832 | tf_op jit(solution)/shard_map/ppermute | solution.py:286
  46.0 5.0 %copy-start.9 = (f32[24,128]{1,0:T(8,128)}, f32[24,128]{1,0:T(8,128)S(1)}, u32[]{:S(2)}) copy-start(f32[24,128]{1,0:T(8,128)S(1)} %get-tuple-element.68.rates) | copy-start | bytes 36868
  47.5 3.5 %copy-start.8 = (bf16[400,24]{0,1:T(8,128)(2,1)S(1)}, bf16[400,24]{0,1:T(8,128)(2,1)}, u32[]{:S(2)}) copy-start(bf16[400,24]{0,1:T(8,128)(2,1)} %param.22) | copy-start | bytes 57604
  47.5 3.5 %copy-start.12 = (s32[1,96]{1,0:T(1,128)S(1)}, s32[1,96]{1,0:T(1,128)}, u32[]{:S(2)}) copy-start(s32[1,96]{1,0:T(1,128)} %listed.1) | copy-start | bytes 1156
  61.9 0.6 copy-start.7
  62.5 0.6 copy-start.15
  63.1 67.3 %collective-permute-start.18 = (bf16[24,32,128]{2,1,0:T(8,128)(2,1)}, bf16[24,32,128]{2,1,0:T(8,128)(2,1)S(1)}, u32[]{:S(2)}, u32[]{:S(2)}) collective-permute-start(bf16[24,32,128]{2,1,0:T(8,128)(2,1)} %get-tuple-element.93), channel_id=1, source_target_pairs={{0,32},{32,64},{64,96},{96,0},{1,33},{33,65},{65,97},{97,1},{2,34}... | collective-permute-start | bytes 589832 | tf_op jit(solution)/shard_map/ppermute | solution.py:285
  114.7 15.7 %collective-permute-start.19 = (bf16[24,32,128]{2,1,0:T(8,128)(2,1)}, bf16[24,32,128]{2,1,0:T(8,128)(2,1)}, u32[]{:S(2)}, u32[]{:S(2)}) collective-permute-start(bf16[24,32,128]{2,1,0:T(8,128)(2,1)} %get-tuple-element.94), channel_id=1, source_target_pairs={{32,0},{64,32},{96,64},{0,96},{33,1},{65,33},{97,65},{1,97},{34,2}... | collective-permute-start | bytes 589832 | tf_op jit(solution)/shard_map/ppermute | solution.py:286
  114.7 25.3 %collective-permute-start.20 = (f32[24,8,128]{2,1,0:T(8,128)}, f32[24,8,128]{2,1,0:T(8,128)S(1)}, u32[]{:S(2)}, u32[]{:S(2)}) collective-permute-start(f32[24,8,128]{2,1,0:T(8,128)} %get-tuple-element.97), channel_id=1, source_target_pairs={{0,8},{8,16},{16,24},{24,0},{1,9},{9,17},{17,25},{25,1},{2,10},{10... | collective-permute-start | bytes 294920 | tf_op jit(solution)/shard_map/ppermute | solution.py:285
  114.7 25.3 %collective-permute-start.21 = (f32[24,8,128]{2,1,0:T(8,128)}, f32[24,8,128]{2,1,0:T(8,128)}, u32[]{:S(2)}, u32[]{:S(2)}) collective-permute-start(f32[24,8,128]{2,1,0:T(8,128)} %get-tuple-element.98), channel_id=1, source_target_pairs={{8,0},{16,8},{24,16},{0,24},{9,1},{17,9},{25,17},{1,25},{10,2},{18... | collective-permute-start | bytes 294920 | tf_op jit(solution)/shard_map/ppermute | solution.py:286
  117.4 22.6 %all-to-all-start = ((f32[128,1,128]{2,1,0:T(1,128)}), f32[128,1,128]{2,1,0:T(1,128)S(1)}, u32[]{:S(2)}, u32[]{:S(2)}) async-start(f32[128,1,128]{2,1,0:T(1,128)} %bitcast.19), calls=%async_computation | async-start | bytes 131072 | tf_op jit(solution)/shard_map/all_to_all | solution.py:302
  130.4 9.6 %collective-permute-start.22 = (f32[24,1,256]{2,1,0:T(1,128)}, f32[24,1,256]{2,1,0:T(1,128)S(1)}, u32[]{:S(2)}, u32[]{:S(2)}) collective-permute-start(f32[24,1,256]{2,1,0:T(1,128)} %get-tuple-element.99), channel_id=1, source_target_pairs={{0,1},{1,2},{2,3},{3,4},{4,5},{5,6},{6,7},{7,0},{8,9},{9,10},{10,1... | collective-permute-start | bytes 73736 | tf_op jit(solution)/shard_map/ppermute | solution.py:285
  132.1 7.9 %collective-permute-start.23 = (f32[24,1,256]{2,1,0:T(1,128)}, f32[24,1,256]{2,1,0:T(1,128)S(1)}, u32[]{:S(2)}, u32[]{:S(2)}) collective-permute-start(f32[24,1,256]{2,1,0:T(1,128)} %copy-done.15), channel_id=1, source_target_pairs={{1,0},{2,1},{3,2},{4,3},{5,4},{6,5},{7,6},{0,7},{9,8},{10,9},{11,1... | collective-permute-start | bytes 73736 | tf_op jit(solution)/shard_map/ppermute | solution.py:286
  140.1 0.7 copy-start.10

commit v9 on v8

--- a/solution.py
+++ b/solution.py
@@ -7,7 +7,8 @@
 from jax.experimental.pallas import tpu as pltpu
 from jax.sharding import PartitionSpec as P
 
-GROUP = 12
+GROUP = 24
+LAST_GROUP = 8
 TOGETHER = 12
 LISTED = 96
 NETWORK_MIB = 38
@@ -27,6 +28,16 @@
     rows = lax.broadcasted_iota(jnp.int32, (16, 256), 0)
     pair = jnp.where(rows == 0, low, jnp.where(rows == 1, high, 0.0)).astype(BF16)
     return lax.dot_general(pair, one_hot_ends(), TN, preferred_element_type=F32)
+
+
+def all_z_columns(low, high):
+    n = low.shape[0]
+    rows = lax.broadcasted_iota(jnp.int32, (2 * n, 128 * n), 0)
+    lanes = lax.broadcasted_iota(jnp.int32, (2 * n, 128 * n), 1)
+    place = jnp.where(rows < n, 128 * rows, 128 * (rows - n) + 127)
+    ends = (lanes == place).astype(F32).astype(BF16)
+    pairs = jnp.concatenate([low, high], axis=0).astype(BF16)
+    return lax.dot_general(pairs, ends, TN, preferred_element_type=F32)
 
 
 def z_ends(cells):
@@ -54,31 +65,33 @@
 
 def put_z_faces(out, f, zf, zl):
     ends = z_ends(out[f].reshape(256, 128))
-    zf[f] = ends[0:1]
-    zl[f] = ends[1:2]
-
-
-def prep_kernel(fields, velocity, xf, xl, yf, yl, zf, zl):
-    def put(ref, i, f):
-        xf[f] = ref[i, 0].astype(BF16)
-        xl[f] = ref[i, 7].astype(BF16)
+    zf[f : f + 1] = ends[0:1]
+    zl[f : f + 1] = ends[1:2]
+
+
+def x_faces_kernel(fields, velocity, xf, xl, planes, sems):
+    copies = []
+    for i, x in enumerate((0, 7)):
+        copies.append(pltpu.make_async_copy(fields.at[:, x], planes.at[i, 0:24], sems.at[i, 0]))
+        copies.append(pltpu.make_async_copy(velocity.at[0, x], planes.at[i, 24], sems.at[i, 1]))
+    for copy in copies:
+        copy.start()
+    for copy in copies:
+        copy.wait()
+    xf[...] = planes[0].astype(BF16)
+    xl[...] = planes[1].astype(BF16)
+
+
+def prep_kernel(fields, velocity, yf, yl, zf, zl):
+    for f in range(25):
         for x in range(8):
-            yf[f, x : x + 1] = ref[i, x, 0:1]
-            yl[f, x : x + 1] = ref[i, x, 31:32]
-        ends = z_ends(ref[i].reshape(256, 128))
-        zf[f] = ends[0:1]
-        zl[f] = ends[1:2]
-
-    for f in range(24):
-        put(fields, f, f)
-    xf[24] = velocity[0, 0].astype(BF16)
-    xl[24] = velocity[0, 7].astype(BF16)
-    for x in range(8):
-        yf[24, x : x + 1] = velocity[1, x, 0:1]
-        yl[24, x : x + 1] = velocity[1, x, 31:32]
-    ends = z_ends(velocity[2].reshape(256, 128))
-    zf[24] = ends[0:1]
-    zl[24] = ends[1:2]
+            cells = velocity[1, x] if f == 24 else fields[f, x]
+            yf[f, x : x + 1] = cells[0:1]
+            yl[f, x : x + 1] = cells[31:32]
+        lines = velocity[2] if f == 24 else fields[f]
+        ends = z_ends(lines.reshape(256, 128))
+        zf[f : f + 1] = ends[0:1]
+        zl[f : f + 1] = ends[1:2]
 
 
 def section_kernel(kind, *refs):
@@ -101,7 +114,7 @@
     zcol = refs.pop(0)
 
     if kind == 1:
-        zcol[0] = z_columns(vzlo[24], vzhi[24])
+        v_col = z_columns(vzlo[24:25], vzhi[24:25])
         for x in range(8):
             before = vxlo[24].astype(F32) if x == 0 else velocity[0, x - 1]
             after = vxhi[24].astype(F32) if x == 7 else velocity[0, x + 1]
@@ -109,7 +122,7 @@
                 velocity[1, x], vylo[24, x : x + 1], vyhi[24, x : x + 1], velocity[1, x]
             )
             _, _, z_next, z_prev = shifted(
-                velocity[2, x], vylo[24, x : x + 1], vyhi[24, x : x + 1], zcol[0, 32 * x : 32 * x + 32]
+                velocity[2, x], vylo[24, x : x + 1], vyhi[24, x : x + 1], v_col[32 * x : 32 * x + 32]
             )
             coef[0, x] = 0.05 - 0.5 * after
             coef[1, x] = 0.05 + 0.5 * before
@@ -118,69 +131,54 @@
             coef[4, x] = 0.05 - 0.5 * z_next
             coef[5, x] = 0.05 + 0.5 * z_prev
 
-    def part(p, carry):
-        fs = [p * GROUP + i for i in range(GROUP)]
-        for i, f in enumerate(fs):
-            zcol[i] = z_columns(zlo[f], zhi[f])
+    zcol[...] = all_z_columns(zlo[0:GROUP, :], zhi[0:GROUP, :])
+    for x in range(8):
+        ce = [coef[i, x] for i in range(6)]
+        for f in range(GROUP):
+            centre = q[f, x]
+            before = xlo[f].astype(F32) if x == 0 else q[f, x - 1]
+            after = xhi[f].astype(F32) if x == 7 else q[f, x + 1]
+            z_col = zcol[32 * x : 32 * x + 32, 128 * f : 128 * f + 128]
+            y_next, y_prev, z_next, z_prev = shifted(centre, ylo[f, x : x + 1], yhi[f, x : x + 1], z_col)
+            moved = (
+                0.7 * centre
+                + (ce[0] * after + ce[1] * before)
+                + (ce[2] * y_next + ce[3] * y_prev)
+                + (ce[4] * z_next + ce[5] * z_prev)
+            )
+            if kind == 1:
+                new = moved
+            elif kind == 2:
+                new = 0.75 * start[f, x] + 0.25 * moved
+            else:
+                new = (1.0 / 3.0) * start[f, x] + (2.0 / 3.0) * moved
+            out[f, x] = new
+            if kind < 3:
+                put_faces(new, f, x, xf, xl, yf, yl)
+    if kind < 3:
+        for f in range(GROUP):
+            put_z_faces(out, f, zf, zl)
+
+
+def diffuse_kernel(rates, q, xlo, xhi, ylo, yhi, zlo, zhi, heats, out, activity, zcol):
+    @pl.when(pl.program_id(0) == 0)
+    def _():
+        activity[0, 0] = jnp.sum(heats[...]) * (1.0 / (8.0 * 128.0))
+
+    zcol[...] = all_z_columns(zlo[...], zhi[...])
+    for f in range(LAST_GROUP):
+        rate = rates[pl.program_id(0) * LAST_GROUP + f]
         for x in range(8):
-            ce = [coef[i, x] for i in range(6)]
-            for i, f in enumerate(fs):
-                centre = q[f, x]
-                before = xlo[f].astype(F32) if x == 0 else q[f, x - 1]
-                after = xhi[f].astype(F32) if x == 7 else q[f, x + 1]
-                y_next, y_prev, z_next, z_prev = shifted(
-                    centre, ylo[f, x : x + 1], yhi[f, x : x + 1], zcol[i, 32 * x : 32 * x + 32]
-                )
-                moved = (
-                    0.7 * centre
-                    + (ce[0] * after + ce[1] * before)
-                    + (ce[2] * y_next + ce[3] * y_prev)
-                    + (ce[4] * z_next + ce[5] * z_prev)
-                )
-                if kind == 1:
-                    new = moved
-                elif kind == 2:
-                    new = 0.75 * start[f, x] + 0.25 * moved
-                else:
-                    new = (1.0 / 3.0) * start[f, x] + (2.0 / 3.0) * moved
-                out[f, x] = new
-                if kind < 3:
-                    put_faces(new, f, x, xf, xl, yf, yl)
-        if kind < 3:
-            for f in fs:
-                put_z_faces(out, f, zf, zl)
-        return carry
-
-    lax.fori_loop(0, 24 // GROUP, part, 0)
-
-
-def diffuse_kernel(rates, q, xlo, xhi, ylo, yhi, zlo, zhi, heats, out, activity, zcol):
-    activity[0, 0] = jnp.sum(heats[...]) * (1.0 / (8.0 * 128.0))
-
-    def part(p, carry):
-        for i in range(GROUP):
-            f = p * GROUP + i
-            zcol[i] = z_columns(zlo[f], zhi[f])
-        for i in range(GROUP):
-            f = p * GROUP + i
-            rate = rates[pl.ds(f, 1), :]
-            for x in range(8):
-                centre = q[f, x]
-                before = xlo[f].astype(F32) if x == 0 else q[f, x - 1]
-                after = xhi[f].astype(F32) if x == 7 else q[f, x + 1]
-                y_next, y_prev, z_next, z_prev = shifted(
-                    centre, ylo[f, x : x + 1], yhi[f, x : x + 1], zcol[i, 32 * x : 32 * x + 32]
-                )
-                spread = (after + before) + (y_next + y_prev) + (z_next + z_prev) - 6.0 * centre
-                out[f, x] = centre + rate * spread
-        return carry
-
-    lax.fori_loop(0, 24 // GROUP, part, 0)
-
-
-def columns_kernel(
-    w_in, b_in, w_mid, w_low, b_mid, b_low, b_out, diffusivity, w1, w2, w3, b2, b3, b4, rates
-):
+            centre = q[f, x]
+            before = xlo[f].astype(F32) if x == 0 else q[f, x - 1]
+            after = xhi[f].astype(F32) if x == 7 else q[f, x + 1]
+            z_col = zcol[32 * x : 32 * x + 32, 128 * f : 128 * f + 128]
+            y_next, y_prev, z_next, z_prev = shifted(centre, ylo[f, x : x + 1], yhi[f, x : x + 1], z_col)
+            spread = (after + before) + (y_next + y_prev) + (z_next + z_prev) - 6.0 * centre
+            out[f, x] = centre + rate * spread
+
+
+def columns_kernel(w_in, b_in, w_mid, w_low, b_mid, b_low, b_out, w1, w2, w3, b2, b3, b4):
     bias = 0.5 * b_in[...]
     parts = []
     for _ in range(3):
@@ -194,7 +192,6 @@
         (b_mid, b2, 0.5),
         (b_low, b3, 0.5),
         (b_out, b4, 1.0),
-        (diffusivity, rates, 1.0),
     ):
         out[...] = jnp.broadcast_to(factor * row[...], (128, row.shape[1])).T
 
@@ -242,8 +239,8 @@
             xl[f] = out[pl.ds(base + 224, 32), :].astype(BF16)
             yf[f] = out[pl.ds(base, 8, stride=32), :]
             yl[f] = out[pl.ds(base + 31, 8, stride=32), :]
-            zf[f] = ends[0:1, 256 * j : 256 * j + 256]
-            zl[f] = ends[1:2, 256 * j : 256 * j + 256]
+            zf[pl.ds(f, 1), :] = ends[0:1, 256 * j : 256 * j + 256]
+            zl[pl.ds(f, 1), :] = ends[1:2, 256 * j : 256 * j + 256]
         return carry
 
     heat[...] = jnp.zeros_like(heat)
@@ -273,8 +270,8 @@
         sds((count, 32, 128), BF16),
         sds((count, 8, 128), F32),
         sds((count, 8, 128), F32),
-        sds((count, 1, 256), F32),
-        sds((count, 1, 256), F32),
+        sds((count, 256), F32),
+        sds((count, 256), F32),
     ]
 
 
@@ -293,7 +290,7 @@
         in_specs=[IN_VMEM] * len(args),
         out_specs=[IN_VMEM] * len(out_shapes),
         out_shape=out_shapes,
-        scratch_shapes=[pltpu.VMEM((GROUP, 256, 128), F32)],
+        scratch_shapes=[pltpu.VMEM((256, 128 * GROUP), F32)],
         compiler_params=params(24),
     )(*args)
 
@@ -321,10 +318,18 @@
     owners = owner_table[0]
     owned_by = (owners[None, :] == jnp.arange(128, dtype=jnp.int32)[:, None]).astype(F32)
 
-    faces = pl.pallas_call(
-        prep_kernel, out_shape=face_shapes(25), compiler_params=params(32)
+    x_faces = pl.pallas_call(
+        x_faces_kernel,
+        in_specs=[pl.BlockSpec(memory_space=pltpu.HBM)] * 2,
+        out_specs=[IN_VMEM] * 2,
+        out_shape=face_shapes(25)[:2],
+        scratch_shapes=[pltpu.VMEM((2, 25, 32, 128), F32), pltpu.SemaphoreType.DMA((2, 2))],
+        compiler_params=params(58),
     )(fields, velocity)
-    halo = exchange(faces)
+    more_faces = pl.pallas_call(
+        prep_kernel, out_shape=face_shapes(25)[2:], compiler_params=params(24)
+    )(fields, velocity)
+    halo = exchange(x_faces, ALL[:1]) + exchange(more_faces, ALL[1:])
     one, coef, *faces = section(
         1, (fields, *halo, velocity, *halo), [brick, sds((6, 8, 32, 128), F32), *face_shapes(24)]
     )
@@ -335,16 +340,16 @@
             bias_in.reshape(1, -1),
             weight_mid.T,
             weight_low.T,
-            *(b.reshape(1, -1) for b in (bias_mid, bias_low, bias_out, diffusivity)),
+            *(b.reshape(1, -1) for b in (bias_mid, bias_low, bias_out)),
         )
     )
-    *columns, rates = pl.pallas_call(
+    columns = pl.pallas_call(
         columns_kernel,
         out_shape=[
             sds((weight_in.shape[1], 32), BF16),
             sds(weight_mid.shape[::-1], BF16),
             sds(weight_low.shape[::-1], BF16),
-            *(sds((b.shape[0], 128), F32) for b in (bias_mid, bias_low, bias_out, diffusivity)),
+            *(sds((b.shape[0], 128), F32) for b in (bias_mid, bias_low, bias_out)),
         ],
         compiler_params=params(20),
         cost_estimate=pl.CostEstimate(flops=0, bytes_accessed=8 * 2**20, transcendentals=0),
@@ -360,19 +365,25 @@
         compiler_params=params(NETWORK_MIB),
     )(react_list, flowed.reshape(24 * 256, 128), owned_by, *columns, weight_out.T)
     reacted = reacted.reshape(fields.shape)
-    x_and_y = exchange(faces[:4])
-    *z_faces, x_and_y[0], x_and_y[1] = lax.optimization_barrier((*faces[4:], *x_and_y[:2]))
-    around = x_and_y + exchange(z_faces, ALL[2:])
+    around = exchange(faces)
     heats = swap(sent.reshape(128, 1, 128)).reshape(128, 128)
+    part = LAST_GROUP
+    bricks = pl.BlockSpec((part, 8, 32, 128), lambda g: (g, 0, 0, 0))
+    x_part = pl.BlockSpec((part, 32, 128), lambda g: (g, 0, 0))
+    y_part = pl.BlockSpec((part, 8, 128), lambda g: (g, 0, 0))
+    z_part = pl.BlockSpec((part, 256), lambda g: (g, 0))
+    smem = pl.BlockSpec(memory_space=pltpu.SMEM)
     updated, activity = pl.pallas_call(
         diffuse_kernel,
-        in_specs=[IN_VMEM] * 9,
-        out_specs=[IN_VMEM, pl.BlockSpec(memory_space=pltpu.SMEM)],
+        grid=(24 // part,),
+        in_specs=[smem, bricks, x_part, x_part, y_part, y_part, z_part, z_part]
+        + [pl.BlockSpec((128, 128), lambda g: (0, 0))],
+        out_specs=[bricks, smem],
         out_shape=[brick, sds((1, 1), F32)],
-        scratch_shapes=[pltpu.VMEM((GROUP, 256, 128), F32)],
-        compiler_params=params(24),
+        scratch_shapes=[pltpu.VMEM((256, 128 * part), F32)],
+        compiler_params=params(32),
         cost_estimate=pl.CostEstimate(flops=10**9, bytes_accessed=24 * 2**20, transcendentals=0),
-    )(rates, reacted, *around, heats)
+    )(diffusivity, reacted, *around, heats)
     return (updated, activity.reshape(1))
 
 

time: 146 us -> 144 us (0.986)
  starting transfers between devices: 97.5 us -> 101 us
  local copies, waits for them, and re-layouts: 4.89 us -> 1.95 us
  waiting for transfers between devices: 13.6 us -> 10.7 us
    ppermute x12, starting transfers between devices: 23.4 us -> 82.3 us  [exchange(): got.append(lax.ppermute(first, axis, [((i + 1) % n, i) for i in range(n)]))]
    ppermute x12, starting transfers between devices: 61 us -> 9.5 us  [exchange(): got.append(lax.ppermute(last, axis, [(i, (i + 1) % n) for i in range(n)]))]
    all_to_all x1, waiting for transfers between devices: 7.89 us -> 2.54 us  [swap(): return lax.all_to_all(tiles, ALL, split_axis=0, concat_axis=0, tiled=True)]
    all_to_all x1, starting transfers between devices: 13 us -> 9.1 us  [swap(): return lax.all_to_all(tiles, ALL, split_axis=0, concat_axis=0, tiled=True)]
    unnamed x38 -> x30, local copies, waits for them, and re-layouts: 4.88 us -> 1.94 us
    pallas_call x2 -> x3, Pallas kernels: 5.59 us -> 6.99 us  [the longest x1 4.36 us: local(): pl.pallas_call(diffuse_kernel, grid=(24 // part,), in_specs=[smem, bricks...]
  transfers between devices with their start and end apart: 25 -> 25, of which waited for: 6 -> 8; matrix products, arithmetic and copies ran while one was open for 0% -> 0% of each run, Pallas kernels for 1% -> 1%
where the time goes in v9:
time: 144 us
  starting transfers between devices  101 us (70%)
  Pallas kernels  29.6 us (21%)
  waiting for transfers between devices  10.7 us (7%)
  local copies, waits for them, and re-layouts  1.95 us (1%)
    ppermute x12, starting transfers between devices, exchange(): got.append(lax.ppermute(first, axis, [((i + 1) % n, i) for i in range(n)]))  82.3 us
    pallas_call x1, Pallas kernels, local(): pl.pallas_call(network_kernel, in_specs=[pl.BlockSpec(memory_space=pltpu....  10.7 us
    pallas_call x3, Pallas kernels, section(): pl.pallas_call(functools.partial(section_kernel, kind), in_specs=[IN_VMEM...  10.3 us
    ppermute x12, starting transfers between devices, exchange(): got.append(lax.ppermute(last, axis, [(i, (i + 1) % n) for i in range(n)]))  9.5 us
    all_to_all x1, starting transfers between devices, swap(): return lax.all_to_all(tiles, ALL, split_axis=0, concat_axis=0, tiled=True)  9.1 us
    ppermute x12, waiting for transfers between devices, exchange(): got.append(lax.ppermute(last, axis, [(i, (i + 1) % n) for i in range(n)]))  4.41 us
    pallas_call x1, Pallas kernels, local(): pl.pallas_call(diffuse_kernel, grid=(24 // part,), in_specs=[smem, bricks...  4.36 us
    ppermute x12, waiting for transfers between devices, exchange(): got.append(lax.ppermute(first, axis, [((i + 1) % n, i) for i in range(n)]))  3.73 us
  transfers between devices with their start and end apart: 25, of which 8 were waited for; matrix products, arithmetic and copies ran while one was open for 0% of the time, Pallas kernels for 1%

profile of v9, /device:TPU:1, one launch (start us, length us, event | category | flops | bytes accessed | tf_op | source)
XLA Modules:
  0.0 144.0 jit_solution(6635193899221265933)
XLA Ops:
  0.6 2.1 %shard_map.140 = (bf16[25,32,128]{2,1,0:T(8,128)(2,1)}, bf16[25,32,128]{2,1,0:T(8,128)(2,1)}) custom-call(f32[24,8,32,128]{3,2,1,0:T(8,128)} %refs_1_.3, f32[3,8,32,128]{3,2,1,0:T(8,128)} %refs_7_.1), custom_call_target="tpu_custom_call" | custom-call | tf_op jit(solution)/shard_map/pallas_call | solution.py:321
  2.7 2.1 %collective-permute-start = (bf16[25,32,128]{2,1,0:T(8,128)(2,1)}, bf16[25,32,128]{2,1,0:T(8,128)(2,1)S(1)}, u32[]{:S(2)}, u32[]{:S(2)}) collective-permute-start(bf16[25,32,128]{2,1,0:T(8,128)(2,1)} %get-tuple-element.47), channel_id=1, source_target_pairs={{0,32},{32,64},{64,96},{96,0},{1,33},{33,65},{65,97},{97,1},{2,34}... | collective-permute-start | bytes 614408 | tf_op jit(solution)/shard_map/ppermute | solution.py:282
  4.8 1.3 collective-permute-start.1
  6.2 0.5 shard_map.141
  6.7 0.0 copy-start.13
  6.8 0.0 copy-start.12
  6.8 1.8 %collective-permute-start.2 = (f32[25,8,128]{2,1,0:T(8,128)S(1)}, f32[25,8,128]{2,1,0:T(8,128)S(1)}, u32[]{:S(2)}, u32[]{:S(2)}) collective-permute-start(f32[25,8,128]{2,1,0:T(8,128)S(1)} %get-tuple-element.49), channel_id=1, source_target_pairs={{0,8},{8,16},{16,24},{24,0},{1,9},{9,17},{17,25},{25,1},{2,10},{10... | collective-permute-start | bytes 307208 | tf_op jit(solution)/shard_map/ppermute | solution.py:282
  8.6 2.2 %collective-permute-start.3 = (f32[25,8,128]{2,1,0:T(8,128)S(1)}, f32[25,8,128]{2,1,0:T(8,128)S(1)}, u32[]{:S(2)}, u32[]{:S(2)}) collective-permute-start(f32[25,8,128]{2,1,0:T(8,128)S(1)} %get-tuple-element.50), channel_id=1, source_target_pairs={{8,0},{16,8},{24,16},{0,24},{9,1},{17,9},{25,17},{1,25},{10,2},{18... | collective-permute-start | bytes 307208 | tf_op jit(solution)/shard_map/ppermute | solution.py:283
  10.8 2.7 %collective-permute-start.4 = (f32[25,256]{1,0:T(8,128)S(1)}, f32[25,256]{1,0:T(8,128)S(1)}, u32[]{:S(2)}, u32[]{:S(2)}) collective-permute-start(f32[25,256]{1,0:T(8,128)S(1)} %get-tuple-element.51), channel_id=1, source_target_pairs={{0,1},{1,2},{2,3},{3,4},{4,5},{5,6},{6,7},{7,0},{8,9},{9,10},{10,1... | collective-permute-start | bytes 76808 | tf_op jit(solution)/shard_map/ppermute | solution.py:282
  13.5 1.0 collective-permute-done.4.refs_5_.refs_12_
  14.5 2.3 %collective-permute-start.5 = (f32[25,256]{1,0:T(8,128)S(1)}, f32[25,256]{1,0:T(8,128)S(1)}, u32[]{:S(2)}, u32[]{:S(2)}) collective-permute-start(f32[25,256]{1,0:T(8,128)S(1)} %get-tuple-element.52), channel_id=1, source_target_pairs={{1,0},{2,1},{3,2},{4,3},{5,4},{6,5},{7,6},{0,7},{9,8},{10,9},{11,1... | collective-permute-start | bytes 76808 | tf_op jit(solution)/shard_map/ppermute | solution.py:283
  16.9 1.6 %collective-permute-done.5.refs_6_.refs_13_ = f32[25,256]{1,0:T(8,128)S(1)} collective-permute-done((f32[25,256]{1,0:T(8,128)S(1)}, f32[25,256]{1,0:T(8,128)S(1)}, u32[]{:S(2)}, u32[]{:S(2)}) %collective-permute-start.5) | collective-permute-done | bytes 25632 | tf_op jit(solution)/shard_map/ppermute | solution.py:283
  18.4 0.0 collective-permute-done.2.refs_3_.refs_10_
  18.4 0.0 collective-permute-done.3.refs_4_.refs_11_
  18.4 0.0 collective-permute-done.refs_1_.refs_8_
  18.4 0.0 collective-permute-done.1.refs_2_.refs_9_
  18.5 3.2 %shard_map.142 = (f32[24,8,32,128]{3,2,1,0:T(8,128)S(1)}, f32[6,8,32,128]{3,2,1,0:T(8,128)S(1)}, bf16[24,32,128]{2,1,0:T(8,128)(2,1)S(1)}, bf16[24,32,128]{2,1,0...) custom-call(f32[24,8,32,128]{3,2,1,0:T(8,128)S(1)} %copy-done, ...), custom_call_target="tpu_custom_call" | custom-call | tf_op jit(solution)/shard_map/pallas_call | solution.py:288
  21.6 0.0 collective-permute-start.6
  21.6 2.7 %collective-permute-start.7 = (bf16[24,32,128]{2,1,0:T(8,128)(2,1)S(1)}, bf16[24,32,128]{2,1,0:T(8,128)(2,1)S(1)}, u32[]{:S(2)}, u32[]{:S(2)}) collective-permute-start(bf16[24,32,128]{2,1,0:T(8,128)(2,1)S(1)} %get-tuple-element.56), channel_id=1, source_target_pairs={{32,0},{64,32},{96,64},{0,96},{33,1},{65,33},{97,65},{1,97},{34,2}... | collective-permute-start | bytes 589832 | tf_op jit(solution)/shard_map/ppermute | solution.py:283
  24.3 0.0 collective-permute-start.8
  24.3 2.7 %collective-permute-start.9 = (f32[24,8,128]{2,1,0:T(8,128)S(1)}, f32[24,8,128]{2,1,0:T(8,128)S(1)}, u32[]{:S(2)}, u32[]{:S(2)}) collective-permute-start(f32[24,8,128]{2,1,0:T(8,128)S(1)} %get-tuple-element.58), channel_id=1, source_target_pairs={{8,0},{16,8},{24,16},{0,24},{9,1},{17,9},{25,17},{1,25},{10,2},{18... | collective-permute-start | bytes 294920 | tf_op jit(solution)/shard_map/ppermute | solution.py:283
  27.0 1.1 collective-permute-start.10
  28.1 0.9 collective-permute-done.10.refs_6_
  29.1 3.5 %collective-permute-start.11 = (f32[24,256]{1,0:T(8,128)S(1)}, f32[24,256]{1,0:T(8,128)S(1)}, u32[]{:S(2)}, u32[]{:S(2)}) collective-permute-start(f32[24,256]{1,0:T(8,128)S(1)} %get-tuple-element.60), channel_id=1, source_target_pairs={{1,0},{2,1},{3,2},{4,3},{5,4},{6,5},{7,6},{0,7},{9,8},{10,9},{11,1... | collective-permute-start | bytes 73736 | tf_op jit(solution)/shard_map/ppermute | solution.py:283
  32.6 0.8 collective-permute-done.11.refs_7_
  33.5 0.0 collective-permute-done.8.refs_4_
  33.5 0.0 collective-permute-done.9.refs_5_
  33.5 0.0 collective-permute-done.6.refs_2_
  33.5 0.0 copy-start.14
  33.5 0.0 copy-start.2
  33.5 0.0 copy-start.3
  33.5 0.0 copy-start.4
  33.5 0.0 copy-start.7
  33.5 0.0 copy-start.8
  33.6 3.7 %shard_map.143 = (f32[24,8,32,128]{3,2,1,0:T(8,128)S(1)}, bf16[24,32,128]{2,1,0:T(8,128)(2,1)S(1)}, bf16[24,32,128]{2,1,0:T(8,128)(2,1)S(1)}, f32[24,8,128]{2,1,...) custom-call(f32[24,8,32,128]{3,2,1,0:T(8,128)S(1)} %get-tuple-element.54.refs_0_, ...), custom_call_target="tpu_custom_call" | custom-call | tf_op jit(solution)/shard_map/pallas_call | solution.py:288
  37.2 0.0 collective-permute-start.16
  37.2 0.7 collective-permute-start.17
  37.9 0.0 collective-permute-start.14
  37.9 2.7 %collective-permute-start.15 = (f32[24,8,128]{2,1,0:T(8,128)S(1)}, f32[24,8,128]{2,1,0:T(8,128)S(1)}, u32[]{:S(2)}, u32[]{:S(2)}) collective-permute-start(f32[24,8,128]{2,1,0:T(8,128)S(1)} %get-tuple-element.66), channel_id=1, source_target_pairs={{8,0},{16,8},{24,16},{0,24},{9,1},{17,9},{25,17},{1,25},{10,2},{18... | collective-permute-start | bytes 294920 | tf_op jit(solution)/shard_map/ppermute | solution.py:283
  40.6 2.7 %collective-permute-start.13 = (bf16[24,32,128]{2,1,0:T(8,128)(2,1)S(1)}, bf16[24,32,128]{2,1,0:T(8,128)(2,1)S(1)}, u32[]{:S(2)}, u32[]{:S(2)}) collective-permute-start(bf16[24,32,128]{2,1,0:T(8,128)(2,1)S(1)} %get-tuple-element.64), channel_id=1, source_target_pairs={{32,0},{64,32},{96,64},{0,96},{33,1},{65,33},{97,65},{1,97},{34,2}... | collective-permute-start | bytes 589832 | tf_op jit(solution)/shard_map/ppermute | solution.py:283
  43.3 1.5 %shard_map.145 = (bf16[1600,32]{1,0:T(8,128)(2,1)S(1)}, bf16[800,1600]{1,0:T(8,128)(2,1)S(1)}, bf16[400,800]{1,0:T(8,128)(2,1)S(1)}, f32[800,128]{1,0:T(8,128)S(...) custom-call(bf16[24,1600]{1,0:T(8,128)(2,1)S(1)} %copy-done.4, f32[1,1600]{1,0:T(1,128)S(1)} %reshape.31.b_in, ...), custom_call_target="tpu_custom_call" | custom-call | bytes 8388608 | tf_op jit(solution)/shard_map/pallas_call | solution.py:346
  44.8 0.0 collective-permute-done.17.refs_7_
  44.8 0.0 collective-permute-done.14.refs_4_
  44.9 1.5 %collective-permute-done.12.refs_2_ = bf16[24,32,128]{2,1,0:T(8,128)(2,1)S(1)} collective-permute-done((bf16[24,32,128]{2,1,0:T(8,128)(2,1)S(1)}, bf16[24,32,128]{2,1,0:T(8,128)(2,1)S(1)}, u32[]{:S(2)}, u32[]{:S(2)}) %collective-permute-start.12) | collective-permute-done | bytes 196640 | tf_op jit(solution)/shard_map/ppermute | solution.py:282
  46.3 3.5 %shard_map.144 = f32[24,8,32,128]{3,2,1,0:T(8,128)S(1)} custom-call(f32[24,8,32,128]{3,2,1,0:T(8,128)S(1)} %get-tuple-element.62.refs_0_, f32[24,8,32,128]{3,2,1,0:T(8,128)S(1)} %copy-done, bf16[24,32,128]{2,1,0:T(8,128)(2,1)S(1)} %collective-permute-done.12.refs_2_, bf16[24,32,128]{2,1,0:T(8,128)(2,1)S(1)} %collective-permute-done.13.refs_3_, ...), custom_call_target="tpu_custom_call" | custom-call | tf_op jit(solution)/shard_map/pallas_call | solution.py:288
  49.9 10.7 %shard_map.146 = (f32[6144,128]{1,0:T(8,128)S(1)}, f32[128,128]{1,0:T(8,128)S(1)}, bf16[24,32,128]{2,1,0:T(8,128)(2,1)}, bf16[24,32,128]{2,1,0:T(8,128)(2,1)}, f...) custom-call(s32[1,96]{1,0:T(1,128)S(1)} %copy-done.9, ...), custom_call_target="tpu_custom_call" | custom-call | tf_op jit(solution)/shard_map/pallas_call | solution.py:359
  60.6 0.6 copy-done.5
  61.2 0.6 copy-done.11
  61.9 0.0 collective-permute-start.18
  61.9 55.7 %collective-permute-start.19 = (bf16[24,32,128]{2,1,0:T(8,128)(2,1)}, bf16[24,32,128]{2,1,0:T(8,128)(2,1)}, u32[]{:S(2)}, u32[]{:S(2)}) collective-permute-start(bf16[24,32,128]{2,1,0:T(8,128)(2,1)} %get-tuple-element.84), channel_id=1, source_target_pairs={{32,0},{64,32},{96,64},{0,96},{33,1},{65,33},{97,65},{1,97},{34,2}... | collective-permute-start | bytes 589832 | tf_op jit(solution)/shard_map/ppermute | solution.py:283
  117.6 0.0 collective-permute-start.20
  117.6 2.7 %collective-permute-start.21 = (f32[24,8,128]{2,1,0:T(8,128)}, f32[24,8,128]{2,1,0:T(8,128)}, u32[]{:S(2)}, u32[]{:S(2)}) collective-permute-start(f32[24,8,128]{2,1,0:T(8,128)} %get-tuple-element.86), channel_id=1, source_target_pairs={{8,0},{16,8},{24,16},{0,24},{9,1},{17,9},{25,17},{1,25},{10,2},{18... | collective-permute-start | bytes 294920 | tf_op jit(solution)/shard_map/ppermute | solution.py:283
  120.3 9.1 %all-to-all-start = ((f32[128,1,128]{2,1,0:T(1,128)}), f32[128,1,128]{2,1,0:T(1,128)S(1)}, u32[]{:S(2)}, u32[]{:S(2)}) async-start(f32[128,1,128]{2,1,0:T(1,128)} %bitcast.18), calls=%async_computation | async-start | bytes 131072 | tf_op jit(solution)/shard_map/all_to_all | solution.py:299
  129.4 1.7 %collective-permute-start.22 = (f32[24,256]{1,0:T(8,128)S(1)}, f32[24,256]{1,0:T(8,128)S(1)}, u32[]{:S(2)}, u32[]{:S(2)}) collective-permute-start(f32[24,256]{1,0:T(8,128)S(1)} %get-tuple-element.87), channel_id=1, source_target_pairs={{0,1},{1,2},{2,3},{3,4},{4,5},{5,6},{6,7},{7,0},{8,9},{9,10},{10,1... | collective-permute-start | bytes 73736 | tf_op jit(solution)/shard_map/ppermute | solution.py:282
  131.1 0.9 collective-permute-done.22.zlo
  132.0 3.1 %collective-permute-start.23 = (f32[24,256]{1,0:T(8,128)}, f32[24,256]{1,0:T(8,128)S(1)}, u32[]{:S(2)}, u32[]{:S(2)}) collective-permute-start(f32[24,256]{1,0:T(8,128)} %copy-done.11), channel_id=1, source_target_pairs={{1,0},{2,1},{3,2},{4,3},{5,4},{6,5},{7,6},{0,7},{9,8},{10,9},{11,1... | collective-permute-start | bytes 73736 | tf_op jit(solution)/shard_map/ppermute | solution.py:283
  135.1 1.3 collective-permute-done.23.zhi
  136.4 2.5 %all-to-all-done = f32[128,1,128]{2,1,0:T(1,128)S(1)} async-done(((f32[128,1,128]{2,1,0:T(1,128)}), f32[128,1,128]{2,1,0:T(1,128)S(1)}, u32[]{:S(2)}, u32[]{:S(2)}) %all-to-all-start) | async-done | bytes 65568 | tf_op jit(solution)/shard_map/all_to_all | solution.py:299
  139.0 0.0 collective-permute-done.20.ylo
  139.0 0.0 collective-permute-done.21.yhi
  139.0 0.0 collective-permute-done.18.xlo
  139.0 0.0 copy-start.10
  139.0 0.6 copy-done.10
  139.7 4.4 %shard_map.147 = (f32[24,8,32,128]{3,2,1,0:T(8,128)}, f32[1,1]{1,0:T(1,128)}) custom-call(f32[24]{0:T(128)S(1)} %copy-done.10, f32[24,8,32,128]{3,2,1,0:T(8,128)S(1)} %bitcast.14, bf16[24,32,128]{2,1,0:T(8,128)(2,1)S(1)} %collective-permute-done.18.xlo, bf16[24,32,128]{2,1,0:T(8,128)(2,1)} %collective-permute-done.19.xhi, ...), custom_call_target="tpu_custom_call" | custom-call | flops 1000000000 | bytes 25165824 | tf_op jit(solution)/shard_map/pallas_call | solution.py:376
  (27 shorter events, 0.1 us)
Async XLA Ops:
  0.6 5.6 %copy-start = (f32[24,8,32,128]{3,2,1,0:T(8,128)S(1)}, f32[24,8,32,128]{3,2,1,0:T(8,128)}, u32[]{:S(2)}) copy-start(f32[24,8,32,128]{3,2,1,0:T(8,128)} %refs_1_.3) | copy-start | bytes 9437188
  0.6 5.6 %copy-start.1 = (f32[3,8,32,128]{3,2,1,0:T(8,128)S(1)}, f32[3,8,32,128]{3,2,1,0:T(8,128)}, u32[]{:S(2)}) copy-start(f32[3,8,32,128]{3,2,1,0:T(8,128)} %refs_7_.1) | copy-start | bytes 1179652
  2.7 15.7 %collective-permute-start = (bf16[25,32,128]{2,1,0:T(8,128)(2,1)}, bf16[25,32,128]{2,1,0:T(8,128)(2,1)S(1)}, u32[]{:S(2)}, u32[]{:S(2)}) collective-permute-start(bf16[25,32,128]{2,1,0:T(8,128)(2,1)} %get-tuple-element.47), channel_id=1, source_target_pairs={{0,32},{32,64},{64,96},{96,0},{1,33},{33,65},{65,97},{97,1},{2,34}... | collective-permute-start | bytes 614408 | tf_op jit(solution)/shard_map/ppermute | solution.py:282
  4.8 13.6 %collective-permute-start.1 = (bf16[25,32,128]{2,1,0:T(8,128)(2,1)}, bf16[25,32,128]{2,1,0:T(8,128)(2,1)S(1)}, u32[]{:S(2)}, u32[]{:S(2)}) collective-permute-start(bf16[25,32,128]{2,1,0:T(8,128)(2,1)} %get-tuple-element.48), channel_id=1, source_target_pairs={{32,0},{64,32},{96,64},{0,96},{33,1},{65,33},{97,65},{1,97},{34,2}... | collective-permute-start | bytes 614408 | tf_op jit(solution)/shard_map/ppermute | solution.py:283
  6.7 25.9 %copy-start.13 = (f32[800]{0:T(1024)S(1)}, f32[800]{0:T(1024)}, u32[]{:S(2)}) copy-start(f32[800]{0:T(1024)} %param.19) | copy-start | bytes 9604
  6.8 25.9 %copy-start.12 = (f32[1600]{0:T(1024)S(1)}, f32[1600]{0:T(1024)}, u32[]{:S(2)}) copy-start(f32[1600]{0:T(1024)} %param.17) | copy-start | bytes 19204
  6.8 11.7 %collective-permute-start.2 = (f32[25,8,128]{2,1,0:T(8,128)S(1)}, f32[25,8,128]{2,1,0:T(8,128)S(1)}, u32[]{:S(2)}, u32[]{:S(2)}) collective-permute-start(f32[25,8,128]{2,1,0:T(8,128)S(1)} %get-tuple-element.49), channel_id=1, source_target_pairs={{0,8},{8,16},{16,24},{24,0},{1,9},{9,17},{17,25},{25,1},{2,10},{10... | collective-permute-start | bytes 307208 | tf_op jit(solution)/shard_map/ppermute | solution.py:282
  8.6 9.8 %collective-permute-start.3 = (f32[25,8,128]{2,1,0:T(8,128)S(1)}, f32[25,8,128]{2,1,0:T(8,128)S(1)}, u32[]{:S(2)}, u32[]{:S(2)}) collective-permute-start(f32[25,8,128]{2,1,0:T(8,128)S(1)} %get-tuple-element.50), channel_id=1, source_target_pairs={{8,0},{16,8},{24,16},{0,24},{9,1},{17,9},{25,17},{1,25},{10,2},{18... | collective-permute-start | bytes 307208 | tf_op jit(solution)/shard_map/ppermute | solution.py:283
  10.8 3.7 %collective-permute-start.4 = (f32[25,256]{1,0:T(8,128)S(1)}, f32[25,256]{1,0:T(8,128)S(1)}, u32[]{:S(2)}, u32[]{:S(2)}) collective-permute-start(f32[25,256]{1,0:T(8,128)S(1)} %get-tuple-element.51), channel_id=1, source_target_pairs={{0,1},{1,2},{2,3},{3,4},{4,5},{5,6},{6,7},{7,0},{8,9},{9,10},{10,1... | collective-permute-start | bytes 76808 | tf_op jit(solution)/shard_map/ppermute | solution.py:282
  14.5 3.9 %collective-permute-start.5 = (f32[25,256]{1,0:T(8,128)S(1)}, f32[25,256]{1,0:T(8,128)S(1)}, u32[]{:S(2)}, u32[]{:S(2)}) collective-permute-start(f32[25,256]{1,0:T(8,128)S(1)} %get-tuple-element.52), channel_id=1, source_target_pairs={{1,0},{2,1},{3,2},{4,3},{5,4},{6,5},{7,6},{0,7},{9,8},{10,9},{11,1... | collective-permute-start | bytes 76808 | tf_op jit(solution)/shard_map/ppermute | solution.py:283
  21.6 11.8 %collective-permute-start.6 = (bf16[24,32,128]{2,1,0:T(8,128)(2,1)S(1)}, bf16[24,32,128]{2,1,0:T(8,128)(2,1)S(1)}, u32[]{:S(2)}, u32[]{:S(2)}) collective-permute-start(bf16[24,32,128]{2,1,0:T(8,128)(2,1)S(1)} %get-tuple-element.55), channel_id=1, source_target_pairs={{0,32},{32,64},{64,96},{96,0},{1,33},{33,65},{65,97},{97,1},{2,34}... | collective-permute-start | bytes 589832 | tf_op jit(solution)/shard_map/ppermute | solution.py:282
  21.6 11.8 %collective-permute-start.7 = (bf16[24,32,128]{2,1,0:T(8,128)(2,1)S(1)}, bf16[24,32,128]{2,1,0:T(8,128)(2,1)S(1)}, u32[]{:S(2)}, u32[]{:S(2)}) collective-permute-start(bf16[24,32,128]{2,1,0:T(8,128)(2,1)S(1)} %get-tuple-element.56), channel_id=1, source_target_pairs={{32,0},{64,32},{96,64},{0,96},{33,1},{65,33},{97,65},{1,97},{34,2}... | collective-permute-start | bytes 589832 | tf_op jit(solution)/shard_map/ppermute | solution.py:283
  24.3 9.1 %collective-permute-start.8 = (f32[24,8,128]{2,1,0:T(8,128)S(1)}, f32[24,8,128]{2,1,0:T(8,128)S(1)}, u32[]{:S(2)}, u32[]{:S(2)}) collective-permute-start(f32[24,8,128]{2,1,0:T(8,128)S(1)} %get-tuple-element.57), channel_id=1, source_target_pairs={{0,8},{8,16},{16,24},{24,0},{1,9},{9,17},{17,25},{25,1},{2,10},{10... | collective-permute-start | bytes 294920 | tf_op jit(solution)/shard_map/ppermute | solution.py:282
  24.3 9.1 %collective-permute-start.9 = (f32[24,8,128]{2,1,0:T(8,128)S(1)}, f32[24,8,128]{2,1,0:T(8,128)S(1)}, u32[]{:S(2)}, u32[]{:S(2)}) collective-permute-start(f32[24,8,128]{2,1,0:T(8,128)S(1)} %get-tuple-element.58), channel_id=1, source_target_pairs={{8,0},{16,8},{24,16},{0,24},{9,1},{17,9},{25,17},{1,25},{10,2},{18... | collective-permute-start | bytes 294920 | tf_op jit(solution)/shard_map/ppermute | solution.py:283
  27.0 2.1 %collective-permute-start.10 = (f32[24,256]{1,0:T(8,128)S(1)}, f32[24,256]{1,0:T(8,128)S(1)}, u32[]{:S(2)}, u32[]{:S(2)}) collective-permute-start(f32[24,256]{1,0:T(8,128)S(1)} %get-tuple-element.59), channel_id=1, source_target_pairs={{0,1},{1,2},{2,3},{3,4},{4,5},{5,6},{6,7},{7,0},{8,9},{9,10},{10,1... | collective-permute-start | bytes 73736 | tf_op jit(solution)/shard_map/ppermute | solution.py:282
  29.1 4.4 %collective-permute-start.11 = (f32[24,256]{1,0:T(8,128)S(1)}, f32[24,256]{1,0:T(8,128)S(1)}, u32[]{:S(2)}, u32[]{:S(2)}) collective-permute-start(f32[24,256]{1,0:T(8,128)S(1)} %get-tuple-element.60), channel_id=1, source_target_pairs={{1,0},{2,1},{3,2},{4,3},{5,4},{6,5},{7,6},{0,7},{9,8},{10,9},{11,1... | collective-permute-start | bytes 73736 | tf_op jit(solution)/shard_map/ppermute | solution.py:283
  33.5 9.8 %copy-start.14 = (s32[1,96]{1,0:T(1,128)S(1)}, s32[1,96]{1,0:T(1,128)}, u32[]{:S(2)}) copy-start(s32[1,96]{1,0:T(1,128)} %param.25) | copy-start | bytes 1156
  33.5 9.8 %copy-start.2 = (bf16[1600,800]{0,1:T(8,128)(2,1)S(1)}, bf16[1600,800]{0,1:T(8,128)(2,1)}, u32[]{:S(2)}) copy-start(bf16[1600,800]{0,1:T(8,128)(2,1)} %param.18) | copy-start | bytes 7680004
  33.5 9.8 %copy-start.3 = (bf16[800,400]{0,1:T(8,128)(2,1)S(1)}, bf16[800,400]{0,1:T(8,128)(2,1)}, u32[]{:S(2)}) copy-start(bf16[800,400]{0,1:T(8,128)(2,1)} %param.20) | copy-start | bytes 1920004
  33.5 9.8 %copy-start.4 = (bf16[24,1600]{1,0:T(8,128)(2,1)S(1)}, bf16[24,1600]{1,0:T(8,128)(2,1)}, u32[]{:S(2)}) copy-start(bf16[24,1600]{1,0:T(8,128)(2,1)} %w_in) | copy-start | bytes 230404
  33.5 9.8 %copy-start.7 = (f32[400]{0:T(512)S(1)}, f32[400]{0:T(512)}, u32[]{:S(2)}) copy-start(f32[400]{0:T(512)} %param.21) | copy-start | bytes 4804
  33.5 9.8 %copy-start.8 = (f32[24]{0:T(128)S(1)}, f32[24]{0:T(128)}, u32[]{:S(2)}) copy-start(f32[24]{0:T(128)} %param.23) | copy-start | bytes 292
  37.2 3.4 %collective-permute-start.16 = (f32[24,256]{1,0:T(8,128)S(1)}, f32[24,256]{1,0:T(8,128)S(1)}, u32[]{:S(2)}, u32[]{:S(2)}) collective-permute-start(f32[24,256]{1,0:T(8,128)S(1)} %get-tuple-element.67), channel_id=1, source_target_pairs={{0,1},{1,2},{2,3},{3,4},{4,5},{5,6},{6,7},{7,0},{8,9},{9,10},{10,1... | collective-permute-start | bytes 73736 | tf_op jit(solution)/shard_map/ppermute | solution.py:282
  37.2 7.6 %collective-permute-start.17 = (f32[24,256]{1,0:T(8,128)S(1)}, f32[24,256]{1,0:T(8,128)S(1)}, u32[]{:S(2)}, u32[]{:S(2)}) collective-permute-start(f32[24,256]{1,0:T(8,128)S(1)} %get-tuple-element.68), channel_id=1, source_target_pairs={{1,0},{2,1},{3,2},{4,3},{5,4},{6,5},{7,6},{0,7},{9,8},{10,9},{11,1... | collective-permute-start | bytes 73736 | tf_op jit(solution)/shard_map/ppermute | solution.py:283
  37.9 6.9 %collective-permute-start.14 = (f32[24,8,128]{2,1,0:T(8,128)S(1)}, f32[24,8,128]{2,1,0:T(8,128)S(1)}, u32[]{:S(2)}, u32[]{:S(2)}) collective-permute-start(f32[24,8,128]{2,1,0:T(8,128)S(1)} %get-tuple-element.65), channel_id=1, source_target_pairs={{0,8},{8,16},{16,24},{24,0},{1,9},{9,17},{17,25},{25,1},{2,10},{10... | collective-permute-start | bytes 294920 | tf_op jit(solution)/shard_map/ppermute | solution.py:282
  37.9 6.9 %collective-permute-start.15 = (f32[24,8,128]{2,1,0:T(8,128)S(1)}, f32[24,8,128]{2,1,0:T(8,128)S(1)}, u32[]{:S(2)}, u32[]{:S(2)}) collective-permute-start(f32[24,8,128]{2,1,0:T(8,128)S(1)} %get-tuple-element.66), channel_id=1, source_target_pairs={{8,0},{16,8},{24,16},{0,24},{9,1},{17,9},{25,17},{1,25},{10,2},{18... | collective-permute-start | bytes 294920 | tf_op jit(solution)/shard_map/ppermute | solution.py:283
  40.6 5.7 %collective-permute-start.12 = (bf16[24,32,128]{2,1,0:T(8,128)(2,1)S(1)}, bf16[24,32,128]{2,1,0:T(8,128)(2,1)S(1)}, u32[]{:S(2)}, u32[]{:S(2)}) collective-permute-start(bf16[24,32,128]{2,1,0:T(8,128)(2,1)S(1)} %get-tuple-element.63), channel_id=1, source_target_pairs={{0,32},{32,64},{64,96},{96,0},{1,33},{33,65},{65,97},{97,1},{2,34}... | collective-permute-start | bytes 589832 | tf_op jit(solution)/shard_map/ppermute | solution.py:282
  40.6 5.7 %collective-permute-start.13 = (bf16[24,32,128]{2,1,0:T(8,128)(2,1)S(1)}, bf16[24,32,128]{2,1,0:T(8,128)(2,1)S(1)}, u32[]{:S(2)}, u32[]{:S(2)}) collective-permute-start(bf16[24,32,128]{2,1,0:T(8,128)(2,1)S(1)} %get-tuple-element.64), channel_id=1, source_target_pairs={{32,0},{64,32},{96,64},{0,96},{33,1},{65,33},{97,65},{1,97},{34,2}... | collective-permute-start | bytes 589832 | tf_op jit(solution)/shard_map/ppermute | solution.py:283
  46.3 3.5 %copy-start.6 = (bf16[400,24]{0,1:T(8,128)(2,1)S(1)}, bf16[400,24]{0,1:T(8,128)(2,1)}, u32[]{:S(2)}) copy-start(bf16[400,24]{0,1:T(8,128)(2,1)} %param.22) | copy-start | bytes 57604
  46.3 3.6 %copy-start.9 = (s32[1,96]{1,0:T(1,128)S(1)}, s32[1,96]{1,0:T(1,128)}, u32[]{:S(2)}) copy-start(s32[1,96]{1,0:T(1,128)} %listed.1) | copy-start | bytes 1156
  60.6 0.6 copy-start.5
  61.2 0.6 copy-start.11
  61.9 77.1 %collective-permute-start.18 = (bf16[24,32,128]{2,1,0:T(8,128)(2,1)}, bf16[24,32,128]{2,1,0:T(8,128)(2,1)S(1)}, u32[]{:S(2)}, u32[]{:S(2)}) collective-permute-start(bf16[24,32,128]{2,1,0:T(8,128)(2,1)} %get-tuple-element.83), channel_id=1, source_target_pairs={{0,32},{32,64},{64,96},{96,0},{1,33},{33,65},{65,97},{97,1},{2,34}... | collective-permute-start | bytes 589832 | tf_op jit(solution)/shard_map/ppermute | solution.py:282
  61.9 77.1 %collective-permute-start.19 = (bf16[24,32,128]{2,1,0:T(8,128)(2,1)}, bf16[24,32,128]{2,1,0:T(8,128)(2,1)}, u32[]{:S(2)}, u32[]{:S(2)}) collective-permute-start(bf16[24,32,128]{2,1,0:T(8,128)(2,1)} %get-tuple-element.84), channel_id=1, source_target_pairs={{32,0},{64,32},{96,64},{0,96},{33,1},{65,33},{97,65},{1,97},{34,2}... | collective-permute-start | bytes 589832 | tf_op jit(solution)/shard_map/ppermute | solution.py:283
  117.6 21.4 %collective-permute-start.20 = (f32[24,8,128]{2,1,0:T(8,128)}, f32[24,8,128]{2,1,0:T(8,128)S(1)}, u32[]{:S(2)}, u32[]{:S(2)}) collective-permute-start(f32[24,8,128]{2,1,0:T(8,128)} %get-tuple-element.85), channel_id=1, source_target_pairs={{0,8},{8,16},{16,24},{24,0},{1,9},{9,17},{17,25},{25,1},{2,10},{10... | collective-permute-start | bytes 294920 | tf_op jit(solution)/shard_map/ppermute | solution.py:282
  117.6 21.4 %collective-permute-start.21 = (f32[24,8,128]{2,1,0:T(8,128)}, f32[24,8,128]{2,1,0:T(8,128)}, u32[]{:S(2)}, u32[]{:S(2)}) collective-permute-start(f32[24,8,128]{2,1,0:T(8,128)} %get-tuple-element.86), channel_id=1, source_target_pairs={{8,0},{16,8},{24,16},{0,24},{9,1},{17,9},{25,17},{1,25},{10,2},{18... | collective-permute-start | bytes 294920 | tf_op jit(solution)/shard_map/ppermute | solution.py:283
  120.3 18.7 %all-to-all-start = ((f32[128,1,128]{2,1,0:T(1,128)}), f32[128,1,128]{2,1,0:T(1,128)S(1)}, u32[]{:S(2)}, u32[]{:S(2)}) async-start(f32[128,1,128]{2,1,0:T(1,128)} %bitcast.18), calls=%async_computation | async-start | bytes 131072 | tf_op jit(solution)/shard_map/all_to_all | solution.py:299
  129.4 2.6 %collective-permute-start.22 = (f32[24,256]{1,0:T(8,128)S(1)}, f32[24,256]{1,0:T(8,128)S(1)}, u32[]{:S(2)}, u32[]{:S(2)}) collective-permute-start(f32[24,256]{1,0:T(8,128)S(1)} %get-tuple-element.87), channel_id=1, source_target_pairs={{0,1},{1,2},{2,3},{3,4},{4,5},{5,6},{6,7},{7,0},{8,9},{9,10},{10,1... | collective-permute-start | bytes 73736 | tf_op jit(solution)/shard_map/ppermute | solution.py:282
  132.0 4.4 %collective-permute-start.23 = (f32[24,256]{1,0:T(8,128)}, f32[24,256]{1,0:T(8,128)S(1)}, u32[]{:S(2)}, u32[]{:S(2)}) collective-permute-start(f32[24,256]{1,0:T(8,128)} %copy-done.11), channel_id=1, source_target_pairs={{1,0},{2,1},{3,2},{4,3},{5,4},{6,5},{7,6},{0,7},{9,8},{10,9},{11,1... | collective-permute-start | bytes 73736 | tf_op jit(solution)/shard_map/ppermute | solution.py:283
  139.0 0.7 copy-start.10

commit v10 on v9

--- a/solution.py
+++ b/solution.py
@@ -160,11 +160,11 @@
             put_z_faces(out, f, zf, zl)
 
 
-def diffuse_kernel(rates, q, xlo, xhi, ylo, yhi, zlo, zhi, heats, out, activity, zcol):
-    @pl.when(pl.program_id(0) == 0)
-    def _():
-        activity[0, 0] = jnp.sum(heats[...]) * (1.0 / (8.0 * 128.0))
-
+def activity_kernel(heats, activity):
+    activity[0, 0] = jnp.sum(heats[...]) * (1.0 / (8.0 * 128.0))
+
+
+def diffuse_kernel(rates, q, xlo, xhi, ylo, yhi, zlo, zhi, out, zcol):
     zcol[...] = all_z_columns(zlo[...], zhi[...])
     for f in range(LAST_GROUP):
         rate = rates[pl.program_id(0) * LAST_GROUP + f]
@@ -365,7 +365,9 @@
         compiler_params=params(NETWORK_MIB),
     )(react_list, flowed.reshape(24 * 256, 128), owned_by, *columns, weight_out.T)
     reacted = reacted.reshape(fields.shape)
-    around = exchange(faces)
+    x_and_y = exchange(faces[:4])
+    *z_faces, x_and_y[0], x_and_y[1] = lax.optimization_barrier((*faces[4:], *x_and_y[:2]))
+    around = x_and_y + exchange(z_faces, ALL[2:])
     heats = swap(sent.reshape(128, 1, 128)).reshape(128, 128)
     part = LAST_GROUP
     bricks = pl.BlockSpec((part, 8, 32, 128), lambda g: (g, 0, 0, 0))
@@ -373,17 +375,18 @@
     y_part = pl.BlockSpec((part, 8, 128), lambda g: (g, 0, 0))
     z_part = pl.BlockSpec((part, 256), lambda g: (g, 0))
     smem = pl.BlockSpec(memory_space=pltpu.SMEM)
-    updated, activity = pl.pallas_call(
+    updated = pl.pallas_call(
         diffuse_kernel,
         grid=(24 // part,),
-        in_specs=[smem, bricks, x_part, x_part, y_part, y_part, z_part, z_part]
-        + [pl.BlockSpec((128, 128), lambda g: (0, 0))],
-        out_specs=[bricks, smem],
-        out_shape=[brick, sds((1, 1), F32)],
+        in_specs=[smem, bricks, x_part, x_part, y_part, y_part, z_part, z_part],
+        out_specs=bricks,
+        out_shape=brick,
         scratch_shapes=[pltpu.VMEM((256, 128 * part), F32)],
         compiler_params=params(32),
-        cost_estimate=pl.CostEstimate(flops=10**9, bytes_accessed=24 * 2**20, transcendentals=0),
-    )(diffusivity, reacted, *around, heats)
+        cost_estimate=pl.CostEstimate(flops=10**7, bytes_accessed=6 * 2**20, transcendentals=0),
+    )(diffusivity, reacted, *around)
+    heats, updated = lax.optimization_barrier((heats, updated))
+    activity = pl.pallas_call(activity_kernel, out_specs=smem, out_shape=sds((1, 1), F32))(heats)
     return (updated, activity.reshape(1))
 
 

time: 144 us -> 141 us (0.979)
  starting transfers between devices: 101 us -> 89.7 us
  Pallas kernels: 29.6 us -> 38.4 us
    ppermute x12, starting transfers between devices: 82.3 us -> 25 us  [exchange(): got.append(lax.ppermute(first, axis, [((i + 1) % n, i) for i in range(n)]))]
    ppermute x12, starting transfers between devices: 9.5 us -> 53.8 us  [exchange(): got.append(lax.ppermute(last, axis, [(i, (i + 1) % n) for i in range(n)]))]
    pallas_call x1, Pallas kernels: 10.7 us -> 18.3 us  [local(): pl.pallas_call(network_kernel, in_specs=[pl.BlockSpec(memory_space=pltpu....]
    all_to_all x1, waiting for transfers between devices: 2.54 us -> 0.01 us  [swap(): return lax.all_to_all(tiles, ALL, split_axis=0, concat_axis=0, tiled=True)]
    all_to_all x1, starting transfers between devices: 9.1 us -> 10.9 us  [swap(): return lax.all_to_all(tiles, ALL, split_axis=0, concat_axis=0, tiled=True)]
    pallas_call x0 -> x1, Pallas kernels: none -> 1.49 us  [local(): pl.pallas_call(activity_kernel, out_specs=smem, out_shape=sds((1, 1), F32))]
  transfers between devices with their start and end apart: 25 -> 25, of which waited for: 8 -> 7; matrix products, arithmetic and copies ran while one was open for 0% -> 0% of each run, Pallas kernels for 1% -> 4%
where the time goes in v10:
time: 141 us
  starting transfers between devices  89.7 us (64%)
  Pallas kernels  38.4 us (27%)
  waiting for transfers between devices  9.75 us (7%)
  local copies, waits for them, and re-layouts  1.9 us (1%)
    ppermute x12, starting transfers between devices, exchange(): got.append(lax.ppermute(last, axis, [(i, (i + 1) % n) for i in range(n)]))  53.8 us
    ppermute x12, starting transfers between devices, exchange(): got.append(lax.ppermute(first, axis, [((i + 1) % n, i) for i in range(n)]))  25 us
    pallas_call x1, Pallas kernels, local(): pl.pallas_call(network_kernel, in_specs=[pl.BlockSpec(memory_space=pltpu....  18.3 us
    all_to_all x1, starting transfers between devices, swap(): return lax.all_to_all(tiles, ALL, split_axis=0, concat_axis=0, tiled=True)  10.9 us
    pallas_call x3, Pallas kernels, section(): pl.pallas_call(functools.partial(section_kernel, kind), in_specs=[IN_VMEM...  10.3 us
    ppermute x12, waiting for transfers between devices, exchange(): got.append(lax.ppermute(first, axis, [((i + 1) % n, i) for i in range(n)]))  5.15 us
    ppermute x12, waiting for transfers between devices, exchange(): got.append(lax.ppermute(last, axis, [(i, (i + 1) % n) for i in range(n)]))  4.6 us
    pallas_call x1, Pallas kernels, local(): pl.pallas_call(diffuse_kernel, grid=(24 // part,), in_specs=[smem, bricks...  4.14 us
  transfers between devices with their start and end apart: 25, of which 7 were waited for; matrix products, arithmetic and copies ran while one was open for 0% of the time, Pallas kernels for 4%

profile of v10, /device:TPU:1, one launch (start us, length us, event | category | flops | bytes accessed | tf_op | source)
XLA Modules:
  0.0 140.8 jit_solution(7388773478947196641)
XLA Ops:
  0.6 2.1 %shard_map.140 = (bf16[25,32,128]{2,1,0:T(8,128)(2,1)}, bf16[25,32,128]{2,1,0:T(8,128)(2,1)}) custom-call(f32[24,8,32,128]{3,2,1,0:T(8,128)} %refs_1_.3, f32[3,8,32,128]{3,2,1,0:T(8,128)} %refs_7_.1), custom_call_target="tpu_custom_call" | custom-call | tf_op jit(solution)/shard_map/pallas_call | solution.py:321
  2.7 2.1 %collective-permute-start = (bf16[25,32,128]{2,1,0:T(8,128)(2,1)}, bf16[25,32,128]{2,1,0:T(8,128)(2,1)S(1)}, u32[]{:S(2)}, u32[]{:S(2)}) collective-permute-start(bf16[25,32,128]{2,1,0:T(8,128)(2,1)} %get-tuple-element.51), channel_id=1, source_target_pairs={{0,32},{32,64},{64,96},{96,0},{1,33},{33,65},{65,97},{97,1},{2,34}... | collective-permute-start | bytes 614408 | tf_op jit(solution)/shard_map/ppermute | solution.py:282
  4.8 1.3 collective-permute-start.1
  6.2 0.5 shard_map.141
  6.7 0.0 copy-start.14
  6.8 0.0 copy-start.13
  6.8 1.8 %collective-permute-start.2 = (f32[25,8,128]{2,1,0:T(8,128)S(1)}, f32[25,8,128]{2,1,0:T(8,128)S(1)}, u32[]{:S(2)}, u32[]{:S(2)}) collective-permute-start(f32[25,8,128]{2,1,0:T(8,128)S(1)} %get-tuple-element.53), channel_id=1, source_target_pairs={{0,8},{8,16},{16,24},{24,0},{1,9},{9,17},{17,25},{25,1},{2,10},{10... | collective-permute-start | bytes 307208 | tf_op jit(solution)/shard_map/ppermute | solution.py:282
  8.6 2.2 %collective-permute-start.3 = (f32[25,8,128]{2,1,0:T(8,128)S(1)}, f32[25,8,128]{2,1,0:T(8,128)S(1)}, u32[]{:S(2)}, u32[]{:S(2)}) collective-permute-start(f32[25,8,128]{2,1,0:T(8,128)S(1)} %get-tuple-element.54), channel_id=1, source_target_pairs={{8,0},{16,8},{24,16},{0,24},{9,1},{17,9},{25,17},{1,25},{10,2},{18... | collective-permute-start | bytes 307208 | tf_op jit(solution)/shard_map/ppermute | solution.py:283
  10.8 2.7 %collective-permute-start.4 = (f32[25,256]{1,0:T(8,128)S(1)}, f32[25,256]{1,0:T(8,128)S(1)}, u32[]{:S(2)}, u32[]{:S(2)}) collective-permute-start(f32[25,256]{1,0:T(8,128)S(1)} %get-tuple-element.55), channel_id=1, source_target_pairs={{0,1},{1,2},{2,3},{3,4},{4,5},{5,6},{6,7},{7,0},{8,9},{9,10},{10,1... | collective-permute-start | bytes 76808 | tf_op jit(solution)/shard_map/ppermute | solution.py:282
  13.5 1.0 collective-permute-done.4.refs_5_.refs_12_
  14.5 2.3 %collective-permute-start.5 = (f32[25,256]{1,0:T(8,128)S(1)}, f32[25,256]{1,0:T(8,128)S(1)}, u32[]{:S(2)}, u32[]{:S(2)}) collective-permute-start(f32[25,256]{1,0:T(8,128)S(1)} %get-tuple-element.56), channel_id=1, source_target_pairs={{1,0},{2,1},{3,2},{4,3},{5,4},{6,5},{7,6},{0,7},{9,8},{10,9},{11,1... | collective-permute-start | bytes 76808 | tf_op jit(solution)/shard_map/ppermute | solution.py:283
  16.9 1.6 %collective-permute-done.5.refs_6_.refs_13_ = f32[25,256]{1,0:T(8,128)S(1)} collective-permute-done((f32[25,256]{1,0:T(8,128)S(1)}, f32[25,256]{1,0:T(8,128)S(1)}, u32[]{:S(2)}, u32[]{:S(2)}) %collective-permute-start.5) | collective-permute-done | bytes 25632 | tf_op jit(solution)/shard_map/ppermute | solution.py:283
  18.4 0.0 collective-permute-done.2.refs_3_.refs_10_
  18.4 0.0 collective-permute-done.3.refs_4_.refs_11_
  18.4 0.0 collective-permute-done.refs_1_.refs_8_
  18.4 0.0 collective-permute-done.1.refs_2_.refs_9_
  18.5 3.2 %shard_map.142 = (f32[24,8,32,128]{3,2,1,0:T(8,128)S(1)}, f32[6,8,32,128]{3,2,1,0:T(8,128)S(1)}, bf16[24,32,128]{2,1,0:T(8,128)(2,1)S(1)}, bf16[24,32,128]{2,1,0...) custom-call(f32[24,8,32,128]{3,2,1,0:T(8,128)S(1)} %copy-done, ...), custom_call_target="tpu_custom_call" | custom-call | tf_op jit(solution)/shard_map/pallas_call | solution.py:288
  21.6 0.0 collective-permute-start.6
  21.6 2.7 %collective-permute-start.7 = (bf16[24,32,128]{2,1,0:T(8,128)(2,1)S(1)}, bf16[24,32,128]{2,1,0:T(8,128)(2,1)S(1)}, u32[]{:S(2)}, u32[]{:S(2)}) collective-permute-start(bf16[24,32,128]{2,1,0:T(8,128)(2,1)S(1)} %get-tuple-element.60), channel_id=1, source_target_pairs={{32,0},{64,32},{96,64},{0,96},{33,1},{65,33},{97,65},{1,97},{34,2}... | collective-permute-start | bytes 589832 | tf_op jit(solution)/shard_map/ppermute | solution.py:283
  24.3 0.0 collective-permute-start.8
  24.3 2.7 %collective-permute-start.9 = (f32[24,8,128]{2,1,0:T(8,128)S(1)}, f32[24,8,128]{2,1,0:T(8,128)S(1)}, u32[]{:S(2)}, u32[]{:S(2)}) collective-permute-start(f32[24,8,128]{2,1,0:T(8,128)S(1)} %get-tuple-element.62), channel_id=1, source_target_pairs={{8,0},{16,8},{24,16},{0,24},{9,1},{17,9},{25,17},{1,25},{10,2},{18... | collective-permute-start | bytes 294920 | tf_op jit(solution)/shard_map/ppermute | solution.py:283
  27.0 1.1 collective-permute-start.10
  28.1 0.9 collective-permute-done.10.refs_6_
  29.1 3.5 %collective-permute-start.11 = (f32[24,256]{1,0:T(8,128)S(1)}, f32[24,256]{1,0:T(8,128)S(1)}, u32[]{:S(2)}, u32[]{:S(2)}) collective-permute-start(f32[24,256]{1,0:T(8,128)S(1)} %get-tuple-element.64), channel_id=1, source_target_pairs={{1,0},{2,1},{3,2},{4,3},{5,4},{6,5},{7,6},{0,7},{9,8},{10,9},{11,1... | collective-permute-start | bytes 73736 | tf_op jit(solution)/shard_map/ppermute | solution.py:283
  32.6 0.8 collective-permute-done.11.refs_7_
  33.5 0.0 collective-permute-done.8.refs_4_
  33.5 0.0 collective-permute-done.9.refs_5_
  33.5 0.0 collective-permute-done.7.refs_3_
  33.5 0.0 copy-start.15
  33.5 0.0 copy-start.2
  33.5 0.0 copy-start.3
  33.5 0.0 copy-start.4
  33.5 0.0 copy-start.7
  33.5 0.0 copy-start.8
  33.6 3.7 %shard_map.143 = (f32[24,8,32,128]{3,2,1,0:T(8,128)S(1)}, bf16[24,32,128]{2,1,0:T(8,128)(2,1)S(1)}, bf16[24,32,128]{2,1,0:T(8,128)(2,1)S(1)}, f32[24,8,128]{2,1,...) custom-call(f32[24,8,32,128]{3,2,1,0:T(8,128)S(1)} %get-tuple-element.58.refs_0_, ...), custom_call_target="tpu_custom_call" | custom-call | tf_op jit(solution)/shard_map/pallas_call | solution.py:288
  37.2 0.0 collective-permute-start.16
  37.2 0.7 collective-permute-start.17
  37.9 2.7 %collective-permute-start.15 = (f32[24,8,128]{2,1,0:T(8,128)S(1)}, f32[24,8,128]{2,1,0:T(8,128)S(1)}, u32[]{:S(2)}, u32[]{:S(2)}) collective-permute-start(f32[24,8,128]{2,1,0:T(8,128)S(1)} %get-tuple-element.70), channel_id=1, source_target_pairs={{8,0},{16,8},{24,16},{0,24},{9,1},{17,9},{25,17},{1,25},{10,2},{18... | collective-permute-start | bytes 294920 | tf_op jit(solution)/shard_map/ppermute | solution.py:283
  40.6 0.0 collective-permute-start.12
  40.6 0.0 collective-permute-done.16.refs_6_
  40.6 2.7 %collective-permute-start.13 = (bf16[24,32,128]{2,1,0:T(8,128)(2,1)S(1)}, bf16[24,32,128]{2,1,0:T(8,128)(2,1)S(1)}, u32[]{:S(2)}, u32[]{:S(2)}) collective-permute-start(bf16[24,32,128]{2,1,0:T(8,128)(2,1)S(1)} %get-tuple-element.68), channel_id=1, source_target_pairs={{32,0},{64,32},{96,64},{0,96},{33,1},{65,33},{97,65},{1,97},{34,2}... | collective-permute-start | bytes 589832 | tf_op jit(solution)/shard_map/ppermute | solution.py:283
  43.3 1.5 %shard_map.145 = (bf16[1600,32]{1,0:T(8,128)(2,1)S(1)}, bf16[800,1600]{1,0:T(8,128)(2,1)S(1)}, bf16[400,800]{1,0:T(8,128)(2,1)S(1)}, f32[800,128]{1,0:T(8,128)S(...) custom-call(bf16[24,1600]{1,0:T(8,128)(2,1)S(1)} %copy-done.4, f32[1,1600]{1,0:T(1,128)S(1)} %reshape.31.b_in, ...), custom_call_target="tpu_custom_call" | custom-call | bytes 8388608 | tf_op jit(solution)/shard_map/pallas_call | solution.py:346
  44.8 0.0 collective-permute-done.17.refs_7_
  44.8 0.0 collective-permute-done.15.refs_5_
  44.9 1.5 %collective-permute-done.12.refs_2_ = bf16[24,32,128]{2,1,0:T(8,128)(2,1)S(1)} collective-permute-done((bf16[24,32,128]{2,1,0:T(8,128)(2,1)S(1)}, bf16[24,32,128]{2,1,0:T(8,128)(2,1)S(1)}, u32[]{:S(2)}, u32[]{:S(2)}) %collective-permute-start.12) | collective-permute-done | bytes 196640 | tf_op jit(solution)/shard_map/ppermute | solution.py:282
  46.3 0.0 collective-permute-done.13.refs_3_
  46.3 3.5 %shard_map.144 = f32[24,8,32,128]{3,2,1,0:T(8,128)S(1)} custom-call(f32[24,8,32,128]{3,2,1,0:T(8,128)S(1)} %get-tuple-element.66.refs_0_, f32[24,8,32,128]{3,2,1,0:T(8,128)S(1)} %copy-done, bf16[24,32,128]{2,1,0:T(8,128)(2,1)S(1)} %collective-permute-done.12.refs_2_, bf16[24,32,128]{2,1,0:T(8,128)(2,1)S(1)} %collective-permute-done.13.refs_3_, ...), custom_call_target="tpu_custom_call" | custom-call | tf_op jit(solution)/shard_map/pallas_call | solution.py:288
  49.9 0.0 copy-start.10
  49.9 18.3 %shard_map.146 = (f32[6144,128]{1,0:T(8,128)S(1)}, f32[128,128]{1,0:T(8,128)S(1)}, bf16[24,32,128]{2,1,0:T(8,128)(2,1)}, bf16[24,32,128]{2,1,0:T(8,128)(2,1)}, f...) custom-call(s32[1,96]{1,0:T(1,128)S(1)} %copy-done.9, ...), custom_call_target="tpu_custom_call" | custom-call | tf_op jit(solution)/shard_map/pallas_call | solution.py:359
  68.2 0.6 copy-done.5
  68.8 0.6 copy-done.11
  69.4 0.6 copy-done.12
  70.0 0.0 collective-permute-start.18
  70.0 2.7 %collective-permute-start.19 = (bf16[24,32,128]{2,1,0:T(8,128)(2,1)}, bf16[24,32,128]{2,1,0:T(8,128)(2,1)S(1)}, u32[]{:S(2)}, u32[]{:S(2)}) collective-permute-start(bf16[24,32,128]{2,1,0:T(8,128)(2,1)} %get-tuple-element.91), channel_id=1, source_target_pairs={{32,0},{64,32},{96,64},{0,96},{33,1},{65,33},{97,65},{1,97},{34,2}... | collective-permute-start | bytes 589832 | tf_op jit(solution)/shard_map/ppermute | solution.py:283
  72.7 44.3 %collective-permute-start.20 = (f32[24,8,128]{2,1,0:T(8,128)}, f32[24,8,128]{2,1,0:T(8,128)}, u32[]{:S(2)}, u32[]{:S(2)}) collective-permute-start(f32[24,8,128]{2,1,0:T(8,128)} %get-tuple-element.94), channel_id=1, source_target_pairs={{0,8},{8,16},{16,24},{24,0},{1,9},{9,17},{17,25},{25,1},{2,10},{10... | collective-permute-start | bytes 294920 | tf_op jit(solution)/shard_map/ppermute | solution.py:282
  117.0 1.5 %collective-permute-start.21 = (f32[24,8,128]{2,1,0:T(8,128)}, f32[24,8,128]{2,1,0:T(8,128)}, u32[]{:S(2)}, u32[]{:S(2)}) collective-permute-start(f32[24,8,128]{2,1,0:T(8,128)} %get-tuple-element.95), channel_id=1, source_target_pairs={{8,0},{16,8},{24,16},{0,24},{9,1},{17,9},{25,17},{1,25},{10,2},{18... | collective-permute-start | bytes 294920 | tf_op jit(solution)/shard_map/ppermute | solution.py:283
  118.5 10.9 %all-to-all-start = ((f32[128,1,128]{2,1,0:T(1,128)}), f32[128,1,128]{2,1,0:T(1,128)}, u32[]{:S(2)}, u32[]{:S(2)}) async-start(f32[128,1,128]{2,1,0:T(1,128)} %bitcast.17), calls=%async_computation | async-start | bytes 131072 | tf_op jit(solution)/shard_map/all_to_all | solution.py:299
  129.5 0.0 collective-permute-done.19.xhi
  129.5 1.6 %collective-permute-start.22 = (f32[24,256]{1,0:T(8,128)}, f32[24,256]{1,0:T(8,128)S(1)}, u32[]{:S(2)}, u32[]{:S(2)}) collective-permute-start(f32[24,256]{1,0:T(8,128)} %copy-done.12), channel_id=1, source_target_pairs={{0,1},{1,2},{2,3},{3,4},{4,5},{5,6},{6,7},{7,0},{8,9},{9,10},{10,1... | collective-permute-start | bytes 73736 | tf_op jit(solution)/shard_map/ppermute | solution.py:282
  131.1 1.1 collective-permute-done.22.zlo
  132.3 2.7 %collective-permute-done.23.zhi = f32[24,256]{1,0:T(8,128)S(1)} collective-permute-done((f32[24,256]{1,0:T(8,128)}, f32[24,256]{1,0:T(8,128)S(1)}, u32[]{:S(2)}, u32[]{:S(2)}) %collective-permute-start.23) | collective-permute-done | bytes 24608 | tf_op jit(solution)/shard_map/ppermute | solution.py:283
  135.0 4.1 %shard_map.147 = f32[24,8,32,128]{3,2,1,0:T(8,128)} custom-call(f32[24]{0:T(128)S(1)} %copy-done.10, f32[24,8,32,128]{3,2,1,0:T(8,128)S(1)} %bitcast.14, bf16[24,32,128]{2,1,0:T(8,128)(2,1)S(1)} %collective-permute-done.18.xlo, bf16[24,32,128]{2,1,0:T(8,128)(2,1)S(1)} %collective-permute-done.19.xhi, f32[24,8,128]{2,1,0:T(8,128)} %collective-permute-done.20.ylo, ...), custom_call_target="tpu_custom_call" | custom-call | flops 10000000 | bytes 6291456 | tf_op jit(solution)/shard_map/pallas_call | solution.py:378
  139.2 0.0 all-to-all-done
  139.2 1.5 %shard_map.148 = f32[1,1]{1,0:T(1,128)} custom-call(f32[128,128]{1,0:T(8,128)} %bitcast.9.heats), custom_call_target="tpu_custom_call" | custom-call | tf_op jit(solution)/shard_map/pallas_call | solution.py:389
  (30 shorter events, 0.1 us)
Async XLA Ops:
  0.6 5.6 %copy-start = (f32[24,8,32,128]{3,2,1,0:T(8,128)S(1)}, f32[24,8,32,128]{3,2,1,0:T(8,128)}, u32[]{:S(2)}) copy-start(f32[24,8,32,128]{3,2,1,0:T(8,128)} %refs_1_.3) | copy-start | bytes 9437188
  0.6 5.6 %copy-start.1 = (f32[3,8,32,128]{3,2,1,0:T(8,128)S(1)}, f32[3,8,32,128]{3,2,1,0:T(8,128)}, u32[]{:S(2)}) copy-start(f32[3,8,32,128]{3,2,1,0:T(8,128)} %refs_7_.1) | copy-start | bytes 1179652
  2.7 15.7 %collective-permute-start = (bf16[25,32,128]{2,1,0:T(8,128)(2,1)}, bf16[25,32,128]{2,1,0:T(8,128)(2,1)S(1)}, u32[]{:S(2)}, u32[]{:S(2)}) collective-permute-start(bf16[25,32,128]{2,1,0:T(8,128)(2,1)} %get-tuple-element.51), channel_id=1, source_target_pairs={{0,32},{32,64},{64,96},{96,0},{1,33},{33,65},{65,97},{97,1},{2,34}... | collective-permute-start | bytes 614408 | tf_op jit(solution)/shard_map/ppermute | solution.py:282
  4.8 13.6 %collective-permute-start.1 = (bf16[25,32,128]{2,1,0:T(8,128)(2,1)}, bf16[25,32,128]{2,1,0:T(8,128)(2,1)S(1)}, u32[]{:S(2)}, u32[]{:S(2)}) collective-permute-start(bf16[25,32,128]{2,1,0:T(8,128)(2,1)} %get-tuple-element.52), channel_id=1, source_target_pairs={{32,0},{64,32},{96,64},{0,96},{33,1},{65,33},{97,65},{1,97},{34,2}... | collective-permute-start | bytes 614408 | tf_op jit(solution)/shard_map/ppermute | solution.py:283
  6.7 25.9 %copy-start.14 = (f32[800]{0:T(1024)S(1)}, f32[800]{0:T(1024)}, u32[]{:S(2)}) copy-start(f32[800]{0:T(1024)} %param.19) | copy-start | bytes 9604
  6.8 25.9 %copy-start.13 = (f32[1600]{0:T(1024)S(1)}, f32[1600]{0:T(1024)}, u32[]{:S(2)}) copy-start(f32[1600]{0:T(1024)} %param.17) | copy-start | bytes 19204
  6.8 11.7 %collective-permute-start.2 = (f32[25,8,128]{2,1,0:T(8,128)S(1)}, f32[25,8,128]{2,1,0:T(8,128)S(1)}, u32[]{:S(2)}, u32[]{:S(2)}) collective-permute-start(f32[25,8,128]{2,1,0:T(8,128)S(1)} %get-tuple-element.53), channel_id=1, source_target_pairs={{0,8},{8,16},{16,24},{24,0},{1,9},{9,17},{17,25},{25,1},{2,10},{10... | collective-permute-start | bytes 307208 | tf_op jit(solution)/shard_map/ppermute | solution.py:282
  8.6 9.8 %collective-permute-start.3 = (f32[25,8,128]{2,1,0:T(8,128)S(1)}, f32[25,8,128]{2,1,0:T(8,128)S(1)}, u32[]{:S(2)}, u32[]{:S(2)}) collective-permute-start(f32[25,8,128]{2,1,0:T(8,128)S(1)} %get-tuple-element.54), channel_id=1, source_target_pairs={{8,0},{16,8},{24,16},{0,24},{9,1},{17,9},{25,17},{1,25},{10,2},{18... | collective-permute-start | bytes 307208 | tf_op jit(solution)/shard_map/ppermute | solution.py:283
  10.8 3.7 %collective-permute-start.4 = (f32[25,256]{1,0:T(8,128)S(1)}, f32[25,256]{1,0:T(8,128)S(1)}, u32[]{:S(2)}, u32[]{:S(2)}) collective-permute-start(f32[25,256]{1,0:T(8,128)S(1)} %get-tuple-element.55), channel_id=1, source_target_pairs={{0,1},{1,2},{2,3},{3,4},{4,5},{5,6},{6,7},{7,0},{8,9},{9,10},{10,1... | collective-permute-start | bytes 76808 | tf_op jit(solution)/shard_map/ppermute | solution.py:282
  14.5 3.9 %collective-permute-start.5 = (f32[25,256]{1,0:T(8,128)S(1)}, f32[25,256]{1,0:T(8,128)S(1)}, u32[]{:S(2)}, u32[]{:S(2)}) collective-permute-start(f32[25,256]{1,0:T(8,128)S(1)} %get-tuple-element.56), channel_id=1, source_target_pairs={{1,0},{2,1},{3,2},{4,3},{5,4},{6,5},{7,6},{0,7},{9,8},{10,9},{11,1... | collective-permute-start | bytes 76808 | tf_op jit(solution)/shard_map/ppermute | solution.py:283
  21.6 11.8 %collective-permute-start.6 = (bf16[24,32,128]{2,1,0:T(8,128)(2,1)S(1)}, bf16[24,32,128]{2,1,0:T(8,128)(2,1)S(1)}, u32[]{:S(2)}, u32[]{:S(2)}) collective-permute-start(bf16[24,32,128]{2,1,0:T(8,128)(2,1)S(1)} %get-tuple-element.59), channel_id=1, source_target_pairs={{0,32},{32,64},{64,96},{96,0},{1,33},{33,65},{65,97},{97,1},{2,34}... | collective-permute-start | bytes 589832 | tf_op jit(solution)/shard_map/ppermute | solution.py:282
  21.6 11.8 %collective-permute-start.7 = (bf16[24,32,128]{2,1,0:T(8,128)(2,1)S(1)}, bf16[24,32,128]{2,1,0:T(8,128)(2,1)S(1)}, u32[]{:S(2)}, u32[]{:S(2)}) collective-permute-start(bf16[24,32,128]{2,1,0:T(8,128)(2,1)S(1)} %get-tuple-element.60), channel_id=1, source_target_pairs={{32,0},{64,32},{96,64},{0,96},{33,1},{65,33},{97,65},{1,97},{34,2}... | collective-permute-start | bytes 589832 | tf_op jit(solution)/shard_map/ppermute | solution.py:283
  24.3 9.1 %collective-permute-start.8 = (f32[24,8,128]{2,1,0:T(8,128)S(1)}, f32[24,8,128]{2,1,0:T(8,128)S(1)}, u32[]{:S(2)}, u32[]{:S(2)}) collective-permute-start(f32[24,8,128]{2,1,0:T(8,128)S(1)} %get-tuple-element.61), channel_id=1, source_target_pairs={{0,8},{8,16},{16,24},{24,0},{1,9},{9,17},{17,25},{25,1},{2,10},{10... | collective-permute-start | bytes 294920 | tf_op jit(solution)/shard_map/ppermute | solution.py:282
  24.3 9.1 %collective-permute-start.9 = (f32[24,8,128]{2,1,0:T(8,128)S(1)}, f32[24,8,128]{2,1,0:T(8,128)S(1)}, u32[]{:S(2)}, u32[]{:S(2)}) collective-permute-start(f32[24,8,128]{2,1,0:T(8,128)S(1)} %get-tuple-element.62), channel_id=1, source_target_pairs={{8,0},{16,8},{24,16},{0,24},{9,1},{17,9},{25,17},{1,25},{10,2},{18... | collective-permute-start | bytes 294920 | tf_op jit(solution)/shard_map/ppermute | solution.py:283
  27.0 2.1 %collective-permute-start.10 = (f32[24,256]{1,0:T(8,128)S(1)}, f32[24,256]{1,0:T(8,128)S(1)}, u32[]{:S(2)}, u32[]{:S(2)}) collective-permute-start(f32[24,256]{1,0:T(8,128)S(1)} %get-tuple-element.63), channel_id=1, source_target_pairs={{0,1},{1,2},{2,3},{3,4},{4,5},{5,6},{6,7},{7,0},{8,9},{9,10},{10,1... | collective-permute-start | bytes 73736 | tf_op jit(solution)/shard_map/ppermute | solution.py:282
  29.1 4.4 %collective-permute-start.11 = (f32[24,256]{1,0:T(8,128)S(1)}, f32[24,256]{1,0:T(8,128)S(1)}, u32[]{:S(2)}, u32[]{:S(2)}) collective-permute-start(f32[24,256]{1,0:T(8,128)S(1)} %get-tuple-element.64), channel_id=1, source_target_pairs={{1,0},{2,1},{3,2},{4,3},{5,4},{6,5},{7,6},{0,7},{9,8},{10,9},{11,1... | collective-permute-start | bytes 73736 | tf_op jit(solution)/shard_map/ppermute | solution.py:283
  33.5 9.8 %copy-start.15 = (s32[1,96]{1,0:T(1,128)S(1)}, s32[1,96]{1,0:T(1,128)}, u32[]{:S(2)}) copy-start(s32[1,96]{1,0:T(1,128)} %param.25) | copy-start | bytes 1156
  33.5 9.8 %copy-start.2 = (bf16[1600,800]{0,1:T(8,128)(2,1)S(1)}, bf16[1600,800]{0,1:T(8,128)(2,1)}, u32[]{:S(2)}) copy-start(bf16[1600,800]{0,1:T(8,128)(2,1)} %param.18) | copy-start | bytes 7680004
  33.5 9.8 %copy-start.3 = (bf16[800,400]{0,1:T(8,128)(2,1)S(1)}, bf16[800,400]{0,1:T(8,128)(2,1)}, u32[]{:S(2)}) copy-start(bf16[800,400]{0,1:T(8,128)(2,1)} %param.20) | copy-start | bytes 1920004
  33.5 9.8 %copy-start.4 = (bf16[24,1600]{1,0:T(8,128)(2,1)S(1)}, bf16[24,1600]{1,0:T(8,128)(2,1)}, u32[]{:S(2)}) copy-start(bf16[24,1600]{1,0:T(8,128)(2,1)} %w_in) | copy-start | bytes 230404
  33.5 9.8 %copy-start.7 = (f32[400]{0:T(512)S(1)}, f32[400]{0:T(512)}, u32[]{:S(2)}) copy-start(f32[400]{0:T(512)} %param.21) | copy-start | bytes 4804
  33.5 9.8 %copy-start.8 = (f32[24]{0:T(128)S(1)}, f32[24]{0:T(128)}, u32[]{:S(2)}) copy-start(f32[24]{0:T(128)} %param.23) | copy-start | bytes 292
  37.2 3.4 %collective-permute-start.16 = (f32[24,256]{1,0:T(8,128)S(1)}, f32[24,256]{1,0:T(8,128)S(1)}, u32[]{:S(2)}, u32[]{:S(2)}) collective-permute-start(f32[24,256]{1,0:T(8,128)S(1)} %get-tuple-element.71), channel_id=1, source_target_pairs={{0,1},{1,2},{2,3},{3,4},{4,5},{5,6},{6,7},{7,0},{8,9},{9,10},{10,1... | collective-permute-start | bytes 73736 | tf_op jit(solution)/shard_map/ppermute | solution.py:282
  37.2 7.6 %collective-permute-start.17 = (f32[24,256]{1,0:T(8,128)S(1)}, f32[24,256]{1,0:T(8,128)S(1)}, u32[]{:S(2)}, u32[]{:S(2)}) collective-permute-start(f32[24,256]{1,0:T(8,128)S(1)} %get-tuple-element.72), channel_id=1, source_target_pairs={{1,0},{2,1},{3,2},{4,3},{5,4},{6,5},{7,6},{0,7},{9,8},{10,9},{11,1... | collective-permute-start | bytes 73736 | tf_op jit(solution)/shard_map/ppermute | solution.py:283
  37.9 6.9 %collective-permute-start.14 = (f32[24,8,128]{2,1,0:T(8,128)S(1)}, f32[24,8,128]{2,1,0:T(8,128)S(1)}, u32[]{:S(2)}, u32[]{:S(2)}) collective-permute-start(f32[24,8,128]{2,1,0:T(8,128)S(1)} %get-tuple-element.69), channel_id=1, source_target_pairs={{0,8},{8,16},{16,24},{24,0},{1,9},{9,17},{17,25},{25,1},{2,10},{10... | collective-permute-start | bytes 294920 | tf_op jit(solution)/shard_map/ppermute | solution.py:282
  37.9 6.9 %collective-permute-start.15 = (f32[24,8,128]{2,1,0:T(8,128)S(1)}, f32[24,8,128]{2,1,0:T(8,128)S(1)}, u32[]{:S(2)}, u32[]{:S(2)}) collective-permute-start(f32[24,8,128]{2,1,0:T(8,128)S(1)} %get-tuple-element.70), channel_id=1, source_target_pairs={{8,0},{16,8},{24,16},{0,24},{9,1},{17,9},{25,17},{1,25},{10,2},{18... | collective-permute-start | bytes 294920 | tf_op jit(solution)/shard_map/ppermute | solution.py:283
  40.6 5.7 %collective-permute-start.12 = (bf16[24,32,128]{2,1,0:T(8,128)(2,1)S(1)}, bf16[24,32,128]{2,1,0:T(8,128)(2,1)S(1)}, u32[]{:S(2)}, u32[]{:S(2)}) collective-permute-start(bf16[24,32,128]{2,1,0:T(8,128)(2,1)S(1)} %get-tuple-element.67), channel_id=1, source_target_pairs={{0,32},{32,64},{64,96},{96,0},{1,33},{33,65},{65,97},{97,1},{2,34}... | collective-permute-start | bytes 589832 | tf_op jit(solution)/shard_map/ppermute | solution.py:282
  40.6 5.7 %collective-permute-start.13 = (bf16[24,32,128]{2,1,0:T(8,128)(2,1)S(1)}, bf16[24,32,128]{2,1,0:T(8,128)(2,1)S(1)}, u32[]{:S(2)}, u32[]{:S(2)}) collective-permute-start(bf16[24,32,128]{2,1,0:T(8,128)(2,1)S(1)} %get-tuple-element.68), channel_id=1, source_target_pairs={{32,0},{64,32},{96,64},{0,96},{33,1},{65,33},{97,65},{1,97},{34,2}... | collective-permute-start | bytes 589832 | tf_op jit(solution)/shard_map/ppermute | solution.py:283
  46.3 3.5 %copy-start.6 = (bf16[400,24]{0,1:T(8,128)(2,1)S(1)}, bf16[400,24]{0,1:T(8,128)(2,1)}, u32[]{:S(2)}) copy-start(bf16[400,24]{0,1:T(8,128)(2,1)} %param.22) | copy-start | bytes 57604
  46.3 3.5 %copy-start.9 = (s32[1,96]{1,0:T(1,128)S(1)}, s32[1,96]{1,0:T(1,128)}, u32[]{:S(2)}) copy-start(s32[1,96]{1,0:T(1,128)} %listed.1) | copy-start | bytes 1156
  49.9 85.1 %copy-start.10 = (f32[24]{0:T(128)S(1)}, f32[24]{0:T(128)}, u32[]{:S(2)}) copy-start(f32[24]{0:T(128)} %rates.1) | copy-start | bytes 292
  68.2 0.6 copy-start.5
  68.8 0.6 copy-start.11
  69.4 0.6 copy-start.12
  70.0 59.4 %collective-permute-start.18 = (bf16[24,32,128]{2,1,0:T(8,128)(2,1)}, bf16[24,32,128]{2,1,0:T(8,128)(2,1)S(1)}, u32[]{:S(2)}, u32[]{:S(2)}) collective-permute-start(bf16[24,32,128]{2,1,0:T(8,128)(2,1)} %get-tuple-element.90), channel_id=1, source_target_pairs={{0,32},{32,64},{64,96},{96,0},{1,33},{33,65},{65,97},{97,1},{2,34}... | collective-permute-start | bytes 589832 | tf_op jit(solution)/shard_map/ppermute | solution.py:282
  70.0 59.4 %collective-permute-start.19 = (bf16[24,32,128]{2,1,0:T(8,128)(2,1)}, bf16[24,32,128]{2,1,0:T(8,128)(2,1)S(1)}, u32[]{:S(2)}, u32[]{:S(2)}) collective-permute-start(bf16[24,32,128]{2,1,0:T(8,128)(2,1)} %get-tuple-element.91), channel_id=1, source_target_pairs={{32,0},{64,32},{96,64},{0,96},{33,1},{65,33},{97,65},{1,97},{34,2}... | collective-permute-start | bytes 589832 | tf_op jit(solution)/shard_map/ppermute | solution.py:283
  72.7 58.4 %collective-permute-start.20 = (f32[24,8,128]{2,1,0:T(8,128)}, f32[24,8,128]{2,1,0:T(8,128)}, u32[]{:S(2)}, u32[]{:S(2)}) collective-permute-start(f32[24,8,128]{2,1,0:T(8,128)} %get-tuple-element.94), channel_id=1, source_target_pairs={{0,8},{8,16},{16,24},{24,0},{1,9},{9,17},{17,25},{25,1},{2,10},{10... | collective-permute-start | bytes 294920 | tf_op jit(solution)/shard_map/ppermute | solution.py:282
  117.0 14.1 %collective-permute-start.21 = (f32[24,8,128]{2,1,0:T(8,128)}, f32[24,8,128]{2,1,0:T(8,128)}, u32[]{:S(2)}, u32[]{:S(2)}) collective-permute-start(f32[24,8,128]{2,1,0:T(8,128)} %get-tuple-element.95), channel_id=1, source_target_pairs={{8,0},{16,8},{24,16},{0,24},{9,1},{17,9},{25,17},{1,25},{10,2},{18... | collective-permute-start | bytes 294920 | tf_op jit(solution)/shard_map/ppermute | solution.py:283
  118.5 20.7 %all-to-all-start = ((f32[128,1,128]{2,1,0:T(1,128)}), f32[128,1,128]{2,1,0:T(1,128)}, u32[]{:S(2)}, u32[]{:S(2)}) async-start(f32[128,1,128]{2,1,0:T(1,128)} %bitcast.17), calls=%async_computation | async-start | bytes 131072 | tf_op jit(solution)/shard_map/all_to_all | solution.py:299
  129.5 2.8 %collective-permute-start.22 = (f32[24,256]{1,0:T(8,128)}, f32[24,256]{1,0:T(8,128)S(1)}, u32[]{:S(2)}, u32[]{:S(2)}) collective-permute-start(f32[24,256]{1,0:T(8,128)} %copy-done.12), channel_id=1, source_target_pairs={{0,1},{1,2},{2,3},{3,4},{4,5},{5,6},{6,7},{7,0},{8,9},{9,10},{10,1... | collective-permute-start | bytes 73736 | tf_op jit(solution)/shard_map/ppermute | solution.py:282
  131.1 3.9 %collective-permute-start.23 = (f32[24,256]{1,0:T(8,128)}, f32[24,256]{1,0:T(8,128)S(1)}, u32[]{:S(2)}, u32[]{:S(2)}) collective-permute-start(f32[24,256]{1,0:T(8,128)} %copy-done.11), channel_id=1, source_target_pairs={{1,0},{2,1},{3,2},{4,3},{5,4},{6,5},{7,6},{0,7},{9,8},{10,9},{11,1... | collective-permute-start | bytes 73736 | tf_op jit(solution)/shard_map/ppermute | solution.py:283

commit v11 on v10

--- a/solution.py
+++ b/solution.py
@@ -9,9 +9,9 @@
 
 GROUP = 24
 LAST_GROUP = 8
-TOGETHER = 12
+TOGETHER = 16
 LISTED = 96
-NETWORK_MIB = 38
+NETWORK_MIB = 42
 ALL = ("gx", "gy", "gz")
 F32, BF16 = jnp.float32, jnp.bfloat16
 TN = (((0,), (0,)), ((), ()))

time: 141 us -> 142 us (level)
  starting transfers between devices: 89.7 us -> 96 us
  Pallas kernels: 38.4 us -> 33.3 us
    ppermute x12, starting transfers between devices: 25 us -> 68.9 us  [exchange(): got.append(lax.ppermute(first, axis, [((i + 1) % n, i) for i in range(n)]))]
    ppermute x12, starting transfers between devices: 53.8 us -> 14.7 us  [exchange(): got.append(lax.ppermute(last, axis, [(i, (i + 1) % n) for i in range(n)]))]
    pallas_call x1, Pallas kernels: 18.3 us -> 13.2 us  [local(): pl.pallas_call(network_kernel, in_specs=[pl.BlockSpec(memory_space=pltpu....]
    all_to_all x1, starting transfers between devices: 10.9 us -> 12.5 us  [swap(): return lax.all_to_all(tiles, ALL, split_axis=0, concat_axis=0, tiled=True)]
where the time goes in v11:
time: 142 us
  starting transfers between devices  96 us (68%)
  Pallas kernels  33.3 us (23%)
  waiting for transfers between devices  9.77 us (7%)
  local copies, waits for them, and re-layouts  1.9 us (1%)
    ppermute x12, starting transfers between devices, exchange(): got.append(lax.ppermute(first, axis, [((i + 1) % n, i) for i in range(n)]))  68.9 us
    ppermute x12, starting transfers between devices, exchange(): got.append(lax.ppermute(last, axis, [(i, (i + 1) % n) for i in range(n)]))  14.7 us
    pallas_call x1, Pallas kernels, local(): pl.pallas_call(network_kernel, in_specs=[pl.BlockSpec(memory_space=pltpu....  13.2 us
    all_to_all x1, starting transfers between devices, swap(): return lax.all_to_all(tiles, ALL, split_axis=0, concat_axis=0, tiled=True)  12.5 us
    pallas_call x3, Pallas kernels, section(): pl.pallas_call(functools.partial(section_kernel, kind), in_specs=[IN_VMEM...  10.3 us
    ppermute x12, waiting for transfers between devices, exchange(): got.append(lax.ppermute(first, axis, [((i + 1) % n, i) for i in range(n)]))  5.17 us
    ppermute x12, waiting for transfers between devices, exchange(): got.append(lax.ppermute(last, axis, [(i, (i + 1) % n) for i in range(n)]))  4.6 us
    pallas_call x1, Pallas kernels, local(): pl.pallas_call(diffuse_kernel, grid=(24 // part,), in_specs=[smem, bricks...  4.15 us
  transfers between devices with their start and end apart: 25, of which 7 were waited for; matrix products, arithmetic and copies ran while one was open for 0% of the time, Pallas kernels for 4%

profile of v11, /device:TPU:1, one launch (start us, length us, event | category | flops | bytes accessed | tf_op | source)
XLA Modules:
  0.0 142.1 jit_solution(4769742186117590043)
XLA Ops:
  0.6 2.1 %shard_map.140 = (bf16[25,32,128]{2,1,0:T(8,128)(2,1)}, bf16[25,32,128]{2,1,0:T(8,128)(2,1)}) custom-call(f32[24,8,32,128]{3,2,1,0:T(8,128)} %refs_1_.3, f32[3,8,32,128]{3,2,1,0:T(8,128)} %refs_7_.1), custom_call_target="tpu_custom_call" | custom-call | tf_op jit(solution)/shard_map/pallas_call | solution.py:321
  2.7 2.1 %collective-permute-start = (bf16[25,32,128]{2,1,0:T(8,128)(2,1)}, bf16[25,32,128]{2,1,0:T(8,128)(2,1)S(1)}, u32[]{:S(2)}, u32[]{:S(2)}) collective-permute-start(bf16[25,32,128]{2,1,0:T(8,128)(2,1)} %get-tuple-element.51), channel_id=1, source_target_pairs={{0,32},{32,64},{64,96},{96,0},{1,33},{33,65},{65,97},{97,1},{2,34}... | collective-permute-start | bytes 614408 | tf_op jit(solution)/shard_map/ppermute | solution.py:282
  4.8 1.3 collective-permute-start.1
  6.2 0.5 shard_map.141
  6.7 0.0 copy-start.14
  6.8 0.0 copy-start.13
  6.8 1.8 %collective-permute-start.2 = (f32[25,8,128]{2,1,0:T(8,128)S(1)}, f32[25,8,128]{2,1,0:T(8,128)S(1)}, u32[]{:S(2)}, u32[]{:S(2)}) collective-permute-start(f32[25,8,128]{2,1,0:T(8,128)S(1)} %get-tuple-element.53), channel_id=1, source_target_pairs={{0,8},{8,16},{16,24},{24,0},{1,9},{9,17},{17,25},{25,1},{2,10},{10... | collective-permute-start | bytes 307208 | tf_op jit(solution)/shard_map/ppermute | solution.py:282
  8.6 2.2 %collective-permute-start.3 = (f32[25,8,128]{2,1,0:T(8,128)S(1)}, f32[25,8,128]{2,1,0:T(8,128)S(1)}, u32[]{:S(2)}, u32[]{:S(2)}) collective-permute-start(f32[25,8,128]{2,1,0:T(8,128)S(1)} %get-tuple-element.54), channel_id=1, source_target_pairs={{8,0},{16,8},{24,16},{0,24},{9,1},{17,9},{25,17},{1,25},{10,2},{18... | collective-permute-start | bytes 307208 | tf_op jit(solution)/shard_map/ppermute | solution.py:283
  10.8 2.7 %collective-permute-start.4 = (f32[25,256]{1,0:T(8,128)S(1)}, f32[25,256]{1,0:T(8,128)S(1)}, u32[]{:S(2)}, u32[]{:S(2)}) collective-permute-start(f32[25,256]{1,0:T(8,128)S(1)} %get-tuple-element.55), channel_id=1, source_target_pairs={{0,1},{1,2},{2,3},{3,4},{4,5},{5,6},{6,7},{7,0},{8,9},{9,10},{10,1... | collective-permute-start | bytes 76808 | tf_op jit(solution)/shard_map/ppermute | solution.py:282
  13.5 1.0 collective-permute-done.4.refs_5_.refs_12_
  14.5 2.3 %collective-permute-start.5 = (f32[25,256]{1,0:T(8,128)S(1)}, f32[25,256]{1,0:T(8,128)S(1)}, u32[]{:S(2)}, u32[]{:S(2)}) collective-permute-start(f32[25,256]{1,0:T(8,128)S(1)} %get-tuple-element.56), channel_id=1, source_target_pairs={{1,0},{2,1},{3,2},{4,3},{5,4},{6,5},{7,6},{0,7},{9,8},{10,9},{11,1... | collective-permute-start | bytes 76808 | tf_op jit(solution)/shard_map/ppermute | solution.py:283
  16.9 1.6 %collective-permute-done.5.refs_6_.refs_13_ = f32[25,256]{1,0:T(8,128)S(1)} collective-permute-done((f32[25,256]{1,0:T(8,128)S(1)}, f32[25,256]{1,0:T(8,128)S(1)}, u32[]{:S(2)}, u32[]{:S(2)}) %collective-permute-start.5) | collective-permute-done | bytes 25632 | tf_op jit(solution)/shard_map/ppermute | solution.py:283
  18.4 0.0 collective-permute-done.2.refs_3_.refs_10_
  18.4 0.0 collective-permute-done.3.refs_4_.refs_11_
  18.4 0.0 collective-permute-done.refs_1_.refs_8_
  18.4 0.0 collective-permute-done.1.refs_2_.refs_9_
  18.5 3.2 %shard_map.142 = (f32[24,8,32,128]{3,2,1,0:T(8,128)S(1)}, f32[6,8,32,128]{3,2,1,0:T(8,128)S(1)}, bf16[24,32,128]{2,1,0:T(8,128)(2,1)S(1)}, bf16[24,32,128]{2,1,0...) custom-call(f32[24,8,32,128]{3,2,1,0:T(8,128)S(1)} %copy-done, ...), custom_call_target="tpu_custom_call" | custom-call | tf_op jit(solution)/shard_map/pallas_call | solution.py:288
  21.6 0.0 collective-permute-start.6
  21.6 2.7 %collective-permute-start.7 = (bf16[24,32,128]{2,1,0:T(8,128)(2,1)S(1)}, bf16[24,32,128]{2,1,0:T(8,128)(2,1)S(1)}, u32[]{:S(2)}, u32[]{:S(2)}) collective-permute-start(bf16[24,32,128]{2,1,0:T(8,128)(2,1)S(1)} %get-tuple-element.60), channel_id=1, source_target_pairs={{32,0},{64,32},{96,64},{0,96},{33,1},{65,33},{97,65},{1,97},{34,2}... | collective-permute-start | bytes 589832 | tf_op jit(solution)/shard_map/ppermute | solution.py:283
  24.3 0.0 collective-permute-start.8
  24.3 2.7 %collective-permute-start.9 = (f32[24,8,128]{2,1,0:T(8,128)S(1)}, f32[24,8,128]{2,1,0:T(8,128)S(1)}, u32[]{:S(2)}, u32[]{:S(2)}) collective-permute-start(f32[24,8,128]{2,1,0:T(8,128)S(1)} %get-tuple-element.62), channel_id=1, source_target_pairs={{8,0},{16,8},{24,16},{0,24},{9,1},{17,9},{25,17},{1,25},{10,2},{18... | collective-permute-start | bytes 294920 | tf_op jit(solution)/shard_map/ppermute | solution.py:283
  27.0 1.1 collective-permute-start.10
  28.1 0.9 collective-permute-done.10.refs_6_
  29.1 3.5 %collective-permute-start.11 = (f32[24,256]{1,0:T(8,128)S(1)}, f32[24,256]{1,0:T(8,128)S(1)}, u32[]{:S(2)}, u32[]{:S(2)}) collective-permute-start(f32[24,256]{1,0:T(8,128)S(1)} %get-tuple-element.64), channel_id=1, source_target_pairs={{1,0},{2,1},{3,2},{4,3},{5,4},{6,5},{7,6},{0,7},{9,8},{10,9},{11,1... | collective-permute-start | bytes 73736 | tf_op jit(solution)/shard_map/ppermute | solution.py:283
  32.6 0.8 collective-permute-done.11.refs_7_
  33.5 0.0 collective-permute-done.8.refs_4_
  33.5 0.0 collective-permute-done.7.refs_3_
  33.5 0.0 copy-start.15
  33.5 0.0 copy-start.2
  33.5 0.0 copy-start.3
  33.5 0.0 copy-start.4
  33.5 0.0 copy-start.7
  33.5 0.0 copy-start.8
  33.6 3.7 %shard_map.143 = (f32[24,8,32,128]{3,2,1,0:T(8,128)S(1)}, bf16[24,32,128]{2,1,0:T(8,128)(2,1)S(1)}, bf16[24,32,128]{2,1,0:T(8,128)(2,1)S(1)}, f32[24,8,128]{2,1,...) custom-call(f32[24,8,32,128]{3,2,1,0:T(8,128)S(1)} %get-tuple-element.58.refs_0_, ...), custom_call_target="tpu_custom_call" | custom-call | tf_op jit(solution)/shard_map/pallas_call | solution.py:288
  37.2 0.0 collective-permute-start.16
  37.2 0.7 collective-permute-start.17
  37.9 2.7 %collective-permute-start.15 = (f32[24,8,128]{2,1,0:T(8,128)S(1)}, f32[24,8,128]{2,1,0:T(8,128)S(1)}, u32[]{:S(2)}, u32[]{:S(2)}) collective-permute-start(f32[24,8,128]{2,1,0:T(8,128)S(1)} %get-tuple-element.70), channel_id=1, source_target_pairs={{8,0},{16,8},{24,16},{0,24},{9,1},{17,9},{25,17},{1,25},{10,2},{18... | collective-permute-start | bytes 294920 | tf_op jit(solution)/shard_map/ppermute | solution.py:283
  40.6 0.0 collective-permute-start.12
  40.6 2.7 %collective-permute-start.13 = (bf16[24,32,128]{2,1,0:T(8,128)(2,1)S(1)}, bf16[24,32,128]{2,1,0:T(8,128)(2,1)S(1)}, u32[]{:S(2)}, u32[]{:S(2)}) collective-permute-start(bf16[24,32,128]{2,1,0:T(8,128)(2,1)S(1)} %get-tuple-element.68), channel_id=1, source_target_pairs={{32,0},{64,32},{96,64},{0,96},{33,1},{65,33},{97,65},{1,97},{34,2}... | collective-permute-start | bytes 589832 | tf_op jit(solution)/shard_map/ppermute | solution.py:283
  43.3 1.5 %shard_map.145 = (bf16[1600,32]{1,0:T(8,128)(2,1)S(1)}, bf16[800,1600]{1,0:T(8,128)(2,1)S(1)}, bf16[400,800]{1,0:T(8,128)(2,1)S(1)}, f32[800,128]{1,0:T(8,128)S(...) custom-call(bf16[24,1600]{1,0:T(8,128)(2,1)S(1)} %copy-done.4, f32[1,1600]{1,0:T(1,128)S(1)} %reshape.31.b_in, ...), custom_call_target="tpu_custom_call" | custom-call | bytes 8388608 | tf_op jit(solution)/shard_map/pallas_call | solution.py:346
  44.8 0.0 collective-permute-done.17.refs_7_
  44.9 1.5 %collective-permute-done.12.refs_2_ = bf16[24,32,128]{2,1,0:T(8,128)(2,1)S(1)} collective-permute-done((bf16[24,32,128]{2,1,0:T(8,128)(2,1)S(1)}, bf16[24,32,128]{2,1,0:T(8,128)(2,1)S(1)}, u32[]{:S(2)}, u32[]{:S(2)}) %collective-permute-start.12) | collective-permute-done | bytes 196640 | tf_op jit(solution)/shard_map/ppermute | solution.py:282
  46.3 0.0 collective-permute-done.13.refs_3_
  46.3 3.5 %shard_map.144 = f32[24,8,32,128]{3,2,1,0:T(8,128)S(1)} custom-call(f32[24,8,32,128]{3,2,1,0:T(8,128)S(1)} %get-tuple-element.66.refs_0_, f32[24,8,32,128]{3,2,1,0:T(8,128)S(1)} %copy-done, bf16[24,32,128]{2,1,0:T(8,128)(2,1)S(1)} %collective-permute-done.12.refs_2_, bf16[24,32,128]{2,1,0:T(8,128)(2,1)S(1)} %collective-permute-done.13.refs_3_, ...), custom_call_target="tpu_custom_call" | custom-call | tf_op jit(solution)/shard_map/pallas_call | solution.py:288
  49.9 0.0 copy-start.10
  49.9 13.2 %shard_map.146 = (f32[6144,128]{1,0:T(8,128)S(1)}, f32[128,128]{1,0:T(8,128)S(1)}, bf16[24,32,128]{2,1,0:T(8,128)(2,1)}, bf16[24,32,128]{2,1,0:T(8,128)(2,1)}, f...) custom-call(s32[1,96]{1,0:T(1,128)S(1)} %copy-done.9, ...), custom_call_target="tpu_custom_call" | custom-call | tf_op jit(solution)/shard_map/pallas_call | solution.py:359
  63.1 0.6 copy-done.5
  63.7 0.6 copy-done.11
  64.3 0.6 copy-done.12
  64.9 2.7 %collective-permute-start.19 = (bf16[24,32,128]{2,1,0:T(8,128)(2,1)}, bf16[24,32,128]{2,1,0:T(8,128)(2,1)S(1)}, u32[]{:S(2)}, u32[]{:S(2)}) collective-permute-start(bf16[24,32,128]{2,1,0:T(8,128)(2,1)} %get-tuple-element.91), channel_id=1, source_target_pairs={{32,0},{64,32},{96,64},{0,96},{33,1},{65,33},{97,65},{1,97},{34,2}... | collective-permute-start | bytes 589832 | tf_op jit(solution)/shard_map/ppermute | solution.py:283
  67.6 5.2 %collective-permute-start.20 = (f32[24,8,128]{2,1,0:T(8,128)}, f32[24,8,128]{2,1,0:T(8,128)}, u32[]{:S(2)}, u32[]{:S(2)}) collective-permute-start(f32[24,8,128]{2,1,0:T(8,128)} %get-tuple-element.94), channel_id=1, source_target_pairs={{0,8},{8,16},{16,24},{24,0},{1,9},{9,17},{17,25},{25,1},{2,10},{10... | collective-permute-start | bytes 294920 | tf_op jit(solution)/shard_map/ppermute | solution.py:282
  72.8 45.4 %collective-permute-start.21 = (f32[24,8,128]{2,1,0:T(8,128)}, f32[24,8,128]{2,1,0:T(8,128)}, u32[]{:S(2)}, u32[]{:S(2)}) collective-permute-start(f32[24,8,128]{2,1,0:T(8,128)} %get-tuple-element.95), channel_id=1, source_target_pairs={{8,0},{16,8},{24,16},{0,24},{9,1},{17,9},{25,17},{1,25},{10,2},{18... | collective-permute-start | bytes 294920 | tf_op jit(solution)/shard_map/ppermute | solution.py:283
  118.2 12.5 %all-to-all-start = ((f32[128,1,128]{2,1,0:T(1,128)}), f32[128,1,128]{2,1,0:T(1,128)}, u32[]{:S(2)}, u32[]{:S(2)}) async-start(f32[128,1,128]{2,1,0:T(1,128)} %bitcast.17), calls=%async_computation | async-start | bytes 131072 | tf_op jit(solution)/shard_map/all_to_all | solution.py:299
  130.7 0.0 collective-permute-done.18.xlo
  130.7 0.0 collective-permute-done.19.xhi
  130.7 1.7 %collective-permute-start.22 = (f32[24,256]{1,0:T(8,128)}, f32[24,256]{1,0:T(8,128)S(1)}, u32[]{:S(2)}, u32[]{:S(2)}) collective-permute-start(f32[24,256]{1,0:T(8,128)} %copy-done.12), channel_id=1, source_target_pairs={{0,1},{1,2},{2,3},{3,4},{4,5},{5,6},{6,7},{7,0},{8,9},{9,10},{10,1... | collective-permute-start | bytes 73736 | tf_op jit(solution)/shard_map/ppermute | solution.py:282
  132.4 0.0 collective-permute-start.23
  132.4 0.0 collective-permute-done.20.ylo
  132.4 0.0 collective-permute-done.21.yhi
  132.4 1.1 collective-permute-done.22.zlo
  133.5 2.8 %collective-permute-done.23.zhi = f32[24,256]{1,0:T(8,128)S(1)} collective-permute-done((f32[24,256]{1,0:T(8,128)}, f32[24,256]{1,0:T(8,128)S(1)}, u32[]{:S(2)}, u32[]{:S(2)}) %collective-permute-start.23) | collective-permute-done | bytes 24608 | tf_op jit(solution)/shard_map/ppermute | solution.py:283
  136.3 4.2 %shard_map.147 = f32[24,8,32,128]{3,2,1,0:T(8,128)} custom-call(f32[24]{0:T(128)S(1)} %copy-done.10, f32[24,8,32,128]{3,2,1,0:T(8,128)S(1)} %bitcast.14, bf16[24,32,128]{2,1,0:T(8,128)(2,1)S(1)} %collective-permute-done.18.xlo, bf16[24,32,128]{2,1,0:T(8,128)(2,1)S(1)} %collective-permute-done.19.xhi, f32[24,8,128]{2,1,0:T(8,128)} %collective-permute-done.20.ylo, ...), custom_call_target="tpu_custom_call" | custom-call | flops 10000000 | bytes 6291456 | tf_op jit(solution)/shard_map/pallas_call | solution.py:378
  140.4 0.0 all-to-all-done
  140.4 1.5 %shard_map.148 = f32[1,1]{1,0:T(1,128)} custom-call(f32[128,128]{1,0:T(8,128)} %bitcast.9.heats), custom_call_target="tpu_custom_call" | custom-call | tf_op jit(solution)/shard_map/pallas_call | solution.py:389
  (30 shorter events, 0.1 us)
Async XLA Ops:
  0.6 5.6 %copy-start = (f32[24,8,32,128]{3,2,1,0:T(8,128)S(1)}, f32[24,8,32,128]{3,2,1,0:T(8,128)}, u32[]{:S(2)}) copy-start(f32[24,8,32,128]{3,2,1,0:T(8,128)} %refs_1_.3) | copy-start | bytes 9437188
  0.6 5.6 %copy-start.1 = (f32[3,8,32,128]{3,2,1,0:T(8,128)S(1)}, f32[3,8,32,128]{3,2,1,0:T(8,128)}, u32[]{:S(2)}) copy-start(f32[3,8,32,128]{3,2,1,0:T(8,128)} %refs_7_.1) | copy-start | bytes 1179652
  2.7 15.7 %collective-permute-start = (bf16[25,32,128]{2,1,0:T(8,128)(2,1)}, bf16[25,32,128]{2,1,0:T(8,128)(2,1)S(1)}, u32[]{:S(2)}, u32[]{:S(2)}) collective-permute-start(bf16[25,32,128]{2,1,0:T(8,128)(2,1)} %get-tuple-element.51), channel_id=1, source_target_pairs={{0,32},{32,64},{64,96},{96,0},{1,33},{33,65},{65,97},{97,1},{2,34}... | collective-permute-start | bytes 614408 | tf_op jit(solution)/shard_map/ppermute | solution.py:282
  4.8 13.6 %collective-permute-start.1 = (bf16[25,32,128]{2,1,0:T(8,128)(2,1)}, bf16[25,32,128]{2,1,0:T(8,128)(2,1)S(1)}, u32[]{:S(2)}, u32[]{:S(2)}) collective-permute-start(bf16[25,32,128]{2,1,0:T(8,128)(2,1)} %get-tuple-element.52), channel_id=1, source_target_pairs={{32,0},{64,32},{96,64},{0,96},{33,1},{65,33},{97,65},{1,97},{34,2}... | collective-permute-start | bytes 614408 | tf_op jit(solution)/shard_map/ppermute | solution.py:283
  6.7 25.9 %copy-start.14 = (f32[800]{0:T(1024)S(1)}, f32[800]{0:T(1024)}, u32[]{:S(2)}) copy-start(f32[800]{0:T(1024)} %param.19) | copy-start | bytes 9604
  6.8 25.9 %copy-start.13 = (f32[1600]{0:T(1024)S(1)}, f32[1600]{0:T(1024)}, u32[]{:S(2)}) copy-start(f32[1600]{0:T(1024)} %param.17) | copy-start | bytes 19204
  6.8 11.7 %collective-permute-start.2 = (f32[25,8,128]{2,1,0:T(8,128)S(1)}, f32[25,8,128]{2,1,0:T(8,128)S(1)}, u32[]{:S(2)}, u32[]{:S(2)}) collective-permute-start(f32[25,8,128]{2,1,0:T(8,128)S(1)} %get-tuple-element.53), channel_id=1, source_target_pairs={{0,8},{8,16},{16,24},{24,0},{1,9},{9,17},{17,25},{25,1},{2,10},{10... | collective-permute-start | bytes 307208 | tf_op jit(solution)/shard_map/ppermute | solution.py:282
  8.6 9.8 %collective-permute-start.3 = (f32[25,8,128]{2,1,0:T(8,128)S(1)}, f32[25,8,128]{2,1,0:T(8,128)S(1)}, u32[]{:S(2)}, u32[]{:S(2)}) collective-permute-start(f32[25,8,128]{2,1,0:T(8,128)S(1)} %get-tuple-element.54), channel_id=1, source_target_pairs={{8,0},{16,8},{24,16},{0,24},{9,1},{17,9},{25,17},{1,25},{10,2},{18... | collective-permute-start | bytes 307208 | tf_op jit(solution)/shard_map/ppermute | solution.py:283
  10.8 3.7 %collective-permute-start.4 = (f32[25,256]{1,0:T(8,128)S(1)}, f32[25,256]{1,0:T(8,128)S(1)}, u32[]{:S(2)}, u32[]{:S(2)}) collective-permute-start(f32[25,256]{1,0:T(8,128)S(1)} %get-tuple-element.55), channel_id=1, source_target_pairs={{0,1},{1,2},{2,3},{3,4},{4,5},{5,6},{6,7},{7,0},{8,9},{9,10},{10,1... | collective-permute-start | bytes 76808 | tf_op jit(solution)/shard_map/ppermute | solution.py:282
  14.5 3.9 %collective-permute-start.5 = (f32[25,256]{1,0:T(8,128)S(1)}, f32[25,256]{1,0:T(8,128)S(1)}, u32[]{:S(2)}, u32[]{:S(2)}) collective-permute-start(f32[25,256]{1,0:T(8,128)S(1)} %get-tuple-element.56), channel_id=1, source_target_pairs={{1,0},{2,1},{3,2},{4,3},{5,4},{6,5},{7,6},{0,7},{9,8},{10,9},{11,1... | collective-permute-start | bytes 76808 | tf_op jit(solution)/shard_map/ppermute | solution.py:283
  21.6 11.8 %collective-permute-start.6 = (bf16[24,32,128]{2,1,0:T(8,128)(2,1)S(1)}, bf16[24,32,128]{2,1,0:T(8,128)(2,1)S(1)}, u32[]{:S(2)}, u32[]{:S(2)}) collective-permute-start(bf16[24,32,128]{2,1,0:T(8,128)(2,1)S(1)} %get-tuple-element.59), channel_id=1, source_target_pairs={{0,32},{32,64},{64,96},{96,0},{1,33},{33,65},{65,97},{97,1},{2,34}... | collective-permute-start | bytes 589832 | tf_op jit(solution)/shard_map/ppermute | solution.py:282
  21.6 11.8 %collective-permute-start.7 = (bf16[24,32,128]{2,1,0:T(8,128)(2,1)S(1)}, bf16[24,32,128]{2,1,0:T(8,128)(2,1)S(1)}, u32[]{:S(2)}, u32[]{:S(2)}) collective-permute-start(bf16[24,32,128]{2,1,0:T(8,128)(2,1)S(1)} %get-tuple-element.60), channel_id=1, source_target_pairs={{32,0},{64,32},{96,64},{0,96},{33,1},{65,33},{97,65},{1,97},{34,2}... | collective-permute-start | bytes 589832 | tf_op jit(solution)/shard_map/ppermute | solution.py:283
  24.3 9.1 %collective-permute-start.8 = (f32[24,8,128]{2,1,0:T(8,128)S(1)}, f32[24,8,128]{2,1,0:T(8,128)S(1)}, u32[]{:S(2)}, u32[]{:S(2)}) collective-permute-start(f32[24,8,128]{2,1,0:T(8,128)S(1)} %get-tuple-element.61), channel_id=1, source_target_pairs={{0,8},{8,16},{16,24},{24,0},{1,9},{9,17},{17,25},{25,1},{2,10},{10... | collective-permute-start | bytes 294920 | tf_op jit(solution)/shard_map/ppermute | solution.py:282
  24.3 9.1 %collective-permute-start.9 = (f32[24,8,128]{2,1,0:T(8,128)S(1)}, f32[24,8,128]{2,1,0:T(8,128)S(1)}, u32[]{:S(2)}, u32[]{:S(2)}) collective-permute-start(f32[24,8,128]{2,1,0:T(8,128)S(1)} %get-tuple-element.62), channel_id=1, source_target_pairs={{8,0},{16,8},{24,16},{0,24},{9,1},{17,9},{25,17},{1,25},{10,2},{18... | collective-permute-start | bytes 294920 | tf_op jit(solution)/shard_map/ppermute | solution.py:283
  27.0 2.1 %collective-permute-start.10 = (f32[24,256]{1,0:T(8,128)S(1)}, f32[24,256]{1,0:T(8,128)S(1)}, u32[]{:S(2)}, u32[]{:S(2)}) collective-permute-start(f32[24,256]{1,0:T(8,128)S(1)} %get-tuple-element.63), channel_id=1, source_target_pairs={{0,1},{1,2},{2,3},{3,4},{4,5},{5,6},{6,7},{7,0},{8,9},{9,10},{10,1... | collective-permute-start | bytes 73736 | tf_op jit(solution)/shard_map/ppermute | solution.py:282
  29.1 4.4 %collective-permute-start.11 = (f32[24,256]{1,0:T(8,128)S(1)}, f32[24,256]{1,0:T(8,128)S(1)}, u32[]{:S(2)}, u32[]{:S(2)}) collective-permute-start(f32[24,256]{1,0:T(8,128)S(1)} %get-tuple-element.64), channel_id=1, source_target_pairs={{1,0},{2,1},{3,2},{4,3},{5,4},{6,5},{7,6},{0,7},{9,8},{10,9},{11,1... | collective-permute-start | bytes 73736 | tf_op jit(solution)/shard_map/ppermute | solution.py:283
  33.5 9.8 %copy-start.15 = (s32[1,96]{1,0:T(1,128)S(1)}, s32[1,96]{1,0:T(1,128)}, u32[]{:S(2)}) copy-start(s32[1,96]{1,0:T(1,128)} %param.25) | copy-start | bytes 1156
  33.5 9.8 %copy-start.2 = (bf16[1600,800]{0,1:T(8,128)(2,1)S(1)}, bf16[1600,800]{0,1:T(8,128)(2,1)}, u32[]{:S(2)}) copy-start(bf16[1600,800]{0,1:T(8,128)(2,1)} %param.18) | copy-start | bytes 7680004
  33.5 9.8 %copy-start.3 = (bf16[800,400]{0,1:T(8,128)(2,1)S(1)}, bf16[800,400]{0,1:T(8,128)(2,1)}, u32[]{:S(2)}) copy-start(bf16[800,400]{0,1:T(8,128)(2,1)} %param.20) | copy-start | bytes 1920004
  33.5 9.8 %copy-start.4 = (bf16[24,1600]{1,0:T(8,128)(2,1)S(1)}, bf16[24,1600]{1,0:T(8,128)(2,1)}, u32[]{:S(2)}) copy-start(bf16[24,1600]{1,0:T(8,128)(2,1)} %w_in) | copy-start | bytes 230404
  33.5 9.8 %copy-start.7 = (f32[400]{0:T(512)S(1)}, f32[400]{0:T(512)}, u32[]{:S(2)}) copy-start(f32[400]{0:T(512)} %param.21) | copy-start | bytes 4804
  33.5 9.8 %copy-start.8 = (f32[24]{0:T(128)S(1)}, f32[24]{0:T(128)}, u32[]{:S(2)}) copy-start(f32[24]{0:T(128)} %param.23) | copy-start | bytes 292
  37.2 3.4 %collective-permute-start.16 = (f32[24,256]{1,0:T(8,128)S(1)}, f32[24,256]{1,0:T(8,128)S(1)}, u32[]{:S(2)}, u32[]{:S(2)}) collective-permute-start(f32[24,256]{1,0:T(8,128)S(1)} %get-tuple-element.71), channel_id=1, source_target_pairs={{0,1},{1,2},{2,3},{3,4},{4,5},{5,6},{6,7},{7,0},{8,9},{9,10},{10,1... | collective-permute-start | bytes 73736 | tf_op jit(solution)/shard_map/ppermute | solution.py:282
  37.2 7.6 %collective-permute-start.17 = (f32[24,256]{1,0:T(8,128)S(1)}, f32[24,256]{1,0:T(8,128)S(1)}, u32[]{:S(2)}, u32[]{:S(2)}) collective-permute-start(f32[24,256]{1,0:T(8,128)S(1)} %get-tuple-element.72), channel_id=1, source_target_pairs={{1,0},{2,1},{3,2},{4,3},{5,4},{6,5},{7,6},{0,7},{9,8},{10,9},{11,1... | collective-permute-start | bytes 73736 | tf_op jit(solution)/shard_map/ppermute | solution.py:283
  37.9 6.9 %collective-permute-start.14 = (f32[24,8,128]{2,1,0:T(8,128)S(1)}, f32[24,8,128]{2,1,0:T(8,128)S(1)}, u32[]{:S(2)}, u32[]{:S(2)}) collective-permute-start(f32[24,8,128]{2,1,0:T(8,128)S(1)} %get-tuple-element.69), channel_id=1, source_target_pairs={{0,8},{8,16},{16,24},{24,0},{1,9},{9,17},{17,25},{25,1},{2,10},{10... | collective-permute-start | bytes 294920 | tf_op jit(solution)/shard_map/ppermute | solution.py:282
  37.9 6.9 %collective-permute-start.15 = (f32[24,8,128]{2,1,0:T(8,128)S(1)}, f32[24,8,128]{2,1,0:T(8,128)S(1)}, u32[]{:S(2)}, u32[]{:S(2)}) collective-permute-start(f32[24,8,128]{2,1,0:T(8,128)S(1)} %get-tuple-element.70), channel_id=1, source_target_pairs={{8,0},{16,8},{24,16},{0,24},{9,1},{17,9},{25,17},{1,25},{10,2},{18... | collective-permute-start | bytes 294920 | tf_op jit(solution)/shard_map/ppermute | solution.py:283
  40.6 5.7 %collective-permute-start.12 = (bf16[24,32,128]{2,1,0:T(8,128)(2,1)S(1)}, bf16[24,32,128]{2,1,0:T(8,128)(2,1)S(1)}, u32[]{:S(2)}, u32[]{:S(2)}) collective-permute-start(bf16[24,32,128]{2,1,0:T(8,128)(2,1)S(1)} %get-tuple-element.67), channel_id=1, source_target_pairs={{0,32},{32,64},{64,96},{96,0},{1,33},{33,65},{65,97},{97,1},{2,34}... | collective-permute-start | bytes 589832 | tf_op jit(solution)/shard_map/ppermute | solution.py:282
  40.6 5.7 %collective-permute-start.13 = (bf16[24,32,128]{2,1,0:T(8,128)(2,1)S(1)}, bf16[24,32,128]{2,1,0:T(8,128)(2,1)S(1)}, u32[]{:S(2)}, u32[]{:S(2)}) collective-permute-start(bf16[24,32,128]{2,1,0:T(8,128)(2,1)S(1)} %get-tuple-element.68), channel_id=1, source_target_pairs={{32,0},{64,32},{96,64},{0,96},{33,1},{65,33},{97,65},{1,97},{34,2}... | collective-permute-start | bytes 589832 | tf_op jit(solution)/shard_map/ppermute | solution.py:283
  46.3 3.5 %copy-start.6 = (bf16[400,24]{0,1:T(8,128)(2,1)S(1)}, bf16[400,24]{0,1:T(8,128)(2,1)}, u32[]{:S(2)}) copy-start(bf16[400,24]{0,1:T(8,128)(2,1)} %param.22) | copy-start | bytes 57604
  46.3 3.5 %copy-start.9 = (s32[1,96]{1,0:T(1,128)S(1)}, s32[1,96]{1,0:T(1,128)}, u32[]{:S(2)}) copy-start(s32[1,96]{1,0:T(1,128)} %listed.1) | copy-start | bytes 1156
  49.9 86.4 %copy-start.10 = (f32[24]{0:T(128)S(1)}, f32[24]{0:T(128)}, u32[]{:S(2)}) copy-start(f32[24]{0:T(128)} %rates.1) | copy-start | bytes 292
  63.1 0.6 copy-start.5
  63.7 0.6 copy-start.11
  64.3 0.6 copy-start.12
  64.9 65.7 %collective-permute-start.18 = (bf16[24,32,128]{2,1,0:T(8,128)(2,1)}, bf16[24,32,128]{2,1,0:T(8,128)(2,1)S(1)}, u32[]{:S(2)}, u32[]{:S(2)}) collective-permute-start(bf16[24,32,128]{2,1,0:T(8,128)(2,1)} %get-tuple-element.90), channel_id=1, source_target_pairs={{0,32},{32,64},{64,96},{96,0},{1,33},{33,65},{65,97},{97,1},{2,34}... | collective-permute-start | bytes 589832 | tf_op jit(solution)/shard_map/ppermute | solution.py:282
  64.9 65.7 %collective-permute-start.19 = (bf16[24,32,128]{2,1,0:T(8,128)(2,1)}, bf16[24,32,128]{2,1,0:T(8,128)(2,1)S(1)}, u32[]{:S(2)}, u32[]{:S(2)}) collective-permute-start(bf16[24,32,128]{2,1,0:T(8,128)(2,1)} %get-tuple-element.91), channel_id=1, source_target_pairs={{32,0},{64,32},{96,64},{0,96},{33,1},{65,33},{97,65},{1,97},{34,2}... | collective-permute-start | bytes 589832 | tf_op jit(solution)/shard_map/ppermute | solution.py:283
  67.6 64.8 %collective-permute-start.20 = (f32[24,8,128]{2,1,0:T(8,128)}, f32[24,8,128]{2,1,0:T(8,128)}, u32[]{:S(2)}, u32[]{:S(2)}) collective-permute-start(f32[24,8,128]{2,1,0:T(8,128)} %get-tuple-element.94), channel_id=1, source_target_pairs={{0,8},{8,16},{16,24},{24,0},{1,9},{9,17},{17,25},{25,1},{2,10},{10... | collective-permute-start | bytes 294920 | tf_op jit(solution)/shard_map/ppermute | solution.py:282
  72.8 59.6 %collective-permute-start.21 = (f32[24,8,128]{2,1,0:T(8,128)}, f32[24,8,128]{2,1,0:T(8,128)}, u32[]{:S(2)}, u32[]{:S(2)}) collective-permute-start(f32[24,8,128]{2,1,0:T(8,128)} %get-tuple-element.95), channel_id=1, source_target_pairs={{8,0},{16,8},{24,16},{0,24},{9,1},{17,9},{25,17},{1,25},{10,2},{18... | collective-permute-start | bytes 294920 | tf_op jit(solution)/shard_map/ppermute | solution.py:283
  118.2 22.3 %all-to-all-start = ((f32[128,1,128]{2,1,0:T(1,128)}), f32[128,1,128]{2,1,0:T(1,128)}, u32[]{:S(2)}, u32[]{:S(2)}) async-start(f32[128,1,128]{2,1,0:T(1,128)} %bitcast.17), calls=%async_computation | async-start | bytes 131072 | tf_op jit(solution)/shard_map/all_to_all | solution.py:299
  130.7 2.9 %collective-permute-start.22 = (f32[24,256]{1,0:T(8,128)}, f32[24,256]{1,0:T(8,128)S(1)}, u32[]{:S(2)}, u32[]{:S(2)}) collective-permute-start(f32[24,256]{1,0:T(8,128)} %copy-done.12), channel_id=1, source_target_pairs={{0,1},{1,2},{2,3},{3,4},{4,5},{5,6},{6,7},{7,0},{8,9},{9,10},{10,1... | collective-permute-start | bytes 73736 | tf_op jit(solution)/shard_map/ppermute | solution.py:282
  132.4 3.9 %collective-permute-start.23 = (f32[24,256]{1,0:T(8,128)}, f32[24,256]{1,0:T(8,128)S(1)}, u32[]{:S(2)}, u32[]{:S(2)}) collective-permute-start(f32[24,256]{1,0:T(8,128)} %copy-done.11), channel_id=1, source_target_pairs={{1,0},{2,1},{3,2},{4,3},{5,4},{6,5},{7,6},{0,7},{9,8},{10,9},{11,1... | collective-permute-start | bytes 73736 | tf_op jit(solution)/shard_map/ppermute | solution.py:283
